TPU v7x, 32 devices: a whole 2x2x4 slice. The times are simulated.
32 devices in a mesh: dp: 8 (over y, x, core), mp: 4 (over z).
Axes of the slice: x: 2, y: 2, z: 4, core: 2. Of those that a mesh axis runs over, the one named last changes fastest.
Arguments:
- tokens: bfloat16 [10240, 1024], P('dp'), may hold values from -6 to 6
- text_states: bfloat16 [40, 128, 1024], P('dp'), may hold values from -6 to 6
- lengths: int32 [40], P('dp'), may hold values from 0 to 1024, as said below
- text_mask: int32 [40, 128], P('dp'), may hold values 0 or 1
- ln_gain: float32 [3, 1024], replicated, may hold values from 0.5 to 1.5
- ln_shift: float32 [3, 1024], replicated, may hold values from -2.5 to 2.5
- w_qkv: bfloat16 [1024, 3, 1024], P(None, None, 'mp'), may hold values from -0.1875 to 0.1875
- w_out: bfloat16 [1024, 1024], P('mp'), may hold values from -1 to 1
- w_cross_q: bfloat16 [1024, 1024], P(None, 'mp'), may hold values from -0.1875 to 0.1875
- w_cross_kv: bfloat16 [1024, 2, 1024], P(None, None, 'mp'), may hold values from -0.1875 to 0.1875
- w_cross_out: bfloat16 [1024, 1024], P('mp'), may hold values from -1 to 1
- w_up: bfloat16 [1024, 4096], P(None, 'mp'), may hold values from -0.1875 to 0.1875
- w_down: bfloat16 [4096, 1024], P('mp'), may hold values from -0.09375 to 0.09375
- cotangent: bfloat16 [10240, 1024], P('dp'), may hold values from -6 to 6
Outputs:
- output: bfloat16 [10240, 1024], P('dp')
- grad_tokens: float32 [10240, 1024], P('dp')
- grad_text: float32 [40, 128, 1024], P('dp')
- grad_gain: float32 [3, 1024], P(None, 'dp')
- grad_shift: float32 [3, 1024], P(None, 'dp')
- grad_qkv: float32 [1024, 3, 1024], P('dp', None, 'mp')
- grad_out: float32 [1024, 1024], P(('mp', 'dp'))
- grad_cross_q: float32 [1024, 1024], P('dp', 'mp')
- grad_cross_kv: float32 [1024, 2, 1024], P('dp', None, 'mp')
- grad_cross_out: float32 [1024, 1024], P(('mp', 'dp'))
- grad_up: float32 [1024, 4096], P('dp', 'mp')
- grad_down: float32 [4096, 1024], P(('mp', 'dp'))
Inputs may be any that keep to these rules, and one draw needn't show every extreme that they name: `lengths`: each group of 5 entries (the slots of one index of dp) holds items of 256 or 1024 tokens followed by zeros, at most one of 1024, and sums to 1280.
All inputs are finite; a program needn't handle non-finite values. No bound on the sum of `text_mask` on one device may be relied on, other than what follows from the above.
Results may differ from a plain program's by a relative error of at most 0.019.
Values sent between devices are 32-bit elements; how exact they have to be, the bound alone decides.
No kernel may reach another device: no remote copies, remote signals or barrier semaphores. Data moves between devices by JAX's collectives and lax.ppermute only.
A program may use at most 192 MiB of HBM per device.

v0:
```python
from functools import partial

import jax
import jax.numpy as jnp
from jax import lax
from jax.sharding import PartitionSpec as P

HEAD = 64
QBLK = 640


epsilon = 1e-05
masked_score = -1e30


def norm_forward(value, gain, shift):
    center = value - jnp.mean(value, axis=-1, keepdims=True)
    spread = jnp.mean(center * center, axis=-1, keepdims=True)
    inverse = lax.rsqrt(spread + epsilon)
    unit_rows = center * inverse
    return ((unit_rows * gain + shift).astype(jnp.bfloat16), unit_rows, inverse)


def norm_backward(incoming, unit_rows, inverse, gain):
    scaled = incoming * gain
    inner = (
        scaled
        - jnp.mean(scaled, axis=-1, keepdims=True)
        - unit_rows * jnp.mean(scaled * unit_rows, axis=-1, keepdims=True)
    )
    return (inner * inverse, jnp.sum(incoming * unit_rows, axis=0), jnp.sum(incoming, axis=0))


def block_scores(query_part, key_set, allowed_part, scale):
    scores = (
        jnp.einsum("qhe,khe->hqk", query_part, key_set, preferred_element_type=jnp.float32) * scale
    )
    return jnp.where(allowed_part[None], scores, masked_score)


def attend_forward(query, key_set, value_set, allowed):
    row_count, head_count, head_size = query.shape
    width = QBLK
    scale = head_size ** (-0.5)

    def one_block(index):
        start = index * width
        query_part = lax.dynamic_slice_in_dim(query, start, width, 0)
        scores = block_scores(query_part, key_set, allowed(start, width), scale)
        peak = jnp.max(scores, axis=-1, keepdims=True)
        weights = jnp.exp(scores - peak)
        weight_total = jnp.sum(weights, axis=-1, keepdims=True)
        chances = (weights / weight_total).astype(jnp.bfloat16)
        result = jnp.einsum("hqk,khe->qhe", chances, value_set, preferred_element_type=jnp.float32)
        return (result.astype(jnp.bfloat16), (peak + jnp.log(weight_total))[:, :, 0])

    results, log_totals = lax.map(one_block, jnp.arange(row_count // width))
    return (results.reshape(row_count, head_count, head_size), log_totals)


def attend_backward(query, key_set, value_set, allowed, log_totals, out_grad):
    row_count, head_count, head_size = query.shape
    width = QBLK
    scale = head_size ** (-0.5)

    def one_block(carry, index):
        key_grad, value_grad = carry
        start = index * width
        query_part = lax.dynamic_slice_in_dim(query, start, width, 0)
        grad_part = lax.dynamic_slice_in_dim(out_grad, start, width, 0)
        scores = block_scores(query_part, key_set, allowed(start, width), scale)
        chances = jnp.exp(scores - log_totals[index][:, :, None])
        pushed = jnp.einsum(
            "qhe,khe->hqk", grad_part, value_set, preferred_element_type=jnp.float32
        )
        score_grad = (
            chances * (pushed - jnp.sum(chances * pushed, axis=-1, keepdims=True))
        ).astype(jnp.bfloat16)
        query_grad = (
            jnp.einsum("hqk,khe->qhe", score_grad, key_set, preferred_element_type=jnp.float32)
            * scale
        )
        key_grad = (
            key_grad
            + jnp.einsum("hqk,qhe->khe", score_grad, query_part, preferred_element_type=jnp.float32)
            * scale
        )
        value_grad = value_grad + jnp.einsum(
            "hqk,qhe->khe",
            chances.astype(jnp.bfloat16),
            grad_part,
            preferred_element_type=jnp.float32,
        )
        return ((key_grad, value_grad), query_grad)

    zero_keys = jnp.zeros(key_set.shape, jnp.float32)
    (key_grad, value_grad), query_grads = lax.scan(
        one_block, (zero_keys, zero_keys), jnp.arange(row_count // width)
    )
    return (query_grads.reshape(row_count, head_count, head_size), key_grad, value_grad)


def local(
    tokens,
    text_states,
    lengths,
    text_mask,
    ln_gain,
    ln_shift,
    w_qkv,
    w_out,
    w_cross_q,
    w_cross_kv,
    w_cross_out,
    w_up,
    w_down,
    cotangent,
):
    row_count = tokens.shape[0]
    local_width = w_out.shape[0]
    local_heads = local_width // HEAD
    slot_count = lengths.shape[0]
    text_length = text_mask.shape[1]
    places = jnp.arange(row_count, dtype=jnp.int32)
    item_ends = jnp.cumsum(lengths)
    item_of = jnp.sum((places[:, None] >= item_ends[None, :]).astype(jnp.int32), axis=1)
    text_places = jnp.arange(slot_count * text_length, dtype=jnp.int32)
    text_owner = text_places // text_length
    live_key = (text_mask.reshape(-1) == 1) | (text_places % text_length == 0)

    def self_allowed(start, width):
        rows_here = lax.dynamic_slice_in_dim(places, start, width)
        items_here = lax.dynamic_slice_in_dim(item_of, start, width)
        return (items_here[:, None] == item_of[None, :]) & (places[None, :] <= rows_here[:, None])

    def cross_allowed(start, width):
        items_here = lax.dynamic_slice_in_dim(item_of, start, width)
        return (items_here[:, None] == text_owner[None, :]) & live_key[None, :]

    def split_heads(value):
        return value.reshape(value.shape[0], local_heads, HEAD)

    residual = tokens.astype(jnp.float32)
    normed_first, first_unit, first_inverse = norm_forward(residual, ln_gain[0], ln_shift[0])
    triple = jnp.einsum(
        "rd,dtc->rtc", normed_first, w_qkv, preferred_element_type=jnp.float32
    ).astype(jnp.bfloat16)
    self_query = split_heads(triple[:, 0])
    self_key = split_heads(triple[:, 1])
    self_value = split_heads(triple[:, 2])
    mixed, self_logs = attend_forward(self_query, self_key, self_value, self_allowed)
    mixed_flat = mixed.reshape(row_count, local_width)
    after_self = residual + lax.psum(
        jnp.dot(mixed_flat, w_out, preferred_element_type=jnp.float32), "mp"
    )
    normed_second, second_unit, second_inverse = norm_forward(after_self, ln_gain[1], ln_shift[1])
    cross_query = jnp.dot(normed_second, w_cross_q, preferred_element_type=jnp.float32).astype(
        jnp.bfloat16
    )
    text_flat = text_states.reshape(slot_count * text_length, text_states.shape[2])
    text_pair = jnp.einsum(
        "sd,dtc->stc", text_flat, w_cross_kv, preferred_element_type=jnp.float32
    ).astype(jnp.bfloat16)
    cross_key = split_heads(text_pair[:, 0])
    cross_value = split_heads(text_pair[:, 1])
    looked, cross_logs = attend_forward(
        split_heads(cross_query), cross_key, cross_value, cross_allowed
    )
    looked_flat = looked.reshape(row_count, local_width)
    after_cross = after_self + lax.psum(
        jnp.dot(looked_flat, w_cross_out, preferred_element_type=jnp.float32), "mp"
    )
    normed_third, third_unit, third_inverse = norm_forward(after_cross, ln_gain[2], ln_shift[2])
    pre_act = jnp.dot(normed_third, w_up, preferred_element_type=jnp.float32)
    activated, gelu_pull = jax.vjp(partial(jax.nn.gelu, approximate=True), pre_act)
    hidden = activated.astype(jnp.bfloat16)
    result = after_cross + lax.psum(
        jnp.dot(hidden, w_down, preferred_element_type=jnp.float32), "mp"
    )
    upstream = cotangent.astype(jnp.float32)
    upstream_low = cotangent
    down_grad = jnp.einsum("rf,rd->fd", hidden, upstream_low, preferred_element_type=jnp.float32)
    hidden_grad = jnp.einsum("rd,fd->rf", upstream_low, w_down, preferred_element_type=jnp.float32)
    pre_grad = gelu_pull(hidden_grad)[0].astype(jnp.bfloat16)
    up_grad = jnp.einsum("rd,rf->df", normed_third, pre_grad, preferred_element_type=jnp.float32)
    third_part = jnp.einsum("rf,df->rd", pre_grad, w_up, preferred_element_type=jnp.float32)
    third_grad = lax.psum(third_part, "mp")
    back_third, gain_third, shift_third = norm_backward(
        third_grad, third_unit, third_inverse, ln_gain[2]
    )
    upstream = upstream + back_third
    upstream_low = upstream.astype(jnp.bfloat16)
    cross_out_grad = jnp.einsum(
        "rc,rd->cd", looked_flat, upstream_low, preferred_element_type=jnp.float32
    )
    looked_grad = jnp.einsum(
        "rd,cd->rc", upstream_low, w_cross_out, preferred_element_type=jnp.float32
    ).astype(jnp.bfloat16)
    query_grad, key_grad, value_grad = attend_backward(
        split_heads(cross_query),
        cross_key,
        cross_value,
        cross_allowed,
        cross_logs,
        split_heads(looked_grad),
    )
    query_low = query_grad.reshape(row_count, local_width).astype(jnp.bfloat16)
    pair_grad = jnp.stack(
        [key_grad.reshape(-1, local_width), value_grad.reshape(-1, local_width)], axis=1
    ).astype(jnp.bfloat16)
    cross_q_grad = jnp.einsum(
        "rd,rc->dc", normed_second, query_low, preferred_element_type=jnp.float32
    )
    cross_kv_grad = jnp.einsum(
        "sd,stc->dtc", text_flat, pair_grad, preferred_element_type=jnp.float32
    )
    second_part = jnp.einsum("rc,dc->rd", query_low, w_cross_q, preferred_element_type=jnp.float32)
    text_part = jnp.einsum("stc,dtc->sd", pair_grad, w_cross_kv, preferred_element_type=jnp.float32)
    second_grad, text_grad = lax.psum((second_part, text_part), "mp")
    back_second, gain_second, shift_second = norm_backward(
        second_grad, second_unit, second_inverse, ln_gain[1]
    )
    upstream = upstream + back_second
    upstream_low = upstream.astype(jnp.bfloat16)
    out_grad = jnp.einsum("rc,rd->cd", mixed_flat, upstream_low, preferred_element_type=jnp.float32)
    mixed_grad = jnp.einsum(
        "rd,cd->rc", upstream_low, w_out, preferred_element_type=jnp.float32
    ).astype(jnp.bfloat16)
    query_grad, key_grad, value_grad = attend_backward(
        self_query, self_key, self_value, self_allowed, self_logs, split_heads(mixed_grad)
    )
    triple_grad = jnp.stack(
        [
            query_grad.reshape(row_count, local_width),
            key_grad.reshape(row_count, local_width),
            value_grad.reshape(row_count, local_width),
        ],
        axis=1,
    ).astype(jnp.bfloat16)
    qkv_grad = jnp.einsum(
        "rd,rtc->dtc", normed_first, triple_grad, preferred_element_type=jnp.float32
    )
    first_part = jnp.einsum("rtc,dtc->rd", triple_grad, w_qkv, preferred_element_type=jnp.float32)
    first_grad = lax.psum(first_part, "mp")
    back_first, gain_first, shift_first = norm_backward(
        first_grad, first_unit, first_inverse, ln_gain[0]
    )
    token_grad = upstream + back_first
    gain_grad = jnp.stack([gain_first, gain_second, gain_third])
    shift_grad = jnp.stack([shift_first, shift_second, shift_third])
    (
        gain_total,
        shift_total,
        qkv_total,
        out_total,
        cross_q_total,
        cross_kv_total,
        cross_out_total,
        up_total,
        down_total,
    ) = (
        lax.psum_scatter(gain_grad, "dp", scatter_dimension=1, tiled=True),
        lax.psum_scatter(shift_grad, "dp", scatter_dimension=1, tiled=True),
        lax.psum_scatter(qkv_grad, "dp", scatter_dimension=0, tiled=True),
        lax.psum_scatter(out_grad, "dp", scatter_dimension=0, tiled=True),
        lax.psum_scatter(cross_q_grad, "dp", scatter_dimension=0, tiled=True),
        lax.psum_scatter(cross_kv_grad, "dp", scatter_dimension=0, tiled=True),
        lax.psum_scatter(cross_out_grad, "dp", scatter_dimension=0, tiled=True),
        lax.psum_scatter(up_grad, "dp", scatter_dimension=0, tiled=True),
        lax.psum_scatter(down_grad, "dp", scatter_dimension=0, tiled=True),
    )
    return (
        result.astype(jnp.bfloat16),
        token_grad,
        text_grad.reshape(slot_count, text_length, text_states.shape[2]),
        gain_total,
        shift_total,
        qkv_total,
        out_total,
        cross_q_total,
        cross_kv_total,
        cross_out_total,
        up_total,
        down_total,
    )


def solution(mesh):
    placed = (
        P("dp", None),
        P("dp", None, None),
        P("dp"),
        P("dp", None),
        P(),
        P(),
        P(None, None, "mp"),
        P("mp", None),
        P(None, "mp"),
        P(None, None, "mp"),
        P("mp", None),
        P(None, "mp"),
        P("mp", None),
        P("dp", None),
    )
    return jax.shard_map(
        local,
        mesh=mesh,
        in_specs=placed,
        out_specs=(
            P("dp", None),
            P("dp", None),
            P("dp", None, None),
            P(None, "dp"),
            P(None, "dp"),
            P("dp", None, "mp"),
            P(("mp", "dp"), None),
            P("dp", "mp"),
            P("dp", None, "mp"),
            P(("mp", "dp"), None),
            P("dp", "mp"),
            P(("mp", "dp"), None),
        ),
        check_vma=False,
    )
```

profile of v0, /device:TPU:0, one launch (start us, length us, event | category | flops | bytes accessed | tf_op | source)
XLA Modules:
  0.0 1886.1 jit_solution(1155321429784555472)
XLA Ops:
  19.7 54.3 %while.57 = (s32[]{:T(128)}, bf16[2,640,4,64]{1,3,2,0:T(8,128)(2,1)}, f32[2,4,640]{2,1,0:T(4,128)S(1)}, s32[2]{0:T(128)S(1)}, s32[1280]{0:T(1024)S(1)}, /*index=...) while((s32[]{:T(128)}, ...), condition=%wide.region_7.8_spmd.clone, body=%wide.region_4.7_spmd.clone.sunk | while | flops 880801280 | bytes 49915144 | solution.py:57
  22.0 8.3 fusion.216
  30.3 8.5 fusion.217
  38.8 7.2 fusion.218
  49.0 8.3 fusion.216
  57.3 8.5 fusion.217
  65.9 7.2 fusion.218
  77.1 4.3 fusion.132
  85.1 188.2 %all-reduce.7.cloned.1.call-done = f32[1280,1024]{1,0:T(8,128)} async-done(((f32[1280,1024]{1,0:T(8,128)}), f32[1280,1024]{1,0:T(8,128)}) %all-reduce.7.cloned.1.call-update) | async-done | bytes 5242896 | tf_op jit(solution)/shard_map/psum | solution.py:153
  282.0 14.9 while.58
  303.9 7.6 fusion.134
  311.5 180.3 %all-reduce.9.cloned.1.call-done = f32[1280,1024]{1,0:T(8,128)} async-done(((f32[1280,1024]{1,0:T(8,128)}), f32[1280,1024]{1,0:T(8,128)}) %all-reduce.9.cloned.1.call-update) | async-done | bytes 5242896 | tf_op jit(solution)/shard_map/psum | solution.py:170
  491.9 4.7 fusion.126
  501.0 8.0 fusion.99
  510.4 4.7 fusion.135
  515.4 187.8 %all-reduce.11.cloned.1.call-done = f32[1280,1024]{1,0:T(8,128)} async-done(((f32[1280,1024]{1,0:T(8,128)}), f32[1280,1024]{1,0:T(8,128)}) %all-reduce.11.cloned.1.call-update) | async-done | bytes 5242896 | tf_op jit(solution)/shard_map/psum | solution.py:187
  703.3 5.9 multiply_reduce_fusion.2
  717.6 27.3 %while.59 = (s32[]{:T(128)}, f32[640,4,64]{0,2,1:T(8,128)S(1)}, f32[640,4,64]{0,2,1:T(8,128)}, bf16[2,640,4,64]{1,3,2,0:T(8,128)(2,1)}, s32[2]{0:T(128)S(1)}, /*...) while((s32[]{:T(128)}, f32[640,4,64]{0,2,1:T(8,128)S(1)}, ...), condition=%wide.region_24.25_spmd.clone, body=%wide.region_22.24_spmd.clone.sunk | while | flops 1074956800 | bytes 66932244 | solution.py:97
  746.8 4.5 fusion.136
  751.8 8.8 fusion.123
  764.9 174.5 %all-reduce.13.cloned.1.call-done = f32[1280,1024]{1,0:T(8,128)} async-done(((f32[1280,1024]{1,0:T(8,128)}), f32[1280,1024]{1,0:T(8,128)}) %all-reduce.13.cloned.1.call-update) | async-done | bytes 5242896 | tf_op jit(solution)/shard_map/psum | solution.py:219
  939.4 6.0 multiply_reduce_fusion.3
  945.4 5.1 multiply_add_fusion
  955.5 64.2 %while.60 = (s32[]{:T(128)}, f32[1280,4,64]{0,2,1:T(8,128)}, f32[1280,4,64]{0,2,1:T(8,128)}, bf16[2,640,4,64]{1,3,2,0:T(8,128)(2,1)}, s32[2]{0:T(128)S(1)}, /*in...) while((s32[]{:T(128)}, f32[1280,4,64]{0,2,1:T(8,128)}, ...), condition=%wide.region_30.31_spmd.clone.clone, body=%wide.region_28.30_spmd.clone.clone.sunk | while | flops 2130900480 | bytes 138030576 | solution.py:97
  962.4 8.0 multiply_reduce_fusion.14
  970.5 6.3 multiply_convert_fusion.8
  976.8 6.2 fusion.248
  994.6 8.0 multiply_reduce_fusion.14
  1002.6 6.3 multiply_convert_fusion.8
  1008.9 6.2 fusion.248
  1026.4 6.2 convolution_bitcast_fusion
  1036.6 439.6 %all-reduce.15.cloned.1.call-done = (f32[1280,1024]{1,0:T(8,128)}, f32[1280,1024]{1,0:T(8,128)}, f32[5,128,1024]{2,1,0:T(8,128)}) async-done(((f32[1280,1024]{1,0:T(8,128)}, f32[1280,1024]{1,0:T(8,128)}, f32[5,128,1024]{2,1,0:T(8,128)}), (f32[1280,1024]{1,0:T(8,128)}, f32[1280,1024]{1,0:T(8,128)}, f32[5,128,1024]{2,1,0:T(8,128)})) %all-reduce.15.cloned.1.call-update) | async-done | bytes 13107216 | tf_op jit(solution)/shard_map/psum | solution.py:177
  1476.2 4.5 fusion.91
  1483.0 8.8 fusion.124
  1491.9 8.8 fusion.122
  1501.1 4.3 fusion.104
  1509.3 4.4 fusion.101
  1513.7 6.0 fusion.110
  1521.6 6.6 add_convert_fusion
  1528.3 5.4 fusion.90
  1533.7 23.3 %reduce-scatter.30.cloned.1.call-done = f32[128,3]{1,0:T(8,128)} async-done(((f32[1024,3]{1,0:T(8,128)}), f32[128,3]{1,0:T(8,128)}) %reduce-scatter.30.cloned.1.call-update) | async-done | bytes 1552
  1558.5 35.7 %reduce-scatter.28.cloned.1.call-done = f32[128,3]{1,0:T(8,128)} async-done(((f32[1024,3]{1,0:T(8,128)}), f32[128,3]{1,0:T(8,128)}) %reduce-scatter.28.cloned.1.call-update) | async-done | bytes 1552
  1595.8 54.2 %reduce-scatter.24.cloned.1.call-done = f32[128,1024]{1,0:T(8,128)} async-done(((f32[1024,1024]{1,0:T(8,128)}), f32[128,1024]{1,0:T(8,128)}) %reduce-scatter.24.cloned.1.call-update) | async-done | bytes 524304 | tf_op jit(solution)/shard_map/reduce_scatter | solution.py:269
  1649.9 55.1 %reduce-scatter.26.cloned.1.call-done = f32[128,1024]{1,0:T(8,128)} async-done(((f32[1024,1024]{1,0:T(8,128)}), f32[128,1024]{1,0:T(8,128)}) %reduce-scatter.26.cloned.1.call-update) | async-done | bytes 524304 | tf_op jit(solution)/shard_map/reduce_scatter | solution.py:270
  1705.1 40.2 %reduce-scatter.22.cloned.1.call-done = f32[32,1024]{1,0:T(8,128)} async-done(((f32[256,1024]{1,0:T(8,128)}), f32[32,1024]{1,0:T(8,128)}) %reduce-scatter.22.cloned.1.call-update) | async-done | bytes 131088 | tf_op jit(solution)/shard_map/reduce_scatter | solution.py:268
  1745.2 40.0 %reduce-scatter.18.cloned.1.call-done = f32[128,256]{1,0:T(8,128)} async-done(((f32[1024,256]{1,0:T(8,128)}), f32[128,256]{1,0:T(8,128)}) %reduce-scatter.18.cloned.1.call-update) | async-done | bytes 131088 | tf_op jit(solution)/shard_map/reduce_scatter | solution.py:266
  1785.2 40.1 %reduce-scatter.16.cloned.1.call-done = f32[32,1024]{1,0:T(8,128)} async-done(((f32[256,1024]{1,0:T(8,128)}), f32[32,1024]{1,0:T(8,128)}) %reduce-scatter.16.cloned.1.call-update) | async-done | bytes 131088 | tf_op jit(solution)/shard_map/reduce_scatter | solution.py:265
  1825.4 50.5 %reduce-scatter.14.cloned.1.call-done = f32[128,3,256]{2,0,1:T(8,128)} async-done(((f32[1024,3,256]{2,0,1:T(8,128)}), f32[128,3,256]{2,0,1:T(8,128)}) %reduce-scatter.14.cloned.1.call-update) | async-done | bytes 393232 | tf_op jit(solution)/shard_map/reduce_scatter | solution.py:264
  (372 shorter events, 143.8 us)
Async XLA Ops:
  7.2 490.1 %copy-start = (bf16[1024,1024]{1,0:T(8,128)(2,1)S(1)}, bf16[1024,1024]{1,0:T(8,128)(2,1)}, u32[]{:S(2)}) copy-start(bf16[1024,1024]{1,0:T(8,128)(2,1)} %param.33) | copy-start | bytes 6291460
  7.2 6.7 copy-start.76
  7.2 266.0 %all-reduce.7.cloned.1.call-start = ((), (), s32[]{:S(2)}) async-start(), calls=%async_computation.9 | async-start | bytes 10485760 | tf_op jit(solution)/shard_map/psum | solution.py:153
  8.2 6.8 copy-start.8
  8.2 6.8 copy-start.82
  10.6 7.1 copy-start.54
  30.3 8.5 copy-start.37
  57.3 8.5 copy-start.37
  73.9 7.5 copy-start.3
  73.9 7.5 copy-start.10
  73.9 7.5 copy-start.50
  81.4 410.4 %all-reduce.9.cloned.1.call-start = ((), (), s32[]{:S(2)}) async-start(), calls=%async_computation.10 | async-start | bytes 10485760 | tf_op jit(solution)/shard_map/psum | solution.py:170
  303.8 399.4 %all-reduce.11.cloned.1.call-start = ((), (), s32[]{:S(2)}) async-start(), calls=%async_computation.11 | async-start | bytes 10485760 | tf_op jit(solution)/shard_map/psum | solution.py:187
  496.5 12.4 copy-start.5
  496.6 212.6 %copy-start.56 = (f32[1280]{0:T(1024)}, f32[1280]{0:T(1024)S(1)}, u32[]{:S(2)}) copy-start(f32[1280]{0:T(1024)S(1)} %broadcast_multiply_fusion.6) | copy-start | bytes 15364
  497.3 211.9 %copy-start.62 = (f32[1280]{0:T(1024)}, f32[1280]{0:T(1024)S(1)}, u32[]{:S(2)}) copy-start(f32[1280]{0:T(1024)S(1)} %add_rsqrt_fusion) | copy-start | bytes 15364
  515.2 424.2 %all-reduce.13.cloned.1.call-start = ((), (), s32[]{:S(2)}) async-start(), calls=%async_computation.12 | async-start | bytes 10485760 | tf_op jit(solution)/shard_map/psum | solution.py:219
  751.3 724.8 %all-reduce.15.cloned.1.call-start = ((), (), s32[]{:S(2)}) async-start(), calls=%async_computation.22 | async-start | bytes 26214400 | tf_op jit(solution)/shard_map/psum | solution.py:177
  751.8 9.1 copy-start.47
  760.6 178.8 %copy-start.53 = (f32[1280]{0:T(1024)S(1)}, f32[1280]{0:T(1024)}, u32[]{:S(2)}) copy-start(f32[1280]{0:T(1024)} %copy-done.52) | copy-start | bytes 15364
  760.6 178.8 %copy-start.59 = (f32[1280]{0:T(1024)S(1)}, f32[1280]{0:T(1024)}, u32[]{:S(2)}) copy-start(f32[1280]{0:T(1024)} %copy-done.58) | copy-start | bytes 15364
  760.7 178.8 %copy-start.65 = (f32[1,1024]{1,0:T(1,128)S(1)}, f32[1,1024]{1,0:T(1,128)}, u32[]{:S(2)}) copy-start(f32[1,1024]{1,0:T(1,128)} %get-tuple-element.578) | copy-start | bytes 12292
  760.9 184.5 %copy-start.27 = (bf16[640,1,256]{2,0,1:T(8,128)(2,1)}, bf16[640,1,256]{2,0,1:T(8,128)(2,1)S(1)}, u32[]{:S(2)}) copy-start(bf16[640,1,256]{2,0,1:T(8,128)(2,1)S(1)} %copy.92) | copy-start | bytes 983044
  761.1 184.2 %copy-start.29 = (bf16[640,1,256]{2,0,1:T(8,128)(2,1)}, bf16[640,1,256]{2,0,1:T(8,128)(2,1)S(1)}, u32[]{:S(2)}) copy-start(bf16[640,1,256]{2,0,1:T(8,128)(2,1)S(1)} %copy.93) | copy-start | bytes 983044
  945.4 7.4 copy-start.42
  1032.6 443.6 %copy-start.55 = (f32[1280]{0:T(1024)S(1)}, f32[1280]{0:T(1024)}, u32[]{:S(2)}) copy-start(f32[1280]{0:T(1024)} %copy-done.54) | copy-start | bytes 15364
  1032.6 443.6 %copy-start.61 = (f32[1280]{0:T(1024)S(1)}, f32[1280]{0:T(1024)}, u32[]{:S(2)}) copy-start(f32[1280]{0:T(1024)} %copy-done.60) | copy-start | bytes 15364
  1032.6 443.6 %copy-start.67 = (f32[1,1024]{1,0:T(1,128)S(1)}, f32[1,1024]{1,0:T(1,128)}, u32[]{:S(2)}) copy-start(f32[1,1024]{1,0:T(1,128)} %copy-done.66) | copy-start | bytes 12292
  1032.6 487.1 %reduce-scatter.20.cloned.1.call-start = ((), (), s32[]{:S(2)}) async-start(), calls=%async_computation.16 | async-start | bytes 2359296 | tf_op jit(solution)/shard_map/reduce_scatter | solution.py:267
  1036.4 444.2 %copy-start.71 = (f32[1024]{0:T(1024)S(1)}, f32[1024]{0:T(1024)}, u32[]{:S(2)}) copy-start(f32[1024]{0:T(1024)} %get-tuple-element.471) | copy-start | bytes 12292
  1036.4 444.2 %copy-start.73 = (f32[1024]{0:T(1024)S(1)}, f32[1024]{0:T(1024)}, u32[]{:S(2)}) copy-start(f32[1024]{0:T(1024)} %get-tuple-element.470) | copy-start | bytes 12292
  1036.4 445.4 %copy-start.70 = (f32[1024]{0:T(1024)S(1)}, f32[1024]{0:T(1024)}, u32[]{:S(2)}) copy-start(f32[1024]{0:T(1024)} %get-tuple-element.462) | copy-start | bytes 12292
  1036.4 445.4 %copy-start.72 = (f32[1024]{0:T(1024)S(1)}, f32[1024]{0:T(1024)}, u32[]{:S(2)}) copy-start(f32[1024]{0:T(1024)} %get-tuple-element.460) | copy-start | bytes 12292
  1036.5 446.5 %copy-start.57 = (f32[1280]{0:T(1024)S(1)}, f32[1280]{0:T(1024)}, u32[]{:S(2)}) copy-start(f32[1280]{0:T(1024)} %copy-done.56) | copy-start | bytes 15364
  1036.5 446.5 %copy-start.63 = (f32[1280]{0:T(1024)S(1)}, f32[1280]{0:T(1024)}, u32[]{:S(2)}) copy-start(f32[1280]{0:T(1024)} %copy-done.62) | copy-start | bytes 15364
  1036.5 446.5 %copy-start.69 = (f32[1,1024]{1,0:T(1,128)S(1)}, f32[1,1024]{1,0:T(1,128)}, u32[]{:S(2)}) copy-start(f32[1,1024]{1,0:T(1,128)} %get-tuple-element.576) | copy-start | bytes 12292
  1036.5 446.5 %copy-start.81 = (f32[1,1024]{1,0:T(1,128)S(1)}, f32[1,1024]{1,0:T(1,128)}, u32[]{:S(2)}) copy-start(f32[1,1024]{1,0:T(1,128)} %get-tuple-element.579) | copy-start | bytes 12292
  1036.5 520.5 %reduce-scatter.30.cloned.1.call-start = ((), (), s32[]{:S(2)}) async-start(), calls=%async_computation.21 | async-start | bytes 589824
  1481.8 112.5 %reduce-scatter.28.cloned.1.call-start = ((), (), s32[]{:S(2)}) async-start(), calls=%async_computation.20 | async-start | bytes 589824
  1482.9 167.0 %reduce-scatter.24.cloned.1.call-start = ((), (), s32[]{:S(2)}) async-start(), calls=%async_computation.18 | async-start | bytes 4718592 | tf_op jit(solution)/shard_map/reduce_scatter | solution.py:269
  1491.9 9.2 copy-start.24
  1491.9 213.2 %reduce-scatter.26.cloned.1.call-start = ((), (), s32[]{:S(2)}) async-start(), calls=%async_computation.19 | async-start | bytes 4718592 | tf_op jit(solution)/shard_map/reduce_scatter | solution.py:270
  1500.8 244.4 %reduce-scatter.22.cloned.1.call-start = ((), (), s32[]{:S(2)}) async-start(), calls=%async_computation.17 | async-start | bytes 1179648 | tf_op jit(solution)/shard_map/reduce_scatter | solution.py:268
  1505.4 279.8 %reduce-scatter.18.cloned.1.call-start = ((), (), s32[]{:S(2)}) async-start(), calls=%async_computation.15 | async-start | bytes 1179648 | tf_op jit(solution)/shard_map/reduce_scatter | solution.py:266
  1509.2 316.2 %reduce-scatter.16.cloned.1.call-start = ((), (), s32[]{:S(2)}) async-start(), calls=%async_computation.14 | async-start | bytes 1179648 | tf_op jit(solution)/shard_map/reduce_scatter | solution.py:265
  1513.6 362.2 %reduce-scatter.14.cloned.1.call-start = ((), (), s32[]{:S(2)}) async-start(), calls=%async_computation.13 | async-start | bytes 3538944 | tf_op jit(solution)/shard_map/reduce_scatter | solution.py:264
  1519.7 8.6 slice-start
  1528.3 351.1 %copy-start.1 = (bf16[1024,1024]{1,0:T(8,128)(2,1)S(1)}, bf16[1024,1024]{1,0:T(8,128)(2,1)}, u32[]{:S(2)}) copy-start(bf16[1024,1024]{1,0:T(8,128)(2,1)} %param.33) | copy-start | bytes 6291460
  (68 other events, 201.0 us)
Sparse Core Ops, SparseCore 0:
  81.6 191.6 all-reduce.6
  304.0 187.8 all-reduce.8
  515.3 187.9 all-reduce.10
  751.5 187.8 all-reduce.12
  1032.7 443.4 all-reduce.14
  1479.3 40.1 reduce-scatter.19
  1522.9 34.1 reduce-scatter.29
  1560.1 34.1 reduce-scatter.27
  1598.6 51.3 reduce-scatter.23
  1653.7 51.2 reduce-scatter.25
  1709.1 36.0 reduce-scatter.21
  1749.2 36.0 reduce-scatter.17
  1789.3 36.0 reduce-scatter.15
  1829.5 46.2 reduce-scatter.13
where the time goes:
time: 1890 us
  waiting for transfers between devices  1510 us (80%)
  matrix products  193 us (10%)
  other arithmetic  96.3 us (5%)
  local copies, waits for them, and re-layouts  56.5 us (3%)
    psum x1, waiting for transfers between devices, local(): lax.psum(jnp.dot(hidden, w_down, preferred_element_type=jnp.float32), 'mp')  440 us
    psum x1, waiting for transfers between devices, local(): lax.psum(jnp.dot(mixed_flat, w_out, preferred_element_type=jnp.float32),...  188 us
    psum x1, waiting for transfers between devices, local(): third_grad = lax.psum(third_part, 'mp')  188 us
    psum x1, waiting for transfers between devices, local(): lax.psum(jnp.dot(looked_flat, w_cross_out, preferred_element_type=jnp.flo...  180 us
    psum x1, waiting for transfers between devices, local(): second_grad, text_grad = lax.psum((second_part, text_part), 'mp')  175 us
    unnamed x16, waiting for transfers between devices  59.3 us
    reduce_scatter x1, waiting for transfers between devices, local(): lax.psum_scatter(down_grad, 'dp', scatter_dimension=0, tiled=True)  55.1 us
    reduce_scatter x1, waiting for transfers between devices, local(): lax.psum_scatter(up_grad, 'dp', scatter_dimension=0, tiled=True)  54.2 us
  transfers between devices with their start and end apart: 14, of which 13 were waited for; matrix products, arithmetic and copies ran while one was open for 4% of the time, Pallas kernels for 0%

commit v1 on v0

v1 whole, which is shorter than its diff:
```python
from functools import partial

import jax
import jax.numpy as jnp
from jax import lax
from jax.experimental import pallas as pl
from jax.experimental.pallas import tpu as pltpu
from jax.sharding import PartitionSpec as P

HEAD = 64
BLK = 256
SLOTS8 = 8
EPS = 1e-05
NEG = -1e30
F32 = jnp.float32
BF16 = jnp.bfloat16
MIB = 1024 * 1024

NN = (((1,), (0,)), ((), ()))
NT = (((1,), (1,)), ((), ()))
TN = (((0,), (0,)), ((), ()))


def dot(a, b, dims=NN):
    return lax.dot_general(a, b, dims, preferred_element_type=F32)


def params(mib=56, semantics=None):
    return pltpu.CompilerParams(vmem_limit_bytes=mib * MIB, dimension_semantics=semantics)


def shape(dims, dtype=F32):
    return jax.ShapeDtypeStruct(dims, dtype)


def smem():
    return pl.BlockSpec(memory_space=pltpu.SMEM)


def whole(dims):
    rank = len(dims)
    return pl.BlockSpec(dims, lambda *_: (0,) * rank)


def at(dims, index):
    return pl.BlockSpec(dims, lambda *_: index)


def rows_of(tile, width):
    return pl.BlockSpec((tile, width), lambda i, *_: (i, 0))


def norm_stats(value):
    center = value - jnp.mean(value, axis=-1, keepdims=True)
    spread = jnp.mean(center * center, axis=-1, keepdims=True)
    inverse = lax.rsqrt(spread + EPS)
    return center * inverse, inverse


def norm_forward(value, gain, shift):
    unit, _ = norm_stats(value)
    return (unit * gain + shift).astype(BF16)


def norm_backward(incoming, value, gain):
    unit, inverse = norm_stats(value)
    scaled = incoming * gain
    pushed = incoming * unit
    inner = (
        scaled
        - jnp.mean(scaled, axis=-1, keepdims=True)
        - unit * jnp.mean(scaled * unit, axis=-1, keepdims=True)
    )
    return (
        inner * inverse,
        jnp.sum(pushed, axis=0, keepdims=True),
        jnp.sum(incoming, axis=0, keepdims=True),
    )


def norm_kernel(tokens_ref, gain_ref, shift_ref, first_ref):
    first_ref[...] = norm_forward(tokens_ref[...].astype(F32), gain_ref[...], shift_ref[...])


def norm_first(tokens, gain, shift):
    rows, width = tokens.shape
    return pl.pallas_call(
        norm_kernel,
        grid=(rows // BLK,),
        in_specs=[rows_of(BLK, width), whole((1, width)), whole((1, width))],
        out_specs=rows_of(BLK, width),
        out_shape=shape((rows, width), BF16),
        name="norm_first",
    )(tokens, gain, shift)


def head_row(width, head, value):
    lane = lax.broadcasted_iota(jnp.int32, (1, width), 1)
    return jnp.where(lane // HEAD == head, value, 0.0)


def masked(block, row):
    return (block.astype(F32) * row).astype(BF16)


def item_at(lengths, place):
    item, start, end = 0, 0, 0
    for slot in range(lengths.shape[0]):
        end = end + lengths[slot]
        past = end <= place
        item = item + past.astype(jnp.int32)
        start = jnp.where(past, end, start)
    return item, start


def fill(target, slots, me, rows):
    for index, ref in enumerate(slots):
        place = pl.multiple_of((me ^ index) * rows, rows)
        for k in range(ref.shape[0]):
            target[k, pl.ds(place, rows), :] = ref[k].astype(BF16)


def causal():
    shape2 = (BLK, BLK)
    return lax.broadcasted_iota(jnp.int32, shape2, 0) <= lax.broadcasted_iota(
        jnp.int32, shape2, 1
    )


def lanes_of(head):
    return slice(head * HEAD, (head + 1) * HEAD)


def self_block(qb, count, qkv, turned, mixed, logs):
    q0 = pl.multiple_of(qb * BLK, BLK)
    k0 = pl.multiple_of((qb - (count - 1)) * BLK, BLK)
    width = qkv.shape[2]
    query = qkv[0, pl.ds(q0, BLK), :]
    diag = qkv[1, pl.ds(q0, BLK), :]
    pre_len = (count - 1) * BLK
    keep = causal()
    pieces = []
    for head in range(width // HEAD):
        part = masked(query, head_row(width, head, HEAD**-0.5))
        near = jnp.where(keep, dot(diag, part, NT), NEG)
        peak = jnp.max(near, axis=0, keepdims=True)
        if pre_len:
            far = dot(qkv[1, pl.ds(k0, pre_len), :], part, NT)
            peak = jnp.maximum(peak, jnp.max(far, axis=0, keepdims=True))
        near = jnp.exp(near - peak)
        total = jnp.sum(near, axis=0, keepdims=True)
        result = dot(turned[lanes_of(head), pl.ds(q0, BLK)], near.astype(BF16))
        if pre_len:
            far = jnp.exp(far - peak)
            total = total + jnp.sum(far, axis=0, keepdims=True)
            result = result + dot(
                turned[lanes_of(head), pl.ds(k0, pre_len)], far.astype(BF16)
            )
        pieces.append(result * (1.0 / total))
        logs[head : head + 1, pl.ds(q0, BLK)] = peak + jnp.log(total)
    mixed[pl.ds(q0, BLK), :] = jnp.concatenate(pieces, axis=0).T.astype(BF16)


def front_body(lengths, first, text, weights, cross, qkv, mixed, logs, pair, turned):
    rows = first.shape[0]
    for m in range(3):
        qkv[m] = dot(first[...], weights[m]).astype(BF16)
    for m in range(2):
        pair[m] = dot(text[...], cross[m + 1]).astype(BF16)
    turned[...] = qkv[2].T

    @pl.loop(0, rows // BLK)
    def _(qb):
        _, start = item_at(lengths, qb * BLK)
        count = qb - start // BLK + 1
        for n in range(1, 5):

            @pl.when(count == n)
            def _():
                self_block(qb, n, qkv, turned, mixed, logs)


def front_kernel(me, lengths, first, text, *refs):
    slots, (weights, cross, *rest) = refs[:16], refs[16:]
    rows = slots[0].shape[1]
    fill(weights, slots[:8], me[0], rows)
    fill(cross, slots[8:], me[0], rows)
    front_body(lengths, first, text, weights, cross, *rest)


def front_outs(rows, text_rows, width):
    return [
        shape((3, rows, width), BF16),
        shape((rows, width), BF16),
        shape((8, rows), F32),
        shape((2, text_rows, width), BF16),
    ]


def vmem():
    return pl.BlockSpec(memory_space=pltpu.VMEM)


def front_own(lengths, first, text, weights, cross):
    rows, _ = first.shape
    width = weights.shape[2]
    return pl.pallas_call(
        front_body,
        in_specs=[smem()] + [vmem()] * 4,
        out_specs=[vmem()] * 4,
        out_shape=front_outs(rows, text.shape[0], width),
        scratch_shapes=[pltpu.VMEM((width, rows), BF16)],
        compiler_params=params(),
        name="front_own",
    )(lengths, first, text, weights, cross)


def halves(slots):
    arrays, specs = [], []
    for half, group in enumerate(slots):
        for index, array in enumerate(group):
            size = group[6].shape
            arrays.append(array)
            specs.append(at(size, (half if index < 6 else 0, 0, 0)))
    return arrays, specs


def front(me, lengths, first, text, slots):
    rows, depth = first.shape
    arrays, specs = halves(slots)
    width = arrays[0].shape[2]
    outs = [shape((3, depth, width), BF16)] * 2 + front_outs(rows, text.shape[0], width)
    return pl.pallas_call(
        front_kernel,
        grid=(1,),
        in_specs=[smem(), smem(), vmem(), vmem()] + specs,
        out_specs=[vmem()] * 6,
        out_shape=outs,
        scratch_shapes=[pltpu.VMEM((width, rows), BF16)],
        compiler_params=params(),
        name="front",
    )(me, lengths, first, text, *arrays)


def middle_kernel(me, lengths, live, tokens, gain1, shift1, gain2, shift2, own_out, own_co, *refs):
    mixed, refs = refs[:4], refs[4:]
    queries, refs = refs[:4], refs[4:]
    pairs, refs = refs[:4], refs[4:]
    slots, refs = refs[:48], refs[48:]
    w_out, w_co, after_self, after_cross, second, third, cross_query, looked, logs, turned = refs
    step = pl.program_id(0)

    @pl.when(step == 0)
    def _():
        width = own_out.shape[0]
        w_out[:width, :] = own_out[...]
        w_co[:width, :] = own_co[...]
        for j in range(3):
            for half, target in enumerate((w_out, w_co)):
                for index in range(SLOTS8):
                    ref = slots[j * 16 + half * 8 + index]
                    rows = ref.shape[1]
                    place = pl.multiple_of((j + 1) * width + (me[0] ^ index) * rows, rows)
                    target[pl.ds(place, rows), :] = ref[0].astype(BF16)
        for j in range(4):
            turned[j] = pairs[j][1].T

    part = jnp.concatenate([ref[...] for ref in mixed], axis=1)
    residual = tokens[...].astype(F32) + dot(part, w_out[...])
    after_self[...] = residual
    normed = norm_forward(residual, gain1[...], shift1[...])
    second[...] = normed
    text = TEXT
    item, _ = item_at(lengths, step * BLK)
    t0 = pl.multiple_of(item * text, text)
    alive = live[pl.ds(t0, text), :] > 0.0
    for j in range(4):
        query = dot(normed, queries[j][0]).astype(BF16)
        width = query.shape[1]
        cols = slice(j * width, (j + 1) * width)
        cross_query[:, cols] = query
        keys = pairs[j][0, pl.ds(t0, text), :]
        pieces = []
        for head in range(width // HEAD):
            row = masked(query, head_row(width, head, HEAD**-0.5))
            score = jnp.where(alive, dot(keys, row, NT), NEG)
            peak = jnp.max(score, axis=0, keepdims=True)
            score = jnp.exp(score - peak)
            total = jnp.sum(score, axis=0, keepdims=True)
            result = dot(turned[j, lanes_of(head), pl.ds(t0, text)], score.astype(BF16))
            pieces.append(result * (1.0 / total))
            index = j * (width // HEAD) + head
            logs[index : index + 1, :] = peak + jnp.log(total)
        looked[:, cols] = jnp.concatenate(pieces, axis=0).T.astype(BF16)
    residual = residual + dot(looked[...], w_co[...])
    after_cross[...] = residual
    third[...] = norm_forward(residual, gain2[...], shift2[...])


TEXT = 128


def middle(me, lengths, live, tokens, norms, own_out, own_co, mixed, crosses, pairs, slots):
    rows, depth = tokens.shape
    width = own_out.shape[0]
    text_rows = live.shape[0]
    inner = 4 * width
    row = whole((1, depth))
    arrays, specs = [], []
    for entry in slots:
        more, more_specs = halves(entry)
        arrays += more
        specs += more_specs
    return pl.pallas_call(
        middle_kernel,
        grid=(rows // BLK,),
        in_specs=[smem(), smem(), whole((text_rows, 1)), rows_of(BLK, depth)]
        + [row] * 4
        + [whole((width, depth))] * 2
        + [rows_of(BLK, width)] * 4
        + [at((1, depth, width), (0, 0, 0))] * 4
        + [whole((2, text_rows, width))] * 4
        + specs,
        out_specs=[whole((inner, depth))] * 2
        + [rows_of(BLK, depth)] * 4
        + [rows_of(BLK, inner)] * 2
        + [pl.BlockSpec((inner // HEAD, BLK), lambda i: (0, i))],
        out_shape=[shape((inner, depth), BF16)] * 2
        + [shape((rows, depth)), shape((rows, depth))]
        + [shape((rows, depth), BF16)] * 2
        + [shape((rows, inner), BF16)] * 2
        + [shape((inner // HEAD, rows))],
        scratch_shapes=[pltpu.VMEM((4, width, text_rows), BF16)],
        compiler_params=params(),
        name="middle",
    )(me, lengths, live, tokens, *norms, own_out, own_co, *mixed, *crosses, *pairs, *arrays)


ROOT = 0.7978845608028654
CUBE = 0.044715


def gelu_both(value):
    square = value * value
    bend = jnp.tanh(value * (ROOT + (ROOT * CUBE) * square))
    half = 0.5 + 0.5 * bend
    slope = half + (0.5 * value) * (1.0 - bend * bend) * (ROOT + (3.0 * ROOT * CUBE) * square)
    return value * half, slope


def feed_rows(third, cot, up, down):
    pre_act = dot(third, up)
    hidden, slope = gelu_both(pre_act)
    hidden = hidden.astype(BF16)
    pre_grad = (dot(cot, down, NT) * slope).astype(BF16)
    return hidden, pre_grad, dot(hidden, down), dot(pre_grad, up, NT)


def feed_own_kernel(third, cot, after, up, down, out, grad, up_grad, down_grad):
    hidden, pre_grad, result, pushed = feed_rows(third[...], cot[...], up[...], down[...])
    out[...] = after[...] + result
    grad[...] = pushed
    first = pl.program_id(0) == 0
    more_up = dot(third[...], pre_grad, TN)
    more_down = dot(hidden, cot[...], TN)

    @pl.when(first)
    def _():
        up_grad[...] = more_up
        down_grad[...] = more_down

    @pl.when(jnp.logical_not(first))
    def _():
        up_grad[...] += more_up
        down_grad[...] += more_down


FEED = 320


def feed_own(third, cot, after, up, down):
    rows, depth = third.shape
    inner = up.shape[1]
    tile = rows_of(FEED, depth)
    return pl.pallas_call(
        feed_own_kernel,
        grid=(rows // FEED,),
        in_specs=[tile, tile, tile, whole((depth, inner)), whole((inner, depth))],
        out_specs=[tile, tile, whole((depth, inner)), whole((inner, depth))],
        out_shape=[
            shape((rows, depth)),
            shape((rows, depth)),
            shape((depth, inner)),
            shape((inner, depth)),
        ],
        compiler_params=params(),
        name="feed_own",
    )(third, cot, after, up, down)


def feed_kernel(me, third, cot, out_in, grad_in, *refs):
    slots, (out, grad, up, down) = refs[:16], refs[16:]

    @pl.when(pl.program_id(0) == 0)
    def _():
        rows = slots[0].shape[1]
        fill(up, slots[:8], me[0], rows)
        fill(down, slots[8:], me[0], rows)

    _, _, result, pushed = feed_rows(third[...], cot[...], up[0], down[0])
    out[...] = (out_in[...] + result).astype(out.dtype)
    grad[...] = grad_in[...] + pushed


def feed(me, third, cot, out, grad, slots, dtype):
    rows, depth = third.shape
    arrays, specs = halves(slots)
    inner = arrays[0].shape[2]
    tile = rows_of(FEED, depth)
    return pl.pallas_call(
        feed_kernel,
        grid=(rows // FEED,),
        in_specs=[smem(), tile, tile, tile, tile] + specs,
        out_specs=[tile, tile],
        out_shape=[shape((rows, depth), dtype), shape((rows, depth))],
        scratch_shapes=[
            pltpu.VMEM((1, depth, inner), BF16),
            pltpu.VMEM((1, 8 * arrays[8].shape[1], depth), BF16),
        ],
        compiler_params=params(),
        name="feed",
    )(me, third, cot, out, grad, *arrays)


def back_kernel(
    lengths, live, third_grad, cot, after_cross, after_self, second, cross_query, looked0, mixed0,
    logs, gain1, gain2, w_out, w_co, *refs,
):
    queries, refs = refs[:4], refs[4:]
    pairs, refs = refs[:4], refs[4:]
    up_grad, mixed_grad, pair_grad, co_grad, cq_grad, out_grad, sums, total, turned = refs
    step = pl.program_id(0)
    text = TEXT

    @pl.when(step == 0)
    def _():
        total[...] = jnp.zeros_like(total)
        co_grad[...] = jnp.zeros_like(co_grad)
        cq_grad[...] = jnp.zeros_like(cq_grad)
        out_grad[...] = jnp.zeros_like(out_grad)
        sums[...] = jnp.zeros_like(sums)
        for j in range(4):
            turned[j] = pairs[j][0].T

    pulled, gain_sum, shift_sum = norm_backward(third_grad[...], after_cross[...], gain2[...])
    sums[0:1, :] += gain_sum
    sums[1:2, :] += shift_sum
    upstream = cot[...].astype(F32) + pulled
    low = upstream.astype(BF16)
    co_grad[...] += dot(looked0[...], low, TN)
    looked_grad = dot(low, w_co[...], NT).astype(BF16)
    item, _ = item_at(lengths, step * BLK)
    t0 = pl.multiple_of(item * text, text)
    alive = live[pl.ds(t0, text), :] > 0.0
    second_grad = jnp.zeros(upstream.shape, F32)
    for j in range(4):
        width = queries[j].shape[2]
        cols = slice(j * width, (j + 1) * width)
        query = cross_query[:, cols]
        grads = looked_grad[:, cols]
        keys = pairs[j][0, pl.ds(t0, text), :]
        values = pairs[j][1, pl.ds(t0, text), :]
        pieces = []
        key_sum = jnp.zeros((text, width), F32)
        value_sum = jnp.zeros((text, width), F32)
        for head in range(width // HEAD):
            row = masked(query, head_row(width, head, HEAD**-0.5))
            grad = masked(grads, head_row(width, head, 1.0))
            index = j * (width // HEAD) + head
            score = jnp.where(alive, dot(keys, row, NT), NEG)
            chance = jnp.exp(score - logs[index : index + 1, :])
            pushed = dot(values, grad, NT)
            weighted = chance * pushed
            mean = jnp.sum(weighted, axis=0, keepdims=True)
            score_grad = (weighted - chance * mean).astype(BF16)
            pieces.append(dot(turned[j, lanes_of(head), pl.ds(t0, text)], score_grad))
            key_sum = key_sum + dot(score_grad, row)
            value_sum = value_sum + dot(chance.astype(BF16), grad)
        total[j, 0, pl.ds(t0, text), :] += key_sum
        total[j, 1, pl.ds(t0, text), :] += value_sum
        query_grad = (jnp.concatenate(pieces, axis=0).T * HEAD**-0.5).astype(BF16)
        if j == 0:
            cq_grad[...] += dot(second[...], query_grad, TN)
        second_grad = second_grad + dot(query_grad, queries[j][0], NT)

    pulled, gain_sum, shift_sum = norm_backward(second_grad, after_self[...], gain1[...])
    sums[2:3, :] += gain_sum
    sums[3:4, :] += shift_sum
    upstream = upstream + pulled
    up_grad[...] = upstream
    low = upstream.astype(BF16)
    out_grad[...] += dot(mixed0[...], low, TN)
    mixed_grad[...] = dot(low, w_out[...], NT).astype(BF16)

    @pl.when(step == pl.num_programs(0) - 1)
    def _():
        pair_grad[...] = total[...].astype(BF16)


def back(
    lengths, live, third_grad, cot, after_cross, after_self, second, cross_query, looked, mixed0,
    logs, gain1, gain2, w_out, w_co, crosses, pairs,
):
    rows, depth = cot.shape
    text_rows = live.shape[0]
    width = mixed0.shape[1]
    inner = 4 * width
    tile = rows_of(BLK, depth)
    row = whole((1, depth))
    return pl.pallas_call(
        back_kernel,
        grid=(rows // BLK,),
        in_specs=[smem(), whole((text_rows, 1))]
        + [tile] * 5
        + [rows_of(BLK, inner), rows_of(BLK, width), rows_of(BLK, width)]
        + [pl.BlockSpec((inner // HEAD, BLK), lambda i: (0, i)), row, row]
        + [whole((inner, depth))] * 2
        + [at((1, depth, width), (0, 0, 0))] * 4
        + [whole((2, text_rows, width))] * 4,
        out_specs=[tile, rows_of(BLK, inner), whole((4, 2, text_rows, width))]
        + [whole((width, depth)), whole((depth, width)), whole((width, depth)), whole((8, depth))],
        out_shape=[
            shape((rows, depth)),
            shape((rows, inner), BF16),
            shape((4, 2, text_rows, width), BF16),
            shape((width, depth)),
            shape((depth, width)),
            shape((width, depth)),
            shape((8, depth)),
        ],
        scratch_shapes=[
            pltpu.VMEM((4, 2, text_rows, width), F32),
            pltpu.VMEM((4, width, text_rows), BF16),
        ],
        compiler_params=params(),
        name="back",
    )(
        lengths, live, third_grad, cot, after_cross, after_self, second, cross_query, looked,
        mixed0, logs, gain1, gain2, w_out, w_co, *crosses, *pairs,
    )


def text_kernel(text, pair_grad, *refs):
    crosses, (text_grad, kv_grad) = refs[:4], refs[4:]
    total = jnp.zeros(text_grad.shape, F32)
    for j in range(4):
        for m in range(2):
            total = total + dot(pair_grad[j, m], crosses[j][m + 1], NT)
    text_grad[...] = total
    for m in range(2):
        kv_grad[m] = dot(text[...], pair_grad[0, m], TN)


def text_back(text, pair_grad, crosses):
    text_rows, depth = text.shape
    width = pair_grad.shape[3]
    return pl.pallas_call(
        text_kernel,
        in_specs=[vmem()] * 6,
        out_specs=[vmem()] * 2,
        out_shape=[shape((text_rows, depth)), shape((2, depth, width))],
        compiler_params=params(),
        name="text_back",
    )(text, pair_grad, *crosses)


def self_back_pair(qb, kb, diag, qkv, rows, grads, logs, means, turned, query_sum, key_sum, value_sum):
    q0 = pl.multiple_of(qb * BLK, BLK)
    k0 = pl.multiple_of(kb * BLK, BLK)
    keys = qkv[1, pl.ds(k0, BLK), :]
    values = qkv[2, pl.ds(k0, BLK), :]
    more_keys = 0.0
    more_values = 0.0
    for head in range(rows.shape[0]):
        score = dot(keys, rows[head], NT)
        if diag:
            score = jnp.where(causal(), score, NEG)
        chance = jnp.exp(score - logs[head : head + 1, pl.ds(q0, BLK)])
        pushed = dot(values, grads[head], NT)
        score_grad = (chance * (pushed - means[head : head + 1, :])).astype(BF16)
        query_sum[lanes_of(head), :] += dot(turned[lanes_of(head), pl.ds(k0, BLK)], score_grad)
        more_keys = more_keys + dot(score_grad, rows[head])
        more_values = more_values + dot(chance.astype(BF16), grads[head])
    key_sum[pl.ds(k0, BLK), :] += more_keys
    value_sum[pl.ds(k0, BLK), :] += more_values


def self_back_body(
    lengths, qkv, mixed, out_grad, logs, weights, triple, turned, rows, grads, means, query_sum,
    key_sum, value_sum,
):
    row_count, width = mixed.shape
    turned[...] = qkv[1].T
    key_sum[...] = jnp.zeros_like(key_sum)
    value_sum[...] = jnp.zeros_like(value_sum)

    @pl.loop(0, row_count // BLK)
    def _(qb):
        q0 = pl.multiple_of(qb * BLK, BLK)
        _, start = item_at(lengths, q0)
        query = qkv[0, pl.ds(q0, BLK), :]
        grad = out_grad[pl.ds(q0, BLK), :]
        flat = (grad.astype(F32) * mixed[pl.ds(q0, BLK), :].astype(F32)).T
        for head in range(width // HEAD):
            rows[head] = masked(query, head_row(width, head, HEAD**-0.5))
            grads[head] = masked(grad, head_row(width, head, 1.0))
            means[head : head + 1, :] = jnp.sum(flat[lanes_of(head), :], axis=0, keepdims=True)
        query_sum[...] = jnp.zeros_like(query_sum)
        rest = (qkv, rows, grads, logs, means, turned, query_sum, key_sum, value_sum)

        @pl.loop(start // BLK, qb)
        def _(kb):
            self_back_pair(qb, kb, False, *rest)

        self_back_pair(qb, qb, True, *rest)
        triple[0, pl.ds(q0, BLK), :] = (query_sum[...].T * HEAD**-0.5).astype(BF16)

    triple[1] = key_sum[...].astype(BF16)
    triple[2] = value_sum[...].astype(BF16)


def self_scratch(rows, width):
    heads = width // HEAD
    return [
        pltpu.VMEM((3, rows, width), BF16),
        pltpu.VMEM((width, rows), BF16),
        pltpu.VMEM((heads, BLK, width), BF16),
        pltpu.VMEM((heads, BLK, width), BF16),
        pltpu.VMEM((8, BLK), F32),
        pltpu.VMEM((width, BLK), F32),
        pltpu.VMEM((rows, width), F32),
        pltpu.VMEM((rows, width), F32),
    ]


def self_own_kernel(lengths, qkv, mixed, out_grad, logs, weights, first, total, qkv_grad, *scratch):
    self_back_body(lengths, qkv, mixed, out_grad, logs, weights, *scratch)
    triple = scratch[0]
    for m in range(3):
        qkv_grad[m] = dot(first[...], triple[m], TN)
    total[...] = sum(dot(triple[m], weights[m], NT) for m in range(3))


def self_own(lengths, qkv, mixed, out_grad, logs, weights, first):
    rows, depth = first.shape
    width = mixed.shape[1]
    return pl.pallas_call(
        self_own_kernel,
        grid=(1,),
        in_specs=[smem()]
        + [whole((3, rows, width)), whole((rows, width)), at((rows, width), (0, 0))]
        + [whole((8, rows)), whole((3, depth, width)), whole((rows, depth))],
        out_specs=[whole((rows, depth)), whole((3, depth, width))],
        out_shape=[shape((rows, depth)), shape((3, depth, width))],
        scratch_shapes=self_scratch(rows, width),
        compiler_params=params(),
        name="self_own",
    )(lengths, qkv, mixed, out_grad, logs, weights, first)


def self_kernel(lengths, qkv, mixed, out_grad, logs, weights, before, total, *scratch):
    self_back_body(lengths, qkv, mixed, out_grad, logs, weights, *scratch)
    triple = scratch[0]
    total[...] = before[...] + sum(dot(triple[m], weights[m], NT) for m in range(3))


def self_back(lengths, qkv, mixed, out_grad, logs, weights, before, j):
    rows, depth = before.shape
    width = mixed.shape[1]
    return pl.pallas_call(
        self_kernel,
        grid=(1,),
        in_specs=[smem()]
        + [whole((3, rows, width)), whole((rows, width)), at((rows, width), (0, j))]
        + [whole((8, rows)), whole((3, depth, width)), whole((rows, depth))],
        out_specs=whole((rows, depth)),
        out_shape=shape((rows, depth)),
        scratch_shapes=self_scratch(rows, width),
        compiler_params=params(),
        name="self_back",
    )(lengths, qkv, mixed, out_grad, logs, weights, before)


def last_kernel(first_grad, tokens, upstream, gain, token_grad, sums):
    @pl.when(pl.program_id(0) == 0)
    def _():
        sums[...] = jnp.zeros_like(sums)

    pulled, gain_sum, shift_sum = norm_backward(
        first_grad[...], tokens[...].astype(F32), gain[...]
    )
    token_grad[...] = upstream[...] + pulled
    sums[0:1, :] += gain_sum
    sums[1:2, :] += shift_sum


def last(first_grad, tokens, upstream, gain):
    rows, depth = tokens.shape
    tile = rows_of(BLK, depth)
    return pl.pallas_call(
        last_kernel,
        grid=(rows // BLK,),
        in_specs=[tile, tile, tile, whole((1, depth))],
        out_specs=[tile, whole((8, depth))],
        out_shape=[shape((rows, depth)), shape((8, depth))],
        compiler_params=params(),
        name="last",
    )(first_grad, tokens, upstream, gain)


UP = [(i, (i + 1) % 4) for i in range(4)]
DOWN = [(i, (i - 1) % 4) for i in range(4)]


def across(value, bit):
    return lax.ppermute(value, "dp", [(i, i ^ bit) for i in range(8)])


def spread(piece):
    half = piece.shape[0] // 2
    by_x = across(piece, 2)
    by_y = across(piece, 4)
    far_one = across(by_y[:half], 2)
    far_two = across(by_x[half:], 4)
    held = [piece, by_x, by_y, far_one, far_two]
    other = [across(value, 1) for value in held]
    common = [held[0], other[0], held[1], other[1], held[2], other[2]]
    return common + [held[3], other[3]], common + [held[4], other[4]]


def sliced(shard):
    rows = shard.shape[1] // SLOTS8
    half = shard.shape[0] // 2
    parts = [shard[:, s * rows : (s + 1) * rows] for s in range(SLOTS8)]
    return (
        parts[:6] + [part[:half] for part in parts[6:]],
        parts[:6] + [part[half:] for part in parts[6:]],
    )


def gather(shard, me, planar):
    if planar:
        rows = shard.shape[1] // SLOTS8
        shard = lax.dynamic_slice_in_dim(shard, me * rows, rows, 1)
    piece = shard.astype(F32)
    one = lax.ppermute(piece, "mp", UP)
    three = lax.ppermute(piece, "mp", DOWN)
    two = lax.ppermute(one, "mp", UP)
    return [spread(value) if planar else sliced(value) for value in (one, two, three)]


def scattered(value, axis):
    return lax.psum_scatter(value, "dp", scatter_dimension=axis, tiled=True)


def local(
    planar, tokens, text_states, lengths, text_mask, ln_gain, ln_shift, w_qkv, w_out, w_cross_q,
    w_cross_kv, w_cross_out, w_up, w_down, cotangent,
):
    slot_count, text_length = text_mask.shape
    place = lax.axis_index("dp") if planar else jnp.int32(0)
    me = jnp.reshape(place, (1,)).astype(jnp.int32)
    gains = [ln_gain[n : n + 1] for n in range(3)]
    shifts = [ln_shift[n : n + 1] for n in range(3)]
    text = text_states.reshape(slot_count * text_length, text_states.shape[2])
    position = lax.broadcasted_iota(jnp.int32, text_mask.shape, 1)
    live = ((text_mask == 1) | (position == 0)).astype(F32).reshape(-1, 1)
    own_qkv = jnp.transpose(w_qkv, (1, 0, 2))
    own_cross = jnp.concatenate([w_cross_q[None], jnp.transpose(w_cross_kv, (1, 0, 2))], axis=0)

    attention = gather(jnp.concatenate([own_qkv, own_cross], axis=0), place, planar)
    outer = gather(jnp.stack([w_out, w_cross_out]), place, planar)
    feeds = gather(jnp.stack([w_up, w_down]), place, planar)

    first = norm_first(tokens, gains[0], shifts[0])
    qkvs, mixeds, logs, pairs = ([None] * 4 for _ in range(4))
    weights, crosses = [own_qkv] + [None] * 3, [own_cross] + [None] * 3
    qkvs[0], mixeds[0], logs[0], pairs[0] = front_own(lengths, first, text, own_qkv, own_cross)
    for j in (1, 3, 2):
        weights[j], crosses[j], qkvs[j], mixeds[j], logs[j], pairs[j] = front(
            me, lengths, first, text, attention[j - 1]
        )
    full_out, full_co, after_self, after_cross, second, third, cross_query, looked, cross_logs = middle(
        me, lengths, live, tokens, (gains[1], shifts[1], gains[2], shifts[2]), w_out, w_cross_out,
        mixeds, crosses, pairs, outer,
    )
    out, grad, up_grad, down_grad = feed_own(third, cotangent, after_cross, w_up, w_down)
    for j in (1, 3, 2):
        out, grad = feed(
            me, third, cotangent, out, grad, feeds[j - 1], BF16 if j == 2 else F32
        )
    upstream, mixed_grad, pair_grad, co_grad, cq_grad, out_grad, sums = back(
        lengths, live, grad, cotangent, after_cross, after_self, second, cross_query, looked,
        mixeds[0], cross_logs, gains[1], gains[2], full_out, full_co, crosses, pairs,
    )
    text_grad, kv_grad = text_back(text, pair_grad, crosses)
    first_grad, qkv_grad = self_own(
        lengths, qkvs[0], mixeds[0], mixed_grad, logs[0], weights[0], first
    )
    for j in (1, 2, 3):
        first_grad = self_back(
            lengths, qkvs[j], mixeds[j], mixed_grad, logs[j], weights[j], first_grad, j
        )
    token_grad, last_sums = last(first_grad, tokens, upstream, gains[0])
    gain_grad = jnp.concatenate([last_sums[0:1], sums[2:3], sums[0:1]], axis=0)
    shift_grad = jnp.concatenate([last_sums[1:2], sums[3:4], sums[1:2]], axis=0)
    return (
        out,
        token_grad,
        text_grad.reshape(text_states.shape),
        scattered(gain_grad, 1),
        scattered(shift_grad, 1),
        jnp.transpose(scattered(qkv_grad, 1), (1, 0, 2)),
        scattered(out_grad, 0),
        scattered(cq_grad, 0),
        jnp.transpose(scattered(kv_grad, 1), (1, 0, 2)),
        scattered(co_grad, 0),
        scattered(up_grad, 0),
        scattered(down_grad, 0),
    )


def solution(mesh):
    placed = (
        P("dp", None),
        P("dp", None, None),
        P("dp"),
        P("dp", None),
        P(),
        P(),
        P(None, None, "mp"),
        P("mp", None),
        P(None, "mp"),
        P(None, None, "mp"),
        P("mp", None),
        P(None, "mp"),
        P("mp", None),
        P("dp", None),
    )
    return jax.shard_map(
        partial(local, mesh.shape["dp"] == SLOTS8),
        mesh=mesh,
        in_specs=placed,
        out_specs=(
            P("dp", None),
            P("dp", None),
            P("dp", None, None),
            P(None, "dp"),
            P(None, "dp"),
            P("dp", None, "mp"),
            P(("mp", "dp"), None),
            P("dp", "mp"),
            P("dp", None, "mp"),
            P(("mp", "dp"), None),
            P("dp", "mp"),
            P(("mp", "dp"), None),
        ),
        check_vma=False,
    )
```

time: 1890 us -> 1120 us (0.59)
  waiting for transfers between devices: 1510 us -> 650 us
  Pallas kernels: 0 us -> 342 us
  matrix products: 193 us -> 0 us
  other arithmetic: 96.3 us -> 2.53 us
  starting transfers between devices: 1.84 us -> 77.7 us
  local copies, waits for them, and re-layouts: 56.5 us -> 21.8 us
    psum x5 -> x0, waiting for transfers between devices: 1170 us -> none  [the longest x1 440 us: local(): lax.psum(jnp.dot(hidden, w_down, preferred_element_type=jnp.float32), 'mp')]
    pallas_call x0 -> x17, Pallas kernels: none -> 342 us  [the longest x3 55.4 us: feed(): pl.pallas_call(feed_kernel, grid=(rows // FEED,), in_specs=[smem(), tile,...]
    ppermute x0 -> x90, waiting for transfers between devices: none -> 223 us  [the longest x81 163 us: across(): return lax.ppermute(value, 'dp', [(i, i ^ bit) for i in range(8)])]
    dot_general x49 -> x0, matrix products: 193 us -> none  [the longest x8 37.5 us: block_scores(): jnp.einsum('qhe,khe->hqk', query_part, key_set, preferred_element_type=jn...]
    ppermute x0 -> x90, starting transfers between devices: none -> 77.2 us  [the longest x81 45.1 us: across(): return lax.ppermute(value, 'dp', [(i, i ^ bit) for i in range(8)])]
    reduce_sum x14 -> x0, other arithmetic: 51 us -> none  [the longest x4 19.8 us: one_block(): weight_total = jnp.sum(weights, axis=-1, keepdims=True)]
    unnamed x16 -> x11, waiting for transfers between devices: 59.3 us -> 105 us
    reduce_scatter x7, waiting for transfers between devices: 280 us -> 323 us  [scattered(): return lax.psum_scatter(value, 'dp', scatter_dimension=axis, tiled=True)]
  transfers between devices with their start and end apart: 14 -> 99, of which waited for: 13 -> 50; matrix products, arithmetic and copies ran while one was open for 4% -> 2% of each run, Pallas kernels for 0% -> 17%
where the time goes in v1:
time: 1120 us; the launch traced here: 1110 us
  waiting for transfers between devices  650 us (58%)
  Pallas kernels  342 us (31%)
  starting transfers between devices  77.7 us (7%)
  local copies, waits for them, and re-layouts  21.8 us (2%)
  between operations  15 us (1%)
    reduce_scatter x7, waiting for transfers between devices, scattered(): return lax.psum_scatter(value, 'dp', scatter_dimension=axis, tiled=True)  323 us
    ppermute x81, waiting for transfers between devices, across(): return lax.ppermute(value, 'dp', [(i, i ^ bit) for i in range(8)])  163 us
    unnamed x11, waiting for transfers between devices  105 us
    pallas_call x3, Pallas kernels, feed(): pl.pallas_call(feed_kernel, grid=(rows // FEED,), in_specs=[smem(), tile,...  55.4 us
    pallas_call x1, Pallas kernels, back(): pl.pallas_call(back_kernel, grid=(rows // BLK,), in_specs=[smem(), whole(...  53.3 us
    pallas_call x3, Pallas kernels, self_back(): pl.pallas_call(self_kernel, grid=(1,), in_specs=[smem()] + [whole((3, row...  52.5 us
    pallas_call x3, Pallas kernels, front(): pl.pallas_call(front_kernel, grid=(1,), in_specs=[smem(), smem(), vmem(),...  47.8 us
    ppermute x81, starting transfers between devices, across(): return lax.ppermute(value, 'dp', [(i, i ^ bit) for i in range(8)])  45.1 us
  transfers between devices with their start and end apart: 99, of which 50 were waited for; matrix products, arithmetic and copies ran while one was open for 2% of the time, Pallas kernels for 17%

profile of v1, /device:TPU:0, one launch (start us, length us, event | category | flops | bytes accessed | tf_op | source)
XLA Modules:
  0.0 1109.2 jit_solution(10706949021864570986)
XLA Ops:
  8.3 3.1 collective-permute-start.30
  13.5 7.2 collective-permute-done.30.refs_12_.refs_20_
  39.7 6.6 collective-permute-start.20
  57.8 5.9 collective-permute-done.refs_0_.refs_8_
  63.8 18.9 %collective-permute-start.70 = (f32[2,128,1024]{2,1,0:T(8,128)S(1)}, f32[2,128,1024]{2,1,0:T(8,128)S(1)}, u32[]{:S(2)}, u32[]{:S(2)}) collective-permute-start(f32[2,128,1024]{2,1,0:T(8,128)S(1)} %fusion.1), channel_id=1, source_target_pairs={{0,3},{1,0},{2,1},{3,2},{4,7},{5,4},{6,5},{7,6},{8,11},{9,8},{10,9... | collective-permute-start | bytes 3145736 | tf_op jit(solution)/shard_map/ppermute | solution.py:757
  85.0 3.8 collective-permute-done.46.refs_34_
  95.1 8.1 collective-permute-done.60.refs_0_.refs_8_
  103.2 19.8 %collective-permute-done.70.refs_0_.refs_8_ = f32[2,128,1024]{2,1,0:T(8,128)S(1)} collective-permute-done((f32[2,128,1024]{2,1,0:T(8,128)S(1)}, f32[2,128,1024]{2,1,0:T(8,128)S(1)}, u32[]{:S(2)}, u32[]{:S(2)}) %collective-permute-start.70) | collective-permute-done | bytes 1048608 | tf_op jit(solution)/shard_map/ppermute | solution.py:757
  123.4 17.7 %collective-permute-done.10.refs_0_.refs_8_ = f32[6,128,256]{2,1,0:T(8,128)S(1)} collective-permute-done((f32[6,128,256]{2,1,0:T(8,128)S(1)}, f32[6,128,256]{2,1,0:T(8,128)S(1)}, u32[]{:S(2)}, u32[]{:S(2)}) %collective-permute-start.10) | collective-permute-done | bytes 786464 | tf_op jit(solution)/shard_map/ppermute | solution.py:758
  145.5 16.1 %collective-permute-done.22.refs_2_.refs_10_ = f32[6,128,256]{2,1,0:T(8,128)S(1)} collective-permute-done((f32[6,128,256]{2,1,0:T(8,128)S(1)}, f32[6,128,256]{2,1,0:T(8,128)S(1)}, u32[]{:S(2)}, u32[]{:S(2)}) %collective-permute-start.22) | collective-permute-done | bytes 786464 | tf_op jit(solution)/shard_map/ppermute | solution.py:726
  163.7 6.4 collective-permute-done.6.refs_6_
  170.5 6.6 collective-permute-done.8.refs_14_
  179.0 6.7 collective-permute-done.28.refs_14_
  186.2 14.7 %collective-permute-done.62.refs_2_.refs_10_ = f32[2,128,1024]{2,1,0:T(8,128)S(1)} collective-permute-done((f32[2,128,1024]{2,1,0:T(8,128)S(1)}, f32[2,128,1024]{2,1,0:T(8,128)S(1)}, u32[]{:S(2)}, u32[]{:S(2)}) %collective-permute-start.62) | collective-permute-done | bytes 1048608 | tf_op jit(solution)/shard_map/ppermute | solution.py:726
  201.5 6.5 collective-permute-done.74.refs_4_.refs_12_
  208.6 14.8 %collective-permute-done.72.refs_2_.refs_10_ = f32[2,128,1024]{2,1,0:T(8,128)S(1)} collective-permute-done((f32[2,128,1024]{2,1,0:T(8,128)S(1)}, f32[2,128,1024]{2,1,0:T(8,128)S(1)}, u32[]{:S(2)}, u32[]{:S(2)}) %collective-permute-start.72) | collective-permute-done | bytes 1048608 | tf_op jit(solution)/shard_map/ppermute | solution.py:726
  224.5 13.5 %collective-permute-done.12.refs_2_.refs_10_ = f32[6,128,256]{2,1,0:T(8,128)S(1)} collective-permute-done((f32[6,128,256]{2,1,0:T(8,128)S(1)}, f32[6,128,256]{2,1,0:T(8,128)S(1)}, u32[]{:S(2)}, u32[]{:S(2)}) %collective-permute-start.12) | collective-permute-done | bytes 786464 | tf_op jit(solution)/shard_map/ppermute | solution.py:726
  247.1 9.0 collective-permute-done.66.refs_6_
  258.1 9.3 collective-permute-done.76.refs_6_
  268.4 6.5 collective-permute-done.16.refs_6_
  279.6 21.3 %collective-permute-done.84.refs_4_.refs_12_ = f32[2,128,1024]{2,1,0:T(8,128)} collective-permute-done((f32[2,128,1024]{2,1,0:T(8,128)}, f32[2,128,1024]{2,1,0:T(8,128)}, u32[]{:S(2)}, u32[]{:S(2)}) %collective-permute-start.84) | collective-permute-done | bytes 1048608 | tf_op jit(solution)/shard_map/ppermute | solution.py:726
  311.3 8.9 collective-permute-done.86.refs_6_
  322.5 5.8 norm_first.1.first
  329.6 13.5 %front_own.1 = (bf16[3,1280,256]{2,1,0:T(8,128)(2,1)}, bf16[1280,256]{1,0:T(8,128)(2,1)}, f32[8,1280]{1,0:T(8,128)}, bf16[2,640,256]{2,1,0:T(8,128)(2,1)}) custom-call(s32[5]{0:T(128)} %lengths.19, bf16[1280,1024]{1,0:T(8,128)(2,1)} %norm_first.1.first, bf16[640,1024]{1,0:T(8,128)(2,1)} %bitcast.25, bf16[3,1024,256]{2,1,0:T(8,128)(2,1)} %bitcast.30, ...), custom_call_target="tpu_custom_call" | custom-call | tf_op jit(solution)/shard_map/front_own/pallas_call | solution.py:207
  343.1 16.1 %front.3 = (bf16[3,1024,256]{2,1,0:T(8,128)(2,1)}, bf16[3,1024,256]{2,1,0:T(8,128)(2,1)}, bf16[3,1280,256]{2,1,0:T(8,128)(2,1)}, bf16[1280,256]{1,0:T(8,128)(2,1...) custom-call(s32[1]{0:T(128)} %bitcast.4.me, s32[5]{0:T(128)} %lengths.19, bf16[1280,1024]{1,0:T(8,128)(2,1)} %norm_first.1.first, ...), custom_call_target="tpu_custom_call" | custom-call | tf_op jit(solution)/shard_map/front/pallas_call | solution.py:233
  359.2 15.8 %front.5 = (bf16[3,1024,256]{2,1,0:T(8,128)(2,1)}, bf16[3,1024,256]{2,1,0:T(8,128)(2,1)}, bf16[3,1280,256]{2,1,0:T(8,128)(2,1)}, bf16[1280,256]{1,0:T(8,128)(2,1...) custom-call(s32[1]{0:T(128)} %bitcast.4.me, s32[5]{0:T(128)} %lengths.19, bf16[1280,1024]{1,0:T(8,128)(2,1)} %norm_first.1.first, ...), custom_call_target="tpu_custom_call" | custom-call | tf_op jit(solution)/shard_map/front/pallas_call | solution.py:233
  375.0 16.0 %front.4 = (bf16[3,1024,256]{2,1,0:T(8,128)(2,1)}, bf16[3,1024,256]{2,1,0:T(8,128)(2,1)}, bf16[3,1280,256]{2,1,0:T(8,128)(2,1)}, bf16[1280,256]{1,0:T(8,128)(2,1...) custom-call(s32[1]{0:T(128)} %bitcast.4.me, s32[5]{0:T(128)} %lengths.19, bf16[1280,1024]{1,0:T(8,128)(2,1)} %norm_first.1.first, ...), custom_call_target="tpu_custom_call" | custom-call | tf_op jit(solution)/shard_map/front/pallas_call | solution.py:233
  391.0 43.2 %middle.1 = (bf16[1024,1024]{1,0:T(8,128)(2,1)}, bf16[1024,1024]{1,0:T(8,128)(2,1)}, f32[1280,1024]{1,0:T(8,128)}, f32[1280,1024]{1,0:T(8,128)}, bf16[1280,1024]...) custom-call(s32[1]{0:T(128)} %bitcast.4.me, ...), custom_call_target="tpu_custom_call" | custom-call | tf_op jit(solution)/shard_map/middle/pallas_call | solution.py:314
  434.2 32.2 %feed_own.1 = (f32[1280,1024]{1,0:T(8,128)}, f32[1280,1024]{1,0:T(8,128)}, f32[1024,1024]{1,0:T(8,128)}, f32[1024,1024]{1,0:T(8,128)}) custom-call(bf16[1280,1024]{1,0:T(8,128)(2,1)} %get-tuple-element.77.third, bf16[1280,1024]{1,0:T(8,128)(2,1)} %cot.9, f32[1280,1024]{1,0:T(8,128)} %get-tuple-element.78.after.after_cross, bf16[1024,1024]{1,0:T(8,128)(2,1)} %up.1, ...), custom_call_target="tpu_custom_call" | custom-call | tf_op jit(solution)/shard_map/feed_own/pallas_call | solution.py:385
  466.4 18.6 %feed.3 = (f32[1280,1024]{1,0:T(8,128)}, f32[1280,1024]{1,0:T(8,128)}) custom-call(s32[1]{0:T(128)} %bitcast.4.me, bf16[1280,1024]{1,0:T(8,128)(2,1)} %get-tuple-element.77.third, bf16[1280,1024]{1,0:T(8,128)(2,1)} %cot.9, f32[1280,1024]{1,0:T(8,128)} %get-tuple-element.79.out_in, f32[1280,1024]{1,0:T(8,128)} %get-tuple-element.80.grad_in, ...), custom_call_target="tpu_custom_call" | custom-call | tf_op jit(solution)/shard_map/feed/pallas_call | solution.py:420
  485.1 18.3 %feed.4 = (f32[1280,1024]{1,0:T(8,128)}, f32[1280,1024]{1,0:T(8,128)}) custom-call(s32[1]{0:T(128)} %bitcast.4.me, bf16[1280,1024]{1,0:T(8,128)(2,1)} %get-tuple-element.77.third, bf16[1280,1024]{1,0:T(8,128)(2,1)} %cot.9, f32[1280,1024]{1,0:T(8,128)} %get-tuple-element.81.out_in, f32[1280,1024]{1,0:T(8,128)} %get-tuple-element.82.grad_in, ...), custom_call_target="tpu_custom_call" | custom-call | tf_op jit(solution)/shard_map/feed/pallas_call | solution.py:420
  504.4 18.5 %feed.5 = (bf16[1280,1024]{1,0:T(8,128)(2,1)}, f32[1280,1024]{1,0:T(8,128)}) custom-call(s32[1]{0:T(128)} %bitcast.4.me, bf16[1280,1024]{1,0:T(8,128)(2,1)} %get-tuple-element.77.third, bf16[1280,1024]{1,0:T(8,128)(2,1)} %cot.9, f32[1280,1024]{1,0:T(8,128)} %get-tuple-element.83.out_in, f32[1280,1024]{1,0:T(8,128)} %get-tuple-element.84.grad_in, ...), custom_call_target="tpu_custom_call" | custom-call | tf_op jit(solution)/shard_map/feed/pallas_call | solution.py:420
  522.8 53.3 %back.1 = (f32[1280,1024]{1,0:T(8,128)}, bf16[1280,1024]{1,0:T(8,128)(2,1)}, bf16[4,2,640,256]{3,2,1,0:T(8,128)(2,1)}, f32[256,1024]{1,0:T(8,128)}, f32[1024,256...) custom-call(s32[5]{0:T(128)} %lengths.19, f32[640,1]{1,0:T(8,128)} %bitcast.38, ...), custom_call_target="tpu_custom_call" | custom-call | tf_op jit(solution)/shard_map/back/pallas_call | solution.py:520
  576.1 18.9 %self_own.1 = (f32[1280,1024]{1,0:T(8,128)}, f32[3,1024,256]{2,1,0:T(8,128)}) custom-call(s32[5]{0:T(128)} %lengths.19, bf16[3,1280,256]{2,1,0:T(8,128)(2,1)} %get-tuple-element.104.qkv, bf16[1280,256]{1,0:T(8,128)(2,1)} %get-tuple-element.66.refs_0_.mixed0.mixed, bf16[1280,1024]{1,0:T(8,128)(2,1)} %get-tuple-element.95.out_grad, ...), custom_call_target="tpu_custom_call" | custom-call | tf_op jit(solution)/shard_map/self_own/pallas_call | solution.py:657
  595.1 17.3 %self_back.3.before = f32[1280,1024]{1,0:T(8,128)} custom-call(s32[5]{0:T(128)} %lengths.19, bf16[3,1280,256]{2,1,0:T(8,128)(2,1)} %get-tuple-element.101.qkv, bf16[1280,256]{1,0:T(8,128)(2,1)} %get-tuple-element.67.refs_1_.mixed, bf16[1280,1024]{1,0:T(8,128)(2,1)} %get-tuple-element.95.out_grad, f32[8,1280]{1,0:T(8,128)} %get-tuple-element.102.logs, ...), custom_call_target="tpu_custom_call" | custom-call | tf_op jit(solution)/shard_map/self_back/pallas_call | solution.py:680
  612.4 17.8 %self_back.4.before = f32[1280,1024]{1,0:T(8,128)} custom-call(s32[5]{0:T(128)} %lengths.19, bf16[3,1280,256]{2,1,0:T(8,128)(2,1)} %get-tuple-element.98.qkv, bf16[1280,256]{1,0:T(8,128)(2,1)} %get-tuple-element.68.refs_2_.mixed, bf16[1280,1024]{1,0:T(8,128)(2,1)} %get-tuple-element.95.out_grad, f32[8,1280]{1,0:T(8,128)} %get-tuple-element.99.logs, ...), custom_call_target="tpu_custom_call" | custom-call | tf_op jit(solution)/shard_map/self_back/pallas_call | solution.py:680
  630.3 17.3 %self_back.5.first_grad = f32[1280,1024]{1,0:T(8,128)} custom-call(s32[5]{0:T(128)} %lengths.19, bf16[3,1280,256]{2,1,0:T(8,128)(2,1)} %get-tuple-element.86.qkv, bf16[1280,256]{1,0:T(8,128)(2,1)} %get-tuple-element.69.refs_3_.mixed, bf16[1280,1024]{1,0:T(8,128)(2,1)} %get-tuple-element.95.out_grad, f32[8,1280]{1,0:T(8,128)} %get-tuple-element.96.logs, ...), custom_call_target="tpu_custom_call" | custom-call | tf_op jit(solution)/shard_map/self_back/pallas_call | solution.py:680
  647.6 10.0 last.1
  660.9 9.1 text_back.1
  674.0 64.9 %reduce-scatter.28.cloned.1.call-done = f32[128,3]{1,0:T(8,128)} async-done(((f32[1024,3]{1,0:T(8,128)}), f32[128,3]{1,0:T(8,128)}) %reduce-scatter.28.cloned.1.call-update) | async-done | bytes 1552
  740.4 36.1 %reduce-scatter.30.cloned.1.call-done = f32[128,3]{1,0:T(8,128)} async-done(((f32[1024,3]{1,0:T(8,128)}), f32[128,3]{1,0:T(8,128)}) %reduce-scatter.30.cloned.1.call-update) | async-done | bytes 1552
  777.9 43.0 %reduce-scatter.20.cloned.1.call-done = f32[2,128,256]{2,1,0:T(8,128)} async-done(((f32[2,1024,256]{2,1,0:T(8,128)}), f32[2,128,256]{2,1,0:T(8,128)}) %reduce-scatter.20.cloned.1.call-update) | async-done | bytes 262160 | tf_op jit(solution)/shard_map/reduce_scatter | solution.py:763
  822.8 38.2 %reduce-scatter.16.cloned.1.call-done = f32[32,1024]{1,0:T(8,128)} async-done(((f32[256,1024]{1,0:T(8,128)}), f32[32,1024]{1,0:T(8,128)}) %reduce-scatter.16.cloned.1.call-update) | async-done | bytes 131088 | tf_op jit(solution)/shard_map/reduce_scatter | solution.py:763
  861.0 40.0 %reduce-scatter.18.cloned.1.call-done = f32[128,256]{1,0:T(8,128)} async-done(((f32[1024,256]{1,0:T(8,128)}), f32[128,256]{1,0:T(8,128)}) %reduce-scatter.18.cloned.1.call-update) | async-done | bytes 131088 | tf_op jit(solution)/shard_map/reduce_scatter | solution.py:763
  900.9 40.0 %reduce-scatter.22.cloned.1.call-done = f32[32,1024]{1,0:T(8,128)} async-done(((f32[256,1024]{1,0:T(8,128)}), f32[32,1024]{1,0:T(8,128)}) %reduce-scatter.22.cloned.1.call-update) | async-done | bytes 131088 | tf_op jit(solution)/shard_map/reduce_scatter | solution.py:763
  940.9 50.6 %reduce-scatter.14.cloned.1.call-done = f32[3,128,256]{2,1,0:T(8,128)} async-done(((f32[3,1024,256]{2,1,0:T(8,128)}), f32[3,128,256]{2,1,0:T(8,128)}) %reduce-scatter.14.cloned.1.call-update) | async-done | bytes 393232 | tf_op jit(solution)/shard_map/reduce_scatter | solution.py:763
  991.5 55.3 %reduce-scatter.24.cloned.1.call-done = f32[128,1024]{1,0:T(8,128)} async-done(((f32[1024,1024]{1,0:T(8,128)}), f32[128,1024]{1,0:T(8,128)}) %reduce-scatter.24.cloned.1.call-update) | async-done | bytes 524304 | tf_op jit(solution)/shard_map/reduce_scatter | solution.py:763
  1046.8 55.7 %reduce-scatter.26.cloned.1.call-done = f32[128,1024]{1,0:T(8,128)} async-done(((f32[1024,1024]{1,0:T(8,128)}), f32[128,1024]{1,0:T(8,128)}) %reduce-scatter.26.cloned.1.call-update) | async-done | bytes 524304 | tf_op jit(solution)/shard_map/reduce_scatter | solution.py:763
  (355 shorter events, 97.4 us)
Async XLA Ops:
  7.2 731.7 %reduce-scatter.28.cloned.1.call-start = ((), (), s32[]{:S(2)}) async-start(), calls=%async_computation.16 | async-start | bytes 589824
  39.4 24.4 %collective-permute-start = (f32[6,128,256]{2,1,0:T(8,128)S(1)}, f32[6,128,256]{2,1,0:T(8,128)S(1)}, u32[]{:S(2)}, u32[]{:S(2)}) collective-permute-start(f32[6,128,256]{2,1,0:T(8,128)S(1)} %fusion.4), channel_id=1, source_target_pairs={{0,1},{1,2},{2,3},{3,0},{4,5},{5,6},{6,7},{7,4},{8,9},{9,10},{10,1... | collective-permute-start | bytes 2359304 | tf_op jit(solution)/shard_map/ppermute | solution.py:756
  39.7 42.9 %collective-permute-start.20 = (f32[6,128,256]{2,1,0:T(8,128)S(1)}, f32[6,128,256]{2,1,0:T(8,128)S(1)}, u32[]{:S(2)}, u32[]{:S(2)}) collective-permute-start(f32[6,128,256]{2,1,0:T(8,128)S(1)} %fusion.4), channel_id=1, source_target_pairs={{0,3},{1,0},{2,1},{3,2},{4,7},{5,4},{6,5},{7,6},{8,11},{9,8},{10,9... | collective-permute-start | bytes 2359304 | tf_op jit(solution)/shard_map/ppermute | solution.py:757
  56.7 46.5 %collective-permute-start.60 = (f32[2,128,1024]{2,1,0:T(8,128)S(1)}, f32[2,128,1024]{2,1,0:T(8,128)S(1)}, u32[]{:S(2)}, u32[]{:S(2)}) collective-permute-start(f32[2,128,1024]{2,1,0:T(8,128)S(1)} %fusion.1), channel_id=1, source_target_pairs={{0,1},{1,2},{2,3},{3,0},{4,5},{5,6},{6,7},{7,4},{8,9},{9,10},{10,1... | collective-permute-start | bytes 3145736 | tf_op jit(solution)/shard_map/ppermute | solution.py:756
  57.3 25.5 %collective-permute-start.37 = (f32[1,32,1024]{2,1,0:T(8,128)S(1)}, f32[1,32,1024]{2,1,0:T(8,128)S(1)}, u32[]{:S(2)}, u32[]{:S(2)}) collective-permute-start(f32[1,32,1024]{2,1,0:T(8,128)S(1)} %collective-permute-done.36.refs_18_), channel_id=1, source_target_pairs={{0,4},{4,0},{8,12},{12,8},{16,20},{20,16},{24,28},{28,24},{1,5},{5... | collective-permute-start | bytes 393224 | tf_op jit(solution)/shard_map/ppermute | solution.py:726
  57.6 26.7 %collective-permute-start.39 = (f32[1,32,1024]{2,1,0:T(8,128)S(1)}, f32[1,32,1024]{2,1,0:T(8,128)S(1)}, u32[]{:S(2)}, u32[]{:S(2)}) collective-permute-start(f32[1,32,1024]{2,1,0:T(8,128)S(1)} %collective-permute-done.38.refs_26_), channel_id=1, source_target_pairs={{0,4},{4,0},{8,12},{12,8},{16,20},{20,16},{24,28},{28,24},{1,5},{5... | collective-permute-start | bytes 393224 | tf_op jit(solution)/shard_map/ppermute | solution.py:726
  63.8 59.1 %collective-permute-start.70 = (f32[2,128,1024]{2,1,0:T(8,128)S(1)}, f32[2,128,1024]{2,1,0:T(8,128)S(1)}, u32[]{:S(2)}, u32[]{:S(2)}) collective-permute-start(f32[2,128,1024]{2,1,0:T(8,128)S(1)} %fusion.1), channel_id=1, source_target_pairs={{0,3},{1,0},{2,1},{3,2},{4,7},{5,4},{6,5},{7,6},{8,11},{9,8},{10,9... | collective-permute-start | bytes 3145736 | tf_op jit(solution)/shard_map/ppermute | solution.py:757
  90.1 51.0 %collective-permute-start.10 = (f32[6,128,256]{2,1,0:T(8,128)S(1)}, f32[6,128,256]{2,1,0:T(8,128)S(1)}, u32[]{:S(2)}, u32[]{:S(2)}) collective-permute-start(f32[6,128,256]{2,1,0:T(8,128)S(1)} %collective-permute-done.refs_0_.refs_8_), channel_id=1, source_target_pairs={{0,1},{1,2},{2,3},{3,0},{4,5},{5,6},{6,7},{7,4},{8,9},{9,10},{10,1... | collective-permute-start | bytes 2359304 | tf_op jit(solution)/shard_map/ppermute | solution.py:758
  91.8 50.8 %collective-permute-start.4 = (f32[6,128,256]{2,1,0:T(8,128)S(1)}, f32[6,128,256]{2,1,0:T(8,128)S(1)}, u32[]{:S(2)}, u32[]{:S(2)}) collective-permute-start(f32[6,128,256]{2,1,0:T(8,128)S(1)} %collective-permute-done.refs_0_.refs_8_), channel_id=1, source_target_pairs={{0,16},{4,20},{8,24},{12,28},{16,0},{20,4},{24,8},{28,12},{1,17},{... | collective-permute-start | bytes 2359304 | tf_op jit(solution)/shard_map/ppermute | solution.py:726
  93.9 48.8 %collective-permute-start.2 = (f32[6,128,256]{2,1,0:T(8,128)S(1)}, f32[6,128,256]{2,1,0:T(8,128)S(1)}, u32[]{:S(2)}, u32[]{:S(2)}) collective-permute-start(f32[6,128,256]{2,1,0:T(8,128)S(1)} %collective-permute-done.refs_0_.refs_8_), channel_id=1, source_target_pairs={{0,8},{4,12},{8,0},{12,4},{16,24},{20,28},{24,16},{28,20},{1,9},{5... | collective-permute-start | bytes 2359304 | tf_op jit(solution)/shard_map/ppermute | solution.py:726
  103.2 40.1 %collective-permute-start.1 = (f32[6,128,256]{2,1,0:T(8,128)S(1)}, f32[6,128,256]{2,1,0:T(8,128)S(1)}, u32[]{:S(2)}, u32[]{:S(2)}) collective-permute-start(f32[6,128,256]{2,1,0:T(8,128)S(1)} %collective-permute-done.refs_0_.refs_8_), channel_id=1, source_target_pairs={{0,4},{4,0},{8,12},{12,8},{16,20},{20,16},{24,28},{28,24},{1,5},{5... | collective-permute-start | bytes 2359304 | tf_op jit(solution)/shard_map/ppermute | solution.py:726
  122.9 20.9 %collective-permute-start.24 = (f32[6,128,256]{2,1,0:T(8,128)S(1)}, f32[6,128,256]{2,1,0:T(8,128)S(1)}, u32[]{:S(2)}, u32[]{:S(2)}) collective-permute-start(f32[6,128,256]{2,1,0:T(8,128)S(1)} %collective-permute-done.20.refs_0_.refs_8_), channel_id=1, source_target_pairs={{0,16},{4,20},{8,24},{12,28},{16,0},{20,4},{24,8},{28,12},{1,17},{... | collective-permute-start | bytes 2359304 | tf_op jit(solution)/shard_map/ppermute | solution.py:726
  141.1 20.5 %collective-permute-start.22 = (f32[6,128,256]{2,1,0:T(8,128)S(1)}, f32[6,128,256]{2,1,0:T(8,128)S(1)}, u32[]{:S(2)}, u32[]{:S(2)}) collective-permute-start(f32[6,128,256]{2,1,0:T(8,128)S(1)} %collective-permute-done.20.refs_0_.refs_8_), channel_id=1, source_target_pairs={{0,8},{4,12},{8,0},{12,4},{16,24},{20,28},{24,16},{28,20},{1,9},{5... | collective-permute-start | bytes 2359304 | tf_op jit(solution)/shard_map/ppermute | solution.py:726
  142.6 20.5 %collective-permute-start.21 = (f32[6,128,256]{2,1,0:T(8,128)S(1)}, f32[6,128,256]{2,1,0:T(8,128)}, u32[]{:S(2)}, u32[]{:S(2)}) collective-permute-start(f32[6,128,256]{2,1,0:T(8,128)S(1)} %collective-permute-done.20.refs_0_.refs_8_), channel_id=1, source_target_pairs={{0,4},{4,0},{8,12},{12,8},{16,20},{20,16},{24,28},{28,24},{1,5},{5... | collective-permute-start | bytes 2359304 | tf_op jit(solution)/shard_map/ppermute | solution.py:726
  142.7 43.5 %collective-permute-start.64 = (f32[2,128,1024]{2,1,0:T(8,128)S(1)}, f32[2,128,1024]{2,1,0:T(8,128)S(1)}, u32[]{:S(2)}, u32[]{:S(2)}) collective-permute-start(f32[2,128,1024]{2,1,0:T(8,128)S(1)} %collective-permute-done.60.refs_0_.refs_8_), channel_id=1, source_target_pairs={{0,16},{4,20},{8,24},{12,28},{16,0},{20,4},{24,8},{28,12},{1,17},{... | collective-permute-start | bytes 3145736 | tf_op jit(solution)/shard_map/ppermute | solution.py:726
  143.3 26.7 %collective-permute-start.6 = (f32[3,128,256]{2,1,0:T(8,128)S(1)}, f32[3,128,256]{2,1,0:T(8,128)S(1)}, u32[]{:S(2)}, u32[]{:S(2)}) collective-permute-start(f32[3,128,256]{2,1,0:T(8,128)S(1)} %slice.120), channel_id=1, source_target_pairs={{0,8},{4,12},{8,0},{12,4},{16,24},{20,28},{24,16},{28,20},{1,9},{5... | collective-permute-start | bytes 1179656 | tf_op jit(solution)/shard_map/ppermute | solution.py:726
  143.9 33.3 %collective-permute-start.8 = (f32[3,128,256]{2,1,0:T(8,128)S(1)}, f32[3,128,256]{2,1,0:T(8,128)S(1)}, u32[]{:S(2)}, u32[]{:S(2)}) collective-permute-start(f32[3,128,256]{2,1,0:T(8,128)S(1)} %slice.121), channel_id=1, source_target_pairs={{0,16},{4,20},{8,24},{12,28},{16,0},{20,4},{24,8},{28,12},{1,17},{... | collective-permute-start | bytes 1179656 | tf_op jit(solution)/shard_map/ppermute | solution.py:726
  163.1 37.8 %collective-permute-start.62 = (f32[2,128,1024]{2,1,0:T(8,128)S(1)}, f32[2,128,1024]{2,1,0:T(8,128)S(1)}, u32[]{:S(2)}, u32[]{:S(2)}) collective-permute-start(f32[2,128,1024]{2,1,0:T(8,128)S(1)} %collective-permute-done.60.refs_0_.refs_8_), channel_id=1, source_target_pairs={{0,8},{4,12},{8,0},{12,4},{16,24},{20,28},{24,16},{28,20},{1,9},{5... | collective-permute-start | bytes 3145736 | tf_op jit(solution)/shard_map/ppermute | solution.py:726
  177.2 23.8 %collective-permute-start.61 = (f32[2,128,1024]{2,1,0:T(8,128)S(1)}, f32[2,128,1024]{2,1,0:T(8,128)}, u32[]{:S(2)}, u32[]{:S(2)}) collective-permute-start(f32[2,128,1024]{2,1,0:T(8,128)S(1)} %collective-permute-done.60.refs_0_.refs_8_), channel_id=1, source_target_pairs={{0,4},{4,0},{8,12},{12,8},{16,20},{20,16},{24,28},{28,24},{1,5},{5... | collective-permute-start | bytes 3145736 | tf_op jit(solution)/shard_map/ppermute | solution.py:726
  178.5 29.6 %collective-permute-start.74 = (f32[2,128,1024]{2,1,0:T(8,128)S(1)}, f32[2,128,1024]{2,1,0:T(8,128)S(1)}, u32[]{:S(2)}, u32[]{:S(2)}) collective-permute-start(f32[2,128,1024]{2,1,0:T(8,128)S(1)} %collective-permute-done.70.refs_0_.refs_8_), channel_id=1, source_target_pairs={{0,16},{4,20},{8,24},{12,28},{16,0},{20,4},{24,8},{28,12},{1,17},{... | collective-permute-start | bytes 3145736 | tf_op jit(solution)/shard_map/ppermute | solution.py:726
  185.7 37.7 %collective-permute-start.72 = (f32[2,128,1024]{2,1,0:T(8,128)S(1)}, f32[2,128,1024]{2,1,0:T(8,128)S(1)}, u32[]{:S(2)}, u32[]{:S(2)}) collective-permute-start(f32[2,128,1024]{2,1,0:T(8,128)S(1)} %collective-permute-done.70.refs_0_.refs_8_), channel_id=1, source_target_pairs={{0,8},{4,12},{8,0},{12,4},{16,24},{20,28},{24,16},{28,20},{1,9},{5... | collective-permute-start | bytes 3145736 | tf_op jit(solution)/shard_map/ppermute | solution.py:726
  186.2 37.2 %collective-permute-start.71 = (f32[2,128,1024]{2,1,0:T(8,128)S(1)}, f32[2,128,1024]{2,1,0:T(8,128)S(1)}, u32[]{:S(2)}, u32[]{:S(2)}) collective-permute-start(f32[2,128,1024]{2,1,0:T(8,128)S(1)} %collective-permute-done.70.refs_0_.refs_8_), channel_id=1, source_target_pairs={{0,4},{4,0},{8,12},{12,8},{16,20},{20,16},{24,28},{28,24},{1,5},{5... | collective-permute-start | bytes 3145736 | tf_op jit(solution)/shard_map/ppermute | solution.py:726
  200.9 23.0 %collective-permute-start.80 = (f32[2,128,1024]{2,1,0:T(8,128)S(1)}, f32[2,128,1024]{2,1,0:T(8,128)}, u32[]{:S(2)}, u32[]{:S(2)}) collective-permute-start(f32[2,128,1024]{2,1,0:T(8,128)S(1)} %collective-permute-done.60.refs_0_.refs_8_), channel_id=1, source_target_pairs={{0,1},{1,2},{2,3},{3,0},{4,5},{5,6},{6,7},{7,4},{8,9},{9,10},{10,1... | collective-permute-start | bytes 3145736 | tf_op jit(solution)/shard_map/ppermute | solution.py:758
  201.0 23.6 %collective-permute-start.14 = (f32[6,128,256]{2,1,0:T(8,128)S(1)}, f32[6,128,256]{2,1,0:T(8,128)S(1)}, u32[]{:S(2)}, u32[]{:S(2)}) collective-permute-start(f32[6,128,256]{2,1,0:T(8,128)S(1)} %collective-permute-done.10.refs_0_.refs_8_), channel_id=1, source_target_pairs={{0,16},{4,20},{8,24},{12,28},{16,0},{20,4},{24,8},{28,12},{1,17},{... | collective-permute-start | bytes 2359304 | tf_op jit(solution)/shard_map/ppermute | solution.py:726
  208.1 29.9 %collective-permute-start.12 = (f32[6,128,256]{2,1,0:T(8,128)S(1)}, f32[6,128,256]{2,1,0:T(8,128)S(1)}, u32[]{:S(2)}, u32[]{:S(2)}) collective-permute-start(f32[6,128,256]{2,1,0:T(8,128)S(1)} %collective-permute-done.10.refs_0_.refs_8_), channel_id=1, source_target_pairs={{0,8},{4,12},{8,0},{12,4},{16,24},{20,28},{24,16},{28,20},{1,9},{5... | collective-permute-start | bytes 2359304 | tf_op jit(solution)/shard_map/ppermute | solution.py:726
  243.9 23.5 %collective-permute-start.76 = (f32[1,128,1024]{2,1,0:T(8,128)S(1)}, f32[1,128,1024]{2,1,0:T(8,128)S(1)}, u32[]{:S(2)}, u32[]{:S(2)}) collective-permute-start(f32[1,128,1024]{2,1,0:T(8,128)S(1)} %slice.134), channel_id=1, source_target_pairs={{0,8},{4,12},{8,0},{12,4},{16,24},{20,28},{24,16},{28,20},{1,9},{5... | collective-permute-start | bytes 1572872 | tf_op jit(solution)/shard_map/ppermute | solution.py:726
  245.4 32.0 %collective-permute-start.63 = (f32[2,128,1024]{2,1,0:T(8,128)S(1)}, f32[2,128,1024]{2,1,0:T(8,128)S(1)}, u32[]{:S(2)}, u32[]{:S(2)}) collective-permute-start(f32[2,128,1024]{2,1,0:T(8,128)S(1)} %collective-permute-done.62.refs_2_.refs_10_), channel_id=1, source_target_pairs={{0,4},{4,0},{8,12},{12,8},{16,20},{20,16},{24,28},{28,24},{1,5},{5... | collective-permute-start | bytes 3145736 | tf_op jit(solution)/shard_map/ppermute | solution.py:726
  245.5 22.9 %collective-permute-start.78 = (f32[1,128,1024]{2,1,0:T(8,128)S(1)}, f32[1,128,1024]{2,1,0:T(8,128)S(1)}, u32[]{:S(2)}, u32[]{:S(2)}) collective-permute-start(f32[1,128,1024]{2,1,0:T(8,128)S(1)} %slice.135), channel_id=1, source_target_pairs={{0,16},{4,20},{8,24},{12,28},{16,0},{20,4},{24,8},{28,12},{1,17},{... | collective-permute-start | bytes 1572872 | tf_op jit(solution)/shard_map/ppermute | solution.py:726
  256.1 18.9 %collective-permute-start.16 = (f32[3,128,256]{2,1,0:T(8,128)S(1)}, f32[3,128,256]{2,1,0:T(8,128)S(1)}, u32[]{:S(2)}, u32[]{:S(2)}) collective-permute-start(f32[3,128,256]{2,1,0:T(8,128)S(1)} %slice.122), channel_id=1, source_target_pairs={{0,8},{4,12},{8,0},{12,4},{16,24},{20,28},{24,16},{28,20},{1,9},{5... | collective-permute-start | bytes 1179656 | tf_op jit(solution)/shard_map/ppermute | solution.py:726
  258.0 20.9 %collective-permute-start.65 = (f32[2,128,1024]{2,1,0:T(8,128)S(1)}, f32[2,128,1024]{2,1,0:T(8,128)S(1)}, u32[]{:S(2)}, u32[]{:S(2)}) collective-permute-start(f32[2,128,1024]{2,1,0:T(8,128)S(1)} %collective-permute-done.64.refs_4_.refs_12_), channel_id=1, source_target_pairs={{0,4},{4,0},{8,12},{12,8},{16,20},{20,16},{24,28},{28,24},{1,5},{5... | collective-permute-start | bytes 3145736 | tf_op jit(solution)/shard_map/ppermute | solution.py:726
  276.9 24.0 %collective-permute-start.84 = (f32[2,128,1024]{2,1,0:T(8,128)}, f32[2,128,1024]{2,1,0:T(8,128)}, u32[]{:S(2)}, u32[]{:S(2)}) collective-permute-start(f32[2,128,1024]{2,1,0:T(8,128)} %collective-permute-done.80.refs_0_.refs_8_), channel_id=1, source_target_pairs={{0,16},{4,20},{8,24},{12,28},{16,0},{20,4},{24,8},{28,12},{1,17},{... | collective-permute-start | bytes 3145736 | tf_op jit(solution)/shard_map/ppermute | solution.py:726
  277.4 23.7 %collective-permute-start.82 = (f32[2,128,1024]{2,1,0:T(8,128)}, f32[2,128,1024]{2,1,0:T(8,128)}, u32[]{:S(2)}, u32[]{:S(2)}) collective-permute-start(f32[2,128,1024]{2,1,0:T(8,128)} %collective-permute-done.80.refs_0_.refs_8_), channel_id=1, source_target_pairs={{0,8},{4,12},{8,0},{12,4},{16,24},{20,28},{24,16},{28,20},{1,9},{5... | collective-permute-start | bytes 3145736 | tf_op jit(solution)/shard_map/ppermute | solution.py:726
  278.9 23.5 %collective-permute-start.13 = (f32[6,128,256]{2,1,0:T(8,128)S(1)}, f32[6,128,256]{2,1,0:T(8,128)S(1)}, u32[]{:S(2)}, u32[]{:S(2)}) collective-permute-start(f32[6,128,256]{2,1,0:T(8,128)S(1)} %collective-permute-done.12.refs_2_.refs_10_), channel_id=1, source_target_pairs={{0,4},{4,0},{8,12},{12,8},{16,20},{20,16},{24,28},{28,24},{1,5},{5... | collective-permute-start | bytes 2359304 | tf_op jit(solution)/shard_map/ppermute | solution.py:726
  279.0 22.4 %collective-permute-start.17 = (f32[3,128,256]{2,1,0:T(8,128)S(1)}, f32[3,128,256]{2,1,0:T(8,128)S(1)}, u32[]{:S(2)}, u32[]{:S(2)}) collective-permute-start(f32[3,128,256]{2,1,0:T(8,128)S(1)} %collective-permute-done.16.refs_6_), channel_id=1, source_target_pairs={{0,4},{4,0},{8,12},{12,8},{16,20},{20,16},{24,28},{28,24},{1,5},{5... | collective-permute-start | bytes 1179656 | tf_op jit(solution)/shard_map/ppermute | solution.py:726
  279.5 22.7 %collective-permute-start.19 = (f32[3,128,256]{2,1,0:T(8,128)S(1)}, f32[3,128,256]{2,1,0:T(8,128)S(1)}, u32[]{:S(2)}, u32[]{:S(2)}) collective-permute-start(f32[3,128,256]{2,1,0:T(8,128)S(1)} %collective-permute-done.18.refs_14_), channel_id=1, source_target_pairs={{0,4},{4,0},{8,12},{12,8},{16,20},{20,16},{24,28},{28,24},{1,5},{5... | collective-permute-start | bytes 1179656 | tf_op jit(solution)/shard_map/ppermute | solution.py:726
  308.9 194.5 %collective-permute-start.81 = (f32[2,128,1024]{2,1,0:T(8,128)}, f32[2,128,1024]{2,1,0:T(8,128)S(1)}, u32[]{:S(2)}, u32[]{:S(2)}) collective-permute-start(f32[2,128,1024]{2,1,0:T(8,128)} %collective-permute-done.80.refs_0_.refs_8_), channel_id=1, source_target_pairs={{0,4},{4,0},{8,12},{12,8},{16,20},{20,16},{24,28},{28,24},{1,5},{5... | collective-permute-start | bytes 3145736 | tf_op jit(solution)/shard_map/ppermute | solution.py:726
  309.0 194.4 %collective-permute-start.83 = (f32[2,128,1024]{2,1,0:T(8,128)}, f32[2,128,1024]{2,1,0:T(8,128)}, u32[]{:S(2)}, u32[]{:S(2)}) collective-permute-start(f32[2,128,1024]{2,1,0:T(8,128)} %collective-permute-done.82.refs_2_.refs_10_), channel_id=1, source_target_pairs={{0,4},{4,0},{8,12},{12,8},{16,20},{20,16},{24,28},{28,24},{1,5},{5... | collective-permute-start | bytes 3145736 | tf_op jit(solution)/shard_map/ppermute | solution.py:726
  309.6 193.9 %collective-permute-start.85 = (f32[2,128,1024]{2,1,0:T(8,128)}, f32[2,128,1024]{2,1,0:T(8,128)}, u32[]{:S(2)}, u32[]{:S(2)}) collective-permute-start(f32[2,128,1024]{2,1,0:T(8,128)} %collective-permute-done.84.refs_4_.refs_12_), channel_id=1, source_target_pairs={{0,4},{4,0},{8,12},{12,8},{16,20},{20,16},{24,28},{28,24},{1,5},{5... | collective-permute-start | bytes 3145736 | tf_op jit(solution)/shard_map/ppermute | solution.py:726
  320.2 183.2 %collective-permute-start.87 = (f32[1,128,1024]{2,1,0:T(8,128)}, f32[1,128,1024]{2,1,0:T(8,128)}, u32[]{:S(2)}, u32[]{:S(2)}) collective-permute-start(f32[1,128,1024]{2,1,0:T(8,128)} %collective-permute-done.86.refs_6_), channel_id=1, source_target_pairs={{0,4},{4,0},{8,12},{12,8},{16,20},{20,16},{24,28},{28,24},{1,5},{5... | collective-permute-start | bytes 1572872 | tf_op jit(solution)/shard_map/ppermute | solution.py:726
  321.3 182.1 %collective-permute-start.89 = (f32[1,128,1024]{2,1,0:T(8,128)}, f32[1,128,1024]{2,1,0:T(8,128)}, u32[]{:S(2)}, u32[]{:S(2)}) collective-permute-start(f32[1,128,1024]{2,1,0:T(8,128)} %collective-permute-done.88.refs_14_), channel_id=1, source_target_pairs={{0,4},{4,0},{8,12},{12,8},{16,20},{20,16},{24,28},{28,24},{1,5},{5... | collective-permute-start | bytes 1572872 | tf_op jit(solution)/shard_map/ppermute | solution.py:726
  659.5 116.9 %reduce-scatter.30.cloned.1.call-start = ((), (), s32[]{:S(2)}) async-start(), calls=%async_computation.17 | async-start | bytes 589824
  660.6 160.3 %reduce-scatter.20.cloned.1.call-start = ((), (), s32[]{:S(2)}) async-start(), calls=%async_computation.12 | async-start | bytes 2359296 | tf_op jit(solution)/shard_map/reduce_scatter | solution.py:763
  670.0 191.0 %reduce-scatter.16.cloned.1.call-start = ((), (), s32[]{:S(2)}) async-start(), calls=%async_computation.10 | async-start | bytes 1179648 | tf_op jit(solution)/shard_map/reduce_scatter | solution.py:763
  670.6 230.4 %reduce-scatter.18.cloned.1.call-start = ((), (), s32[]{:S(2)}) async-start(), calls=%async_computation.11 | async-start | bytes 1179648 | tf_op jit(solution)/shard_map/reduce_scatter | solution.py:763
  671.1 269.8 %reduce-scatter.22.cloned.1.call-start = ((), (), s32[]{:S(2)}) async-start(), calls=%async_computation.13 | async-start | bytes 1179648 | tf_op jit(solution)/shard_map/reduce_scatter | solution.py:763
  671.7 319.8 %reduce-scatter.14.cloned.1.call-start = ((), (), s32[]{:S(2)}) async-start(), calls=%async_computation.9 | async-start | bytes 3538944 | tf_op jit(solution)/shard_map/reduce_scatter | solution.py:763
  672.5 374.3 %reduce-scatter.24.cloned.1.call-start = ((), (), s32[]{:S(2)}) async-start(), calls=%async_computation.14 | async-start | bytes 4718592 | tf_op jit(solution)/shard_map/reduce_scatter | solution.py:763
  673.2 429.3 %reduce-scatter.26.cloned.1.call-start = ((), (), s32[]{:S(2)}) async-start(), calls=%async_computation.15 | async-start | bytes 4718592 | tf_op jit(solution)/shard_map/reduce_scatter | solution.py:763
  (122 other events, 4137.6 us)
Sparse Core Ops, SparseCore 0:
  659.7 79.1 reduce-scatter.27
  742.3 34.1 reduce-scatter.29
  779.7 41.1 reduce-scatter.19
  824.9 36.0 reduce-scatter.15
  864.9 35.9 reduce-scatter.17
  904.9 35.9 reduce-scatter.21
  945.2 46.2 reduce-scatter.13
  995.4 51.2 reduce-scatter.23
  1051.1 51.3 reduce-scatter.25

commit v2 on v1

--- a/solution.py
+++ b/solution.py
@@ -9,7 +9,6 @@
 
 HEAD = 64
 BLK = 256
-SLOTS8 = 8
 EPS = 1e-05
 NEG = -1e30
 F32 = jnp.float32
@@ -27,6 +26,12 @@
 
 def params(mib=56, semantics=None):
     return pltpu.CompilerParams(vmem_limit_bytes=mib * MIB, dimension_semantics=semantics)
+
+
+def cost(us):
+    return pl.CostEstimate(
+        flops=int(us * 1.15e9), transcendentals=0, bytes_accessed=int(us * 3.6e6)
+    )
 
 
 def shape(dims, dtype=F32):
@@ -91,6 +96,7 @@
         out_specs=rows_of(BLK, width),
         out_shape=shape((rows, width), BF16),
         name="norm_first",
+        cost_estimate=cost(6),
     )(tokens, gain, shift)
 
 
@@ -113,11 +119,34 @@
     return item, start
 
 
-def fill(target, slots, me, rows):
-    for index, ref in enumerate(slots):
-        place = pl.multiple_of((me ^ index) * rows, rows)
-        for k in range(ref.shape[0]):
-            target[k, pl.ds(place, rows), :] = ref[k].astype(BF16)
+def offsets(core):
+    return (0, 1 + core, 2 - core, 3)
+
+
+def fill(targets, refs, chip, core):
+    for ref, offset in zip(refs, offsets(core)):
+        rows = ref.shape[1]
+        place = pl.multiple_of((chip ^ offset) * rows, rows)
+        for k, target in enumerate(targets):
+            target[pl.ds(place, rows), :] = ref[k].astype(BF16)
+
+
+def fill_two(first, second, mine, other, me, flip=1):
+    chip, core = me[0], me[1]
+
+    @pl.when(core == 0)
+    def _():
+        fill(first, mine, chip, 0)
+        fill(second, other, chip, 1)
+
+    @pl.when(core == 1)
+    def _():
+        fill(second[::flip], mine, chip, 1)
+        fill(first[::flip], other, chip, 0)
+
+
+def planes(ref):
+    return [ref.at[k] for k in range(ref.shape[0])]
 
 
 def causal():
@@ -161,12 +190,10 @@
     mixed[pl.ds(q0, BLK), :] = jnp.concatenate(pieces, axis=0).T.astype(BF16)
 
 
-def front_body(lengths, first, text, weights, cross, qkv, mixed, logs, pair, turned):
+def front_body(lengths, first, weights, qkv, mixed, logs, turned):
     rows = first.shape[0]
     for m in range(3):
         qkv[m] = dot(first[...], weights[m]).astype(BF16)
-    for m in range(2):
-        pair[m] = dot(text[...], cross[m + 1]).astype(BF16)
     turned[...] = qkv[2].T
 
     @pl.loop(0, rows // BLK)
@@ -180,73 +207,85 @@
                 self_block(qb, n, qkv, turned, mixed, logs)
 
 
-def front_kernel(me, lengths, first, text, *refs):
-    slots, (weights, cross, *rest) = refs[:16], refs[16:]
-    rows = slots[0].shape[1]
-    fill(weights, slots[:8], me[0], rows)
-    fill(cross, slots[8:], me[0], rows)
-    front_body(lengths, first, text, weights, cross, *rest)
-
-
-def front_outs(rows, text_rows, width):
-    return [
+def front_kernel(own, me, lengths, first, *refs):
+    slots, (weights, *rest) = refs[:4], refs[4:]
+    core = me[1] if own else 1 - me[1]
+    fill(planes(weights), slots, me[0], core)
+    front_body(lengths, first, weights, *rest)
+
+
+def front_two_kernel(me, lengths, first, *refs):
+    mine, other, (weights, cross, *rest) = refs[:4], refs[4:8], refs[8:]
+    fill_two(planes(weights), planes(cross), mine, other, me)
+    front_body(lengths, first, weights, *rest)
+
+
+def vmem():
+    return pl.BlockSpec(memory_space=pltpu.VMEM)
+
+
+def front_call(kernel, name, us, prefix, first, arrays, weight_count):
+    rows, depth = first.shape
+    width = arrays[0].shape[2]
+    outs = [shape((3, depth, width), BF16)] * weight_count + [
         shape((3, rows, width), BF16),
         shape((rows, width), BF16),
         shape((8, rows), F32),
-        shape((2, text_rows, width), BF16),
     ]
-
-
-def vmem():
-    return pl.BlockSpec(memory_space=pltpu.VMEM)
-
-
-def front_own(lengths, first, text, weights, cross):
-    rows, _ = first.shape
-    width = weights.shape[2]
-    return pl.pallas_call(
-        front_body,
-        in_specs=[smem()] + [vmem()] * 4,
-        out_specs=[vmem()] * 4,
-        out_shape=front_outs(rows, text.shape[0], width),
-        scratch_shapes=[pltpu.VMEM((width, rows), BF16)],
-        compiler_params=params(),
-        name="front_own",
-    )(lengths, first, text, weights, cross)
-
-
-def halves(slots):
-    arrays, specs = [], []
-    for half, group in enumerate(slots):
-        for index, array in enumerate(group):
-            size = group[6].shape
-            arrays.append(array)
-            specs.append(at(size, (half if index < 6 else 0, 0, 0)))
-    return arrays, specs
-
-
-def front(me, lengths, first, text, slots):
-    rows, depth = first.shape
-    arrays, specs = halves(slots)
-    width = arrays[0].shape[2]
-    outs = [shape((3, depth, width), BF16)] * 2 + front_outs(rows, text.shape[0], width)
-    return pl.pallas_call(
-        front_kernel,
-        grid=(1,),
-        in_specs=[smem(), smem(), vmem(), vmem()] + specs,
-        out_specs=[vmem()] * 6,
+    return pl.pallas_call(
+        kernel,
+        in_specs=[smem()] * len(prefix) + [vmem()] * (1 + len(arrays)),
+        out_specs=[vmem()] * len(outs),
         out_shape=outs,
         scratch_shapes=[pltpu.VMEM((width, rows), BF16)],
         compiler_params=params(),
-        name="front",
-    )(me, lengths, first, text, *arrays)
+        name=name,
+        cost_estimate=cost(us),
+    )(*prefix, first, *arrays)
+
+
+def front_own(lengths, first, weights):
+    return front_call(front_body, "front_own", 12, (lengths,), first, [weights], 0)
+
+
+def front(own, me, lengths, first, arrays):
+    kernel = partial(front_kernel, own)
+    return front_call(kernel, "front", 14, (me, lengths), first, arrays, 1)
+
+
+def front_two(me, lengths, first, arrays):
+    return front_call(front_two_kernel, "front_two", 15, (me, lengths), first, arrays, 2)
+
+
+def text_front_kernel(me, text, own, two, *refs):
+    mine, other, (cross_a, cross_b, *pairs) = refs[:4], refs[4:8], refs[8:]
+    fill(planes(cross_a), mine, me[0], me[1])
+    fill(planes(cross_b), other, me[0], 1 - me[1])
+    for pair, cross in zip(pairs, (own, cross_a, two, cross_b)):
+        for m in range(2):
+            pair[m] = dot(text[...], cross[m + 1]).astype(BF16)
+
+
+def text_front(me, text, own, two, arrays):
+    rows = text.shape[0]
+    width = own.shape[2]
+    outs = [shape(own.shape, BF16)] * 2 + [shape((2, rows, width), BF16)] * 4
+    return pl.pallas_call(
+        text_front_kernel,
+        in_specs=[smem()] + [vmem()] * 11,
+        out_specs=[vmem()] * 6,
+        out_shape=outs,
+        compiler_params=params(),
+        name="text_front",
+        cost_estimate=cost(8),
+    )(me, text, own, two, *arrays)
 
 
 def middle_kernel(me, lengths, live, tokens, gain1, shift1, gain2, shift2, own_out, own_co, *refs):
     mixed, refs = refs[:4], refs[4:]
     queries, refs = refs[:4], refs[4:]
     pairs, refs = refs[:4], refs[4:]
-    slots, refs = refs[:48], refs[48:]
+    mine, other, refs = refs[:4], refs[4:8], refs[8:]
     w_out, w_co, after_self, after_cross, second, third, cross_query, looked, logs, turned = refs
     step = pl.program_id(0)
 
@@ -255,13 +294,10 @@
         width = own_out.shape[0]
         w_out[:width, :] = own_out[...]
         w_co[:width, :] = own_co[...]
-        for j in range(3):
-            for half, target in enumerate((w_out, w_co)):
-                for index in range(SLOTS8):
-                    ref = slots[j * 16 + half * 8 + index]
-                    rows = ref.shape[1]
-                    place = pl.multiple_of((j + 1) * width + (me[0] ^ index) * rows, rows)
-                    target[pl.ds(place, rows), :] = ref[0].astype(BF16)
+        parts = [
+            [target.at[pl.ds((j + 1) * width, width)] for j in range(3)] for target in (w_out, w_co)
+        ]
+        fill_two(*parts, mine, other, me, flip=-1)
         for j in range(4):
             turned[j] = pairs[j][1].T
 
@@ -300,17 +336,12 @@
 TEXT = 128
 
 
-def middle(me, lengths, live, tokens, norms, own_out, own_co, mixed, crosses, pairs, slots):
+def middle(me, lengths, live, tokens, norms, own_out, own_co, mixed, crosses, pairs, arrays):
     rows, depth = tokens.shape
     width = own_out.shape[0]
     text_rows = live.shape[0]
     inner = 4 * width
     row = whole((1, depth))
-    arrays, specs = [], []
-    for entry in slots:
-        more, more_specs = halves(entry)
-        arrays += more
-        specs += more_specs
     return pl.pallas_call(
         middle_kernel,
         grid=(rows // BLK,),
@@ -320,7 +351,7 @@
         + [rows_of(BLK, width)] * 4
         + [at((1, depth, width), (0, 0, 0))] * 4
         + [whole((2, text_rows, width))] * 4
-        + specs,
+        + [whole(arrays[0].shape)] * 8,
         out_specs=[whole((inner, depth))] * 2
         + [rows_of(BLK, depth)] * 4
         + [rows_of(BLK, inner)] * 2
@@ -333,6 +364,7 @@
         scratch_shapes=[pltpu.VMEM((4, width, text_rows), BF16)],
         compiler_params=params(),
         name="middle",
+        cost_estimate=cost(43),
     )(me, lengths, live, tokens, *norms, own_out, own_co, *mixed, *crosses, *pairs, *arrays)
 
 
@@ -356,7 +388,7 @@
     return hidden, pre_grad, dot(hidden, down), dot(pre_grad, up, NT)
 
 
-def feed_own_kernel(third, cot, after, up, down, out, grad, up_grad, down_grad):
+def feed_own_kernel(third, cot, after, up, down, out, grad, both):
     hidden, pre_grad, result, pushed = feed_rows(third[...], cot[...], up[...], down[...])
     out[...] = after[...] + result
     grad[...] = pushed
@@ -366,13 +398,13 @@
 
     @pl.when(first)
     def _():
-        up_grad[...] = more_up
-        down_grad[...] = more_down
+        both[0] = more_up
+        both[1] = more_down
 
     @pl.when(jnp.logical_not(first))
     def _():
-        up_grad[...] += more_up
-        down_grad[...] += more_down
+        both[0] += more_up
+        both[1] += more_down
 
 
 FEED = 320
@@ -386,68 +418,61 @@
         feed_own_kernel,
         grid=(rows // FEED,),
         in_specs=[tile, tile, tile, whole((depth, inner)), whole((inner, depth))],
-        out_specs=[tile, tile, whole((depth, inner)), whole((inner, depth))],
-        out_shape=[
-            shape((rows, depth)),
-            shape((rows, depth)),
-            shape((depth, inner)),
-            shape((inner, depth)),
-        ],
+        out_specs=[tile, tile, whole((2, depth, inner))],
+        out_shape=[shape((rows, depth)), shape((rows, depth)), shape((2, depth, inner))],
         compiler_params=params(),
         name="feed_own",
+        cost_estimate=cost(32),
     )(third, cot, after, up, down)
 
 
-def feed_kernel(me, third, cot, out_in, grad_in, *refs):
-    slots, (out, grad, up, down) = refs[:16], refs[16:]
+def feed_kernel(kind, me, third, cot, out_in, grad_in, *refs):
+    slots, (out, grad, both) = refs[:-3], refs[-3:]
 
     @pl.when(pl.program_id(0) == 0)
     def _():
-        rows = slots[0].shape[1]
-        fill(up, slots[:8], me[0], rows)
-        fill(down, slots[8:], me[0], rows)
-
-    _, _, result, pushed = feed_rows(third[...], cot[...], up[0], down[0])
+        up, down = planes(both)
+        if kind == 2:
+            fill_two([up], [down], slots[:4], slots[4:], me)
+        else:
+            fill([up, down], slots, me[0], me[1] if kind == 0 else 1 - me[1])
+
+    _, _, result, pushed = feed_rows(third[...], cot[...], both[0], both[1])
     out[...] = (out_in[...] + result).astype(out.dtype)
     grad[...] = grad_in[...] + pushed
 
 
-def feed(me, third, cot, out, grad, slots, dtype):
+def feed(kind, me, third, cot, out, grad, arrays, dtype):
     rows, depth = third.shape
-    arrays, specs = halves(slots)
     inner = arrays[0].shape[2]
     tile = rows_of(FEED, depth)
     return pl.pallas_call(
-        feed_kernel,
+        partial(feed_kernel, kind),
         grid=(rows // FEED,),
-        in_specs=[smem(), tile, tile, tile, tile] + specs,
+        in_specs=[smem(), tile, tile, tile, tile] + [whole(arrays[0].shape)] * len(arrays),
         out_specs=[tile, tile],
         out_shape=[shape((rows, depth), dtype), shape((rows, depth))],
-        scratch_shapes=[
-            pltpu.VMEM((1, depth, inner), BF16),
-            pltpu.VMEM((1, 8 * arrays[8].shape[1], depth), BF16),
-        ],
+        scratch_shapes=[pltpu.VMEM((2, depth, inner), BF16)],
         compiler_params=params(),
         name="feed",
+        cost_estimate=cost(18),
     )(me, third, cot, out, grad, *arrays)
 
 
 def back_kernel(
-    lengths, live, third_grad, cot, after_cross, after_self, second, cross_query, looked0, mixed0,
-    logs, gain1, gain2, w_out, w_co, *refs,
+    lengths, live, third_grad, cot, after_cross, after_self, cross_query, looked0, mixed0, logs,
+    gain1, gain2, w_out, w_co, *refs,
 ):
     queries, refs = refs[:4], refs[4:]
     pairs, refs = refs[:4], refs[4:]
-    up_grad, mixed_grad, pair_grad, co_grad, cq_grad, out_grad, sums, total, turned = refs
+    up_grad, mixed_grad, pair_grad, row_grads, query_grads, sums, total, turned = refs
     step = pl.program_id(0)
     text = TEXT
 
     @pl.when(step == 0)
     def _():
         total[...] = jnp.zeros_like(total)
-        co_grad[...] = jnp.zeros_like(co_grad)
-        cq_grad[...] = jnp.zeros_like(cq_grad)
-        out_grad[...] = jnp.zeros_like(out_grad)
+        row_grads[...] = jnp.zeros_like(row_grads)
         sums[...] = jnp.zeros_like(sums)
         for j in range(4):
             turned[j] = pairs[j][0].T
@@ -457,7 +482,7 @@
     sums[1:2, :] += shift_sum
     upstream = cot[...].astype(F32) + pulled
     low = upstream.astype(BF16)
-    co_grad[...] += dot(looked0[...], low, TN)
+    row_grads[1] += dot(looked0[...], low, TN)
     looked_grad = dot(low, w_co[...], NT).astype(BF16)
     item, _ = item_at(lengths, step * BLK)
     t0 = pl.multiple_of(item * text, text)
@@ -490,7 +515,7 @@
         total[j, 1, pl.ds(t0, text), :] += value_sum
         query_grad = (jnp.concatenate(pieces, axis=0).T * HEAD**-0.5).astype(BF16)
         if j == 0:
-            cq_grad[...] += dot(second[...], query_grad, TN)
+            query_grads[...] = query_grad
         second_grad = second_grad + dot(query_grad, queries[j][0], NT)
 
     pulled, gain_sum, shift_sum = norm_backward(second_grad, after_self[...], gain1[...])
@@ -499,7 +524,7 @@
     upstream = upstream + pulled
     up_grad[...] = upstream
     low = upstream.astype(BF16)
-    out_grad[...] += dot(mixed0[...], low, TN)
+    row_grads[0] += dot(mixed0[...], low, TN)
     mixed_grad[...] = dot(low, w_out[...], NT).astype(BF16)
 
     @pl.when(step == pl.num_programs(0) - 1)
@@ -508,8 +533,8 @@
 
 
 def back(
-    lengths, live, third_grad, cot, after_cross, after_self, second, cross_query, looked, mixed0,
-    logs, gain1, gain2, w_out, w_co, crosses, pairs,
+    lengths, live, third_grad, cot, after_cross, after_self, cross_query, looked, mixed0, logs,
+    gain1, gain2, w_out, w_co, crosses, pairs,
 ):
     rows, depth = cot.shape
     text_rows = live.shape[0]
@@ -521,21 +546,20 @@
         back_kernel,
         grid=(rows // BLK,),
         in_specs=[smem(), whole((text_rows, 1))]
-        + [tile] * 5
+        + [tile] * 4
         + [rows_of(BLK, inner), rows_of(BLK, width), rows_of(BLK, width)]
         + [pl.BlockSpec((inner // HEAD, BLK), lambda i: (0, i)), row, row]
         + [whole((inner, depth))] * 2
         + [at((1, depth, width), (0, 0, 0))] * 4
         + [whole((2, text_rows, width))] * 4,
         out_specs=[tile, rows_of(BLK, inner), whole((4, 2, text_rows, width))]
-        + [whole((width, depth)), whole((depth, width)), whole((width, depth)), whole((8, depth))],
+        + [whole((2, width, depth)), rows_of(BLK, width), whole((8, depth))],
         out_shape=[
             shape((rows, depth)),
             shape((rows, inner), BF16),
             shape((4, 2, text_rows, width), BF16),
-            shape((width, depth)),
-            shape((depth, width)),
-            shape((width, depth)),
+            shape((2, width, depth)),
+            shape((rows, width), BF16),
             shape((8, depth)),
         ],
         scratch_shapes=[
@@ -544,34 +568,37 @@
         ],
         compiler_params=params(),
         name="back",
+        cost_estimate=cost(53),
     )(
-        lengths, live, third_grad, cot, after_cross, after_self, second, cross_query, looked,
-        mixed0, logs, gain1, gain2, w_out, w_co, *crosses, *pairs,
-    )
-
-
-def text_kernel(text, pair_grad, *refs):
-    crosses, (text_grad, kv_grad) = refs[:4], refs[4:]
+        lengths, live, third_grad, cot, after_cross, after_self, cross_query, looked, mixed0, logs,
+        gain1, gain2, w_out, w_co, *crosses, *pairs,
+    )
+
+
+def text_kernel(text, pair_grad, second, query_grad, *refs):
+    crosses, (text_grad, cross_grad) = refs[:4], refs[4:]
     total = jnp.zeros(text_grad.shape, F32)
     for j in range(4):
         for m in range(2):
             total = total + dot(pair_grad[j, m], crosses[j][m + 1], NT)
     text_grad[...] = total
+    cross_grad[0] = dot(second[...], query_grad[...], TN)
     for m in range(2):
-        kv_grad[m] = dot(text[...], pair_grad[0, m], TN)
-
-
-def text_back(text, pair_grad, crosses):
+        cross_grad[m + 1] = dot(text[...], pair_grad[0, m], TN)
+
+
+def text_back(text, pair_grad, second, query_grad, crosses):
     text_rows, depth = text.shape
     width = pair_grad.shape[3]
     return pl.pallas_call(
         text_kernel,
-        in_specs=[vmem()] * 6,
+        in_specs=[vmem()] * 8,
         out_specs=[vmem()] * 2,
-        out_shape=[shape((text_rows, depth)), shape((2, depth, width))],
+        out_shape=[shape((text_rows, depth)), shape((3, depth, width))],
         compiler_params=params(),
         name="text_back",
-    )(text, pair_grad, *crosses)
+        cost_estimate=cost(9),
+    )(text, pair_grad, second, query_grad, *crosses)
 
 
 def self_back_pair(qb, kb, diag, qkv, rows, grads, logs, means, turned, query_sum, key_sum, value_sum):
@@ -643,29 +670,42 @@
     ]
 
 
-def self_own_kernel(lengths, qkv, mixed, out_grad, logs, weights, first, total, qkv_grad, *scratch):
-    self_back_body(lengths, qkv, mixed, out_grad, logs, weights, *scratch)
-    triple = scratch[0]
+def self_own_kernel(me, lengths, qkv, mixed, out_grad, logs, weights, first, total, keep, send, *scratch):
+    self_back_body(lengths, qkv, mixed, out_grad, logs, weights, *scratch[:-1])
+    triple, whole_grad = scratch[0], scratch[-1]
     for m in range(3):
-        qkv_grad[m] = dot(first[...], triple[m], TN)
+        whole_grad[m] = dot(first[...], triple[m], TN)
+    put_pieces(whole_grad, keep, send, me)
     total[...] = sum(dot(triple[m], weights[m], NT) for m in range(3))
 
 
-def self_own(lengths, qkv, mixed, out_grad, logs, weights, first):
+def put_pieces(source, keep, send, me):
+    chip, core = me[0], me[1]
+    rows = keep.shape[2]
+    for target, owner in ((keep, core), (send, 1 - core)):
+        for index, offset in enumerate((0, 2 - owner, 1 + owner, 3)):
+            place = pl.multiple_of(((chip ^ offset) * 2 + owner) * rows, rows)
+            for k in range(keep.shape[1]):
+                target[index, k] = source[k, pl.ds(place, rows), :]
+
+
+def self_own(me, lengths, qkv, mixed, out_grad, logs, weights, first):
     rows, depth = first.shape
     width = mixed.shape[1]
+    pieces = (4, 3, depth // 8, width)
     return pl.pallas_call(
         self_own_kernel,
         grid=(1,),
-        in_specs=[smem()]
+        in_specs=[smem(), smem()]
         + [whole((3, rows, width)), whole((rows, width)), at((rows, width), (0, 0))]
         + [whole((8, rows)), whole((3, depth, width)), whole((rows, depth))],
-        out_specs=[whole((rows, depth)), whole((3, depth, width))],
-        out_shape=[shape((rows, depth)), shape((3, depth, width))],
-        scratch_shapes=self_scratch(rows, width),
+        out_specs=[whole((rows, depth)), whole(pieces), whole(pieces)],
+        out_shape=[shape((rows, depth)), shape(pieces), shape(pieces)],
+        scratch_shapes=self_scratch(rows, width) + [pltpu.VMEM((3, depth, width), F32)],
         compiler_params=params(),
         name="self_own",
-    )(lengths, qkv, mixed, out_grad, logs, weights, first)
+        cost_estimate=cost(20),
+    )(me, lengths, qkv, mixed, out_grad, logs, weights, first)
 
 
 def self_kernel(lengths, qkv, mixed, out_grad, logs, weights, before, total, *scratch):
@@ -688,6 +728,7 @@
         scratch_shapes=self_scratch(rows, width),
         compiler_params=params(),
         name="self_back",
+        cost_estimate=cost(17.5),
     )(lengths, qkv, mixed, out_grad, logs, weights, before)
 
 
@@ -715,52 +756,104 @@
         out_shape=[shape((rows, depth)), shape((8, depth))],
         compiler_params=params(),
         name="last",
+        cost_estimate=cost(10),
     )(first_grad, tokens, upstream, gain)
 
 
-UP = [(i, (i + 1) % 4) for i in range(4)]
-DOWN = [(i, (i - 1) % 4) for i in range(4)]
-
-
-def across(value, bit):
-    return lax.ppermute(value, "dp", [(i, i ^ bit) for i in range(8)])
+DP = 8
+MP = 4
+
+
+def ring(step):
+    pairs = []
+    for i in range(DP):
+        for z in range(MP):
+            to = (z + (step if i % 2 == 0 else -step)) % MP
+            pairs.append((i * MP + z, i * MP + to))
+    return pairs
+
+
+def straight(step):
+    return [(z, (z + step) % MP) for z in range(MP)]
+
+
+def beside(first):
+    return [(i, i ^ (2 if (i % 2 == 0) == first else 4)) for i in range(DP)]
+
+
+def swap(value):
+    return lax.ppermute(value, "dp", [(i, i ^ 1) for i in range(DP)])
 
 
 def spread(piece):
-    half = piece.shape[0] // 2
-    by_x = across(piece, 2)
-    by_y = across(piece, 4)
-    far_one = across(by_y[:half], 2)
-    far_two = across(by_x[half:], 4)
-    held = [piece, by_x, by_y, far_one, far_two]
-    other = [across(value, 1) for value in held]
-    common = [held[0], other[0], held[1], other[1], held[2], other[2]]
-    return common + [held[3], other[3]], common + [held[4], other[4]]
-
-
-def sliced(shard):
-    rows = shard.shape[1] // SLOTS8
-    half = shard.shape[0] // 2
-    parts = [shard[:, s * rows : (s + 1) * rows] for s in range(SLOTS8)]
+    near = lax.ppermute(piece, "dp", beside(True))
+    side = lax.ppermute(piece, "dp", beside(False))
+    far = lax.ppermute(side, "dp", beside(True))
+    mine = [piece, near, side, far]
+    return mine, [swap(value) for value in mine]
+
+
+def cut(shard, chip):
+    rows = shard.shape[1] // 4
+    return lax.dynamic_slice_in_dim(shard, chip * rows, rows, 1).astype(F32)
+
+
+def sets(shard, other):
+    def parts(value, order):
+        rows = value.shape[1] // 4
+        return [value[:, k * rows : (k + 1) * rows] for k in order]
+
+    return parts(shard, (0, 1, 2, 3)), parts(other, (0, 2, 1, 3))
+
+
+def gather_whole(qkv, cross, outer, feeds):
+    def along(value, step):
+        return lax.ppermute(value.astype(F32), "mp", straight(step))
+
+    def joined(value):
+        return jnp.concatenate([along(value[None], step) for step in (1, 2, 3)], axis=0)
+
     return (
-        parts[:6] + [part[:half] for part in parts[6:]],
-        parts[:6] + [part[half:] for part in parts[6:]],
-    )
-
-
-def gather(shard, me, planar):
-    if planar:
-        rows = shard.shape[1] // SLOTS8
-        shard = lax.dynamic_slice_in_dim(shard, me * rows, rows, 1)
-    piece = shard.astype(F32)
-    one = lax.ppermute(piece, "mp", UP)
-    three = lax.ppermute(piece, "mp", DOWN)
-    two = lax.ppermute(one, "mp", UP)
-    return [spread(value) if planar else sliced(value) for value in (one, two, three)]
+        sets(along(qkv, 1), along(qkv, 3)),
+        sets(along(qkv, 2), along(cross, 2)),
+        sets(along(cross, 1), along(cross, 3)),
+        sets(joined(outer[0]), joined(outer[1])),
+        sets(along(feeds, 1), along(feeds, 3)),
+        sets(along(feeds[:1], 2), along(feeds[1:], 2)),
+    )
+
+
+def gather(qkv, cross, outer, feeds, chip, core):
+    axes = ("dp", "mp")
+    own_qkv, own_cross = cut(qkv, chip), cut(cross, chip)
+    own_outer = cut(lax.dynamic_slice_in_dim(outer, core, 1, 0), chip)
+    own_feeds = cut(feeds, chip)
+    qkv_one = lax.ppermute(own_qkv, axes, ring(1))
+    cross_one = lax.ppermute(own_cross, axes, ring(1))
+    two = lax.ppermute(jnp.where(core == 0, qkv_one, cross_one), axes, ring(1))
+    outer_one = lax.ppermute(own_outer, "mp", straight(1))
+    outer_three = lax.ppermute(own_outer, "mp", straight(3))
+    outer_two = lax.ppermute(outer_one, "mp", straight(1))
+    feed_one = lax.ppermute(own_feeds, axes, ring(1))
+    feed_two = lax.ppermute(lax.dynamic_slice_in_dim(feed_one, core, 1, 0), axes, ring(1))
+    outers = jnp.concatenate([outer_one, outer_two, outer_three], axis=0)
+    return [spread(piece) for piece in (qkv_one, two, cross_one, outers, feed_one, feed_two)]
 
 
 def scattered(value, axis):
     return lax.psum_scatter(value, "dp", scatter_dimension=axis, tiled=True)
+
+
+def pair_sum(keep, send):
+    part = keep + swap(send)
+    part = part[:2] + lax.ppermute(part[2:], "dp", beside(True))
+    return part[0] + lax.ppermute(part[1], "dp", beside(False))
+
+
+def plane_sum(value):
+    for bit in (1, 2, 4):
+        value = value + lax.ppermute(value, "dp", [(i, i ^ bit) for i in range(DP)])
+    return value
 
 
 def local(
@@ -769,7 +862,8 @@
 ):
     slot_count, text_length = text_mask.shape
     place = lax.axis_index("dp") if planar else jnp.int32(0)
-    me = jnp.reshape(place, (1,)).astype(jnp.int32)
+    chip, core = place // 2, place % 2
+    me = jnp.stack([chip, core]).astype(jnp.int32)
     gains = [ln_gain[n : n + 1] for n in range(3)]
     shifts = [ln_shift[n : n + 1] for n in range(3)]
     text = text_states.reshape(slot_count * text_length, text_states.shape[2])
@@ -777,56 +871,75 @@
     live = ((text_mask == 1) | (position == 0)).astype(F32).reshape(-1, 1)
     own_qkv = jnp.transpose(w_qkv, (1, 0, 2))
     own_cross = jnp.concatenate([w_cross_q[None], jnp.transpose(w_cross_kv, (1, 0, 2))], axis=0)
-
-    attention = gather(jnp.concatenate([own_qkv, own_cross], axis=0), place, planar)
-    outer = gather(jnp.stack([w_out, w_cross_out]), place, planar)
-    feeds = gather(jnp.stack([w_up, w_down]), place, planar)
+    shards = (own_qkv, own_cross, jnp.stack([w_out, w_cross_out]), jnp.stack([w_up, w_down]))
+    g_qkv, g_two, g_cross, g_outer, g_feed, g_feed_two = (
+        gather(*shards, chip, core) if planar else gather_whole(*shards)
+    )
 
     first = norm_first(tokens, gains[0], shifts[0])
-    qkvs, mixeds, logs, pairs = ([None] * 4 for _ in range(4))
-    weights, crosses = [own_qkv] + [None] * 3, [own_cross] + [None] * 3
-    qkvs[0], mixeds[0], logs[0], pairs[0] = front_own(lengths, first, text, own_qkv, own_cross)
-    for j in (1, 3, 2):
-        weights[j], crosses[j], qkvs[j], mixeds[j], logs[j], pairs[j] = front(
-            me, lengths, first, text, attention[j - 1]
-        )
+    qkvs, mixeds, logs, weights = ([None] * 4 for _ in range(4))
+    weights[0] = own_qkv
+    qkvs[0], mixeds[0], logs[0] = front_own(lengths, first, own_qkv)
+    weights[1], qkvs[1], mixeds[1], logs[1] = front(True, me, lengths, first, g_qkv[0])
+    weights[3], qkvs[3], mixeds[3], logs[3] = front(False, me, lengths, first, g_qkv[1])
+    weights[2], cross_two, qkvs[2], mixeds[2], logs[2] = front_two(
+        me, lengths, first, g_two[0] + g_two[1]
+    )
+    cross_a, cross_b, *pairs = text_front(
+        me, text, own_cross, cross_two, g_cross[0] + g_cross[1]
+    )
+    crosses = [own_cross, cross_a, cross_two, cross_b]
     full_out, full_co, after_self, after_cross, second, third, cross_query, looked, cross_logs = middle(
         me, lengths, live, tokens, (gains[1], shifts[1], gains[2], shifts[2]), w_out, w_cross_out,
-        mixeds, crosses, pairs, outer,
-    )
-    out, grad, up_grad, down_grad = feed_own(third, cotangent, after_cross, w_up, w_down)
-    for j in (1, 3, 2):
-        out, grad = feed(
-            me, third, cotangent, out, grad, feeds[j - 1], BF16 if j == 2 else F32
-        )
-    upstream, mixed_grad, pair_grad, co_grad, cq_grad, out_grad, sums = back(
-        lengths, live, grad, cotangent, after_cross, after_self, second, cross_query, looked,
-        mixeds[0], cross_logs, gains[1], gains[2], full_out, full_co, crosses, pairs,
-    )
-    text_grad, kv_grad = text_back(text, pair_grad, crosses)
-    first_grad, qkv_grad = self_own(
-        lengths, qkvs[0], mixeds[0], mixed_grad, logs[0], weights[0], first
+        mixeds, crosses, pairs, g_outer[0] + g_outer[1],
+    )
+    out, grad, both_grad = feed_own(third, cotangent, after_cross, w_up, w_down)
+    out, grad = feed(0, me, third, cotangent, out, grad, g_feed[0], F32)
+    out, grad = feed(1, me, third, cotangent, out, grad, g_feed[1], F32)
+    out, grad = feed(
+        2, me, third, cotangent, out, grad, g_feed_two[0] + g_feed_two[1], BF16
+    )
+    upstream, mixed_grad, pair_grad, row_grads, query_grad, sums = back(
+        lengths, live, grad, cotangent, after_cross, after_self, cross_query, looked, mixeds[0],
+        cross_logs, gains[1], gains[2], full_out, full_co, crosses, pairs,
+    )
+    text_grad, cross_grad = text_back(text, pair_grad, second, query_grad, crosses)
+    first_grad, keep, send = self_own(
+        me, lengths, qkvs[0], mixeds[0], mixed_grad, logs[0], weights[0], first
     )
     for j in (1, 2, 3):
         first_grad = self_back(
             lengths, qkvs[j], mixeds[j], mixed_grad, logs[j], weights[j], first_grad, j
         )
     token_grad, last_sums = last(first_grad, tokens, upstream, gains[0])
-    gain_grad = jnp.concatenate([last_sums[0:1], sums[2:3], sums[0:1]], axis=0)
-    shift_grad = jnp.concatenate([last_sums[1:2], sums[3:4], sums[1:2]], axis=0)
+    both_sum = scattered(both_grad, 1)
+    row_sum = scattered(row_grads, 1)
+    cross_sum = scattered(cross_grad, 1)
+    norm_sums = jnp.concatenate(
+        [last_sums[0:1], sums[2:3], sums[0:1], last_sums[1:2], sums[3:4], sums[1:2]], axis=0
+    )
+    if planar:
+        qkv_sum = pair_sum(keep, send)
+        width = norm_sums.shape[1] // DP
+        norm_sum = lax.dynamic_slice_in_dim(plane_sum(norm_sums), place * width, width, 1)
+    else:
+        pieces = [part[k] for k in (0, 2, 1, 3) for part in (keep, send)]
+        pieces = jnp.stack(pieces, axis=1)
+        qkv_sum = scattered(jnp.reshape(pieces, own_qkv.shape), 1)
+        norm_sum = scattered(norm_sums, 1)
     return (
         out,
         token_grad,
         text_grad.reshape(text_states.shape),
-        scattered(gain_grad, 1),
-        scattered(shift_grad, 1),
-        jnp.transpose(scattered(qkv_grad, 1), (1, 0, 2)),
-        scattered(out_grad, 0),
-        scattered(cq_grad, 0),
-        jnp.transpose(scattered(kv_grad, 1), (1, 0, 2)),
-        scattered(co_grad, 0),
-        scattered(up_grad, 0),
-        scattered(down_grad, 0),
+        norm_sum[:3],
+        norm_sum[3:],
+        jnp.transpose(qkv_sum, (1, 0, 2)),
+        row_sum[0],
+        cross_sum[0],
+        jnp.transpose(cross_sum[1:], (1, 0, 2)),
+        row_sum[1],
+        both_sum[0],
+        both_sum[1],
     )
 
 
@@ -848,7 +961,7 @@
         P("dp", None),
     )
     return jax.shard_map(
-        partial(local, mesh.shape["dp"] == SLOTS8),
+        partial(local, mesh.shape["dp"] == DP),
         mesh=mesh,
         in_specs=placed,
         out_specs=(

time: 1120 us -> 647 us (0.58)
  waiting for transfers between devices: 650 us -> 150 us
  Pallas kernels: 342 us -> 389 us
  starting transfers between devices: 77.7 us -> 52.7 us
    reduce_scatter x7 -> x3, waiting for transfers between devices: 323 us -> 11.5 us  [scattered(): return lax.psum_scatter(value, 'dp', scatter_dimension=axis, tiled=True)]
    unnamed x11 -> x3, waiting for transfers between devices: 105 us -> 0.71 us
    ppermute x90 -> x56, waiting for transfers between devices: 223 us -> 138 us  [the longest x1 37.2 us: gather(): two = lax.ppermute(jnp.where(core == 0, qkv_one, cross_one), axes, ring(1))]
    pallas_call x3, Pallas kernels: 52.5 us -> 78.5 us  [self_back(): pl.pallas_call(self_kernel, grid=(1,), in_specs=[smem()] + [whole((3, row...]
    ppermute x90 -> x56, starting transfers between devices: 77.2 us -> 52.5 us  [the longest x25 8.55 us: swap(): return lax.ppermute(value, 'dp', [(i, i ^ 1) for i in range(DP)])]
    pallas_call x9 -> x10, Pallas kernels: 145 us -> 168 us  [the longest x4 65.5 us: front_call(): pl.pallas_call(kernel, in_specs=[smem()] * len(prefix) + [vmem()] * (1 +...]
  transfers between devices with their start and end apart: 99 -> 59, of which waited for: 50 -> 12; matrix products, arithmetic and copies ran while one was open for 2% -> 3% of each run, Pallas kernels for 17% -> 50%
where the time goes in v2:
time: 647 us; the launch traced here: 636 us
  Pallas kernels  389 us (60%)
  waiting for transfers between devices  150 us (23%)
  starting transfers between devices  52.7 us (8%)
  local copies, waits for them, and re-layouts  17.4 us (3%)
  between operations  14.7 us (2%)
  other arithmetic  12.6 us (2%)
    pallas_call x3, Pallas kernels, self_back(): pl.pallas_call(self_kernel, grid=(1,), in_specs=[smem()] + [whole((3, row...  78.5 us
    pallas_call x4, Pallas kernels, front_call(): pl.pallas_call(kernel, in_specs=[smem()] * len(prefix) + [vmem()] * (1 +...  65.5 us
    pallas_call x3, Pallas kernels, feed(): pl.pallas_call(partial(feed_kernel, kind), grid=(rows // FEED,), in_specs...  55.6 us
    pallas_call x1, Pallas kernels, back(): pl.pallas_call(back_kernel, grid=(rows // BLK,), in_specs=[smem(), whole(...  51.8 us
    pallas_call x1, Pallas kernels, middle(): pl.pallas_call(middle_kernel, grid=(rows // BLK,), in_specs=[smem(), smem...  42.9 us
    ppermute x1, waiting for transfers between devices, gather(): two = lax.ppermute(jnp.where(core == 0, qkv_one, cross_one), axes, ring(1))  37.2 us
    ppermute x1, waiting for transfers between devices, gather(): outer_one = lax.ppermute(own_outer, 'mp', straight(1))  34.1 us
    pallas_call x1, Pallas kernels, feed_own(): pl.pallas_call(feed_own_kernel, grid=(rows // FEED,), in_specs=[tile, til...  31.8 us
  transfers between devices with their start and end apart: 59, of which 12 were waited for; matrix products, arithmetic and copies ran while one was open for 3% of the time, Pallas kernels for 50%

profile of v2, /device:TPU:0, one launch (start us, length us, event | category | flops | bytes accessed | tf_op | source)
XLA Modules:
  0.0 636.4 jit_solution(4014034802349343799)
XLA Ops:
  8.6 2.0 fusion.3
  10.6 3.0 collective-permute-start.4
  13.7 1.9 convert_bitcast_fusion
  17.2 1.7 fusion.7
  20.4 2.2 collective-permute-start.26
  22.7 34.1 %collective-permute-done.24 = f32[1,64,1024]{2,1,0:T(8,128)} collective-permute-done((f32[1,64,1024]{2,1,0:T(8,128)}, f32[1,64,1024]{2,1,0:T(8,128)}, u32[]{:S(2)}, u32[]{:S(2)}) %collective-permute-start.24) | collective-permute-done | bytes 262176 | tf_op jit(solution)/shard_map/ppermute | solution.py:834
  56.8 2.6 fusion.1
  59.4 6.9 %collective-permute-start.34 = (f32[2,256,1024]{2,1,0:T(8,128)}, f32[2,256,1024]{2,1,0:T(8,128)S(1)}, u32[]{:S(2)}, u32[]{:S(2)}) collective-permute-start(f32[2,256,1024]{2,1,0:T(8,128)} %fusion.1), channel_id=1, source_target_pairs={{0,1},{1,2},{2,3},{3,0},{4,7},{5,4},{6,5},{7,6},{8,9},{9,10},{10,1... | collective-permute-start | bytes 6291464 | tf_op jit(solution)/shard_map/ppermute | solution.py:837
  67.3 5.6 collective-permute-done.25
  73.9 1.7 collective-permute-start.28
  79.1 10.1 %collective-permute-done.28.refs_14_ = f32[3,64,1024]{2,1,0:T(8,128)S(1)} collective-permute-done((f32[3,64,1024]{2,1,0:T(8,128)S(1)}, f32[3,64,1024]{2,1,0:T(8,128)S(1)}, u32[]{:S(2)}, u32[]{:S(2)}) %collective-permute-start.28) | collective-permute-done | bytes 786464 | tf_op jit(solution)/shard_map/ppermute | solution.py:790
  89.2 2.5 collective-permute-start.18
  91.9 37.2 %collective-permute-done.5.refs_0_ = f32[3,256,256]{2,1,0:T(8,128)S(1)} collective-permute-done((f32[3,256,256]{2,1,0:T(8,128)S(1)}, f32[3,256,256]{2,1,0:T(8,128)S(1)}, u32[]{:S(2)}, u32[]{:S(2)}) %collective-permute-start.5) | collective-permute-done | bytes 786464 | tf_op jit(solution)/shard_map/ppermute | solution.py:833
  131.3 5.6 norm_first.1.first
  139.0 8.3 %collective-permute-done.2.refs_2_ = f32[3,256,256]{2,1,0:T(8,128)} collective-permute-done((f32[3,256,256]{2,1,0:T(8,128)}, f32[3,256,256]{2,1,0:T(8,128)}, u32[]{:S(2)}, u32[]{:S(2)}) %collective-permute-start.2) | collective-permute-done | bytes 786464 | tf_op jit(solution)/shard_map/ppermute | solution.py:790
  147.3 1.6 collective-permute-start.7
  148.9 2.5 collective-permute-start.3
  151.4 15.0 %front_own.1 = (bf16[3,1280,256]{2,1,0:T(8,128)(2,1)}, bf16[1280,256]{1,0:T(8,128)(2,1)}, f32[8,1280]{1,0:T(8,128)}) custom-call(s32[5]{0:T(128)} %lengths.19, bf16[1280,1024]{1,0:T(8,128)(2,1)} %norm_first.1.first, bf16[3,1024,256]{2,1,0:T(8,128)(2,1)} %bitcast.54), custom_call_target="tpu_custom_call" | custom-call | flops 13799999488 | bytes 43200000 | tf_op jit(solution)/shard_map/front_own/pallas_call | solution.py:235
  172.0 2.5 collective-permute-done.3.refs_3_
  175.2 16.2 %front.2 = (bf16[3,1024,256]{2,1,0:T(8,128)(2,1)}, bf16[3,1280,256]{2,1,0:T(8,128)(2,1)}, bf16[1280,256]{1,0:T(8,128)(2,1)}, f32[8,1280]{1,0:T(8,128)}) custom-call(s32[2]{0:T(128)} %pad_add_fusion.me, s32[5]{0:T(128)} %lengths.19, bf16[1280,1024]{1,0:T(8,128)(2,1)} %norm_first.1.first, f32[3,256,256]{2,1,0:T(8,128)} %collective-permute-done.refs_0_, ...), custom_call_target="tpu_custom_call" | custom-call | flops 16099999744 | bytes 50400000 | tf_op jit(solution)/shard_map/front/pallas_call | solution.py:235
  194.6 16.5 %front.3 = (bf16[3,1024,256]{2,1,0:T(8,128)(2,1)}, bf16[3,1280,256]{2,1,0:T(8,128)(2,1)}, bf16[1280,256]{1,0:T(8,128)(2,1)}, f32[8,1280]{1,0:T(8,128)}) custom-call(s32[2]{0:T(128)} %pad_add_fusion.me, s32[5]{0:T(128)} %lengths.19, bf16[1280,1024]{1,0:T(8,128)(2,1)} %norm_first.1.first, f32[3,256,256]{2,1,0:T(8,128)} %collective-permute-done.13.refs_0_, ...), custom_call_target="tpu_custom_call" | custom-call | flops 16099999744 | bytes 50400000 | tf_op jit(solution)/shard_map/front/pallas_call | solution.py:235
  212.7 3.7 collective-permute-start.23
  216.4 17.8 %front_two.1 = (bf16[3,1024,256]{2,1,0:T(8,128)(2,1)}, bf16[3,1024,256]{2,1,0:T(8,128)(2,1)}, bf16[3,1280,256]{2,1,0:T(8,128)(2,1)}, bf16[1280,256]{1,0:T(8,128)(2,1)}, f32[8,1280]{1,0:T(8,128)}) custom-call(s32[2]{0:T(128)} %pad_add_fusion.me, s32[5]{0:T(128)} %lengths.19, bf16[1280,1024]{1,0:T(8,128)(2,1)} %norm_first.1.first, f32[3,256,256]{2,1,0:T(8,128)} %copy-done.23, ...), custom_call_target="tpu_custom_call" | custom-call | flops 17250000896 | bytes 54000000 | tf_op jit(solution)/shard_map/front_two/pallas_call | solution.py:235
  235.1 8.0 %text_front.1 = (bf16[3,1024,256]{2,1,0:T(8,128)(2,1)}, bf16[3,1024,256]{2,1,0:T(8,128)(2,1)}, bf16[2,640,256]{2,1,0:T(8,128)(2,1)}, bf16[2,640,256]{2,1,0:T(8,1...) custom-call(s32[2]{0:T(128)} %pad_add_fusion.me, bf16[640,1024]{1,0:T(8,128)(2,1)} %bitcast.57, ...), custom_call_target="tpu_custom_call" | custom-call | flops 9200000000 | bytes 28800000 | tf_op jit(solution)/shard_map/text_front/pallas_call | solution.py:273
  243.1 1.7 collective-permute-start.35
  245.4 1.7 collective-permute-start.37
  247.1 42.9 %middle.1 = (bf16[1024,1024]{1,0:T(8,128)(2,1)}, bf16[1024,1024]{1,0:T(8,128)(2,1)}, f32[1280,1024]{1,0:T(8,128)}, f32[1280,1024]{1,0:T(8,128)}, bf16[1280,1024]...) custom-call(s32[2]{0:T(128)} %pad_add_fusion.me, ...), custom_call_target="tpu_custom_call" | custom-call | flops 49450000384 | bytes 154800000 | tf_op jit(solution)/shard_map/middle/pallas_call | solution.py:345
  290.6 12.4 %collective-permute-done.37.refs_3_ = f32[2,256,1024]{2,1,0:T(8,128)} collective-permute-done((f32[2,256,1024]{2,1,0:T(8,128)S(1)}, f32[2,256,1024]{2,1,0:T(8,128)}, u32[]{:S(2)}, u32[]{:S(2)}) %collective-permute-start.37) | collective-permute-done | bytes 2097184 | tf_op jit(solution)/shard_map/ppermute | solution.py:791
  303.0 31.8 %feed_own.1 = (f32[1280,1024]{1,0:T(8,128)}, f32[1280,1024]{1,0:T(8,128)}, f32[2,1024,1024]{2,1,0:T(8,128)}) custom-call(bf16[1280,1024]{1,0:T(8,128)(2,1)} %get-tuple-element.76.third, bf16[1280,1024]{1,0:T(8,128)(2,1)} %cot.9, f32[1280,1024]{1,0:T(8,128)} %get-tuple-element.77.after.after_cross, bf16[1024,1024]{1,0:T(8,128)(2,1)} %up.1, ...), custom_call_target="tpu_custom_call" | custom-call | flops 36800000000 | bytes 115200000 | tf_op jit(solution)/shard_map/feed_own/pallas_call | solution.py:417
  334.9 1.7 collective-permute-start.43
  337.0 18.7 %feed.3 = (f32[1280,1024]{1,0:T(8,128)}, f32[1280,1024]{1,0:T(8,128)}) custom-call(s32[2]{0:T(128)} %pad_add_fusion.me, bf16[1280,1024]{1,0:T(8,128)(2,1)} %get-tuple-element.76.third, bf16[1280,1024]{1,0:T(8,128)(2,1)} %cot.9, f32[1280,1024]{1,0:T(8,128)} %get-tuple-element.78.out_in, f32[1280,1024]{1,0:T(8,128)} %get-tuple-element.79.grad_in, ...), custom_call_target="tpu_custom_call" | custom-call | flops 20700000256 | bytes 64800000 | tf_op jit(solution)/shard_map/feed/pallas_call | solution.py:449
  355.8 5.4 collective-permute-done.45.refs_3_
  361.8 18.4 %feed.4 = (f32[1280,1024]{1,0:T(8,128)}, f32[1280,1024]{1,0:T(8,128)}) custom-call(s32[2]{0:T(128)} %pad_add_fusion.me, bf16[1280,1024]{1,0:T(8,128)(2,1)} %get-tuple-element.76.third, bf16[1280,1024]{1,0:T(8,128)(2,1)} %cot.9, f32[1280,1024]{1,0:T(8,128)} %get-tuple-element.80.out_in, f32[1280,1024]{1,0:T(8,128)} %get-tuple-element.81.grad_in, ...), custom_call_target="tpu_custom_call" | custom-call | flops 20700000256 | bytes 64800000 | tf_op jit(solution)/shard_map/feed/pallas_call | solution.py:449
  381.9 18.4 %feed.5 = (bf16[1280,1024]{1,0:T(8,128)(2,1)}, f32[1280,1024]{1,0:T(8,128)}) custom-call(s32[2]{0:T(128)} %pad_add_fusion.me, bf16[1280,1024]{1,0:T(8,128)(2,1)} %get-tuple-element.76.third, bf16[1280,1024]{1,0:T(8,128)(2,1)} %cot.9, f32[1280,1024]{1,0:T(8,128)} %get-tuple-element.82.out_in, f32[1280,1024]{1,0:T(8,128)} %get-tuple-element.83.grad_in, ...), custom_call_target="tpu_custom_call" | custom-call | flops 20700000256 | bytes 64800000 | tf_op jit(solution)/shard_map/feed/pallas_call | solution.py:449
  400.4 51.8 %back.1 = (f32[1280,1024]{1,0:T(8,128)}, bf16[1280,1024]{1,0:T(8,128)(2,1)}, bf16[4,2,640,256]{3,2,1,0:T(8,128)(2,1)}, f32[2,256,1024]{2,1,0:T(8,128)}, bf16[1280,256]{1,0:T(8,128)(2,1)}, /*index=5*/f32[8,1024]{1,0:T(8,128)}) custom-call(s32[5]{0:T(128)} %lengths.19, f32[640,1]{1,0:T(8,128)} %bitcast.53, f32[1280,1024]{1,0:T(8,128)} %get-tuple-element.86.third_grad, ...), custom_call_target="tpu_custom_call" | custom-call | flops 60949999616 | bytes 190800000 | tf_op jit(solution)/shard_map/back/pallas_call | solution.py:545
  452.3 11.2 %text_back.1 = (f32[640,1024]{1,0:T(8,128)}, f32[3,1024,256]{2,1,0:T(8,128)}) custom-call(bf16[640,1024]{1,0:T(8,128)(2,1)} %bitcast.58, bf16[4,2,640,256]{3,2,1,0:T(8,128)(2,1)} %get-tuple-element.107.pair_grad, bf16[1280,1024]{1,0:T(8,128)(2,1)} %get-tuple-element.108.second, bf16[1280,256]{1,0:T(8,128)(2,1)} %get-tuple-element.109.query_grad, ...), custom_call_target="tpu_custom_call" | custom-call | flops 10350000128 | bytes 32400000 | tf_op jit(solution)/shard_map/text_back/pallas_call | solution.py:593
  464.2 27.7 %self_own.1 = (f32[1280,1024]{1,0:T(8,128)}, f32[4,3,128,256]{3,2,1,0:T(8,128)}, f32[4,3,128,256]{3,2,1,0:T(8,128)}) custom-call(s32[2]{0:T(128)} %pad_add_fusion.me, s32[5]{0:T(128)} %lengths.19, bf16[3,1280,256]{2,1,0:T(8,128)(2,1)} %get-tuple-element.102.qkv, bf16[1280,256]{1,0:T(8,128)(2,1)} %get-tuple-element.65.refs_0_.mixed0.mixed, ...), custom_call_target="tpu_custom_call" | custom-call | flops 23000000512 | bytes 72000000 | tf_op jit(solution)/shard_map/self_own/pallas_call | solution.py:696
  492.4 26.0 %self_back.3.before = f32[1280,1024]{1,0:T(8,128)} custom-call(s32[5]{0:T(128)} %lengths.19, bf16[3,1280,256]{2,1,0:T(8,128)(2,1)} %get-tuple-element.99.qkv, bf16[1280,256]{1,0:T(8,128)(2,1)} %get-tuple-element.66.refs_1_.mixed, bf16[1280,1024]{1,0:T(8,128)(2,1)} %get-tuple-element.93.out_grad, f32[8,1280]{1,0:T(8,128)} %get-tuple-element.100.logs, ...), custom_call_target="tpu_custom_call" | custom-call | flops 20124999680 | bytes 63000000 | tf_op jit(solution)/shard_map/self_back/pallas_call | solution.py:720
  518.4 26.3 %self_back.4.before = f32[1280,1024]{1,0:T(8,128)} custom-call(s32[5]{0:T(128)} %lengths.19, bf16[3,1280,256]{2,1,0:T(8,128)(2,1)} %get-tuple-element.96.qkv, bf16[1280,256]{1,0:T(8,128)(2,1)} %get-tuple-element.67.refs_2_.mixed, bf16[1280,1024]{1,0:T(8,128)(2,1)} %get-tuple-element.93.out_grad, f32[8,1280]{1,0:T(8,128)} %get-tuple-element.97.logs, ...), custom_call_target="tpu_custom_call" | custom-call | flops 20124999680 | bytes 63000000 | tf_op jit(solution)/shard_map/self_back/pallas_call | solution.py:720
  544.7 26.1 %self_back.5.first_grad = f32[1280,1024]{1,0:T(8,128)} custom-call(s32[5]{0:T(128)} %lengths.19, bf16[3,1280,256]{2,1,0:T(8,128)(2,1)} %get-tuple-element.85.qkv, bf16[1280,256]{1,0:T(8,128)(2,1)} %get-tuple-element.68.refs_3_.mixed, bf16[1280,1024]{1,0:T(8,128)(2,1)} %get-tuple-element.93.out_grad, f32[8,1280]{1,0:T(8,128)} %get-tuple-element.94.logs, ...), custom_call_target="tpu_custom_call" | custom-call | flops 20124999680 | bytes 63000000 | tf_op jit(solution)/shard_map/self_back/pallas_call | solution.py:720
  572.4 10.0 %last.1 = (f32[1280,1024]{1,0:T(8,128)}, f32[8,1024]{1,0:T(8,128)}) custom-call(f32[1280,1024]{1,0:T(8,128)} %self_back.5.first_grad, bf16[1280,1024]{1,0:T(8,128)(2,1)} %tokens.3, f32[1280,1024]{1,0:T(8,128)} %get-tuple-element.105.upstream, f32[1,1024]{1,0:T(1,128)} %get-tuple-element.155.gain_ref.gain), custom_call_target="tpu_custom_call" | custom-call | flops 11500000256 | bytes 36000000 | tf_op jit(solution)/shard_map/last/pallas_call | solution.py:751
  583.4 16.7 %collective-permute-done.54 = f32[2,3,128,256]{3,2,1,0:T(8,128)S(1)} collective-permute-done((f32[2,3,128,256]{3,2,1,0:T(8,128)S(1)}, f32[2,3,128,256]{3,2,1,0:T(8,128)S(1)}, u32[]{:S(2)}, u32[]{:S(2)}) %collective-permute-start.54) | collective-permute-done | bytes 786464 | tf_op jit(solution)/shard_map/ppermute | solution.py:849
  601.5 3.5 collective-permute-done.51
  605.1 1.7 collective-permute-start.52
  606.8 2.2 collective-permute-done.52
  610.4 1.7 slice_bitcast_fusion.5
  615.6 11.5 %reduce-scatter.8.cloned.1.call-done = f32[2,128,1024]{2,1,0:T(8,128)} async-done(((f32[2,1024,1024]{2,1,0:T(8,128)}), f32[2,128,1024]{2,1,0:T(8,128)}) %reduce-scatter.8.cloned.1.call-update) | async-done | bytes 1048592 | tf_op jit(solution)/shard_map/reduce_scatter | solution.py:844
  627.1 2.3 slice_bitcast_fusion
  (188 shorter events, 40.4 us)
Async XLA Ops:
  7.2 603.2 %reduce-scatter.4.cloned.1.call-start = ((), (), s32[]{:S(2)}) async-start(), calls=%async_computation.3 | async-start | bytes 2359296 | tf_op jit(solution)/shard_map/reduce_scatter | solution.py:844
  10.6 66.5 %collective-permute-start.4 = (f32[3,256,256]{2,1,0:T(8,128)}, f32[3,256,256]{2,1,0:T(8,128)}, u32[]{:S(2)}, u32[]{:S(2)}) collective-permute-start(f32[3,256,256]{2,1,0:T(8,128)} %fusion.3), channel_id=1, source_target_pairs={{0,1},{1,2},{2,3},{3,0},{4,7},{5,4},{6,5},{7,6},{8,9},{9,10},{10,1... | collective-permute-start | bytes 2359304 | tf_op jit(solution)/shard_map/ppermute | solution.py:832
  15.6 61.5 %collective-permute-start = (f32[3,256,256]{2,1,0:T(8,128)}, f32[3,256,256]{2,1,0:T(8,128)}, u32[]{:S(2)}, u32[]{:S(2)}) collective-permute-start(f32[3,256,256]{2,1,0:T(8,128)} %convert_bitcast_fusion), channel_id=1, source_target_pairs={{0,1},{1,2},{2,3},{3,0},{4,7},{5,4},{6,5},{7,6},{8,9},{9,10},{10,1... | collective-permute-start | bytes 2359304 | tf_op jit(solution)/shard_map/ppermute | solution.py:831
  18.9 37.9 %collective-permute-start.24 = (f32[1,64,1024]{2,1,0:T(8,128)}, f32[1,64,1024]{2,1,0:T(8,128)}, u32[]{:S(2)}, u32[]{:S(2)}) collective-permute-start(f32[1,64,1024]{2,1,0:T(8,128)} %fusion.7), channel_id=1, source_target_pairs={{0,1},{1,2},{2,3},{3,0},{4,5},{5,6},{6,7},{7,4},{8,9},{9,10},{10,1... | collective-permute-start | bytes 786440 | tf_op jit(solution)/shard_map/ppermute | solution.py:834
  20.4 53.4 %collective-permute-start.26 = (f32[1,64,1024]{2,1,0:T(8,128)}, f32[1,64,1024]{2,1,0:T(8,128)S(1)}, u32[]{:S(2)}, u32[]{:S(2)}) collective-permute-start(f32[1,64,1024]{2,1,0:T(8,128)} %fusion.7), channel_id=1, source_target_pairs={{0,3},{1,0},{2,1},{3,2},{4,7},{5,4},{6,5},{7,6},{8,11},{9,8},{10,9... | collective-permute-start | bytes 786440 | tf_op jit(solution)/shard_map/ppermute | solution.py:835
  59.4 89.5 %collective-permute-start.34 = (f32[2,256,1024]{2,1,0:T(8,128)}, f32[2,256,1024]{2,1,0:T(8,128)S(1)}, u32[]{:S(2)}, u32[]{:S(2)}) collective-permute-start(f32[2,256,1024]{2,1,0:T(8,128)} %fusion.1), channel_id=1, source_target_pairs={{0,1},{1,2},{2,3},{3,0},{4,7},{5,4},{6,5},{7,6},{8,9},{9,10},{10,1... | collective-permute-start | bytes 6291464 | tf_op jit(solution)/shard_map/ppermute | solution.py:837
  78.4 50.7 %collective-permute-start.5 = (f32[3,256,256]{2,1,0:T(8,128)S(1)}, f32[3,256,256]{2,1,0:T(8,128)S(1)}, u32[]{:S(2)}, u32[]{:S(2)}) collective-permute-start(f32[3,256,256]{2,1,0:T(8,128)S(1)} %broadcast_select_fusion), channel_id=1, source_target_pairs={{0,1},{1,2},{2,3},{3,0},{4,7},{5,4},{6,5},{7,6},{8,9},{9,10},{10,1... | collective-permute-start | bytes 2359304 | tf_op jit(solution)/shard_map/ppermute | solution.py:833
  89.2 47.8 %collective-permute-start.18 = (f32[3,256,256]{2,1,0:T(8,128)}, f32[3,256,256]{2,1,0:T(8,128)}, u32[]{:S(2)}, u32[]{:S(2)}) collective-permute-start(f32[3,256,256]{2,1,0:T(8,128)} %collective-permute-done.4.refs_0_), channel_id=1, source_target_pairs={{0,16},{4,12},{8,24},{12,4},{16,0},{20,28},{24,8},{28,20},{1,17},{... | collective-permute-start | bytes 2359304 | tf_op jit(solution)/shard_map/ppermute | solution.py:790
  91.7 46.8 %collective-permute-start.17 = (f32[3,256,256]{2,1,0:T(8,128)}, f32[3,256,256]{2,1,0:T(8,128)}, u32[]{:S(2)}, u32[]{:S(2)}) collective-permute-start(f32[3,256,256]{2,1,0:T(8,128)} %collective-permute-done.4.refs_0_), channel_id=1, source_target_pairs={{0,8},{4,20},{8,0},{12,28},{16,24},{20,4},{24,16},{28,12},{1,9},{5... | collective-permute-start | bytes 2359304 | tf_op jit(solution)/shard_map/ppermute | solution.py:789
  91.9 46.5 %collective-permute-start.20 = (f32[3,256,256]{2,1,0:T(8,128)}, f32[3,256,256]{2,1,0:T(8,128)}, u32[]{:S(2)}, u32[]{:S(2)}) collective-permute-start(f32[3,256,256]{2,1,0:T(8,128)} %collective-permute-done.4.refs_0_), channel_id=1, source_target_pairs={{0,4},{4,0},{8,12},{12,8},{16,20},{20,16},{24,28},{28,24},{1,5},{5... | collective-permute-start | bytes 2359304 | tf_op jit(solution)/shard_map/ppermute | solution.py:785
  129.1 18.2 %collective-permute-start.2 = (f32[3,256,256]{2,1,0:T(8,128)}, f32[3,256,256]{2,1,0:T(8,128)}, u32[]{:S(2)}, u32[]{:S(2)}) collective-permute-start(f32[3,256,256]{2,1,0:T(8,128)} %collective-permute-done.refs_0_), channel_id=1, source_target_pairs={{0,16},{4,12},{8,24},{12,4},{16,0},{20,28},{24,8},{28,20},{1,17},{... | collective-permute-start | bytes 2359304 | tf_op jit(solution)/shard_map/ppermute | solution.py:790
  136.9 32.4 %collective-permute-start.1 = (f32[3,256,256]{2,1,0:T(8,128)}, f32[3,256,256]{2,1,0:T(8,128)}, u32[]{:S(2)}, u32[]{:S(2)}) collective-permute-start(f32[3,256,256]{2,1,0:T(8,128)} %collective-permute-done.refs_0_), channel_id=1, source_target_pairs={{0,8},{4,20},{8,0},{12,28},{16,24},{20,4},{24,16},{28,12},{1,9},{5... | collective-permute-start | bytes 2359304 | tf_op jit(solution)/shard_map/ppermute | solution.py:789
  138.4 32.3 %collective-permute-start.13 = (f32[3,256,256]{2,1,0:T(8,128)}, f32[3,256,256]{2,1,0:T(8,128)}, u32[]{:S(2)}, u32[]{:S(2)}) collective-permute-start(f32[3,256,256]{2,1,0:T(8,128)} %collective-permute-done.refs_0_), channel_id=1, source_target_pairs={{0,4},{4,0},{8,12},{12,8},{16,20},{20,16},{24,28},{28,24},{1,5},{5... | collective-permute-start | bytes 2359304 | tf_op jit(solution)/shard_map/ppermute | solution.py:785
  138.4 32.3 %collective-permute-start.29 = (f32[3,64,1024]{2,1,0:T(8,128)}, f32[3,64,1024]{2,1,0:T(8,128)}, u32[]{:S(2)}, u32[]{:S(2)}) collective-permute-start(f32[3,64,1024]{2,1,0:T(8,128)} %copy-done.18), channel_id=1, source_target_pairs={{0,8},{4,20},{8,0},{12,28},{16,24},{20,4},{24,16},{28,12},{1,9},{5... | collective-permute-start | bytes 2359304 | tf_op jit(solution)/shard_map/ppermute | solution.py:791
  147.3 24.0 %collective-permute-start.7 = (f32[3,256,256]{2,1,0:T(8,128)}, f32[3,256,256]{2,1,0:T(8,128)}, u32[]{:S(2)}, u32[]{:S(2)}) collective-permute-start(f32[3,256,256]{2,1,0:T(8,128)} %copy-done.23), channel_id=1, source_target_pairs={{0,16},{4,12},{8,24},{12,4},{16,0},{20,28},{24,8},{28,20},{1,17},{... | collective-permute-start | bytes 2359304 | tf_op jit(solution)/shard_map/ppermute | solution.py:790
  148.9 25.6 %collective-permute-start.3 = (f32[3,256,256]{2,1,0:T(8,128)}, f32[3,256,256]{2,1,0:T(8,128)}, u32[]{:S(2)}, u32[]{:S(2)}) collective-permute-start(f32[3,256,256]{2,1,0:T(8,128)} %collective-permute-done.2.refs_2_), channel_id=1, source_target_pairs={{0,8},{4,20},{8,0},{12,28},{16,24},{20,4},{24,16},{28,12},{1,9},{5... | collective-permute-start | bytes 2359304 | tf_op jit(solution)/shard_map/ppermute | solution.py:791
  169.4 22.0 %collective-permute-start.6 = (f32[3,256,256]{2,1,0:T(8,128)S(1)}, f32[3,256,256]{2,1,0:T(8,128)S(1)}, u32[]{:S(2)}, u32[]{:S(2)}) collective-permute-start(f32[3,256,256]{2,1,0:T(8,128)S(1)} %copy-done.24), channel_id=1, source_target_pairs={{0,8},{4,20},{8,0},{12,28},{16,24},{20,4},{24,16},{28,12},{1,9},{5... | collective-permute-start | bytes 2359304 | tf_op jit(solution)/shard_map/ppermute | solution.py:789
  170.8 22.4 %collective-permute-start.15 = (f32[3,256,256]{2,1,0:T(8,128)}, f32[3,256,256]{2,1,0:T(8,128)S(1)}, u32[]{:S(2)}, u32[]{:S(2)}) collective-permute-start(f32[3,256,256]{2,1,0:T(8,128)} %collective-permute-done.2.refs_2_), channel_id=1, source_target_pairs={{0,4},{4,0},{8,12},{12,8},{16,20},{20,16},{24,28},{28,24},{1,5},{5... | collective-permute-start | bytes 2359304 | tf_op jit(solution)/shard_map/ppermute | solution.py:785
  170.8 20.7 %collective-permute-start.14 = (f32[3,256,256]{2,1,0:T(8,128)}, f32[3,256,256]{2,1,0:T(8,128)S(1)}, u32[]{:S(2)}, u32[]{:S(2)}) collective-permute-start(f32[3,256,256]{2,1,0:T(8,128)} %collective-permute-done.1.refs_1_), channel_id=1, source_target_pairs={{0,4},{4,0},{8,12},{12,8},{16,20},{20,16},{24,28},{28,24},{1,5},{5... | collective-permute-start | bytes 2359304 | tf_op jit(solution)/shard_map/ppermute | solution.py:785
  171.3 22.0 %collective-permute-start.8 = (f32[3,256,256]{2,1,0:T(8,128)}, f32[3,256,256]{2,1,0:T(8,128)}, u32[]{:S(2)}, u32[]{:S(2)}) collective-permute-start(f32[3,256,256]{2,1,0:T(8,128)} %collective-permute-done.7.refs_2_), channel_id=1, source_target_pairs={{0,8},{4,20},{8,0},{12,28},{16,24},{20,4},{24,16},{28,12},{1,9},{5... | collective-permute-start | bytes 2359304 | tf_op jit(solution)/shard_map/ppermute | solution.py:791
  174.5 19.1 %collective-permute-start.16 = (f32[3,256,256]{2,1,0:T(8,128)}, f32[3,256,256]{2,1,0:T(8,128)S(1)}, u32[]{:S(2)}, u32[]{:S(2)}) collective-permute-start(f32[3,256,256]{2,1,0:T(8,128)} %collective-permute-done.3.refs_3_), channel_id=1, source_target_pairs={{0,4},{4,0},{8,12},{12,8},{16,20},{20,16},{24,28},{28,24},{1,5},{5... | collective-permute-start | bytes 2359304 | tf_op jit(solution)/shard_map/ppermute | solution.py:785
  191.4 19.7 %collective-permute-start.9 = (f32[3,256,256]{2,1,0:T(8,128)S(1)}, f32[3,256,256]{2,1,0:T(8,128)}, u32[]{:S(2)}, u32[]{:S(2)}) collective-permute-start(f32[3,256,256]{2,1,0:T(8,128)S(1)} %copy-done.24), channel_id=1, source_target_pairs={{0,4},{4,0},{8,12},{12,8},{16,20},{20,16},{24,28},{28,24},{1,5},{5... | collective-permute-start | bytes 2359304 | tf_op jit(solution)/shard_map/ppermute | solution.py:785
  191.5 19.8 %collective-permute-start.19 = (f32[3,256,256]{2,1,0:T(8,128)}, f32[3,256,256]{2,1,0:T(8,128)S(1)}, u32[]{:S(2)}, u32[]{:S(2)}) collective-permute-start(f32[3,256,256]{2,1,0:T(8,128)} %collective-permute-done.18.refs_2_), channel_id=1, source_target_pairs={{0,8},{4,20},{8,0},{12,28},{16,24},{20,4},{24,16},{28,12},{1,9},{5... | collective-permute-start | bytes 2359304 | tf_op jit(solution)/shard_map/ppermute | solution.py:791
  193.1 19.2 %collective-permute-start.11 = (f32[3,256,256]{2,1,0:T(8,128)}, f32[3,256,256]{2,1,0:T(8,128)}, u32[]{:S(2)}, u32[]{:S(2)}) collective-permute-start(f32[3,256,256]{2,1,0:T(8,128)} %collective-permute-done.7.refs_2_), channel_id=1, source_target_pairs={{0,4},{4,0},{8,12},{12,8},{16,20},{20,16},{24,28},{28,24},{1,5},{5... | collective-permute-start | bytes 2359304 | tf_op jit(solution)/shard_map/ppermute | solution.py:785
  193.3 18.4 %collective-permute-start.10 = (f32[3,256,256]{2,1,0:T(8,128)S(1)}, f32[3,256,256]{2,1,0:T(8,128)}, u32[]{:S(2)}, u32[]{:S(2)}) collective-permute-start(f32[3,256,256]{2,1,0:T(8,128)S(1)} %collective-permute-done.6.refs_1_), channel_id=1, source_target_pairs={{0,4},{4,0},{8,12},{12,8},{16,20},{20,16},{24,28},{28,24},{1,5},{5... | collective-permute-start | bytes 2359304 | tf_op jit(solution)/shard_map/ppermute | solution.py:785
  193.6 19.0 %collective-permute-start.12 = (f32[3,256,256]{2,1,0:T(8,128)}, f32[3,256,256]{2,1,0:T(8,128)}, u32[]{:S(2)}, u32[]{:S(2)}) collective-permute-start(f32[3,256,256]{2,1,0:T(8,128)} %collective-permute-done.8.refs_3_), channel_id=1, source_target_pairs={{0,4},{4,0},{8,12},{12,8},{16,20},{20,16},{24,28},{28,24},{1,5},{5... | collective-permute-start | bytes 2359304 | tf_op jit(solution)/shard_map/ppermute | solution.py:785
  211.1 23.1 %collective-permute-start.22 = (f32[3,256,256]{2,1,0:T(8,128)}, f32[3,256,256]{2,1,0:T(8,128)S(1)}, u32[]{:S(2)}, u32[]{:S(2)}) collective-permute-start(f32[3,256,256]{2,1,0:T(8,128)} %collective-permute-done.18.refs_2_), channel_id=1, source_target_pairs={{0,4},{4,0},{8,12},{12,8},{16,20},{20,16},{24,28},{28,24},{1,5},{5... | collective-permute-start | bytes 2359304 | tf_op jit(solution)/shard_map/ppermute | solution.py:785
  211.4 22.8 %collective-permute-start.21 = (f32[3,256,256]{2,1,0:T(8,128)}, f32[3,256,256]{2,1,0:T(8,128)}, u32[]{:S(2)}, u32[]{:S(2)}) collective-permute-start(f32[3,256,256]{2,1,0:T(8,128)} %collective-permute-done.17.refs_1_), channel_id=1, source_target_pairs={{0,4},{4,0},{8,12},{12,8},{16,20},{20,16},{24,28},{28,24},{1,5},{5... | collective-permute-start | bytes 2359304 | tf_op jit(solution)/shard_map/ppermute | solution.py:785
  211.7 33.1 %collective-permute-start.42 = (f32[1,256,1024]{2,1,0:T(8,128)S(1)}, f32[1,256,1024]{2,1,0:T(8,128)}, u32[]{:S(2)}, u32[]{:S(2)}) collective-permute-start(f32[1,256,1024]{2,1,0:T(8,128)S(1)} %constant_dynamic-slice_fusion), channel_id=1, source_target_pairs={{0,1},{1,2},{2,3},{3,0},{4,7},{5,4},{6,5},{7,6},{8,9},{9,10},{10,1... | collective-permute-start | bytes 3145736 | tf_op jit(solution)/shard_map/ppermute | solution.py:838
  212.3 33.1 %collective-permute-start.36 = (f32[2,256,1024]{2,1,0:T(8,128)S(1)}, f32[2,256,1024]{2,1,0:T(8,128)S(1)}, u32[]{:S(2)}, u32[]{:S(2)}) collective-permute-start(f32[2,256,1024]{2,1,0:T(8,128)S(1)} %copy-done.4), channel_id=1, source_target_pairs={{0,16},{4,12},{8,24},{12,4},{16,0},{20,28},{24,8},{28,20},{1,17},{... | collective-permute-start | bytes 6291464 | tf_op jit(solution)/shard_map/ppermute | solution.py:790
  212.7 22.1 %collective-permute-start.23 = (f32[3,256,256]{2,1,0:T(8,128)}, f32[3,256,256]{2,1,0:T(8,128)}, u32[]{:S(2)}, u32[]{:S(2)}) collective-permute-start(f32[3,256,256]{2,1,0:T(8,128)} %copy-done.26), channel_id=1, source_target_pairs={{0,4},{4,0},{8,12},{12,8},{16,20},{20,16},{24,28},{28,24},{1,5},{5... | collective-permute-start | bytes 2359304 | tf_op jit(solution)/shard_map/ppermute | solution.py:785
  243.1 47.0 %collective-permute-start.35 = (f32[2,256,1024]{2,1,0:T(8,128)S(1)}, f32[2,256,1024]{2,1,0:T(8,128)}, u32[]{:S(2)}, u32[]{:S(2)}) collective-permute-start(f32[2,256,1024]{2,1,0:T(8,128)S(1)} %copy-done.4), channel_id=1, source_target_pairs={{0,8},{4,20},{8,0},{12,28},{16,24},{20,4},{24,16},{28,12},{1,9},{5... | collective-permute-start | bytes 6291464 | tf_op jit(solution)/shard_map/ppermute | solution.py:789
  244.8 90.0 %collective-permute-start.38 = (f32[2,256,1024]{2,1,0:T(8,128)S(1)}, f32[2,256,1024]{2,1,0:T(8,128)S(1)}, u32[]{:S(2)}, u32[]{:S(2)}) collective-permute-start(f32[2,256,1024]{2,1,0:T(8,128)S(1)} %copy-done.4), channel_id=1, source_target_pairs={{0,4},{4,0},{8,12},{12,8},{16,20},{20,16},{24,28},{28,24},{1,5},{5... | collective-permute-start | bytes 6291464 | tf_op jit(solution)/shard_map/ppermute | solution.py:785
  244.8 91.8 %collective-permute-start.44 = (f32[1,256,1024]{2,1,0:T(8,128)}, f32[1,256,1024]{2,1,0:T(8,128)S(1)}, u32[]{:S(2)}, u32[]{:S(2)}) collective-permute-start(f32[1,256,1024]{2,1,0:T(8,128)} %collective-permute-done.42.refs_0_), channel_id=1, source_target_pairs={{0,16},{4,12},{8,24},{12,4},{16,0},{20,28},{24,8},{28,20},{1,17},{... | collective-permute-start | bytes 3145736 | tf_op jit(solution)/shard_map/ppermute | solution.py:790
  245.4 57.6 %collective-permute-start.37 = (f32[2,256,1024]{2,1,0:T(8,128)S(1)}, f32[2,256,1024]{2,1,0:T(8,128)}, u32[]{:S(2)}, u32[]{:S(2)}) collective-permute-start(f32[2,256,1024]{2,1,0:T(8,128)S(1)} %collective-permute-done.36.refs_2_), channel_id=1, source_target_pairs={{0,8},{4,20},{8,0},{12,28},{16,24},{20,4},{24,16},{28,12},{1,9},{5... | collective-permute-start | bytes 6291464 | tf_op jit(solution)/shard_map/ppermute | solution.py:791
  290.0 71.7 %collective-permute-start.40 = (f32[2,256,1024]{2,1,0:T(8,128)S(1)}, f32[2,256,1024]{2,1,0:T(8,128)}, u32[]{:S(2)}, u32[]{:S(2)}) collective-permute-start(f32[2,256,1024]{2,1,0:T(8,128)S(1)} %collective-permute-done.36.refs_2_), channel_id=1, source_target_pairs={{0,4},{4,0},{8,12},{12,8},{16,20},{20,16},{24,28},{28,24},{1,5},{5... | collective-permute-start | bytes 6291464 | tf_op jit(solution)/shard_map/ppermute | solution.py:785
  290.1 71.1 %collective-permute-start.39 = (f32[2,256,1024]{2,1,0:T(8,128)}, f32[2,256,1024]{2,1,0:T(8,128)}, u32[]{:S(2)}, u32[]{:S(2)}) collective-permute-start(f32[2,256,1024]{2,1,0:T(8,128)} %collective-permute-done.35.refs_1_), channel_id=1, source_target_pairs={{0,4},{4,0},{8,12},{12,8},{16,20},{20,16},{24,28},{28,24},{1,5},{5... | collective-permute-start | bytes 6291464 | tf_op jit(solution)/shard_map/ppermute | solution.py:785
  303.0 58.8 %collective-permute-start.41 = (f32[2,256,1024]{2,1,0:T(8,128)}, f32[2,256,1024]{2,1,0:T(8,128)}, u32[]{:S(2)}, u32[]{:S(2)}) collective-permute-start(f32[2,256,1024]{2,1,0:T(8,128)} %collective-permute-done.37.refs_3_), channel_id=1, source_target_pairs={{0,4},{4,0},{8,12},{12,8},{16,20},{20,16},{24,28},{28,24},{1,5},{5... | collective-permute-start | bytes 6291464 | tf_op jit(solution)/shard_map/ppermute | solution.py:785
  334.9 20.9 %collective-permute-start.43 = (f32[1,256,1024]{2,1,0:T(8,128)}, f32[1,256,1024]{2,1,0:T(8,128)S(1)}, u32[]{:S(2)}, u32[]{:S(2)}) collective-permute-start(f32[1,256,1024]{2,1,0:T(8,128)} %collective-permute-done.42.refs_0_), channel_id=1, source_target_pairs={{0,8},{4,20},{8,0},{12,28},{16,24},{20,4},{24,16},{28,12},{1,9},{5... | collective-permute-start | bytes 3145736 | tf_op jit(solution)/shard_map/ppermute | solution.py:789
  336.6 24.6 %collective-permute-start.45 = (f32[1,256,1024]{2,1,0:T(8,128)S(1)}, f32[1,256,1024]{2,1,0:T(8,128)S(1)}, u32[]{:S(2)}, u32[]{:S(2)}) collective-permute-start(f32[1,256,1024]{2,1,0:T(8,128)S(1)} %collective-permute-done.44.refs_2_), channel_id=1, source_target_pairs={{0,8},{4,20},{8,0},{12,28},{16,24},{20,4},{24,16},{28,12},{1,9},{5... | collective-permute-start | bytes 3145736 | tf_op jit(solution)/shard_map/ppermute | solution.py:791
  355.8 24.4 %collective-permute-start.46 = (f32[1,256,1024]{2,1,0:T(8,128)}, f32[1,256,1024]{2,1,0:T(8,128)S(1)}, u32[]{:S(2)}, u32[]{:S(2)}) collective-permute-start(f32[1,256,1024]{2,1,0:T(8,128)} %collective-permute-done.42.refs_0_), channel_id=1, source_target_pairs={{0,4},{4,0},{8,12},{12,8},{16,20},{20,16},{24,28},{28,24},{1,5},{5... | collective-permute-start | bytes 3145736 | tf_op jit(solution)/shard_map/ppermute | solution.py:785
  361.2 19.0 %collective-permute-start.48 = (f32[1,256,1024]{2,1,0:T(8,128)S(1)}, f32[1,256,1024]{2,1,0:T(8,128)S(1)}, u32[]{:S(2)}, u32[]{:S(2)}) collective-permute-start(f32[1,256,1024]{2,1,0:T(8,128)S(1)} %collective-permute-done.44.refs_2_), channel_id=1, source_target_pairs={{0,4},{4,0},{8,12},{12,8},{16,20},{20,16},{24,28},{28,24},{1,5},{5... | collective-permute-start | bytes 3145736 | tf_op jit(solution)/shard_map/ppermute | solution.py:785
  361.2 19.0 %collective-permute-start.47 = (f32[1,256,1024]{2,1,0:T(8,128)S(1)}, f32[1,256,1024]{2,1,0:T(8,128)}, u32[]{:S(2)}, u32[]{:S(2)}) collective-permute-start(f32[1,256,1024]{2,1,0:T(8,128)S(1)} %collective-permute-done.43.refs_1_), channel_id=1, source_target_pairs={{0,4},{4,0},{8,12},{12,8},{16,20},{20,16},{24,28},{28,24},{1,5},{5... | collective-permute-start | bytes 3145736 | tf_op jit(solution)/shard_map/ppermute | solution.py:785
  361.7 18.5 %collective-permute-start.49 = (f32[1,256,1024]{2,1,0:T(8,128)S(1)}, f32[1,256,1024]{2,1,0:T(8,128)S(1)}, u32[]{:S(2)}, u32[]{:S(2)}) collective-permute-start(f32[1,256,1024]{2,1,0:T(8,128)S(1)} %collective-permute-done.45.refs_3_), channel_id=1, source_target_pairs={{0,4},{4,0},{8,12},{12,8},{16,20},{20,16},{24,28},{28,24},{1,5},{5... | collective-permute-start | bytes 3145736 | tf_op jit(solution)/shard_map/ppermute | solution.py:785
  452.2 159.9 %reduce-scatter.6.cloned.1.call-start = ((), (), s32[]{:S(2)}) async-start(), calls=%async_computation.4 | async-start | bytes 3538944 | tf_op jit(solution)/shard_map/reduce_scatter | solution.py:844
  463.5 163.7 %reduce-scatter.8.cloned.1.call-start = ((), (), s32[]{:S(2)}) async-start(), calls=%async_computation.5 | async-start | bytes 9437184 | tf_op jit(solution)/shard_map/reduce_scatter | solution.py:844
  491.9 78.9 %collective-permute-start.53 = (f32[4,3,128,256]{3,2,1,0:T(8,128)}, f32[4,3,128,256]{3,2,1,0:T(8,128)S(1)}, u32[]{:S(2)}, u32[]{:S(2)}) collective-permute-start(f32[4,3,128,256]{3,2,1,0:T(8,128)} %get-tuple-element.114), channel_id=1, source_target_pairs={{0,4},{4,0},{8,12},{12,8},{16,20},{20,16},{24,28},{28,24},{1,5},{5... | collective-permute-start | bytes 4718600 | tf_op jit(solution)/shard_map/ppermute | solution.py:785
  571.2 28.9 %collective-permute-start.54 = (f32[2,3,128,256]{3,2,1,0:T(8,128)S(1)}, f32[2,3,128,256]{3,2,1,0:T(8,128)S(1)}, u32[]{:S(2)}, u32[]{:S(2)}) collective-permute-start(f32[2,3,128,256]{3,2,1,0:T(8,128)S(1)} %slice.97), channel_id=1, source_target_pairs={{0,8},{4,20},{8,0},{12,28},{16,24},{20,4},{24,16},{28,12},{1,9},{5... | collective-permute-start | bytes 2359304 | tf_op jit(solution)/shard_map/ppermute | solution.py:849
  (42 other events, 729.8 us)
Sparse Core Ops, SparseCore 0:
  452.3 39.5 reduce-scatter.3
  495.7 46.2 reduce-scatter.5
  545.5 81.5 reduce-scatter.7

commit v3 on v2

--- a/solution.py
+++ b/solution.py
@@ -49,6 +49,40 @@
 
 def at(dims, index):
     return pl.BlockSpec(dims, lambda *_: index)
+
+
+def once(dims):
+    rank = len(dims)
+    return pl.BlockSpec(dims, lambda *_: (0,) * rank, pipeline_mode=pl.Buffered(1))
+
+
+def anywhere():
+    return pl.BlockSpec(memory_space=pl.ANY)
+
+
+def launch(kernel, args, in_specs, out_specs, out_shape, scratch=(), wait=(), carry=(), **options):
+    args, wait, carry = list(args), list(wait), list(carry)
+    count, extra, outs = len(args), len(wait) + len(carry), len(out_shape)
+
+    def body(*refs):
+        results = refs[count + extra : count + extra + outs]
+        kernel(*refs[:count], *results, *refs[count + extra + outs + len(carry) :])
+
+    return pl.pallas_call(
+        body,
+        in_specs=list(in_specs) + [anywhere()] * extra,
+        out_specs=list(out_specs) + [anywhere()] * len(carry),
+        out_shape=list(out_shape) + [shape(value.shape, value.dtype) for value in carry],
+        scratch_shapes=list(scratch),
+        input_output_aliases={count + len(wait) + k: outs + k for k in range(len(carry))},
+        **options,
+    )(*args, *wait, *carry)
+
+
+def gate(wait, carry):
+    return launch(
+        lambda: None, [], [], [], [], wait=wait, carry=[carry], name="gate", cost_estimate=cost(1)
+    )[0]
 
 
 def rows_of(tile, width):
@@ -89,15 +123,16 @@
 
 def norm_first(tokens, gain, shift):
     rows, width = tokens.shape
-    return pl.pallas_call(
+    return launch(
         norm_kernel,
+        [tokens, gain, shift],
+        [rows_of(BLK, width), whole((1, width)), whole((1, width))],
+        [rows_of(BLK, width)],
+        [shape((rows, width), BF16)],
         grid=(rows // BLK,),
-        in_specs=[rows_of(BLK, width), whole((1, width)), whole((1, width))],
-        out_specs=rows_of(BLK, width),
-        out_shape=shape((rows, width), BF16),
         name="norm_first",
         cost_estimate=cost(6),
-    )(tokens, gain, shift)
+    )[0]
 
 
 def head_row(width, head, value):
@@ -123,26 +158,55 @@
     return (0, 1 + core, 2 - core, 3)
 
 
-def fill(targets, refs, chip, core):
-    for ref, offset in zip(refs, offsets(core)):
-        rows = ref.shape[1]
-        place = pl.multiple_of((chip ^ offset) * rows, rows)
-        for k, target in enumerate(targets):
-            target[pl.ds(place, rows), :] = ref[k].astype(BF16)
-
-
-def fill_two(first, second, mine, other, me, flip=1):
-    chip, core = me[0], me[1]
-
+def join_kernel(me, *refs):
+    parts, (target, sems) = refs[:4], refs[4:]
+    copies = []
+    for index, (part, offset) in enumerate(zip(parts, offsets(me[1]))):
+        rows = part.shape[1]
+        place = pl.multiple_of((me[0] ^ offset) * rows, rows)
+        for k in range(part.shape[0]):
+            copies.append(
+                pltpu.make_async_copy(
+                    part.at[k], target.at[k, pl.ds(place, rows)], sems.at[index, k]
+                )
+            )
+    for copy in copies:
+        copy.start()
+    for copy in copies:
+        copy.wait()
+
+
+def join(me, parts, wait):
+    count, rows, width = parts[0].shape
+    return launch(
+        join_kernel,
+        [me, *parts],
+        [smem()] + [anywhere()] * 4,
+        [vmem()],
+        [shape((count, 4 * rows, width))],
+        scratch=[pltpu.SemaphoreType.DMA((4, count))],
+        wait=wait,
+        compiler_params=params(24),
+        name="join",
+        cost_estimate=cost(2),
+    )[0]
+
+
+def take(targets, source, flip=1):
+    for k, target in enumerate(targets[::flip]):
+        target[...] = source[k].astype(BF16)
+
+
+def take_two(first, second, mine, other, core, flip=1):
     @pl.when(core == 0)
     def _():
-        fill(first, mine, chip, 0)
-        fill(second, other, chip, 1)
+        take(first, mine)
+        take(second, other)
 
     @pl.when(core == 1)
     def _():
-        fill(second[::flip], mine, chip, 1)
-        fill(first[::flip], other, chip, 0)
+        take(second, mine, flip)
+        take(first, other, flip)
 
 
 def planes(ref):
@@ -207,85 +271,93 @@
                 self_block(qb, n, qkv, turned, mixed, logs)
 
 
-def front_kernel(own, me, lengths, first, *refs):
-    slots, (weights, *rest) = refs[:4], refs[4:]
-    core = me[1] if own else 1 - me[1]
-    fill(planes(weights), slots, me[0], core)
+def front_kernel(lengths, first, shard, weights, *rest):
+    take(planes(weights), shard)
     front_body(lengths, first, weights, *rest)
 
 
-def front_two_kernel(me, lengths, first, *refs):
-    mine, other, (weights, cross, *rest) = refs[:4], refs[4:8], refs[8:]
-    fill_two(planes(weights), planes(cross), mine, other, me)
-    front_body(lengths, first, weights, *rest)
+def front_two_kernel(me, lengths, first, mine, other, text, weights, cross, qkv, mixed, logs, pair, turned):
+    take_two(planes(weights), planes(cross), mine, other, me[1])
+    text_pair(pair, text, cross)
+    front_body(lengths, first, weights, qkv, mixed, logs, turned)
 
 
 def vmem():
     return pl.BlockSpec(memory_space=pltpu.VMEM)
 
 
-def front_call(kernel, name, us, prefix, first, arrays, weight_count):
+def front_call(kernel, name, us, prefix, first, arrays, weight_count, more, wait, carry=()):
     rows, depth = first.shape
     width = arrays[0].shape[2]
     outs = [shape((3, depth, width), BF16)] * weight_count + [
         shape((3, rows, width), BF16),
         shape((rows, width), BF16),
         shape((8, rows), F32),
-    ]
-    return pl.pallas_call(
+    ] + more
+    return launch(
         kernel,
-        in_specs=[smem()] * len(prefix) + [vmem()] * (1 + len(arrays)),
-        out_specs=[vmem()] * len(outs),
-        out_shape=outs,
-        scratch_shapes=[pltpu.VMEM((width, rows), BF16)],
+        [*prefix, first, *arrays],
+        [smem()] * len(prefix) + [vmem()] * (1 + len(arrays)),
+        [vmem()] * len(outs),
+        outs,
+        scratch=[pltpu.VMEM((width, rows), BF16)],
+        wait=wait,
+        carry=carry,
         compiler_params=params(),
         name=name,
         cost_estimate=cost(us),
-    )(*prefix, first, *arrays)
-
-
-def front_own(lengths, first, weights):
-    return front_call(front_body, "front_own", 12, (lengths,), first, [weights], 0)
-
-
-def front(own, me, lengths, first, arrays):
-    kernel = partial(front_kernel, own)
-    return front_call(kernel, "front", 14, (me, lengths), first, arrays, 1)
-
-
-def front_two(me, lengths, first, arrays):
-    return front_call(front_two_kernel, "front_two", 15, (me, lengths), first, arrays, 2)
-
-
-def text_front_kernel(me, text, own, two, *refs):
-    mine, other, (cross_a, cross_b, *pairs) = refs[:4], refs[4:8], refs[8:]
-    fill(planes(cross_a), mine, me[0], me[1])
-    fill(planes(cross_b), other, me[0], 1 - me[1])
-    for pair, cross in zip(pairs, (own, cross_a, two, cross_b)):
-        for m in range(2):
-            pair[m] = dot(text[...], cross[m + 1]).astype(BF16)
-
-
-def text_front(me, text, own, two, arrays):
+    )
+
+
+def front_own(lengths, first, weights, wait):
+    return front_call(front_body, "front_own", 15, (lengths,), first, [weights], 0, [], wait)
+
+
+def front(lengths, first, shard, wait, carry):
+    return front_call(front_kernel, "front", 16, (lengths,), first, [shard], 1, [], wait, carry)
+
+
+def front_two(me, lengths, first, arrays, text, wait):
+    pair = shape((2, text.shape[0], arrays[0].shape[2]), BF16)
+    return front_call(
+        front_two_kernel, "front_two", 18, (me, lengths), first, [*arrays, text], 2, [pair], wait
+    )
+
+
+def text_pair(pair, text, cross):
+    for m in range(2):
+        pair[m] = dot(text[...], cross[m + 1]).astype(BF16)
+
+
+def text_front_kernel(text, own, mine, other, cross_a, cross_b, *pairs):
+    take(planes(cross_a), mine)
+    take(planes(cross_b), other)
+    for pair, cross in zip(pairs, (own, cross_a, cross_b)):
+        text_pair(pair, text, cross)
+
+
+def text_front(text, own, arrays, wait):
     rows = text.shape[0]
     width = own.shape[2]
-    outs = [shape(own.shape, BF16)] * 2 + [shape((2, rows, width), BF16)] * 4
-    return pl.pallas_call(
+    outs = [shape(own.shape, BF16)] * 2 + [shape((2, rows, width), BF16)] * 3
+    return launch(
         text_front_kernel,
-        in_specs=[smem()] + [vmem()] * 11,
-        out_specs=[vmem()] * 6,
-        out_shape=outs,
+        [text, own, *arrays],
+        [vmem()] * 4,
+        [vmem()] * 5,
+        outs,
+        wait=wait,
         compiler_params=params(),
         name="text_front",
-        cost_estimate=cost(8),
-    )(me, text, own, two, *arrays)
+        cost_estimate=cost(7),
+    )
 
 
 def middle_kernel(me, lengths, live, tokens, gain1, shift1, gain2, shift2, own_out, own_co, *refs):
     mixed, refs = refs[:4], refs[4:]
     queries, refs = refs[:4], refs[4:]
     pairs, refs = refs[:4], refs[4:]
-    mine, other, refs = refs[:4], refs[4:8], refs[8:]
+    mine, other, *refs = refs
     w_out, w_co, after_self, after_cross, second, third, cross_query, looked, logs, turned = refs
     step = pl.program_id(0)
 
@@ -297,7 +369,7 @@
         parts = [
             [target.at[pl.ds((j + 1) * width, width)] for j in range(3)] for target in (w_out, w_co)
         ]
-        fill_two(*parts, mine, other, me, flip=-1)
+        take_two(*parts, mine, other, me[1], flip=-1)
         for j in range(4):
             turned[j] = pairs[j][1].T
 
@@ -336,36 +408,38 @@
 TEXT = 128
 
 
-def middle(me, lengths, live, tokens, norms, own_out, own_co, mixed, crosses, pairs, arrays):
+def middle(me, lengths, live, tokens, norms, own_out, own_co, mixed, crosses, pairs, arrays, wait):
     rows, depth = tokens.shape
     width = own_out.shape[0]
     text_rows = live.shape[0]
     inner = 4 * width
     row = whole((1, depth))
-    return pl.pallas_call(
+    return launch(
         middle_kernel,
-        grid=(rows // BLK,),
-        in_specs=[smem(), smem(), whole((text_rows, 1)), rows_of(BLK, depth)]
+        [me, lengths, live, tokens, *norms, own_out, own_co, *mixed, *crosses, *pairs, *arrays],
+        [smem(), smem(), whole((text_rows, 1)), rows_of(BLK, depth)]
         + [row] * 4
-        + [whole((width, depth))] * 2
+        + [once((width, depth))] * 2
         + [rows_of(BLK, width)] * 4
         + [at((1, depth, width), (0, 0, 0))] * 4
         + [whole((2, text_rows, width))] * 4
-        + [whole(arrays[0].shape)] * 8,
-        out_specs=[whole((inner, depth))] * 2
+        + [once(arrays[0].shape)] * 2,
+        [whole((inner, depth))] * 2
         + [rows_of(BLK, depth)] * 4
         + [rows_of(BLK, inner)] * 2
         + [pl.BlockSpec((inner // HEAD, BLK), lambda i: (0, i))],
-        out_shape=[shape((inner, depth), BF16)] * 2
+        [shape((inner, depth), BF16)] * 2
         + [shape((rows, depth)), shape((rows, depth))]
         + [shape((rows, depth), BF16)] * 2
         + [shape((rows, inner), BF16)] * 2
         + [shape((inner // HEAD, rows))],
-        scratch_shapes=[pltpu.VMEM((4, width, text_rows), BF16)],
+        scratch=[pltpu.VMEM((4, width, text_rows), BF16)],
+        wait=wait,
+        grid=(rows // BLK,),
         compiler_params=params(),
         name="middle",
         cost_estimate=cost(43),
-    )(me, lengths, live, tokens, *norms, own_out, own_co, *mixed, *crosses, *pairs, *arrays)
+    )
 
 
 ROOT = 0.7978845608028654
@@ -388,75 +462,110 @@
     return hidden, pre_grad, dot(hidden, down), dot(pre_grad, up, NT)
 
 
-def feed_own_kernel(third, cot, after, up, down, out, grad, both):
+def feed_own_kernel(me, third, cot, after, up, down, out, grad, keep, send, both):
     hidden, pre_grad, result, pushed = feed_rows(third[...], cot[...], up[...], down[...])
     out[...] = after[...] + result
     grad[...] = pushed
-    first = pl.program_id(0) == 0
+    step = pl.program_id(0)
     more_up = dot(third[...], pre_grad, TN)
     more_down = dot(hidden, cot[...], TN)
 
-    @pl.when(first)
+    @pl.when(step == 0)
     def _():
         both[0] = more_up
         both[1] = more_down
 
-    @pl.when(jnp.logical_not(first))
+    @pl.when(step > 0)
     def _():
         both[0] += more_up
         both[1] += more_down
 
+    @pl.when(step == pl.num_programs(0) - 1)
+    def _():
+        put_pieces(both, keep, send, me)
+
+
+def put_pieces(source, keep, send, me, first=0):
+    chip, core = me[0], me[1]
+    rows = source.shape[1] // 8
+    for target, owner in ((keep, core), (send, 1 - core)):
+        for index, offset in enumerate((0, 2 - owner, 1 + owner, 3)):
+            place = pl.multiple_of(((chip ^ offset) * 2 + owner) * rows, rows)
+            for k in range(source.shape[0]):
+                target[index, first + k] = source[k, pl.ds(place, rows), :]
+
 
 FEED = 320
 
 
-def feed_own(third, cot, after, up, down):
+def feed_own(me, third, cot, after, up, down, wait):
     rows, depth = third.shape
     inner = up.shape[1]
     tile = rows_of(FEED, depth)
-    return pl.pallas_call(
+    pieces = (4, 2, depth // 8, depth)
+    return launch(
         feed_own_kernel,
+        [me, third, cot, after, up, down],
+        [smem(), tile, tile, tile, once((depth, inner)), once((inner, depth))],
+        [tile, tile, once(pieces), once(pieces)],
+        [shape((rows, depth)), shape((rows, depth)), shape(pieces), shape(pieces)],
+        scratch=[pltpu.VMEM((2, depth, inner), F32)],
+        wait=wait,
         grid=(rows // FEED,),
-        in_specs=[tile, tile, tile, whole((depth, inner)), whole((inner, depth))],
-        out_specs=[tile, tile, whole((2, depth, inner))],
-        out_shape=[shape((rows, depth)), shape((rows, depth)), shape((2, depth, inner))],
         compiler_params=params(),
         name="feed_own",
         cost_estimate=cost(32),
-    )(third, cot, after, up, down)
-
-
-def feed_kernel(kind, me, third, cot, out_in, grad_in, *refs):
-    slots, (out, grad, both) = refs[:-3], refs[-3:]
-
+    )
+
+
+def feed_pair_kernel(third, cot, out_in, grad_in, mine, other, out, grad, one, two):
+    @pl.when(pl.program_id(0) == 0)
+    def _():
+        take(planes(one), mine)
+        take(planes(two), other)
+
+    _, _, result, pushed = feed_rows(third[...], cot[...], one[0], one[1])
+    _, _, more_result, more_pushed = feed_rows(third[...], cot[...], two[0], two[1])
+    out[...] = out_in[...] + (result + more_result)
+    grad[...] = grad_in[...] + (pushed + more_pushed)
+
+
+def feed_last_kernel(me, third, cot, out_in, grad_in, mine, other, out, grad, both):
     @pl.when(pl.program_id(0) == 0)
     def _():
         up, down = planes(both)
-        if kind == 2:
-            fill_two([up], [down], slots[:4], slots[4:], me)
-        else:
-            fill([up, down], slots, me[0], me[1] if kind == 0 else 1 - me[1])
+        take_two([up], [down], mine, other, me[1])
 
     _, _, result, pushed = feed_rows(third[...], cot[...], both[0], both[1])
-    out[...] = (out_in[...] + result).astype(out.dtype)
+    out[...] = (out_in[...] + result).astype(BF16)
     grad[...] = grad_in[...] + pushed
 
 
-def feed(kind, me, third, cot, out, grad, arrays, dtype):
+def feed_call(kernel, name, us, prefix, dtype, copies, third, cot, out, grad, arrays, wait, carry=()):
     rows, depth = third.shape
-    inner = arrays[0].shape[2]
     tile = rows_of(FEED, depth)
-    return pl.pallas_call(
-        partial(feed_kernel, kind),
+    return launch(
+        kernel,
+        [*prefix, third, cot, out, grad, *arrays],
+        [smem()] * len(prefix) + [tile] * 4 + [once(arrays[0].shape)] * 2,
+        [tile, tile],
+        [shape((rows, depth), dtype), shape((rows, depth))],
+        scratch=[pltpu.VMEM((2,) + arrays[0].shape[1:], BF16)] * copies,
+        wait=wait,
+        carry=carry,
         grid=(rows // FEED,),
-        in_specs=[smem(), tile, tile, tile, tile] + [whole(arrays[0].shape)] * len(arrays),
-        out_specs=[tile, tile],
-        out_shape=[shape((rows, depth), dtype), shape((rows, depth))],
-        scratch_shapes=[pltpu.VMEM((2, depth, inner), BF16)],
         compiler_params=params(),
-        name="feed",
-        cost_estimate=cost(18),
-    )(me, third, cot, out, grad, *arrays)
+        name=name,
+        cost_estimate=cost(us),
+    )
+
+
+def feed_pair(*operands):
+    return feed_call(feed_pair_kernel, "feed_pair", 30, (), F32, 2, *operands)
+
+
+def feed_last(me, *operands):
+    return feed_call(feed_last_kernel, "feed_last", 18, (me,), BF16, 1, *operands)
 
 
 def back_kernel(
@@ -534,7 +643,7 @@
 
 def back(
     lengths, live, third_grad, cot, after_cross, after_self, cross_query, looked, mixed0, logs,
-    gain1, gain2, w_out, w_co, crosses, pairs,
+    gain1, gain2, w_out, w_co, crosses, pairs, wait,
 ):
     rows, depth = cot.shape
     text_rows = live.shape[0]
@@ -542,19 +651,20 @@
     inner = 4 * width
     tile = rows_of(BLK, depth)
     row = whole((1, depth))
-    return pl.pallas_call(
+    return launch(
         back_kernel,
-        grid=(rows // BLK,),
-        in_specs=[smem(), whole((text_rows, 1))]
+        [lengths, live, third_grad, cot, after_cross, after_self, cross_query, looked, mixed0]
+        + [logs, gain1, gain2, w_out, w_co, *crosses, *pairs],
+        [smem(), whole((text_rows, 1))]
         + [tile] * 4
         + [rows_of(BLK, inner), rows_of(BLK, width), rows_of(BLK, width)]
         + [pl.BlockSpec((inner // HEAD, BLK), lambda i: (0, i)), row, row]
         + [whole((inner, depth))] * 2
         + [at((1, depth, width), (0, 0, 0))] * 4
         + [whole((2, text_rows, width))] * 4,
-        out_specs=[tile, rows_of(BLK, inner), whole((4, 2, text_rows, width))]
+        [tile, rows_of(BLK, inner), whole((4, 2, text_rows, width))]
         + [whole((2, width, depth)), rows_of(BLK, width), whole((8, depth))],
-        out_shape=[
+        [
             shape((rows, depth)),
             shape((rows, inner), BF16),
             shape((4, 2, text_rows, width), BF16),
@@ -562,21 +672,20 @@
             shape((rows, width), BF16),
             shape((8, depth)),
         ],
-        scratch_shapes=[
+        scratch=[
             pltpu.VMEM((4, 2, text_rows, width), F32),
             pltpu.VMEM((4, width, text_rows), BF16),
         ],
+        wait=wait,
+        grid=(rows // BLK,),
         compiler_params=params(),
         name="back",
         cost_estimate=cost(53),
-    )(
-        lengths, live, third_grad, cot, after_cross, after_self, cross_query, looked, mixed0, logs,
-        gain1, gain2, w_out, w_co, *crosses, *pairs,
-    )
-
-
-def text_kernel(text, pair_grad, second, query_grad, *refs):
-    crosses, (text_grad, cross_grad) = refs[:4], refs[4:]
+    )
+
+
+def text_kernel(me, text, pair_grad, second, query_grad, row_grads, qkv_grad, *refs):
+    crosses, (text_grad, keep, send, cross_grad, folded) = refs[:4], refs[4:]
     total = jnp.zeros(text_grad.shape, F32)
     for j in range(4):
         for m in range(2):
@@ -585,20 +694,41 @@
     cross_grad[0] = dot(second[...], query_grad[...], TN)
     for m in range(2):
         cross_grad[m + 1] = dot(text[...], pair_grad[0, m], TN)
-
-
-def text_back(text, pair_grad, second, query_grad, crosses):
+    put_pieces(cross_grad, keep, send, me)
+    put_pieces(qkv_grad, keep, send, me, 3)
+    width = folded.shape[2]
+    rows = row_grads.shape[1] // 8
+    for k in range(2):
+        for piece in range(8):
+            for part in range(4):
+                folded[k, pl.ds((piece * 4 + part) * rows, rows), :] = row_grads[
+                    k, pl.ds(piece * rows, rows), part * width : (part + 1) * width
+                ]
+    put_pieces(folded, keep, send, me, 6)
+
+
+def unfold(piece):
+    rows, width = piece.shape
+    parts = [piece[k * rows // 4 : (k + 1) * rows // 4] for k in range(4)]
+    return jnp.concatenate(parts, axis=1)
+
+
+def text_back(me, text, pair_grad, second, query_grad, row_grads, qkv_grad, crosses, wait):
     text_rows, depth = text.shape
     width = pair_grad.shape[3]
-    return pl.pallas_call(
+    pieces = (4, 8, depth // 8, width)
+    return launch(
         text_kernel,
-        in_specs=[vmem()] * 8,
-        out_specs=[vmem()] * 2,
-        out_shape=[shape((text_rows, depth)), shape((3, depth, width))],
+        [me, text, pair_grad, second, query_grad, row_grads, qkv_grad, *crosses],
+        [smem()] + [vmem()] * 10,
+        [vmem()] * 3,
+        [shape((text_rows, depth)), shape(pieces), shape(pieces)],
+        scratch=[pltpu.VMEM((3, depth, width), F32), pltpu.VMEM((2, depth, width), F32)],
+        wait=wait,
         compiler_params=params(),
         name="text_back",
-        cost_estimate=cost(9),
-    )(text, pair_grad, second, query_grad, *crosses)
+        cost_estimate=cost(15),
+    )
 
 
 def self_back_pair(qb, kb, diag, qkv, rows, grads, logs, means, turned, query_sum, key_sum, value_sum):
@@ -670,42 +800,38 @@
     ]
 
 
-def self_own_kernel(me, lengths, qkv, mixed, out_grad, logs, weights, first, total, keep, send, *scratch):
-    self_back_body(lengths, qkv, mixed, out_grad, logs, weights, *scratch[:-1])
-    triple, whole_grad = scratch[0], scratch[-1]
+def self_own_kernel(lengths, qkv, mixed, out_grad, logs, weights, first, total, qkv_grad, *scratch):
+    self_back_body(lengths, qkv, mixed, out_grad, logs, weights, *scratch)
+    triple = scratch[0]
     for m in range(3):
-        whole_grad[m] = dot(first[...], triple[m], TN)
-    put_pieces(whole_grad, keep, send, me)
+        qkv_grad[m] = dot(first[...], triple[m], TN)
     total[...] = sum(dot(triple[m], weights[m], NT) for m in range(3))
 
 
-def put_pieces(source, keep, send, me):
-    chip, core = me[0], me[1]
-    rows = keep.shape[2]
-    for target, owner in ((keep, core), (send, 1 - core)):
-        for index, offset in enumerate((0, 2 - owner, 1 + owner, 3)):
-            place = pl.multiple_of(((chip ^ offset) * 2 + owner) * rows, rows)
-            for k in range(keep.shape[1]):
-                target[index, k] = source[k, pl.ds(place, rows), :]
-
-
-def self_own(me, lengths, qkv, mixed, out_grad, logs, weights, first):
-    rows, depth = first.shape
-    width = mixed.shape[1]
-    pieces = (4, 3, depth // 8, width)
-    return pl.pallas_call(
-        self_own_kernel,
+def self_call(kernel, name, us, j, outs, operands, wait):
+    lengths, qkv, mixed, out_grad, logs, weights, last_in = operands
+    rows, width = mixed.shape
+    return launch(
+        kernel,
+        operands,
+        [smem()]
+        + [whole(qkv.shape), whole(mixed.shape), at((rows, width), (0, j))]
+        + [whole(logs.shape), whole(weights.shape), whole(last_in.shape)],
+        [whole(out.shape) for out in outs],
+        outs,
+        scratch=self_scratch(rows, width),
+        wait=wait,
         grid=(1,),
-        in_specs=[smem(), smem()]
-        + [whole((3, rows, width)), whole((rows, width)), at((rows, width), (0, 0))]
-        + [whole((8, rows)), whole((3, depth, width)), whole((rows, depth))],
-        out_specs=[whole((rows, depth)), whole(pieces), whole(pieces)],
-        out_shape=[shape((rows, depth)), shape(pieces), shape(pieces)],
-        scratch_shapes=self_scratch(rows, width) + [pltpu.VMEM((3, depth, width), F32)],
         compiler_params=params(),
-        name="self_own",
-        cost_estimate=cost(20),
-    )(me, lengths, qkv, mixed, out_grad, logs, weights, first)
+        name=name,
+        cost_estimate=cost(us),
+    )
+
+
+def self_own(lengths, qkv, mixed, out_grad, logs, weights, first, wait):
+    outs = [shape(first.shape), shape(weights.shape)]
+    operands = (lengths, qkv, mixed, out_grad, logs, weights, first)
+    return self_call(self_own_kernel, "self_own", 28, 0, outs, operands, wait)
 
 
 def self_kernel(lengths, qkv, mixed, out_grad, logs, weights, before, total, *scratch):
@@ -714,22 +840,9 @@
     total[...] = before[...] + sum(dot(triple[m], weights[m], NT) for m in range(3))
 
 
-def self_back(lengths, qkv, mixed, out_grad, logs, weights, before, j):
-    rows, depth = before.shape
-    width = mixed.shape[1]
-    return pl.pallas_call(
-        self_kernel,
-        grid=(1,),
-        in_specs=[smem()]
-        + [whole((3, rows, width)), whole((rows, width)), at((rows, width), (0, j))]
-        + [whole((8, rows)), whole((3, depth, width)), whole((rows, depth))],
-        out_specs=whole((rows, depth)),
-        out_shape=shape((rows, depth)),
-        scratch_shapes=self_scratch(rows, width),
-        compiler_params=params(),
-        name="self_back",
-        cost_estimate=cost(17.5),
-    )(lengths, qkv, mixed, out_grad, logs, weights, before)
+def self_back(lengths, qkv, mixed, out_grad, logs, weights, before, j, wait):
+    operands = (lengths, qkv, mixed, out_grad, logs, weights, before)
+    return self_call(self_kernel, "self_back", 26, j, [shape(before.shape)], operands, wait)[0]
 
 
 def last_kernel(first_grad, tokens, upstream, gain, token_grad, sums):
@@ -745,19 +858,21 @@
     sums[1:2, :] += shift_sum
 
 
-def last(first_grad, tokens, upstream, gain):
+def last(first_grad, tokens, upstream, gain, wait):
     rows, depth = tokens.shape
     tile = rows_of(BLK, depth)
-    return pl.pallas_call(
+    return launch(
         last_kernel,
+        [first_grad, tokens, upstream, gain],
+        [tile, tile, tile, whole((1, depth))],
+        [tile, whole((8, depth))],
+        [shape((rows, depth)), shape((8, depth))],
+        wait=wait,
         grid=(rows // BLK,),
-        in_specs=[tile, tile, tile, whole((1, depth))],
-        out_specs=[tile, whole((8, depth))],
-        out_shape=[shape((rows, depth)), shape((8, depth))],
         compiler_params=params(),
         name="last",
         cost_estimate=cost(10),
-    )(first_grad, tokens, upstream, gain)
+    )
 
 
 DP = 8
@@ -785,69 +900,44 @@
     return lax.ppermute(value, "dp", [(i, i ^ 1) for i in range(DP)])
 
 
-def spread(piece):
-    near = lax.ppermute(piece, "dp", beside(True))
-    side = lax.ppermute(piece, "dp", beside(False))
-    far = lax.ppermute(side, "dp", beside(True))
-    mine = [piece, near, side, far]
-    return mine, [swap(value) for value in mine]
-
-
 def cut(shard, chip):
     rows = shard.shape[1] // 4
     return lax.dynamic_slice_in_dim(shard, chip * rows, rows, 1).astype(F32)
 
 
-def sets(shard, other):
-    def parts(value, order):
-        rows = value.shape[1] // 4
-        return [value[:, k * rows : (k + 1) * rows] for k in order]
-
-    return parts(shard, (0, 1, 2, 3)), parts(other, (0, 2, 1, 3))
-
-
-def gather_whole(qkv, cross, outer, feeds):
-    def along(value, step):
-        return lax.ppermute(value.astype(F32), "mp", straight(step))
-
-    def joined(value):
-        return jnp.concatenate([along(value[None], step) for step in (1, 2, 3)], axis=0)
-
-    return (
-        sets(along(qkv, 1), along(qkv, 3)),
-        sets(along(qkv, 2), along(cross, 2)),
-        sets(along(cross, 1), along(cross, 3)),
-        sets(joined(outer[0]), joined(outer[1])),
-        sets(along(feeds, 1), along(feeds, 3)),
-        sets(along(feeds[:1], 2), along(feeds[1:], 2)),
-    )
-
-
-def gather(qkv, cross, outer, feeds, chip, core):
-    axes = ("dp", "mp")
-    own_qkv, own_cross = cut(qkv, chip), cut(cross, chip)
-    own_outer = cut(lax.dynamic_slice_in_dim(outer, core, 1, 0), chip)
-    own_feeds = cut(feeds, chip)
-    qkv_one = lax.ppermute(own_qkv, axes, ring(1))
-    cross_one = lax.ppermute(own_cross, axes, ring(1))
-    two = lax.ppermute(jnp.where(core == 0, qkv_one, cross_one), axes, ring(1))
-    outer_one = lax.ppermute(own_outer, "mp", straight(1))
-    outer_three = lax.ppermute(own_outer, "mp", straight(3))
-    outer_two = lax.ppermute(outer_one, "mp", straight(1))
-    feed_one = lax.ppermute(own_feeds, axes, ring(1))
-    feed_two = lax.ppermute(lax.dynamic_slice_in_dim(feed_one, core, 1, 0), axes, ring(1))
-    outers = jnp.concatenate([outer_one, outer_two, outer_three], axis=0)
-    return [spread(piece) for piece in (qkv_one, two, cross_one, outers, feed_one, feed_two)]
+def near_of(piece):
+    return lax.ppermute(piece, "dp", beside(True))
+
+
+def side_of(piece):
+    return lax.ppermute(piece, "dp", beside(False))
+
+
+def along(value, step):
+    return lax.ppermute(value, "mp", straight(step))
+
+
+def around(value):
+    return lax.ppermute(value, ("dp", "mp"), ring(1))
+
+
+def in_order(keep, send):
+    pieces = [part[k] for k, m in ((0, 0), (2, 1), (1, 2), (3, 3)) for part, k in ((keep, k), (send, m))]
+    return jnp.concatenate(pieces, axis=1)
 
 
 def scattered(value, axis):
     return lax.psum_scatter(value, "dp", scatter_dimension=axis, tiled=True)
 
 
-def pair_sum(keep, send):
-    part = keep + swap(send)
-    part = part[:2] + lax.ppermute(part[2:], "dp", beside(True))
-    return part[0] + lax.ppermute(part[1], "dp", beside(False))
+def sum_near(keep, sent):
+    part = keep + sent
+    return part[:2], lax.ppermute(part[2:], "dp", beside(True))
+
+
+def sum_side(part, near):
+    part = part + near
+    return part[0], side_of(part[1])
 
 
 def plane_sum(value):
@@ -871,61 +961,156 @@
     live = ((text_mask == 1) | (position == 0)).astype(F32).reshape(-1, 1)
     own_qkv = jnp.transpose(w_qkv, (1, 0, 2))
     own_cross = jnp.concatenate([w_cross_q[None], jnp.transpose(w_cross_kv, (1, 0, 2))], axis=0)
-    shards = (own_qkv, own_cross, jnp.stack([w_out, w_cross_out]), jnp.stack([w_up, w_down]))
-    g_qkv, g_two, g_cross, g_outer, g_feed, g_feed_two = (
-        gather(*shards, chip, core) if planar else gather_whole(*shards)
-    )
-
+    outer, feeds = jnp.stack([w_out, w_cross_out]), jnp.stack([w_up, w_down])
     first = norm_first(tokens, gains[0], shifts[0])
     qkvs, mixeds, logs, weights = ([None] * 4 for _ in range(4))
     weights[0] = own_qkv
-    qkvs[0], mixeds[0], logs[0] = front_own(lengths, first, own_qkv)
-    weights[1], qkvs[1], mixeds[1], logs[1] = front(True, me, lengths, first, g_qkv[0])
-    weights[3], qkvs[3], mixeds[3], logs[3] = front(False, me, lengths, first, g_qkv[1])
-    weights[2], cross_two, qkvs[2], mixeds[2], logs[2] = front_two(
-        me, lengths, first, g_two[0] + g_two[1]
-    )
-    cross_a, cross_b, *pairs = text_front(
-        me, text, own_cross, cross_two, g_cross[0] + g_cross[1]
-    )
+
+    def shards(value):
+        return along(value.astype(F32), 1), along(value.astype(F32), 3)
+
+    if planar:
+        qkv_one = around(cut(own_qkv, chip))
+        qkv_near, qkv_side = near_of(qkv_one), side_of(qkv_one)
+        own_piece = gate([qkv_one], cut(own_cross, chip))
+        cross_one = around(own_piece)
+        wait = [qkv_one]
+    else:
+        wait = []
+    qkvs[0], mixeds[0], logs[0] = front_own(lengths, first, own_qkv, wait)
+    carry = []
+    if planar:
+        mine = join(me, [qkv_one, qkv_near, qkv_side, near_of(qkv_side)], [logs[0], cross_one])
+        g_qkv = mine, swap(mine)
+        cross_near, cross_side = near_of(cross_one), side_of(cross_one)
+        two = around(jnp.where(core == 0, qkv_one, cross_one))
+        wait = [cross_one]
+        carry = [cut(lax.dynamic_slice_in_dim(outer, core, 1, 0), chip)]
+    else:
+        g_qkv = shards(own_qkv)
+    weights[1], qkvs[1], mixeds[1], logs[1], *carried = front(
+        lengths, first, g_qkv[0], wait, carry
+    )
+    if planar:
+        cross_side, two = gate([logs[1]], cross_side), gate([logs[1]], two)
+        cross_far = near_of(cross_side)
+        two_near, two_side = near_of(two), side_of(two)
+        outer_one, outer_three = along(carried[0], 1), along(carried[0], 3)
+        wait = [two, cross_near, cross_side, logs[1]]
+        carry = []
+    weights[3], qkvs[3], mixeds[3], logs[3], *carried = front(
+        lengths, first, g_qkv[1], wait, carry
+    )
+    if planar:
+        mine = join(me, [cross_one, cross_near, cross_side, cross_far], [logs[3], outer_one, outer_three])
+        g_cross = mine, swap(mine)
+        mine = join(me, [two, two_near, two_side, near_of(two_side)], [mine])
+        g_two = mine, swap(mine)
+        outer_two = along(outer_one, 1)
+        feed_one = around(gate([outer_two], cut(feeds, chip)))
+        wait = [two_near, two_side, outer_two]
+    else:
+        g_cross = shards(own_cross)
+        g_two = along(own_qkv.astype(F32), 2), along(own_cross.astype(F32), 2)
+    cross_a, cross_b, *pairs = text_front(text, own_cross, g_cross, wait)
+    if planar:
+        outers = jnp.concatenate([outer_one, outer_two, outer_three], axis=0)
+        outers = gate([cross_a], outers)
+        outer_near, outer_side = near_of(outers), side_of(outers)
+        wait = [outers, feed_one]
+    weights[2], cross_two, qkvs[2], mixeds[2], logs[2], pair_two = front_two(
+        me, lengths, first, g_two, text, wait
+    )
+    pairs = [pairs[0], pairs[1], pair_two, pairs[2]]
     crosses = [own_cross, cross_a, cross_two, cross_b]
+    if planar:
+        outer_side, feed_one = gate([logs[2]], outer_side), gate([logs[2]], feed_one)
+        mine = join(me, [outers, outer_near, outer_side, near_of(outer_side)], [logs[2]])
+        g_outer = mine, swap(mine)
+        feed_near, feed_side = near_of(feed_one), side_of(feed_one)
+        feed_two = around(lax.dynamic_slice_in_dim(feed_one, core, 1, 0))
+        wait = [feed_one]
+    else:
+        g_outer = [
+            jnp.stack([along(value.astype(F32), step) for step in (1, 2, 3)])
+            for value in (w_out, w_cross_out)
+        ]
     full_out, full_co, after_self, after_cross, second, third, cross_query, looked, cross_logs = middle(
         me, lengths, live, tokens, (gains[1], shifts[1], gains[2], shifts[2]), w_out, w_cross_out,
-        mixeds, crosses, pairs, g_outer[0] + g_outer[1],
-    )
-    out, grad, both_grad = feed_own(third, cotangent, after_cross, w_up, w_down)
-    out, grad = feed(0, me, third, cotangent, out, grad, g_feed[0], F32)
-    out, grad = feed(1, me, third, cotangent, out, grad, g_feed[1], F32)
-    out, grad = feed(
-        2, me, third, cotangent, out, grad, g_feed_two[0] + g_feed_two[1], BF16
-    )
+        mixeds, crosses, pairs, g_outer, wait,
+    )
+    if planar:
+        feed_side, feed_two = gate([third], feed_side), gate([third], feed_two)
+        feed_far = near_of(feed_side)
+        last_near, last_side = near_of(feed_two), side_of(feed_two)
+        wait = [feed_near, feed_side, feed_two]
+    out, grad, both_keep, both_send = feed_own(
+        me, third, cotangent, after_cross, w_up, w_down, wait
+    )
+    if planar:
+        mine = join(me, [feed_one, feed_near, feed_side, feed_far], [out, last_near, last_side])
+        g_feed = mine, swap(mine)
+        last_side = gate([out], last_side)
+        last_far = near_of(last_side)
+        wait = [last_near, last_side]
+    else:
+        g_feed = shards(feeds)
+    out, grad, both_send = feed_pair(
+        third, cotangent, out, grad, g_feed, wait, [both_send]
+    )
+    if planar:
+        mine = join(me, [feed_two, last_near, last_side, last_far], [out])
+        g_last = mine, swap(mine)
+    else:
+        g_last = along(feeds[:1].astype(F32), 2), along(feeds[1:].astype(F32), 2)
+        wait = []
+    out, grad = feed_last(me, third, cotangent, out, grad, g_last, [])
+    if planar:
+        both_part, both_near = sum_near(both_keep, swap(both_send))
     upstream, mixed_grad, pair_grad, row_grads, query_grad, sums = back(
         lengths, live, grad, cotangent, after_cross, after_self, cross_query, looked, mixeds[0],
         cross_logs, gains[1], gains[2], full_out, full_co, crosses, pairs,
-    )
-    text_grad, cross_grad = text_back(text, pair_grad, second, query_grad, crosses)
-    first_grad, keep, send = self_own(
-        me, lengths, qkvs[0], mixeds[0], mixed_grad, logs[0], weights[0], first
-    )
+        [both_part] if planar else [],
+    )
+    if planar:
+        both_part, both_side = sum_side(both_part, both_near)
+        wait = [both_near]
+    first_grad, qkv_grad = self_own(
+        lengths, qkvs[0], mixeds[0], mixed_grad, logs[0], weights[0], first, wait
+    )
+    if planar:
+        wait = [both_side]
+    text_grad, keep, send = text_back(
+        me, text, pair_grad, second, query_grad, row_grads, qkv_grad, crosses, wait
+    )
+    waits = [[], [], [], []]
+    if planar:
+        late_swap = swap(send)
+        late_part, late_near = sum_near(keep, late_swap)
+        late_one, late_side = sum_side(late_part, late_near)
+        waits = [[], [late_swap], [late_near], [late_side]]
     for j in (1, 2, 3):
         first_grad = self_back(
-            lengths, qkvs[j], mixeds[j], mixed_grad, logs[j], weights[j], first_grad, j
+            lengths, qkvs[j], mixeds[j], mixed_grad, logs[j], weights[j], first_grad, j,
+            waits[j - 1],
         )
-    token_grad, last_sums = last(first_grad, tokens, upstream, gains[0])
-    both_sum = scattered(both_grad, 1)
-    row_sum = scattered(row_grads, 1)
-    cross_sum = scattered(cross_grad, 1)
+    token_grad, last_sums = last(first_grad, tokens, upstream, gains[0], waits[3])
     norm_sums = jnp.concatenate(
         [last_sums[0:1], sums[2:3], sums[0:1], last_sums[1:2], sums[3:4], sums[1:2]], axis=0
     )
     if planar:
-        qkv_sum = pair_sum(keep, send)
+        both_sum, late_sum = both_part + both_side, late_one + late_side
+        row_sum = [unfold(late_sum[k]) for k in (6, 7)]
         width = norm_sums.shape[1] // DP
         norm_sum = lax.dynamic_slice_in_dim(plane_sum(norm_sums), place * width, width, 1)
     else:
-        pieces = [part[k] for k in (0, 2, 1, 3) for part in (keep, send)]
-        pieces = jnp.stack(pieces, axis=1)
-        qkv_sum = scattered(jnp.reshape(pieces, own_qkv.shape), 1)
+        both_sum = scattered(in_order(both_keep, both_send), 1)
+        late = in_order(keep, send)
+        late_sum = scattered(late[:6], 1)
+        row_sum = [
+            scattered(jnp.concatenate([unfold(part) for part in jnp.split(late[k], 8)]), 0)
+            for k in (6, 7)
+        ]
         norm_sum = scattered(norm_sums, 1)
     return (
         out,
@@ -933,10 +1118,10 @@
         text_grad.reshape(text_states.shape),
         norm_sum[:3],
         norm_sum[3:],
-        jnp.transpose(qkv_sum, (1, 0, 2)),
+        jnp.transpose(late_sum[3:6], (1, 0, 2)),
         row_sum[0],
-        cross_sum[0],
-        jnp.transpose(cross_sum[1:], (1, 0, 2)),
+        late_sum[0],
+        jnp.transpose(late_sum[1:3], (1, 0, 2)),
         row_sum[1],
         both_sum[0],
         both_sum[1],

time: 647 us -> 635 us (0.981)
  waiting for transfers between devices: 150 us -> 124 us
  Pallas kernels: 389 us -> 408 us
  local copies, waits for them, and re-layouts: 17.4 us -> 33.3 us
  between operations: 14.7 us -> 1.47 us
  starting transfers between devices: 52.7 us -> 40.9 us
  other arithmetic: 12.6 us -> 19.4 us
    ppermute x28 -> x30, waiting for transfers between devices: 132 us -> 99.8 us  [the longest x5 54.1 us: around(): return lax.ppermute(value, ('dp', 'mp'), ring(1))]
    ppermute x25 -> x8, waiting for transfers between devices: 0.07 us -> 20.6 us  [swap(): return lax.ppermute(value, 'dp', [(i, i ^ 1) for i in range(DP)])]
    pallas_call x18 -> x33, Pallas kernels: 389 us -> 408 us  [launch(): pl.pallas_call(body, in_specs=list(in_specs) + [anywhere()] * extra, out_...]
    unnamed x68 -> x102, local copies, waits for them, and re-layouts: 7.92 us -> 26 us
    reduce_scatter x3 -> x0, waiting for transfers between devices: 11.5 us -> none  [scattered(): return lax.psum_scatter(value, 'dp', scatter_dimension=axis, tiled=True)]
    add x2 -> x6, other arithmetic: 0.37 us -> 9.55 us  [the longest x2 5.43 us: sum_side(): part = part + near]
    ppermute x25 -> x8, starting transfers between devices: 8.55 us -> 1.41 us  [swap(): return lax.ppermute(value, 'dp', [(i, i ^ 1) for i in range(DP)])]
    ppermute x28 -> x30, starting transfers between devices: 41.4 us -> 36.7 us  [the longest x8 11.6 us: side_of(): return lax.ppermute(piece, 'dp', beside(False))]
  transfers between devices with their start and end apart: 59 -> 41, of which waited for: 12 -> 17; matrix products, arithmetic and copies ran while one was open for 3% -> 3% of each run, Pallas kernels for 50% -> 59%
where the time goes in v3:
time: 635 us; the launch traced here: 628 us
  Pallas kernels  408 us (64%)
  waiting for transfers between devices  124 us (20%)
  starting transfers between devices  40.9 us (6%)
  local copies, waits for them, and re-layouts  33.3 us (5%)
  other arithmetic  19.4 us (3%)
    pallas_call x33, Pallas kernels, launch(): pl.pallas_call(body, in_specs=list(in_specs) + [anywhere()] * extra, out_...  408 us
    ppermute x5, waiting for transfers between devices, around(): return lax.ppermute(value, ('dp', 'mp'), ring(1))  54.1 us
    unnamed x102, local copies, waits for them, and re-layouts  26 us
    ppermute x12, waiting for transfers between devices, near_of(): return lax.ppermute(piece, 'dp', beside(True))  23.1 us
    ppermute x8, waiting for transfers between devices, swap(): return lax.ppermute(value, 'dp', [(i, i ^ 1) for i in range(DP)])  20.6 us
    ppermute x8, waiting for transfers between devices, side_of(): return lax.ppermute(piece, 'dp', beside(False))  13.9 us
  transfers between devices with their start and end apart: 41, of which 17 were waited for; matrix products, arithmetic and copies ran while one was open for 3% of the time, Pallas kernels for 59%

profile of v3, /device:TPU:0, one launch (start us, length us, event | category | flops | bytes accessed | tf_op | source)
XLA Modules:
  0.0 627.6 jit_solution(6489592780684403156)
XLA Ops:
  1.8 3.1 collective-permute-start
  8.6 16.0 %collective-permute-done.refs_3_.refs_0_.refs_1_ = f32[3,256,256]{2,1,0:T(8,128)S(1)} collective-permute-done((f32[3,256,256]{2,1,0:T(8,128)S(1)}, f32[3,256,256]{2,1,0:T(8,128)S(1)}, u32[]{:S(2)}, u32[]{:S(2)}) %collective-permute-start) | collective-permute-done | bytes 786464 | tf_op jit(solution)/shard_map/ppermute | solution.py:921
  26.2 5.5 norm_first.1.refs_1_.refs_2_.refs_6_
  33.3 3.5 collective-permute-done.2.refs_3_
  36.8 2.4 collective-permute-start.3
  39.2 15.0 %front_own.1 = (bf16[3,1280,256]{2,1,0:T(8,128)(2,1)}, bf16[1280,256]{1,0:T(8,128)(2,1)}, f32[8,1280]{1,0:T(8,128)}) custom-call(s32[5]{0:T(128)} %refs_0_.17, bf16[1280,1024]{1,0:T(8,128)(2,1)} %norm_first.1.refs_1_.refs_2_.refs_6_, bf16[3,1024,256]{2,1,0:T(8,128)(2,1)} %bitcast.70, f32[3,256,256]{2,1,0:T(8,128)} %copy-done.16), custom_call_target="tpu_custom_call" | custom-call | flops 17250000896 | bytes 54000000 | tf_op jit(solution)/shard_map/front_own/pallas_call | solution.py:71
  55.1 2.6 join.6.refs_2_
  59.5 2.0 collective-permute-start.5
  63.1 15.9 %front.2 = (bf16[3,1024,256]{2,1,0:T(8,128)(2,1)}, bf16[3,1280,256]{2,1,0:T(8,128)(2,1)}, bf16[1280,256]{1,0:T(8,128)(2,1)}, f32[8,1280]{1,0:T(8,128)}, f32[1,64,1024]{2,1,0:T(8,128)}) custom-call(s32[5]{0:T(128)} %refs_0_.17, bf16[1280,1024]{1,0:T(8,128)(2,1)} %norm_first.1.refs_1_.refs_2_.refs_6_, ...), custom_call_target="tpu_custom_call", output_to_operand_aliasing={{4}: (4, {})} | custom-call | flops 18400000000 | bytes 57600000 | tf_op jit(solution)/shard_map/front/pallas_call | solution.py:71
  79.0 3.0 collective-permute-done.5.refs_1_
  84.1 2.2 collective-permute-start.13
  86.4 2.0 collective-permute-start.14
  88.6 10.4 %collective-permute-done.7.refs_3_.refs_5_ = f32[3,256,256]{2,1,0:T(8,128)S(1)} collective-permute-done((f32[3,256,256]{2,1,0:T(8,128)}, f32[3,256,256]{2,1,0:T(8,128)S(1)}, u32[]{:S(2)}, u32[]{:S(2)}) %collective-permute-start.7) | collective-permute-done | bytes 786464 | tf_op jit(solution)/shard_map/ppermute | solution.py:913
  99.1 2.0 collective-permute-start.8
  101.1 15.9 %front.3 = (bf16[3,1024,256]{2,1,0:T(8,128)(2,1)}, bf16[3,1280,256]{2,1,0:T(8,128)(2,1)}, bf16[1280,256]{1,0:T(8,128)(2,1)}, f32[8,1280]{1,0:T(8,128)}) custom-call(s32[5]{0:T(128)} %refs_0_.17, bf16[1280,1024]{1,0:T(8,128)(2,1)} %norm_first.1.refs_1_.refs_2_.refs_6_, f32[3,1024,256]{2,1,0:T(8,128)} %collective-permute-done.12.refs_2_, ...), custom_call_target="tpu_custom_call" | custom-call | flops 18400000000 | bytes 57600000 | tf_op jit(solution)/shard_map/front/pallas_call | solution.py:71
  117.8 3.7 join.7.refs_5_.refs_2_
  121.7 2.6 join.8.refs_3_
  124.8 4.5 collective-permute-start.17
  130.9 7.2 %collective-permute-done.17.refs_6_.refs_0_ = f32[1,64,1024]{2,1,0:T(8,128)S(1)} collective-permute-done((f32[1,64,1024]{2,1,0:T(8,128)S(1)}, f32[1,64,1024]{2,1,0:T(8,128)S(1)}, u32[]{:S(2)}, u32[]{:S(2)}) %collective-permute-start.17) | collective-permute-done | bytes 262176 | tf_op jit(solution)/shard_map/ppermute | solution.py:917
  139.9 2.5 pad_maximum_fusion.refs_1_.refs_14_.refs_7_
  143.3 7.9 %text_front.1 = (bf16[3,1024,256]{2,1,0:T(8,128)(2,1)}, bf16[3,1024,256]{2,1,0:T(8,128)(2,1)}, bf16[2,640,256]{2,1,0:T(8,128)(2,1)}, bf16[2,640,256]{2,1,0:T(8,128)(2,1)}, bf16[2,640,256]{2,1,0:T(8,128)(2,1)}) custom-call(bf16[640,1024]{1,0:T(8,128)(2,1)} %bitcast.73, bf16[3,1024,256]{2,1,0:T(8,128)(2,1)} %pad_maximum_fusion.refs_1_.refs_14_.refs_7_, ...), custom_call_target="tpu_custom_call" | custom-call | flops 8049999872 | bytes 25200000 | tf_op jit(solution)/shard_map/text_front/pallas_call | solution.py:71
  153.1 35.1 %collective-permute-done.18.refs_7_.refs_1_ = f32[2,256,1024]{2,1,0:T(8,128)S(1)} collective-permute-done((f32[2,256,1024]{2,1,0:T(8,128)}, f32[2,256,1024]{2,1,0:T(8,128)S(1)}, u32[]{:S(2)}, u32[]{:S(2)}) %collective-permute-start.18) | collective-permute-done | bytes 2097184 | tf_op jit(solution)/shard_map/ppermute | solution.py:921
  189.5 19.1 %front_two.1 = (bf16[3,1024,256]{2,1,0:T(8,128)(2,1)}, bf16[3,1024,256]{2,1,0:T(8,128)(2,1)}, bf16[3,1280,256]{2,1,0:T(8,128)(2,1)}, bf16[1280,256]{1,0:T(8,128)...) custom-call(s32[2]{0:T(128)} %copy-done.23, s32[5]{0:T(128)} %refs_0_.17, ...), custom_call_target="tpu_custom_call" | custom-call | flops 20700000256 | bytes 64800000 | tf_op jit(solution)/shard_map/front_two/pallas_call | solution.py:71
  209.6 12.2 %collective-permute-done.21.refs_4_ = f32[3,64,1024]{2,1,0:T(8,128)S(1)} collective-permute-done((f32[3,64,1024]{2,1,0:T(8,128)}, f32[3,64,1024]{2,1,0:T(8,128)S(1)}, u32[]{:S(2)}, u32[]{:S(2)}) %collective-permute-start.21) | collective-permute-done | bytes 786464 | tf_op jit(solution)/shard_map/ppermute | solution.py:909
  222.9 2.6 join.9.refs_22_
  231.5 42.9 %middle.1 = (bf16[1024,1024]{1,0:T(8,128)(2,1)}, bf16[1024,1024]{1,0:T(8,128)(2,1)}, f32[1280,1024]{1,0:T(8,128)}, f32[1280,1024]{1,0:T(8,128)}, bf16[1280,1024]...) custom-call(s32[2]{0:T(128)} %copy-done.23, ...), custom_call_target="tpu_custom_call" | custom-call | flops 49450000384 | bytes 154800000 | tf_op jit(solution)/shard_map/middle/pallas_call | solution.py:71
  278.7 2.0 collective-permute-start.26
  280.7 32.5 %feed_own.1 = (f32[1280,1024]{1,0:T(8,128)}, f32[1280,1024]{1,0:T(8,128)}, f32[4,2,128,1024]{3,2,1,0:T(8,128)}, f32[4,2,128,1024]{3,2,1,0:T(8,128)}) custom-call(s32[2]{0:T(128)} %copy-done.23, bf16[1280,1024]{1,0:T(8,128)(2,1)} %get-tuple-element.82.refs_0_.refs_1_, bf16[1280,1024]{1,0:T(8,128)(2,1)} %refs_3_.3, ...), custom_call_target="tpu_custom_call" | custom-call | flops 36800000000 | bytes 115200000 | tf_op jit(solution)/shard_map/feed_own/pallas_call | solution.py:71
  313.3 10.9 %collective-permute-done.26.refs_4_ = f32[2,256,1024]{2,1,0:T(8,128)S(1)} collective-permute-done((f32[2,256,1024]{2,1,0:T(8,128)}, f32[2,256,1024]{2,1,0:T(8,128)S(1)}, u32[]{:S(2)}, u32[]{:S(2)}) %collective-permute-start.26) | collective-permute-done | bytes 2097184 | tf_op jit(solution)/shard_map/ppermute | solution.py:909
  325.5 2.5 copy-done
  331.1 5.6 join.10.refs_4_
  337.5 12.9 %collective-permute-done.29.refs_5_ = f32[2,1024,1024]{2,1,0:T(8,128)} collective-permute-done((f32[2,1024,1024]{2,1,0:T(8,128)}, f32[2,1024,1024]{2,1,0:T(8,128)}, u32[]{:S(2)}, u32[]{:S(2)}) %collective-permute-start.29) | collective-permute-done | bytes 8388640 | tf_op jit(solution)/shard_map/ppermute | solution.py:900
  350.4 32.7 %feed_pair.1 = (f32[1280,1024]{1,0:T(8,128)}, f32[1280,1024]{1,0:T(8,128)}, f32[4,2,128,1024]{3,2,1,0:T(8,128)}) custom-call(bf16[1280,1024]{1,0:T(8,128)(2,1)} %get-tuple-element.82.refs_0_.refs_1_, bf16[1280,1024]{1,0:T(8,128)(2,1)} %refs_3_.3, f32[1280,1024]{1,0:T(8,128)} %get-tuple-element.84.refs_5_.refs_0_.refs_2_, ...), custom_call_target="tpu_custom_call", output_to_operand_aliasing={{2}: (8, {})} | custom-call | flops 34500001792 | bytes 108000000 | tf_op jit(solution)/shard_map/feed_pair/pallas_call | solution.py:71
  383.3 2.5 copy-done.5
  385.7 2.2 join.11.refs_5_
  388.4 2.1 collective-permute-done.32
  392.2 4.1 collective-permute-done.31.refs_6_
  396.3 1.9 copy-done.48
  398.2 18.3 %feed_last.1 = (bf16[1280,1024]{1,0:T(8,128)(2,1)}, f32[1280,1024]{1,0:T(8,128)}) custom-call(s32[2]{0:T(128)} %copy-done.23, bf16[1280,1024]{1,0:T(8,128)(2,1)} %get-tuple-element.82.refs_0_.refs_1_, bf16[1280,1024]{1,0:T(8,128)(2,1)} %refs_3_.3, f32[1280,1024]{1,0:T(8,128)} %get-tuple-element.87.refs_5_.refs_3_, f32[1280,1024]{1,0:T(8,128)} %get-tuple-element.88.refs_4_, ...), custom_call_target="tpu_custom_call" | custom-call | flops 20700000256 | bytes 64800000 | tf_op jit(solution)/shard_map/feed_last/pallas_call | solution.py:71
  417.9 3.5 slice_add_fusion.1
  422.6 51.8 %back.1 = (f32[1280,1024]{1,0:T(8,128)}, bf16[1280,1024]{1,0:T(8,128)(2,1)}, bf16[4,2,640,256]{3,2,1,0:T(8,128)(2,1)}, f32[2,256,1024]{2,1,0:T(8,128)}, bf16[1280,256]{1,0:T(8,128)(2,1)}, /*index=5*/f32[8,1024]{1,0:T(8,128)}) custom-call(s32[5]{0:T(128)} %refs_0_.17, f32[640,1]{1,0:T(8,128)} %bitcast.69, f32[1280,1024]{1,0:T(8,128)} %get-tuple-element.91.refs_2_, ...), custom_call_target="tpu_custom_call" | custom-call | flops 60949999616 | bytes 190800000 | tf_op jit(solution)/shard_map/back/pallas_call | solution.py:71
  474.5 27.5 %self_own.1 = (f32[1280,1024]{1,0:T(8,128)}, f32[3,1024,256]{2,1,0:T(8,128)}) custom-call(s32[5]{0:T(128)} %refs_0_.17, bf16[3,1280,256]{2,1,0:T(8,128)(2,1)} %get-tuple-element.106.refs_1_, bf16[1280,256]{1,0:T(8,128)(2,1)} %get-tuple-element.66.refs_10_.refs_8_.refs_2_, bf16[1280,1024]{1,0:T(8,128)(2,1)} %get-tuple-element.100.refs_3_, ...), custom_call_target="tpu_custom_call" | custom-call | flops 32199999488 | bytes 100800000 | tf_op jit(solution)/shard_map/self_own/pallas_call | solution.py:71
  502.9 15.2 %text_back.1 = (f32[640,1024]{1,0:T(8,128)}, f32[4,8,128,256]{3,2,1,0:T(8,128)}, f32[4,8,128,256]{3,2,1,0:T(8,128)}) custom-call(s32[2]{0:T(128)} %copy-done.23, bf16[640,1024]{1,0:T(8,128)(2,1)} %bitcast.75, bf16[4,2,640,256]{3,2,1,0:T(8,128)(2,1)} %get-tuple-element.108.refs_2_, bf16[1280,1024]{1,0:T(8,128)(2,1)} %get-tuple-element.109.refs_3_, ...), custom_call_target="tpu_custom_call" | custom-call | flops 17250000896 | bytes 54000000 | tf_op jit(solution)/shard_map/text_back/pallas_call | solution.py:71
  518.2 26.3 %self_back.3.refs_6_ = f32[1280,1024]{1,0:T(8,128)} custom-call(s32[5]{0:T(128)} %refs_0_.17, bf16[3,1280,256]{2,1,0:T(8,128)(2,1)} %get-tuple-element.104.refs_1_, bf16[1280,256]{1,0:T(8,128)(2,1)} %get-tuple-element.68.refs_11_.refs_2_, bf16[1280,1024]{1,0:T(8,128)(2,1)} %get-tuple-element.100.refs_3_, ...), custom_call_target="tpu_custom_call" | custom-call | flops 29899999232 | bytes 93600000 | tf_op jit(solution)/shard_map/self_back/pallas_call | solution.py:71
  547.0 2.9 add.56
  550.2 26.0 %self_back.4.refs_6_ = f32[1280,1024]{1,0:T(8,128)} custom-call(s32[5]{0:T(128)} %refs_0_.17, bf16[3,1280,256]{2,1,0:T(8,128)(2,1)} %get-tuple-element.102.refs_1_, bf16[1280,256]{1,0:T(8,128)(2,1)} %get-tuple-element.73.refs_12_.refs_2_, bf16[1280,1024]{1,0:T(8,128)(2,1)} %get-tuple-element.100.refs_3_, ...), custom_call_target="tpu_custom_call" | custom-call | flops 29899999232 | bytes 93600000 | tf_op jit(solution)/shard_map/self_back/pallas_call | solution.py:71
  579.4 26.4 %self_back.5.refs_0_ = f32[1280,1024]{1,0:T(8,128)} custom-call(s32[5]{0:T(128)} %refs_0_.17, bf16[3,1280,256]{2,1,0:T(8,128)(2,1)} %get-tuple-element.90.refs_1_, bf16[1280,256]{1,0:T(8,128)(2,1)} %get-tuple-element.74.refs_13_.refs_2_, bf16[1280,1024]{1,0:T(8,128)(2,1)} %get-tuple-element.100.refs_3_, f32[8,1280]{1,0:T(8,128)} %get-tuple-element.70.refs_5_.refs_4_, ...), custom_call_target="tpu_custom_call" | custom-call | flops 29899999232 | bytes 93600000 | tf_op jit(solution)/shard_map/self_back/pallas_call | solution.py:71
  606.9 10.0 %last.1 = (f32[1280,1024]{1,0:T(8,128)}, f32[8,1024]{1,0:T(8,128)}) custom-call(f32[1280,1024]{1,0:T(8,128)} %self_back.5.refs_0_, bf16[1280,1024]{1,0:T(8,128)(2,1)} %refs_1_.7, f32[1280,1024]{1,0:T(8,128)} %get-tuple-element.115.refs_2_, f32[1,1024]{1,0:T(1,128)} %get-tuple-element.165.refs_1_.refs_3_, f32[8,128,256]{2,1,0:T(8,128)} %copy-done.40), custom_call_target="tpu_custom_call" | custom-call | flops 11500000256 | bytes 36000000 | tf_op jit(solution)/shard_map/last/pallas_call | solution.py:71
  (205 shorter events, 64.5 us)
Async XLA Ops:
  1.8 22.8 %collective-permute-start = (f32[3,256,256]{2,1,0:T(8,128)S(1)}, f32[3,256,256]{2,1,0:T(8,128)S(1)}, u32[]{:S(2)}, u32[]{:S(2)}) collective-permute-start(f32[3,256,256]{2,1,0:T(8,128)S(1)} %convert_bitcast_fusion), channel_id=1, source_target_pairs={{0,1},{1,2},{2,3},{3,0},{4,7},{5,4},{6,5},{7,6},{8,9},{9,10},{10,1... | collective-permute-start | bytes 2359304 | tf_op jit(solution)/shard_map/ppermute | solution.py:921
  24.6 12.2 %collective-permute-start.2 = (f32[3,256,256]{2,1,0:T(8,128)S(1)}, f32[3,256,256]{2,1,0:T(8,128)S(1)}, u32[]{:S(2)}, u32[]{:S(2)}) collective-permute-start(f32[3,256,256]{2,1,0:T(8,128)S(1)} %collective-permute-done.refs_3_.refs_0_.refs_1_), channel_id=1, source_target_pairs={{0,16},{4,12},{8,24},{12,4},{16,0},{20,28},{24,8},{28,20},{1,17},{... | collective-permute-start | bytes 2359304 | tf_op jit(solution)/shard_map/ppermute | solution.py:913
  26.2 95.5 %copy-start.23 = (s32[2]{0:T(128)}, s32[2]{0:T(128)S(1)}, u32[]{:S(2)}) copy-start(s32[2]{0:T(128)S(1)} %pad_add_fusion.refs_0_) | copy-start | bytes 28
  31.7 22.4 %collective-permute-start.4 = (f32[3,256,256]{2,1,0:T(8,128)}, f32[3,256,256]{2,1,0:T(8,128)S(1)}, u32[]{:S(2)}, u32[]{:S(2)}) collective-permute-start(f32[3,256,256]{2,1,0:T(8,128)} %gate.10), channel_id=1, source_target_pairs={{0,1},{1,2},{2,3},{3,0},{4,7},{5,4},{6,5},{7,6},{8,9},{9,10},{10,1... | collective-permute-start | bytes 2359304 | tf_op jit(solution)/shard_map/ppermute | solution.py:921
  31.7 22.4 %collective-permute-start.1 = (f32[3,256,256]{2,1,0:T(8,128)}, f32[3,256,256]{2,1,0:T(8,128)S(1)}, u32[]{:S(2)}, u32[]{:S(2)}) collective-permute-start(f32[3,256,256]{2,1,0:T(8,128)} %copy-done.16), channel_id=1, source_target_pairs={{0,8},{4,20},{8,0},{12,28},{16,24},{20,4},{24,16},{28,12},{1,9},{5... | collective-permute-start | bytes 2359304 | tf_op jit(solution)/shard_map/ppermute | solution.py:909
  36.8 17.4 %collective-permute-start.3 = (f32[3,256,256]{2,1,0:T(8,128)S(1)}, f32[3,256,256]{2,1,0:T(8,128)S(1)}, u32[]{:S(2)}, u32[]{:S(2)}) collective-permute-start(f32[3,256,256]{2,1,0:T(8,128)S(1)} %collective-permute-done.2.refs_3_), channel_id=1, source_target_pairs={{0,8},{4,20},{8,0},{12,28},{16,24},{20,4},{24,16},{28,12},{1,9},{5... | collective-permute-start | bytes 2359304 | tf_op jit(solution)/shard_map/ppermute | solution.py:909
  57.6 41.4 %collective-permute-start.12 = (f32[3,1024,256]{2,1,0:T(8,128)}, f32[3,1024,256]{2,1,0:T(8,128)}, u32[]{:S(2)}, u32[]{:S(2)}) collective-permute-start(f32[3,1024,256]{2,1,0:T(8,128)} %join.6.refs_2_), channel_id=1, source_target_pairs={{0,4},{4,0},{8,12},{12,8},{16,20},{20,16},{24,28},{28,24},{1,5},{5... | collective-permute-start | bytes 9437192 | tf_op jit(solution)/shard_map/ppermute | solution.py:900
  59.5 22.4 %collective-permute-start.5 = (f32[3,256,256]{2,1,0:T(8,128)S(1)}, f32[3,256,256]{2,1,0:T(8,128)S(1)}, u32[]{:S(2)}, u32[]{:S(2)}) collective-permute-start(f32[3,256,256]{2,1,0:T(8,128)S(1)} %broadcast_select_fusion), channel_id=1, source_target_pairs={{0,1},{1,2},{2,3},{3,0},{4,7},{5,4},{6,5},{7,6},{8,9},{9,10},{10,1... | collective-permute-start | bytes 2359304 | tf_op jit(solution)/shard_map/ppermute | solution.py:921
  61.5 24.8 %collective-permute-start.10 = (f32[3,256,256]{2,1,0:T(8,128)S(1)}, f32[3,256,256]{2,1,0:T(8,128)}, u32[]{:S(2)}, u32[]{:S(2)}) collective-permute-start(f32[3,256,256]{2,1,0:T(8,128)S(1)} %collective-permute-done.4.refs_6_.refs_3_.refs_1_), channel_id=1, source_target_pairs={{0,16},{4,12},{8,24},{12,4},{16,0},{20,28},{24,8},{28,20},{1,17},{... | collective-permute-start | bytes 2359304 | tf_op jit(solution)/shard_map/ppermute | solution.py:913
  63.1 25.3 %collective-permute-start.9 = (f32[3,256,256]{2,1,0:T(8,128)S(1)}, f32[3,256,256]{2,1,0:T(8,128)}, u32[]{:S(2)}, u32[]{:S(2)}) collective-permute-start(f32[3,256,256]{2,1,0:T(8,128)S(1)} %collective-permute-done.4.refs_6_.refs_3_.refs_1_), channel_id=1, source_target_pairs={{0,8},{4,20},{8,0},{12,28},{16,24},{20,4},{24,16},{28,12},{1,9},{5... | collective-permute-start | bytes 2359304 | tf_op jit(solution)/shard_map/ppermute | solution.py:909
  82.9 16.2 %collective-permute-start.7 = (f32[3,256,256]{2,1,0:T(8,128)}, f32[3,256,256]{2,1,0:T(8,128)S(1)}, u32[]{:S(2)}, u32[]{:S(2)}) collective-permute-start(f32[3,256,256]{2,1,0:T(8,128)} %gate.11.refs_3_.refs_1_), channel_id=1, source_target_pairs={{0,16},{4,12},{8,24},{12,4},{16,0},{20,28},{24,8},{28,20},{1,17},{... | collective-permute-start | bytes 2359304 | tf_op jit(solution)/shard_map/ppermute | solution.py:913
  84.1 32.9 %collective-permute-start.13 = (f32[1,64,1024]{2,1,0:T(8,128)S(1)}, f32[1,64,1024]{2,1,0:T(8,128)S(1)}, u32[]{:S(2)}, u32[]{:S(2)}) collective-permute-start(f32[1,64,1024]{2,1,0:T(8,128)S(1)} %copy-done.43), channel_id=1, source_target_pairs={{0,1},{1,2},{2,3},{3,0},{4,5},{5,6},{6,7},{7,4},{8,9},{9,10},{10,1... | collective-permute-start | bytes 786440 | tf_op jit(solution)/shard_map/ppermute | solution.py:917
  86.4 30.6 %collective-permute-start.14 = (f32[1,64,1024]{2,1,0:T(8,128)S(1)}, f32[1,64,1024]{2,1,0:T(8,128)S(1)}, u32[]{:S(2)}, u32[]{:S(2)}) collective-permute-start(f32[1,64,1024]{2,1,0:T(8,128)S(1)} %copy-done.43), channel_id=1, source_target_pairs={{0,3},{1,0},{2,1},{3,2},{4,7},{5,4},{6,5},{7,6},{8,11},{9,8},{10,9... | collective-permute-start | bytes 786440 | tf_op jit(solution)/shard_map/ppermute | solution.py:917
  88.4 28.6 %copy-start.14 = (f32[3,256,256]{2,1,0:T(8,128)S(1)}, f32[3,256,256]{2,1,0:T(8,128)}, u32[]{:S(2)}) copy-start(f32[3,256,256]{2,1,0:T(8,128)} %copy-done.13) | copy-start | bytes 2359300
  88.4 33.2 %collective-permute-start.6 = (f32[3,256,256]{2,1,0:T(8,128)S(1)}, f32[3,256,256]{2,1,0:T(8,128)S(1)}, u32[]{:S(2)}, u32[]{:S(2)}) collective-permute-start(f32[3,256,256]{2,1,0:T(8,128)S(1)} %copy-done.20), channel_id=1, source_target_pairs={{0,8},{4,20},{8,0},{12,28},{16,24},{20,4},{24,16},{28,12},{1,9},{5... | collective-permute-start | bytes 2359304 | tf_op jit(solution)/shard_map/ppermute | solution.py:909
  99.1 18.0 %collective-permute-start.11 = (f32[3,256,256]{2,1,0:T(8,128)}, f32[3,256,256]{2,1,0:T(8,128)S(1)}, u32[]{:S(2)}, u32[]{:S(2)}) collective-permute-start(f32[3,256,256]{2,1,0:T(8,128)} %gate.12.refs_5_.refs_3_), channel_id=1, source_target_pairs={{0,8},{4,20},{8,0},{12,28},{16,24},{20,4},{24,16},{28,12},{1,9},{5... | collective-permute-start | bytes 2359304 | tf_op jit(solution)/shard_map/ppermute | solution.py:909
  99.1 22.6 %collective-permute-start.8 = (f32[3,256,256]{2,1,0:T(8,128)S(1)}, f32[3,256,256]{2,1,0:T(8,128)S(1)}, u32[]{:S(2)}, u32[]{:S(2)}) collective-permute-start(f32[3,256,256]{2,1,0:T(8,128)S(1)} %collective-permute-done.7.refs_3_.refs_5_), channel_id=1, source_target_pairs={{0,8},{4,20},{8,0},{12,28},{16,24},{20,4},{24,16},{28,12},{1,9},{5... | collective-permute-start | bytes 2359304 | tf_op jit(solution)/shard_map/ppermute | solution.py:909
  121.6 21.8 %collective-permute-start.16 = (f32[3,1024,256]{2,1,0:T(8,128)}, f32[3,1024,256]{2,1,0:T(8,128)}, u32[]{:S(2)}, u32[]{:S(2)}) collective-permute-start(f32[3,1024,256]{2,1,0:T(8,128)} %join.7.refs_5_.refs_2_), channel_id=1, source_target_pairs={{0,4},{4,0},{8,12},{12,8},{16,20},{20,16},{24,28},{28,24},{1,5},{5... | collective-permute-start | bytes 9437192 | tf_op jit(solution)/shard_map/ppermute | solution.py:900
  124.3 63.9 %collective-permute-start.15 = (f32[3,1024,256]{2,1,0:T(8,128)}, f32[3,1024,256]{2,1,0:T(8,128)}, u32[]{:S(2)}, u32[]{:S(2)}) collective-permute-start(f32[3,1024,256]{2,1,0:T(8,128)} %join.8.refs_3_), channel_id=1, source_target_pairs={{0,4},{4,0},{8,12},{12,8},{16,20},{20,16},{24,28},{28,24},{1,5},{5... | collective-permute-start | bytes 9437192 | tf_op jit(solution)/shard_map/ppermute | solution.py:900
  124.8 13.2 %collective-permute-start.17 = (f32[1,64,1024]{2,1,0:T(8,128)S(1)}, f32[1,64,1024]{2,1,0:T(8,128)S(1)}, u32[]{:S(2)}, u32[]{:S(2)}) collective-permute-start(f32[1,64,1024]{2,1,0:T(8,128)S(1)} %collective-permute-done.13.refs_6_), channel_id=1, source_target_pairs={{0,1},{1,2},{2,3},{3,0},{4,5},{5,6},{6,7},{7,4},{8,9},{9,10},{10,1... | collective-permute-start | bytes 786440 | tf_op jit(solution)/shard_map/ppermute | solution.py:917
  138.7 49.5 %collective-permute-start.18 = (f32[2,256,1024]{2,1,0:T(8,128)}, f32[2,256,1024]{2,1,0:T(8,128)S(1)}, u32[]{:S(2)}, u32[]{:S(2)}) collective-permute-start(f32[2,256,1024]{2,1,0:T(8,128)} %gate.14), channel_id=1, source_target_pairs={{0,1},{1,2},{2,3},{3,0},{4,7},{5,4},{6,5},{7,6},{8,9},{9,10},{10,1... | collective-permute-start | bytes 6291464 | tf_op jit(solution)/shard_map/ppermute | solution.py:921
  151.2 57.3 %collective-permute-start.20 = (f32[3,64,1024]{2,1,0:T(8,128)}, f32[3,64,1024]{2,1,0:T(8,128)S(1)}, u32[]{:S(2)}, u32[]{:S(2)}) collective-permute-start(f32[3,64,1024]{2,1,0:T(8,128)} %gate.13.refs_6_.refs_1_), channel_id=1, source_target_pairs={{0,16},{4,12},{8,24},{12,4},{16,0},{20,28},{24,8},{28,20},{1,17},{... | collective-permute-start | bytes 2359304 | tf_op jit(solution)/shard_map/ppermute | solution.py:913
  153.1 56.4 %collective-permute-start.19 = (f32[3,64,1024]{2,1,0:T(8,128)}, f32[3,64,1024]{2,1,0:T(8,128)S(1)}, u32[]{:S(2)}, u32[]{:S(2)}) collective-permute-start(f32[3,64,1024]{2,1,0:T(8,128)} %gate.13.refs_6_.refs_1_), channel_id=1, source_target_pairs={{0,8},{4,20},{8,0},{12,28},{16,24},{20,4},{24,16},{28,12},{1,9},{5... | collective-permute-start | bytes 2359304 | tf_op jit(solution)/shard_map/ppermute | solution.py:909
  209.5 12.3 %collective-permute-start.21 = (f32[3,64,1024]{2,1,0:T(8,128)}, f32[3,64,1024]{2,1,0:T(8,128)S(1)}, u32[]{:S(2)}, u32[]{:S(2)}) collective-permute-start(f32[3,64,1024]{2,1,0:T(8,128)} %gate.15.refs_3_), channel_id=1, source_target_pairs={{0,8},{4,20},{8,0},{12,28},{16,24},{20,4},{24,16},{28,12},{1,9},{5... | collective-permute-start | bytes 2359304 | tf_op jit(solution)/shard_map/ppermute | solution.py:909
  225.4 6.1 collective-permute-start.22
  226.5 50.9 %collective-permute-start.24 = (f32[2,256,1024]{2,1,0:T(8,128)}, f32[2,256,1024]{2,1,0:T(8,128)S(1)}, u32[]{:S(2)}, u32[]{:S(2)}) collective-permute-start(f32[2,256,1024]{2,1,0:T(8,128)} %gate.16.refs_24_.refs_1_), channel_id=1, source_target_pairs={{0,16},{4,12},{8,24},{12,4},{16,0},{20,28},{24,8},{28,20},{1,17},{... | collective-permute-start | bytes 6291464 | tf_op jit(solution)/shard_map/ppermute | solution.py:913
  228.3 52.4 %collective-permute-start.23 = (f32[2,256,1024]{2,1,0:T(8,128)}, f32[2,256,1024]{2,1,0:T(8,128)}, u32[]{:S(2)}, u32[]{:S(2)}) collective-permute-start(f32[2,256,1024]{2,1,0:T(8,128)} %gate.16.refs_24_.refs_1_), channel_id=1, source_target_pairs={{0,8},{4,20},{8,0},{12,28},{16,24},{20,4},{24,16},{28,12},{1,9},{5... | collective-permute-start | bytes 6291464 | tf_op jit(solution)/shard_map/ppermute | solution.py:909
  229.7 44.7 %collective-permute-start.25 = (f32[1,256,1024]{2,1,0:T(8,128)S(1)}, f32[1,256,1024]{2,1,0:T(8,128)S(1)}, u32[]{:S(2)}, u32[]{:S(2)}) collective-permute-start(f32[1,256,1024]{2,1,0:T(8,128)S(1)} %constant_dynamic-slice_fusion), channel_id=1, source_target_pairs={{0,1},{1,2},{2,3},{3,0},{4,7},{5,4},{6,5},{7,6},{8,9},{9,10},{10,1... | collective-permute-start | bytes 3145736 | tf_op jit(solution)/shard_map/ppermute | solution.py:921
  275.4 37.8 %collective-permute-start.27 = (f32[1,256,1024]{2,1,0:T(8,128)}, f32[1,256,1024]{2,1,0:T(8,128)}, u32[]{:S(2)}, u32[]{:S(2)}) collective-permute-start(f32[1,256,1024]{2,1,0:T(8,128)} %gate.18.refs_8_.refs_1_), channel_id=1, source_target_pairs={{0,8},{4,20},{8,0},{12,28},{16,24},{20,4},{24,16},{28,12},{1,9},{5... | collective-permute-start | bytes 3145736 | tf_op jit(solution)/shard_map/ppermute | solution.py:909
  275.9 37.4 %collective-permute-start.28 = (f32[1,256,1024]{2,1,0:T(8,128)}, f32[1,256,1024]{2,1,0:T(8,128)S(1)}, u32[]{:S(2)}, u32[]{:S(2)}) collective-permute-start(f32[1,256,1024]{2,1,0:T(8,128)} %gate.18.refs_8_.refs_1_), channel_id=1, source_target_pairs={{0,16},{4,12},{8,24},{12,4},{16,0},{20,28},{24,8},{28,20},{1,17},{... | collective-permute-start | bytes 3145736 | tf_op jit(solution)/shard_map/ppermute | solution.py:913
  278.7 45.4 %collective-permute-start.26 = (f32[2,256,1024]{2,1,0:T(8,128)}, f32[2,256,1024]{2,1,0:T(8,128)S(1)}, u32[]{:S(2)}, u32[]{:S(2)}) collective-permute-start(f32[2,256,1024]{2,1,0:T(8,128)} %gate.17.refs_7_.refs_3_), channel_id=1, source_target_pairs={{0,8},{4,20},{8,0},{12,28},{16,24},{20,4},{24,16},{28,12},{1,9},{5... | collective-permute-start | bytes 6291464 | tf_op jit(solution)/shard_map/ppermute | solution.py:909
  280.7 44.8 %copy-start.4 = (f32[2,256,1024]{2,1,0:T(8,128)S(1)}, f32[2,256,1024]{2,1,0:T(8,128)}, u32[]{:S(2)}) copy-start(f32[2,256,1024]{2,1,0:T(8,128)} %gate.17.refs_7_.refs_3_) | copy-start | bytes 6291460
  280.7 44.8 %copy-start.25 = (s32[2]{0:T(128)S(1)}, s32[2]{0:T(128)}, u32[]{:S(2)}) copy-start(s32[2]{0:T(128)} %copy-done.23) | copy-start | bytes 28
  336.8 13.6 %collective-permute-start.29 = (f32[2,1024,1024]{2,1,0:T(8,128)}, f32[2,1024,1024]{2,1,0:T(8,128)}, u32[]{:S(2)}, u32[]{:S(2)}) collective-permute-start(f32[2,1024,1024]{2,1,0:T(8,128)} %join.10.refs_4_), channel_id=1, source_target_pairs={{0,4},{4,0},{8,12},{12,8},{16,20},{20,16},{24,28},{28,24},{1,5},{5... | collective-permute-start | bytes 25165832 | tf_op jit(solution)/shard_map/ppermute | solution.py:900
  336.9 46.3 %collective-permute-start.30 = (f32[1,256,1024]{2,1,0:T(8,128)}, f32[1,256,1024]{2,1,0:T(8,128)S(1)}, u32[]{:S(2)}, u32[]{:S(2)}) collective-permute-start(f32[1,256,1024]{2,1,0:T(8,128)} %gate.19.refs_7_.refs_3_), channel_id=1, source_target_pairs={{0,8},{4,20},{8,0},{12,28},{16,24},{20,4},{24,16},{28,12},{1,9},{5... | collective-permute-start | bytes 3145736 | tf_op jit(solution)/shard_map/ppermute | solution.py:909
  350.4 32.9 %copy-start.2 = (f32[1,256,1024]{2,1,0:T(8,128)S(1)}, f32[1,256,1024]{2,1,0:T(8,128)}, u32[]{:S(2)}) copy-start(f32[1,256,1024]{2,1,0:T(8,128)} %gate.19.refs_7_.refs_3_) | copy-start | bytes 3145732
  350.4 32.9 %copy-start.10 = (f32[1,256,1024]{2,1,0:T(8,128)S(1)}, f32[1,256,1024]{2,1,0:T(8,128)}, u32[]{:S(2)}) copy-start(f32[1,256,1024]{2,1,0:T(8,128)} %gate.18.refs_8_.refs_1_) | copy-start | bytes 3145732
  383.1 7.4 %collective-permute-start.32 = (f32[4,2,128,1024]{3,2,1,0:T(8,128)}, f32[4,2,128,1024]{3,2,1,0:T(8,128)S(1)}, u32[]{:S(2)}, u32[]{:S(2)}) collective-permute-start(f32[4,2,128,1024]{3,2,1,0:T(8,128)} %get-tuple-element.99), channel_id=1, source_target_pairs={{0,4},{4,0},{8,12},{12,8},{16,20},{20,16},{24,28},{28,24},{1,5},{5... | collective-permute-start | bytes 12582920 | tf_op jit(solution)/shard_map/ppermute | solution.py:900
  387.9 8.3 %collective-permute-start.31 = (f32[1,1024,1024]{2,1,0:T(8,128)S(1)}, f32[1,1024,1024]{2,1,0:T(8,128)S(1)}, u32[]{:S(2)}, u32[]{:S(2)}) collective-permute-start(f32[1,1024,1024]{2,1,0:T(8,128)S(1)} %join.11.refs_5_), channel_id=1, source_target_pairs={{0,4},{4,0},{8,12},{12,8},{16,20},{20,16},{24,28},{28,24},{1,5},{5... | collective-permute-start | bytes 12582920 | tf_op jit(solution)/shard_map/ppermute | solution.py:900
  391.7 26.2 %collective-permute-start.33 = (f32[2,2,128,1024]{3,2,1,0:T(8,128)S(1)}, f32[2,2,128,1024]{3,2,1,0:T(8,128)}, u32[]{:S(2)}, u32[]{:S(2)}) collective-permute-start(f32[2,2,128,1024]{3,2,1,0:T(8,128)S(1)} %slice.183), channel_id=1, source_target_pairs={{0,8},{4,20},{8,0},{12,28},{16,24},{20,4},{24,16},{28,12},{1,9},{5... | collective-permute-start | bytes 6291464 | tf_op jit(solution)/shard_map/ppermute | solution.py:935
  421.5 80.5 %collective-permute-start.34 = (f32[2,128,1024]{2,1,0:T(8,128)S(1)}, f32[2,128,1024]{2,1,0:T(8,128)S(1)}, u32[]{:S(2)}, u32[]{:S(2)}) collective-permute-start(f32[2,128,1024]{2,1,0:T(8,128)S(1)} %slice_bitcast_fusion.3), channel_id=1, source_target_pairs={{0,16},{4,12},{8,24},{12,4},{16,0},{20,28},{24,8},{28,20},{1,17},{... | collective-permute-start | bytes 3145736 | tf_op jit(solution)/shard_map/ppermute | solution.py:913
  518.1 27.5 %collective-permute-start.35 = (f32[4,8,128,256]{3,2,1,0:T(8,128)}, f32[4,8,128,256]{3,2,1,0:T(8,128)}, u32[]{:S(2)}, u32[]{:S(2)}) collective-permute-start(f32[4,8,128,256]{3,2,1,0:T(8,128)} %get-tuple-element.113), channel_id=1, source_target_pairs={{0,4},{4,0},{8,12},{12,8},{16,20},{20,16},{24,28},{28,24},{1,5},{5... | collective-permute-start | bytes 12582920 | tf_op jit(solution)/shard_map/ppermute | solution.py:900
  518.2 26.3 %copy-start.39 = (f32[2,128,1024]{2,1,0:T(8,128)S(1)}, f32[2,128,1024]{2,1,0:T(8,128)}, u32[]{:S(2)}) copy-start(f32[2,128,1024]{2,1,0:T(8,128)} %copy-done.38) | copy-start | bytes 3145732
  550.2 26.2 %collective-permute-start.36 = (f32[2,8,128,256]{3,2,1,0:T(8,128)S(1)}, f32[2,8,128,256]{3,2,1,0:T(8,128)}, u32[]{:S(2)}, u32[]{:S(2)}) collective-permute-start(f32[2,8,128,256]{3,2,1,0:T(8,128)S(1)} %slice.185), channel_id=1, source_target_pairs={{0,8},{4,20},{8,0},{12,28},{16,24},{20,4},{24,16},{28,12},{1,9},{5... | collective-permute-start | bytes 6291464 | tf_op jit(solution)/shard_map/ppermute | solution.py:935
  578.3 27.4 %collective-permute-start.37 = (f32[8,128,256]{2,1,0:T(8,128)S(1)}, f32[8,128,256]{2,1,0:T(8,128)S(1)}, u32[]{:S(2)}, u32[]{:S(2)}) collective-permute-start(f32[8,128,256]{2,1,0:T(8,128)S(1)} %slice_bitcast_fusion.2), channel_id=1, source_target_pairs={{0,16},{4,12},{8,24},{12,4},{16,0},{20,28},{24,8},{28,20},{1,17},{... | collective-permute-start | bytes 3145736 | tf_op jit(solution)/shard_map/ppermute | solution.py:913
  617.7 1.3 collective-permute-start.38
  619.0 3.9 collective-permute-start.39
  622.9 3.9 collective-permute-start.40
  (42 other events, 232.2 us)

commit v4 on v3

--- a/solution.py
+++ b/solution.py
@@ -233,12 +233,15 @@
     pre_len = (count - 1) * BLK
     keep = causal()
     pieces = []
-    for head in range(width // HEAD):
-        part = masked(query, head_row(width, head, HEAD**-0.5))
-        near = jnp.where(keep, dot(diag, part, NT), NEG)
+    heads = range(width // HEAD)
+    parts = [masked(query, head_row(width, head, HEAD**-0.5)) for head in heads]
+    nears = [dot(diag, part, NT) for part in parts]
+    fars = [dot(qkv[1, pl.ds(k0, pre_len), :], part, NT) for part in parts] if pre_len else []
+    for head in heads:
+        near = jnp.where(keep, nears[head], NEG)
         peak = jnp.max(near, axis=0, keepdims=True)
         if pre_len:
-            far = dot(qkv[1, pl.ds(k0, pre_len), :], part, NT)
+            far = fars[head]
             peak = jnp.maximum(peak, jnp.max(far, axis=0, keepdims=True))
         near = jnp.exp(near - peak)
         total = jnp.sum(near, axis=0, keepdims=True)
@@ -382,16 +385,19 @@
     item, _ = item_at(lengths, step * BLK)
     t0 = pl.multiple_of(item * text, text)
     alive = live[pl.ds(t0, text), :] > 0.0
+    width = own_out.shape[0]
+    heads = range(width // HEAD)
+    stages = []
     for j in range(4):
         query = dot(normed, queries[j][0]).astype(BF16)
-        width = query.shape[1]
-        cols = slice(j * width, (j + 1) * width)
-        cross_query[:, cols] = query
+        cross_query[:, j * width : (j + 1) * width] = query
+        rows = [masked(query, head_row(width, head, HEAD**-0.5)) for head in heads]
         keys = pairs[j][0, pl.ds(t0, text), :]
+        stages.append([dot(keys, row, NT) for row in rows])
+    for j in range(4):
         pieces = []
-        for head in range(width // HEAD):
-            row = masked(query, head_row(width, head, HEAD**-0.5))
-            score = jnp.where(alive, dot(keys, row, NT), NEG)
+        for head in heads:
+            score = jnp.where(alive, stages[j][head], NEG)
             peak = jnp.max(score, axis=0, keepdims=True)
             score = jnp.exp(score - peak)
             total = jnp.sum(score, axis=0, keepdims=True)
@@ -399,7 +405,7 @@
             pieces.append(result * (1.0 / total))
             index = j * (width // HEAD) + head
             logs[index : index + 1, :] = peak + jnp.log(total)
-        looked[:, cols] = jnp.concatenate(pieces, axis=0).T.astype(BF16)
+        looked[:, j * width : (j + 1) * width] = jnp.concatenate(pieces, axis=0).T.astype(BF16)
     residual = residual + dot(looked[...], w_co[...])
     after_cross[...] = residual
     third[...] = norm_forward(residual, gain2[...], shift2[...])
@@ -455,10 +461,13 @@
 
 
 def feed_rows(third, cot, up, down):
-    pre_act = dot(third, up)
+    return feed_finish(dot(third, up), dot(cot, down, NT), up, down)
+
+
+def feed_finish(pre_act, hidden_grad, up, down):
     hidden, slope = gelu_both(pre_act)
     hidden = hidden.astype(BF16)
-    pre_grad = (dot(cot, down, NT) * slope).astype(BF16)
+    pre_grad = (hidden_grad * slope).astype(BF16)
     return hidden, pre_grad, dot(hidden, down), dot(pre_grad, up, NT)
 
 
@@ -597,31 +606,38 @@
     t0 = pl.multiple_of(item * text, text)
     alive = live[pl.ds(t0, text), :] > 0.0
     second_grad = jnp.zeros(upstream.shape, F32)
-    for j in range(4):
-        width = queries[j].shape[2]
+    width = queries[0].shape[2]
+    heads = range(width // HEAD)
+
+    def scores(j):
         cols = slice(j * width, (j + 1) * width)
-        query = cross_query[:, cols]
-        grads = looked_grad[:, cols]
+        rows = [masked(cross_query[:, cols], head_row(width, h, HEAD**-0.5)) for h in heads]
+        grads = [masked(looked_grad[:, cols], head_row(width, h, 1.0)) for h in heads]
         keys = pairs[j][0, pl.ds(t0, text), :]
         values = pairs[j][1, pl.ds(t0, text), :]
-        pieces = []
-        key_sum = jnp.zeros((text, width), F32)
-        value_sum = jnp.zeros((text, width), F32)
-        for head in range(width // HEAD):
-            row = masked(query, head_row(width, head, HEAD**-0.5))
-            grad = masked(grads, head_row(width, head, 1.0))
+        return rows, grads, [dot(keys, row, NT) for row in rows], [dot(values, g, NT) for g in grads]
+
+    ahead = scores(0)
+    for j in range(4):
+        rows, grads, score_set, pushed_set = ahead
+        if j < 3:
+            ahead = scores(j + 1)
+        pieces, chances, score_grads = [], [], []
+        for head in heads:
             index = j * (width // HEAD) + head
-            score = jnp.where(alive, dot(keys, row, NT), NEG)
+            score = jnp.where(alive, score_set[head], NEG)
             chance = jnp.exp(score - logs[index : index + 1, :])
-            pushed = dot(values, grad, NT)
-            weighted = chance * pushed
+            weighted = chance * pushed_set[head]
             mean = jnp.sum(weighted, axis=0, keepdims=True)
-            score_grad = (weighted - chance * mean).astype(BF16)
-            pieces.append(dot(turned[j, lanes_of(head), pl.ds(t0, text)], score_grad))
-            key_sum = key_sum + dot(score_grad, row)
-            value_sum = value_sum + dot(chance.astype(BF16), grad)
-        total[j, 0, pl.ds(t0, text), :] += key_sum
-        total[j, 1, pl.ds(t0, text), :] += value_sum
+            score_grads.append((weighted - chance * mean).astype(BF16))
+            chances.append(chance.astype(BF16))
+            pieces.append(dot(turned[j, lanes_of(head), pl.ds(t0, text)], score_grads[head]))
+        total[j, 0, pl.ds(t0, text), :] += dot(
+            jnp.concatenate(score_grads, axis=1), jnp.concatenate(rows, axis=0)
+        )
+        total[j, 1, pl.ds(t0, text), :] += dot(
+            jnp.concatenate(chances, axis=1), jnp.concatenate(grads, axis=0)
+        )
         query_grad = (jnp.concatenate(pieces, axis=0).T * HEAD**-0.5).astype(BF16)
         if j == 0:
             query_grads[...] = query_grad
@@ -684,7 +700,7 @@
     )
 
 
-def text_kernel(me, text, pair_grad, second, query_grad, row_grads, qkv_grad, *refs):
+def text_kernel(me, text, pair_grad, second, query_grad, row_grads, *refs):
     crosses, (text_grad, keep, send, cross_grad, folded) = refs[:4], refs[4:]
     total = jnp.zeros(text_grad.shape, F32)
     for j in range(4):
@@ -695,7 +711,6 @@
     for m in range(2):
         cross_grad[m + 1] = dot(text[...], pair_grad[0, m], TN)
     put_pieces(cross_grad, keep, send, me)
-    put_pieces(qkv_grad, keep, send, me, 3)
     width = folded.shape[2]
     rows = row_grads.shape[1] // 8
     for k in range(2):
@@ -704,7 +719,7 @@
                 folded[k, pl.ds((piece * 4 + part) * rows, rows), :] = row_grads[
                     k, pl.ds(piece * rows, rows), part * width : (part + 1) * width
                 ]
-    put_pieces(folded, keep, send, me, 6)
+    put_pieces(folded, keep, send, me, 3)
 
 
 def unfold(piece):
@@ -713,14 +728,14 @@
     return jnp.concatenate(parts, axis=1)
 
 
-def text_back(me, text, pair_grad, second, query_grad, row_grads, qkv_grad, crosses, wait):
+def text_back(me, text, pair_grad, second, query_grad, row_grads, crosses, wait):
     text_rows, depth = text.shape
     width = pair_grad.shape[3]
-    pieces = (4, 8, depth // 8, width)
+    pieces = (4, 5, depth // 8, width)
     return launch(
         text_kernel,
-        [me, text, pair_grad, second, query_grad, row_grads, qkv_grad, *crosses],
-        [smem()] + [vmem()] * 10,
+        [me, text, pair_grad, second, query_grad, row_grads, *crosses],
+        [smem()] + [vmem()] * 9,
         [vmem()] * 3,
         [shape((text_rows, depth)), shape(pieces), shape(pieces)],
         scratch=[pltpu.VMEM((3, depth, width), F32), pltpu.VMEM((2, depth, width), F32)],
@@ -738,12 +753,12 @@
     values = qkv[2, pl.ds(k0, BLK), :]
     more_keys = 0.0
     more_values = 0.0
-    for head in range(rows.shape[0]):
-        score = dot(keys, rows[head], NT)
+    heads = range(rows.shape[0])
+    stages = [(dot(keys, rows[h], NT), dot(values, grads[h], NT)) for h in heads]
+    for head, (score, pushed) in zip(heads, stages):
         if diag:
             score = jnp.where(causal(), score, NEG)
         chance = jnp.exp(score - logs[head : head + 1, pl.ds(q0, BLK)])
-        pushed = dot(values, grads[head], NT)
         score_grad = (chance * (pushed - means[head : head + 1, :])).astype(BF16)
         query_sum[lanes_of(head), :] += dot(turned[lanes_of(head), pl.ds(k0, BLK)], score_grad)
         more_keys = more_keys + dot(score_grad, rows[head])
@@ -800,26 +815,27 @@
     ]
 
 
-def self_own_kernel(lengths, qkv, mixed, out_grad, logs, weights, first, total, qkv_grad, *scratch):
-    self_back_body(lengths, qkv, mixed, out_grad, logs, weights, *scratch)
-    triple = scratch[0]
+def self_own_kernel(me, lengths, qkv, mixed, out_grad, logs, weights, first, total, keep, send, *scratch):
+    self_back_body(lengths, qkv, mixed, out_grad, logs, weights, *scratch[:-1])
+    triple, qkv_grad = scratch[0], scratch[-1]
     for m in range(3):
         qkv_grad[m] = dot(first[...], triple[m], TN)
+    put_pieces(qkv_grad, keep, send, me)
     total[...] = sum(dot(triple[m], weights[m], NT) for m in range(3))
 
 
-def self_call(kernel, name, us, j, outs, operands, wait):
+def self_call(kernel, name, us, j, outs, operands, wait, prefix=(), scratch=()):
     lengths, qkv, mixed, out_grad, logs, weights, last_in = operands
     rows, width = mixed.shape
     return launch(
         kernel,
-        operands,
-        [smem()]
+        [*prefix, *operands],
+        [smem()] * (len(prefix) + 1)
         + [whole(qkv.shape), whole(mixed.shape), at((rows, width), (0, j))]
         + [whole(logs.shape), whole(weights.shape), whole(last_in.shape)],
         [whole(out.shape) for out in outs],
         outs,
-        scratch=self_scratch(rows, width),
+        scratch=self_scratch(rows, width) + list(scratch),
         wait=wait,
         grid=(1,),
         compiler_params=params(),
@@ -828,10 +844,13 @@
     )
 
 
-def self_own(lengths, qkv, mixed, out_grad, logs, weights, first, wait):
-    outs = [shape(first.shape), shape(weights.shape)]
+def self_own(me, lengths, qkv, mixed, out_grad, logs, weights, first, wait):
+    _, depth, width = weights.shape
+    pieces = shape((4, 3, depth // 8, width))
     operands = (lengths, qkv, mixed, out_grad, logs, weights, first)
-    return self_call(self_own_kernel, "self_own", 28, 0, outs, operands, wait)
+    scratch = [pltpu.VMEM(weights.shape, F32)]
+    outs = [shape(first.shape), pieces, pieces]
+    return self_call(self_own_kernel, "self_own", 22, 0, outs, operands, wait, (me,), scratch)
 
 
 def self_kernel(lengths, qkv, mixed, out_grad, logs, weights, before, total, *scratch):
@@ -845,33 +864,82 @@
     return self_call(self_kernel, "self_back", 26, j, [shape(before.shape)], operands, wait)[0]
 
 
-def last_kernel(first_grad, tokens, upstream, gain, token_grad, sums):
-    @pl.when(pl.program_id(0) == 0)
-    def _():
-        sums[...] = jnp.zeros_like(sums)
-
-    pulled, gain_sum, shift_sum = norm_backward(
-        first_grad[...], tokens[...].astype(F32), gain[...]
-    )
-    token_grad[...] = upstream[...] + pulled
-    sums[0:1, :] += gain_sum
-    sums[1:2, :] += shift_sum
-
-
-def last(first_grad, tokens, upstream, gain, wait):
+def self_rest_kernel(places, lengths, *refs):
+    count = len(places)
+    sets, refs = [refs[4 * k : 4 * k + 4] for k in range(count)], refs[4 * count :]
+    out_grad, before, tokens, upstream, gain, token_grad, sums, *refs = refs
+    held, (total, token_rows, up_rows, sems, out_sems, *scratch) = refs[:5], refs[5:]
+    rows, width = held[1].shape[1:]
+    waits = []
+    for k, (arrays, place) in enumerate(zip(sets, places)):
+        sources = [*arrays, out_grad.at[:, pl.ds(place * width, width)]]
+        waits.append(
+            [
+                pltpu.make_async_copy(source, target.at[k], sems.at[k, m])
+                for m, (source, target) in enumerate(zip(sources, held))
+            ]
+        )
+    ends = [
+        pltpu.make_async_copy(source, target, sems.at[count, m])
+        for m, (source, target) in enumerate(
+            ((before, total), (tokens, token_rows), (upstream, up_rows))
+        )
+    ]
+    for copy in waits[0] + ends[:1] + sum(waits[1:], []) + ends[1:]:
+        copy.start()
+    triple = scratch[0]
+    for k in range(count):
+        for copy in waits[k]:
+            copy.wait()
+        qkv, mixed, logs, weights, grads = (ref.at[k] for ref in held)
+        self_back_body(lengths, qkv, mixed, grads, logs, weights, *scratch)
+        if k == 0:
+            ends[0].wait()
+        total[...] += sum(dot(triple[m], weights[m], NT) for m in range(3))
+    ends[1].wait()
+    ends[2].wait()
+    sums[...] = jnp.zeros_like(sums)
+    outs = []
+    for k in range(rows // BLK):
+        part = slice(k * BLK, (k + 1) * BLK)
+        pulled, gain_sum, shift_sum = norm_backward(
+            total[part, :], token_rows[part, :].astype(F32), gain[...]
+        )
+        sums[0:1, :] += gain_sum
+        sums[1:2, :] += shift_sum
+        up_rows[part, :] = up_rows[part, :] + pulled
+        outs.append(
+            pltpu.make_async_copy(
+                up_rows.at[pl.ds(k * BLK, BLK)], token_grad.at[pl.ds(k * BLK, BLK)], out_sems.at[k]
+            )
+        )
+        outs[-1].start()
+    for copy in outs:
+        copy.wait()
+
+
+def self_rest(places, lengths, sets, out_grad, before, tokens, upstream, gain, wait):
     rows, depth = tokens.shape
-    tile = rows_of(BLK, depth)
+    count = len(places)
+    width = sets[0][1].shape[1]
+    args = [lengths, *sum(sets, []), out_grad, before, tokens, upstream, gain]
+    held = [
+        pltpu.VMEM((count,) + array.shape, array.dtype) for array in sets[0] + [sets[0][1]]
+    ]
     return launch(
-        last_kernel,
-        [first_grad, tokens, upstream, gain],
-        [tile, tile, tile, whole((1, depth))],
-        [tile, whole((8, depth))],
+        partial(self_rest_kernel, places),
+        args,
+        [smem()] + [anywhere()] * (len(args) - 2) + [vmem()],
+        [anywhere(), vmem()],
         [shape((rows, depth)), shape((8, depth))],
+        scratch=held
+        + [pltpu.VMEM((rows, depth), dtype) for dtype in (F32, BF16, F32)]
+        + [pltpu.SemaphoreType.DMA((count + 1, 5)), pltpu.SemaphoreType.DMA((rows // BLK,))]
+        + self_scratch(rows, width),
         wait=wait,
-        grid=(rows // BLK,),
         compiler_params=params(),
-        name="last",
-        cost_estimate=cost(10),
+        name="self_rest",
+        cost_estimate=cost(40),
     )
 
 
@@ -997,7 +1065,7 @@
         two_near, two_side = near_of(two), side_of(two)
         outer_one, outer_three = along(carried[0], 1), along(carried[0], 3)
         wait = [two, cross_near, cross_side, logs[1]]
-        carry = []
+        carry = [cut(feeds, chip)]
     weights[3], qkvs[3], mixeds[3], logs[3], *carried = front(
         lengths, first, g_qkv[1], wait, carry
     )
@@ -1007,8 +1075,8 @@
         mine = join(me, [two, two_near, two_side, near_of(two_side)], [mine])
         g_two = mine, swap(mine)
         outer_two = along(outer_one, 1)
-        feed_one = around(gate([outer_two], cut(feeds, chip)))
-        wait = [two_near, two_side, outer_two]
+        feed_one = around(carried[0])
+        wait = [two_near, two_side]
     else:
         g_cross = shards(own_cross)
         g_two = along(own_qkv.astype(F32), 2), along(own_cross.astype(F32), 2)
@@ -1072,44 +1140,53 @@
         cross_logs, gains[1], gains[2], full_out, full_co, crosses, pairs,
         [both_part] if planar else [],
     )
-    if planar:
-        both_part, both_side = sum_side(both_part, both_near)
+    wait = []
+    if planar:
+        both_part, both_side = sum_side(both_part, gate([sums], both_near))
         wait = [both_near]
-    first_grad, qkv_grad = self_own(
-        lengths, qkvs[0], mixeds[0], mixed_grad, logs[0], weights[0], first, wait
-    )
-    if planar:
-        wait = [both_side]
     text_grad, keep, send = text_back(
-        me, text, pair_grad, second, query_grad, row_grads, qkv_grad, crosses, wait
-    )
-    waits = [[], [], [], []]
+        me, text, pair_grad, second, query_grad, row_grads, crosses, wait
+    )
     if planar:
         late_swap = swap(send)
+        wait = []
+    first_grad, qkv_keep, qkv_send = self_own(
+        me, lengths, qkvs[0], mixeds[0], mixed_grad, logs[0], weights[0], first, wait
+    )
+    if planar:
         late_part, late_near = sum_near(keep, late_swap)
-        late_one, late_side = sum_side(late_part, late_near)
-        waits = [[], [late_swap], [late_near], [late_side]]
-    for j in (1, 2, 3):
-        first_grad = self_back(
-            lengths, qkvs[j], mixeds[j], mixed_grad, logs[j], weights[j], first_grad, j,
-            waits[j - 1],
-        )
-    token_grad, last_sums = last(first_grad, tokens, upstream, gains[0], waits[3])
+        qkv_swap = swap(qkv_send)
+        wait = [late_part, both_side]
+    first_grad = self_back(
+        lengths, qkvs[1], mixeds[1], mixed_grad, logs[1], weights[1], first_grad, 1, wait
+    )
+    if planar:
+        late_one, late_side = sum_side(late_part, gate([first_grad], late_near))
+        qkv_part, qkv_near = sum_near(qkv_keep, gate([first_grad], qkv_swap))
+        wait = [late_one, qkv_part]
+    token_grad, last_sums = self_rest(
+        (2, 3), lengths, [[qkvs[j], mixeds[j], logs[j], weights[j]] for j in (2, 3)],
+        mixed_grad, first_grad, tokens, upstream, gains[0], wait,
+    )
+    if planar:
+        qkv_one, qkv_side = sum_side(qkv_part, gate([last_sums], qkv_near))
     norm_sums = jnp.concatenate(
         [last_sums[0:1], sums[2:3], sums[0:1], last_sums[1:2], sums[3:4], sums[1:2]], axis=0
     )
     if planar:
         both_sum, late_sum = both_part + both_side, late_one + late_side
-        row_sum = [unfold(late_sum[k]) for k in (6, 7)]
+        qkv_sum = qkv_one + qkv_side
+        row_sum = [unfold(late_sum[k]) for k in (3, 4)]
         width = norm_sums.shape[1] // DP
         norm_sum = lax.dynamic_slice_in_dim(plane_sum(norm_sums), place * width, width, 1)
     else:
         both_sum = scattered(in_order(both_keep, both_send), 1)
         late = in_order(keep, send)
-        late_sum = scattered(late[:6], 1)
+        late_sum = scattered(late[:3], 1)
+        qkv_sum = scattered(in_order(qkv_keep, qkv_send), 1)
         row_sum = [
             scattered(jnp.concatenate([unfold(part) for part in jnp.split(late[k], 8)]), 0)
-            for k in (6, 7)
+            for k in (3, 4)
         ]
         norm_sum = scattered(norm_sums, 1)
     return (
@@ -1118,7 +1195,7 @@
         text_grad.reshape(text_states.shape),
         norm_sum[:3],
         norm_sum[3:],
-        jnp.transpose(late_sum[3:6], (1, 0, 2)),
+        jnp.transpose(qkv_sum, (1, 0, 2)),
         row_sum[0],
         late_sum[0],
         jnp.transpose(late_sum[1:3], (1, 0, 2)),

time: 635 us -> 592 us (0.932)
  Pallas kernels: 408 us -> 333 us
  local copies, waits for them, and re-layouts: 33.3 us -> 45 us
  other arithmetic: 19.4 us -> 28.5 us
  starting transfers between devices: 40.9 us -> 49.9 us
    pallas_call x33 -> x34, Pallas kernels: 408 us -> 333 us  [launch(): pl.pallas_call(body, in_specs=list(in_specs) + [anywhere()] * extra, out_...]
    ppermute x3, waiting for transfers between devices: 7.17 us -> 50.6 us  [along(): return lax.ppermute(value, 'mp', straight(step))]
    ppermute x5, waiting for transfers between devices: 54.1 us -> 22.2 us  [around(): return lax.ppermute(value, ('dp', 'mp'), ring(1))]
    ppermute x12, starting transfers between devices: 9.32 us -> 18.6 us  [near_of(): return lax.ppermute(piece, 'dp', beside(True))]
    ppermute x8 -> x9, waiting for transfers between devices: 20.6 us -> 12.7 us  [swap(): return lax.ppermute(value, 'dp', [(i, i ^ 1) for i in range(DP)])]
    unnamed x102 -> x108, local copies, waits for them, and re-layouts: 26 us -> 32.1 us
    ppermute x8 -> x9, waiting for transfers between devices: 13.9 us -> 16.6 us  [side_of(): return lax.ppermute(piece, 'dp', beside(False))]
    ppermute x8 -> x9, starting transfers between devices: 11.6 us -> 13.7 us  [side_of(): return lax.ppermute(piece, 'dp', beside(False))]
  transfers between devices with their start and end apart: 41 -> 44, of which waited for: 17 -> 16; matrix products, arithmetic and copies ran while one was open for 3% -> 6% of each run, Pallas kernels for 59% -> 53%
where the time goes in v4:
time: 592 us; the launch traced here: 586 us
  Pallas kernels  333 us (56%)
  waiting for transfers between devices  129 us (22%)
  starting transfers between devices  49.9 us (8%)
  local copies, waits for them, and re-layouts  45 us (8%)
  other arithmetic  28.5 us (5%)
    pallas_call x34, Pallas kernels, launch(): pl.pallas_call(body, in_specs=list(in_specs) + [anywhere()] * extra, out_...  333 us
    ppermute x3, waiting for transfers between devices, along(): return lax.ppermute(value, 'mp', straight(step))  50.6 us
    unnamed x108, local copies, waits for them, and re-layouts  32.1 us
    ppermute x5, waiting for transfers between devices, around(): return lax.ppermute(value, ('dp', 'mp'), ring(1))  22.2 us
    ppermute x12, waiting for transfers between devices, near_of(): return lax.ppermute(piece, 'dp', beside(True))  21 us
    ppermute x12, starting transfers between devices, near_of(): return lax.ppermute(piece, 'dp', beside(True))  18.6 us
    ppermute x9, waiting for transfers between devices, side_of(): return lax.ppermute(piece, 'dp', beside(False))  16.6 us
    ppermute x9, starting transfers between devices, side_of(): return lax.ppermute(piece, 'dp', beside(False))  13.7 us
  transfers between devices with their start and end apart: 44, of which 16 were waited for; matrix products, arithmetic and copies ran while one was open for 6% of the time, Pallas kernels for 53%

profile of v4, /device:TPU:0, one launch (start us, length us, event | category | flops | bytes accessed | tf_op | source)
XLA Modules:
  0.0 586.3 jit_solution(11152369421200260858)
XLA Ops:
  1.8 3.1 collective-permute-start
  8.6 16.0 %collective-permute-done.refs_3_.refs_0_.refs_1_ = f32[3,256,256]{2,1,0:T(8,128)S(1)} collective-permute-done((f32[3,256,256]{2,1,0:T(8,128)S(1)}, f32[3,256,256]{2,1,0:T(8,128)S(1)}, u32[]{:S(2)}, u32[]{:S(2)}) %collective-permute-start) | collective-permute-done | bytes 786464 | tf_op jit(solution)/shard_map/ppermute | solution.py:989
  26.2 5.6 norm_first.1.refs_1_.refs_2_.refs_7_
  33.3 3.4 collective-permute-done.2.refs_3_
  36.7 2.5 collective-permute-start.3
  39.2 11.9 %front_own.1 = (bf16[3,1280,256]{2,1,0:T(8,128)(2,1)}, bf16[1280,256]{1,0:T(8,128)(2,1)}, f32[8,1280]{1,0:T(8,128)}) custom-call(s32[5]{0:T(128)} %refs_0_.13, bf16[1280,1024]{1,0:T(8,128)(2,1)} %norm_first.1.refs_1_.refs_2_.refs_7_, bf16[3,1024,256]{2,1,0:T(8,128)(2,1)} %bitcast.78, f32[3,256,256]{2,1,0:T(8,128)} %copy-done.16), custom_call_target="tpu_custom_call" | custom-call | flops 17250000896 | bytes 54000000 | tf_op jit(solution)/shard_map/front_own/pallas_call | solution.py:71
  53.2 2.6 join.6.refs_2_
  58.5 2.0 collective-permute-start.5
  62.4 12.8 %front.2 = (bf16[3,1024,256]{2,1,0:T(8,128)(2,1)}, bf16[3,1280,256]{2,1,0:T(8,128)(2,1)}, bf16[1280,256]{1,0:T(8,128)(2,1)}, f32[8,1280]{1,0:T(8,128)}, f32[1,64,1024]{2,1,0:T(8,128)}) custom-call(s32[5]{0:T(128)} %refs_0_.13, bf16[1280,1024]{1,0:T(8,128)(2,1)} %norm_first.1.refs_1_.refs_2_.refs_7_, ...), custom_call_target="tpu_custom_call", output_to_operand_aliasing={{4}: (4, {})} | custom-call | flops 18400000000 | bytes 57600000 | tf_op jit(solution)/shard_map/front/pallas_call | solution.py:71
  75.3 5.6 collective-permute-done.5.refs_1_
  82.1 2.8 fusion.1.refs_7_
  85.4 3.4 collective-permute-start.14
  90.5 5.9 %collective-permute-done.7.refs_3_.refs_5_ = f32[3,256,256]{2,1,0:T(8,128)S(1)} collective-permute-done((f32[3,256,256]{2,1,0:T(8,128)}, f32[3,256,256]{2,1,0:T(8,128)S(1)}, u32[]{:S(2)}, u32[]{:S(2)}) %collective-permute-start.7) | collective-permute-done | bytes 786464 | tf_op jit(solution)/shard_map/ppermute | solution.py:981
  96.5 2.6 collective-permute-start.11
  99.1 12.8 %front.3 = (bf16[3,1024,256]{2,1,0:T(8,128)(2,1)}, bf16[3,1280,256]{2,1,0:T(8,128)(2,1)}, bf16[1280,256]{1,0:T(8,128)(2,1)}, f32[8,1280]{1,0:T(8,128)}, f32[2,256,1024]{2,1,0:T(8,128)}) custom-call(s32[5]{0:T(128)} %refs_0_.13, bf16[1280,1024]{1,0:T(8,128)(2,1)} %norm_first.1.refs_1_.refs_2_.refs_7_, ...), custom_call_target="tpu_custom_call", output_to_operand_aliasing={{4}: (7, {})} | custom-call | flops 18400000000 | bytes 57600000 | tf_op jit(solution)/shard_map/front/pallas_call | solution.py:71
  118.0 4.5 join.8.refs_3_
  123.1 3.5 collective-permute-start.17
  127.9 50.6 %collective-permute-done.17 = f32[1,64,1024]{2,1,0:T(8,128)S(1)} collective-permute-done((f32[1,64,1024]{2,1,0:T(8,128)S(1)}, f32[1,64,1024]{2,1,0:T(8,128)S(1)}, u32[]{:S(2)}, u32[]{:S(2)}) %collective-permute-start.17) | collective-permute-done | bytes 262176 | tf_op jit(solution)/shard_map/ppermute | solution.py:985
  181.2 8.0 %text_front.1 = (bf16[3,1024,256]{2,1,0:T(8,128)(2,1)}, bf16[3,1024,256]{2,1,0:T(8,128)(2,1)}, bf16[2,640,256]{2,1,0:T(8,128)(2,1)}, bf16[2,640,256]{2,1,0:T(8,128)(2,1)}, bf16[2,640,256]{2,1,0:T(8,128)(2,1)}) custom-call(bf16[640,1024]{1,0:T(8,128)(2,1)} %bitcast.81, bf16[3,1024,256]{2,1,0:T(8,128)(2,1)} %pad_maximum_fusion.refs_1_.refs_14_.refs_6_, ...), custom_call_target="tpu_custom_call" | custom-call | flops 8049999872 | bytes 25200000 | tf_op jit(solution)/shard_map/text_front/pallas_call | solution.py:71
  193.7 16.0 %front_two.1 = (bf16[3,1024,256]{2,1,0:T(8,128)(2,1)}, bf16[3,1024,256]{2,1,0:T(8,128)(2,1)}, bf16[3,1280,256]{2,1,0:T(8,128)(2,1)}, bf16[1280,256]{1,0:T(8,128)...) custom-call(s32[2]{0:T(128)} %copy-done.20, s32[5]{0:T(128)} %refs_0_.13, ...), custom_call_target="tpu_custom_call" | custom-call | flops 20700000256 | bytes 64800000 | tf_op jit(solution)/shard_map/front_two/pallas_call | solution.py:71
  212.0 10.9 %collective-permute-done.21.refs_4_ = f32[3,64,1024]{2,1,0:T(8,128)S(1)} collective-permute-done((f32[3,64,1024]{2,1,0:T(8,128)}, f32[3,64,1024]{2,1,0:T(8,128)S(1)}, u32[]{:S(2)}, u32[]{:S(2)}) %collective-permute-start.21) | collective-permute-done | bytes 786464 | tf_op jit(solution)/shard_map/ppermute | solution.py:977
  224.1 2.6 join.9.refs_22_
  232.7 32.0 %middle.1 = (bf16[1024,1024]{1,0:T(8,128)(2,1)}, bf16[1024,1024]{1,0:T(8,128)(2,1)}, f32[1280,1024]{1,0:T(8,128)}, f32[1280,1024]{1,0:T(8,128)}, bf16[1280,1024]...) custom-call(s32[2]{0:T(128)} %copy-done.20, ...), custom_call_target="tpu_custom_call" | custom-call | flops 49450000384 | bytes 154800000 | tf_op jit(solution)/shard_map/middle/pallas_call | solution.py:71
  268.7 7.2 %collective-permute-done.24.refs_1_ = f32[2,256,1024]{2,1,0:T(8,128)S(1)} collective-permute-done((f32[2,256,1024]{2,1,0:T(8,128)}, f32[2,256,1024]{2,1,0:T(8,128)S(1)}, u32[]{:S(2)}, u32[]{:S(2)}) %collective-permute-start.24) | collective-permute-done | bytes 2097184 | tf_op jit(solution)/shard_map/ppermute | solution.py:981
  279.0 32.6 %feed_own.1 = (f32[1280,1024]{1,0:T(8,128)}, f32[1280,1024]{1,0:T(8,128)}, f32[4,2,128,1024]{3,2,1,0:T(8,128)}, f32[4,2,128,1024]{3,2,1,0:T(8,128)}) custom-call(s32[2]{0:T(128)} %copy-done.20, bf16[1280,1024]{1,0:T(8,128)(2,1)} %get-tuple-element.85.refs_0_.refs_1_, bf16[1280,1024]{1,0:T(8,128)(2,1)} %refs_3_.3, ...), custom_call_target="tpu_custom_call" | custom-call | flops 36800000000 | bytes 115200000 | tf_op jit(solution)/shard_map/feed_own/pallas_call | solution.py:71
  311.6 9.2 %collective-permute-done.26.refs_4_ = f32[2,256,1024]{2,1,0:T(8,128)S(1)} collective-permute-done((f32[2,256,1024]{2,1,0:T(8,128)}, f32[2,256,1024]{2,1,0:T(8,128)S(1)}, u32[]{:S(2)}, u32[]{:S(2)}) %collective-permute-start.26) | collective-permute-done | bytes 2097184 | tf_op jit(solution)/shard_map/ppermute | solution.py:977
  322.2 2.5 copy-done
  327.8 5.6 join.10.refs_4_
  335.1 11.9 %collective-permute-done.29.refs_5_ = f32[2,1024,1024]{2,1,0:T(8,128)} collective-permute-done((f32[2,1024,1024]{2,1,0:T(8,128)}, f32[2,1024,1024]{2,1,0:T(8,128)}, u32[]{:S(2)}, u32[]{:S(2)}) %collective-permute-start.29) | collective-permute-done | bytes 8388640 | tf_op jit(solution)/shard_map/ppermute | solution.py:968
  347.1 32.8 %feed_pair.1 = (f32[1280,1024]{1,0:T(8,128)}, f32[1280,1024]{1,0:T(8,128)}, f32[4,2,128,1024]{3,2,1,0:T(8,128)}) custom-call(bf16[1280,1024]{1,0:T(8,128)(2,1)} %get-tuple-element.85.refs_0_.refs_1_, bf16[1280,1024]{1,0:T(8,128)(2,1)} %refs_3_.3, f32[1280,1024]{1,0:T(8,128)} %get-tuple-element.87.refs_5_.refs_0_.refs_2_, ...), custom_call_target="tpu_custom_call", output_to_operand_aliasing={{2}: (8, {})} | custom-call | flops 34500001792 | bytes 108000000 | tf_op jit(solution)/shard_map/feed_pair/pallas_call | solution.py:71
  380.2 2.5 copy-done.5
  382.7 3.9 join.11.refs_5_
  387.4 4.4 add.63
  391.8 2.0 fusion.10
  395.7 18.3 %feed_last.1 = (bf16[1280,1024]{1,0:T(8,128)(2,1)}, f32[1280,1024]{1,0:T(8,128)}) custom-call(s32[2]{0:T(128)} %copy-done.20, bf16[1280,1024]{1,0:T(8,128)(2,1)} %get-tuple-element.85.refs_0_.refs_1_, bf16[1280,1024]{1,0:T(8,128)(2,1)} %refs_3_.3, f32[1280,1024]{1,0:T(8,128)} %get-tuple-element.90.refs_5_.refs_3_, f32[1280,1024]{1,0:T(8,128)} %get-tuple-element.91.refs_4_, ...), custom_call_target="tpu_custom_call" | custom-call | flops 20700000256 | bytes 64800000 | tf_op jit(solution)/shard_map/feed_last/pallas_call | solution.py:71
  413.9 39.3 %back.1 = (f32[1280,1024]{1,0:T(8,128)}, bf16[1280,1024]{1,0:T(8,128)(2,1)}, bf16[4,2,640,256]{3,2,1,0:T(8,128)(2,1)}, f32[2,256,1024]{2,1,0:T(8,128)}, bf16[1280,256]{1,0:T(8,128)(2,1)}, /*index=5*/f32[8,1024]{1,0:T(8,128)}) custom-call(s32[5]{0:T(128)} %refs_0_.13, f32[640,1]{1,0:T(8,128)} %bitcast.77, f32[1280,1024]{1,0:T(8,128)} %get-tuple-element.97.refs_2_, ...), custom_call_target="tpu_custom_call" | custom-call | flops 60949999616 | bytes 190800000 | tf_op jit(solution)/shard_map/back/pallas_call | solution.py:71
  454.6 13.2 %text_back.1 = (f32[640,1024]{1,0:T(8,128)}, f32[4,5,128,256]{3,2,1,0:T(8,128)}, f32[4,5,128,256]{3,2,1,0:T(8,128)}) custom-call(s32[2]{0:T(128)} %copy-done.20, bf16[640,1024]{1,0:T(8,128)(2,1)} %bitcast.83, bf16[4,2,640,256]{3,2,1,0:T(8,128)(2,1)} %get-tuple-element.111.refs_2_, bf16[1280,1024]{1,0:T(8,128)(2,1)} %get-tuple-element.112.refs_3_, ...), custom_call_target="tpu_custom_call" | custom-call | flops 17250000896 | bytes 54000000 | tf_op jit(solution)/shard_map/text_back/pallas_call | solution.py:71
  467.8 2.8 slice_add_fusion.2
  473.4 21.6 %self_own.1 = (f32[1280,1024]{1,0:T(8,128)}, f32[4,3,128,256]{3,2,1,0:T(8,128)}, f32[4,3,128,256]{3,2,1,0:T(8,128)}) custom-call(s32[2]{0:T(128)} %copy-done.20, s32[5]{0:T(128)} %refs_0_.13, bf16[3,1280,256]{2,1,0:T(8,128)(2,1)} %get-tuple-element.109.refs_2_, bf16[1280,256]{1,0:T(8,128)(2,1)} %get-tuple-element.68.refs_10_.refs_8_.refs_3_, ...), custom_call_target="tpu_custom_call" | custom-call | flops 25300000768 | bytes 79200000 | tf_op jit(solution)/shard_map/self_own/pallas_call | solution.py:71
  495.1 2.5 fusion.2
  499.1 2.1 add.64
  503.6 19.5 %self_back.1.refs_0_.refs_10_ = f32[1280,1024]{1,0:T(8,128)} custom-call(s32[5]{0:T(128)} %refs_0_.13, bf16[3,1280,256]{2,1,0:T(8,128)(2,1)} %get-tuple-element.107.refs_1_, bf16[1280,256]{1,0:T(8,128)(2,1)} %get-tuple-element.70.refs_11_.refs_2_, bf16[1280,1024]{1,0:T(8,128)(2,1)} %get-tuple-element.106.refs_4_.refs_3_.refs_9_, ...), custom_call_target="tpu_custom_call" | custom-call | flops 29899999232 | bytes 93600000 | tf_op jit(solution)/shard_map/self_back/pallas_call | solution.py:71
  523.2 2.1 add.67
  531.2 2.2 collective-permute-start.43
  533.4 35.2 %self_rest.1 = (f32[1280,1024]{1,0:T(8,128)}, f32[8,1024]{1,0:T(8,128)}) custom-call(s32[5]{0:T(128)} %refs_0_.13, bf16[3,1280,256]{2,1,0:T(8,128)(2,1)} %get-tuple-element.93.refs_1_, bf16[1280,256]{1,0:T(8,128)(2,1)} %get-tuple-element.76.refs_12_.refs_2_, f32[8,1280]{1,0:T(8,128)} %get-tuple-element.84.refs_0_.refs_5_.refs_3_, ...), custom_call_target="tpu_custom_call" | custom-call | flops 46000001024 | bytes 144000000 | tf_op jit(solution)/shard_map/self_rest/pallas_call | solution.py:71
  572.6 1.9 collective-permute-start.42
  574.5 2.3 collective-permute-done.39
  577.9 3.3 collective-permute-done.40
  (222 shorter events, 82.8 us)
Async XLA Ops:
  1.8 22.8 %collective-permute-start = (f32[3,256,256]{2,1,0:T(8,128)S(1)}, f32[3,256,256]{2,1,0:T(8,128)S(1)}, u32[]{:S(2)}, u32[]{:S(2)}) collective-permute-start(f32[3,256,256]{2,1,0:T(8,128)S(1)} %convert_bitcast_fusion), channel_id=1, source_target_pairs={{0,1},{1,2},{2,3},{3,0},{4,7},{5,4},{6,5},{7,6},{8,9},{9,10},{10,1... | collective-permute-start | bytes 2359304 | tf_op jit(solution)/shard_map/ppermute | solution.py:989
  24.6 12.1 %collective-permute-start.2 = (f32[3,256,256]{2,1,0:T(8,128)S(1)}, f32[3,256,256]{2,1,0:T(8,128)S(1)}, u32[]{:S(2)}, u32[]{:S(2)}) collective-permute-start(f32[3,256,256]{2,1,0:T(8,128)S(1)} %collective-permute-done.refs_3_.refs_0_.refs_1_), channel_id=1, source_target_pairs={{0,16},{4,12},{8,24},{12,4},{16,0},{20,28},{24,8},{28,20},{1,17},{... | collective-permute-start | bytes 2359304 | tf_op jit(solution)/shard_map/ppermute | solution.py:981
  26.2 91.8 %copy-start.20 = (s32[2]{0:T(128)}, s32[2]{0:T(128)S(1)}, u32[]{:S(2)}) copy-start(s32[2]{0:T(128)S(1)} %pad_add_fusion.refs_0_) | copy-start | bytes 28
  31.8 20.0 %collective-permute-start.4 = (f32[3,256,256]{2,1,0:T(8,128)}, f32[3,256,256]{2,1,0:T(8,128)S(1)}, u32[]{:S(2)}, u32[]{:S(2)}) collective-permute-start(f32[3,256,256]{2,1,0:T(8,128)} %gate.13), channel_id=1, source_target_pairs={{0,1},{1,2},{2,3},{3,0},{4,7},{5,4},{6,5},{7,6},{8,9},{9,10},{10,1... | collective-permute-start | bytes 2359304 | tf_op jit(solution)/shard_map/ppermute | solution.py:989
  31.8 20.0 %collective-permute-start.1 = (f32[3,256,256]{2,1,0:T(8,128)}, f32[3,256,256]{2,1,0:T(8,128)S(1)}, u32[]{:S(2)}, u32[]{:S(2)}) collective-permute-start(f32[3,256,256]{2,1,0:T(8,128)} %copy-done.16), channel_id=1, source_target_pairs={{0,8},{4,20},{8,0},{12,28},{16,24},{20,4},{24,16},{28,12},{1,9},{5... | collective-permute-start | bytes 2359304 | tf_op jit(solution)/shard_map/ppermute | solution.py:977
  36.7 15.7 %collective-permute-start.3 = (f32[3,256,256]{2,1,0:T(8,128)S(1)}, f32[3,256,256]{2,1,0:T(8,128)S(1)}, u32[]{:S(2)}, u32[]{:S(2)}) collective-permute-start(f32[3,256,256]{2,1,0:T(8,128)S(1)} %collective-permute-done.2.refs_3_), channel_id=1, source_target_pairs={{0,8},{4,20},{8,0},{12,28},{16,24},{20,4},{24,16},{28,12},{1,9},{5... | collective-permute-start | bytes 2359304 | tf_op jit(solution)/shard_map/ppermute | solution.py:977
  55.8 43.2 %collective-permute-start.12 = (f32[3,1024,256]{2,1,0:T(8,128)}, f32[3,1024,256]{2,1,0:T(8,128)}, u32[]{:S(2)}, u32[]{:S(2)}) collective-permute-start(f32[3,1024,256]{2,1,0:T(8,128)} %join.6.refs_2_), channel_id=1, source_target_pairs={{0,4},{4,0},{8,12},{12,8},{16,20},{20,16},{24,28},{28,24},{1,5},{5... | collective-permute-start | bytes 9437192 | tf_op jit(solution)/shard_map/ppermute | solution.py:968
  58.5 22.3 %collective-permute-start.5 = (f32[3,256,256]{2,1,0:T(8,128)S(1)}, f32[3,256,256]{2,1,0:T(8,128)}, u32[]{:S(2)}, u32[]{:S(2)}) collective-permute-start(f32[3,256,256]{2,1,0:T(8,128)S(1)} %broadcast_select_fusion), channel_id=1, source_target_pairs={{0,1},{1,2},{2,3},{3,0},{4,7},{5,4},{6,5},{7,6},{8,9},{9,10},{10,1... | collective-permute-start | bytes 2359304 | tf_op jit(solution)/shard_map/ppermute | solution.py:989
  60.4 25.0 %collective-permute-start.10 = (f32[3,256,256]{2,1,0:T(8,128)S(1)}, f32[3,256,256]{2,1,0:T(8,128)}, u32[]{:S(2)}, u32[]{:S(2)}) collective-permute-start(f32[3,256,256]{2,1,0:T(8,128)S(1)} %collective-permute-done.4.refs_6_.refs_3_.refs_1_), channel_id=1, source_target_pairs={{0,16},{4,12},{8,24},{12,4},{16,0},{20,28},{24,8},{28,20},{1,17},{... | collective-permute-start | bytes 2359304 | tf_op jit(solution)/shard_map/ppermute | solution.py:981
  61.0 27.9 %collective-permute-start.9 = (f32[3,256,256]{2,1,0:T(8,128)S(1)}, f32[3,256,256]{2,1,0:T(8,128)S(1)}, u32[]{:S(2)}, u32[]{:S(2)}) collective-permute-start(f32[3,256,256]{2,1,0:T(8,128)S(1)} %collective-permute-done.4.refs_6_.refs_3_.refs_1_), channel_id=1, source_target_pairs={{0,8},{4,20},{8,0},{12,28},{16,24},{20,4},{24,16},{28,12},{1,9},{5... | collective-permute-start | bytes 2359304 | tf_op jit(solution)/shard_map/ppermute | solution.py:977
  80.8 15.6 %collective-permute-start.7 = (f32[3,256,256]{2,1,0:T(8,128)}, f32[3,256,256]{2,1,0:T(8,128)S(1)}, u32[]{:S(2)}, u32[]{:S(2)}) collective-permute-start(f32[3,256,256]{2,1,0:T(8,128)} %gate.14.refs_3_.refs_1_), channel_id=1, source_target_pairs={{0,16},{4,12},{8,24},{12,4},{16,0},{20,28},{24,8},{28,20},{1,17},{... | collective-permute-start | bytes 2359304 | tf_op jit(solution)/shard_map/ppermute | solution.py:981
  84.9 27.0 %collective-permute-start.13 = (f32[1,64,1024]{2,1,0:T(8,128)S(1)}, f32[1,64,1024]{2,1,0:T(8,128)S(1)}, u32[]{:S(2)}, u32[]{:S(2)}) collective-permute-start(f32[1,64,1024]{2,1,0:T(8,128)S(1)} %copy-done.46), channel_id=1, source_target_pairs={{0,1},{1,2},{2,3},{3,0},{4,5},{5,6},{6,7},{7,4},{8,9},{9,10},{10,1... | collective-permute-start | bytes 786440 | tf_op jit(solution)/shard_map/ppermute | solution.py:985
  85.4 26.5 %collective-permute-start.14 = (f32[1,64,1024]{2,1,0:T(8,128)S(1)}, f32[1,64,1024]{2,1,0:T(8,128)S(1)}, u32[]{:S(2)}, u32[]{:S(2)}) collective-permute-start(f32[1,64,1024]{2,1,0:T(8,128)S(1)} %copy-done.46), channel_id=1, source_target_pairs={{0,3},{1,0},{2,1},{3,2},{4,7},{5,4},{6,5},{7,6},{8,11},{9,8},{10,9... | collective-permute-start | bytes 786440 | tf_op jit(solution)/shard_map/ppermute | solution.py:985
  88.9 29.0 %collective-permute-start.6 = (f32[3,256,256]{2,1,0:T(8,128)}, f32[3,256,256]{2,1,0:T(8,128)S(1)}, u32[]{:S(2)}, u32[]{:S(2)}) collective-permute-start(f32[3,256,256]{2,1,0:T(8,128)} %gate.14.refs_3_.refs_1_), channel_id=1, source_target_pairs={{0,8},{4,20},{8,0},{12,28},{16,24},{20,4},{24,16},{28,12},{1,9},{5... | collective-permute-start | bytes 2359304 | tf_op jit(solution)/shard_map/ppermute | solution.py:977
  96.5 15.5 %collective-permute-start.11 = (f32[3,256,256]{2,1,0:T(8,128)}, f32[3,256,256]{2,1,0:T(8,128)S(1)}, u32[]{:S(2)}, u32[]{:S(2)}) collective-permute-start(f32[3,256,256]{2,1,0:T(8,128)} %gate.15.refs_5_.refs_3_), channel_id=1, source_target_pairs={{0,8},{4,20},{8,0},{12,28},{16,24},{20,4},{24,16},{28,12},{1,9},{5... | collective-permute-start | bytes 2359304 | tf_op jit(solution)/shard_map/ppermute | solution.py:977
  99.0 19.0 %collective-permute-start.8 = (f32[3,256,256]{2,1,0:T(8,128)S(1)}, f32[3,256,256]{2,1,0:T(8,128)S(1)}, u32[]{:S(2)}, u32[]{:S(2)}) collective-permute-start(f32[3,256,256]{2,1,0:T(8,128)S(1)} %collective-permute-done.7.refs_3_.refs_5_), channel_id=1, source_target_pairs={{0,8},{4,20},{8,0},{12,28},{16,24},{20,4},{24,16},{28,12},{1,9},{5... | collective-permute-start | bytes 2359304 | tf_op jit(solution)/shard_map/ppermute | solution.py:977
  117.8 61.6 %collective-permute-start.16 = (f32[3,1024,256]{2,1,0:T(8,128)S(1)}, f32[3,1024,256]{2,1,0:T(8,128)S(1)}, u32[]{:S(2)}, u32[]{:S(2)}) collective-permute-start(f32[3,1024,256]{2,1,0:T(8,128)S(1)} %join.7.refs_5_.refs_2_), channel_id=1, source_target_pairs={{0,4},{4,0},{8,12},{12,8},{16,20},{20,16},{24,28},{28,24},{1,5},{5... | collective-permute-start | bytes 9437192 | tf_op jit(solution)/shard_map/ppermute | solution.py:968
  122.6 69.8 %collective-permute-start.15 = (f32[3,1024,256]{2,1,0:T(8,128)}, f32[3,1024,256]{2,1,0:T(8,128)}, u32[]{:S(2)}, u32[]{:S(2)}) collective-permute-start(f32[3,1024,256]{2,1,0:T(8,128)} %join.8.refs_3_), channel_id=1, source_target_pairs={{0,4},{4,0},{8,12},{12,8},{16,20},{20,16},{24,28},{28,24},{1,5},{5... | collective-permute-start | bytes 9437192 | tf_op jit(solution)/shard_map/ppermute | solution.py:968
  122.7 69.8 %collective-permute-start.18 = (f32[2,256,1024]{2,1,0:T(8,128)}, f32[2,256,1024]{2,1,0:T(8,128)S(1)}, u32[]{:S(2)}, u32[]{:S(2)}) collective-permute-start(f32[2,256,1024]{2,1,0:T(8,128)} %get-tuple-element.75), channel_id=1, source_target_pairs={{0,1},{1,2},{2,3},{3,0},{4,7},{5,4},{6,5},{7,6},{8,9},{9,10},{10,1... | collective-permute-start | bytes 6291464 | tf_op jit(solution)/shard_map/ppermute | solution.py:989
  123.1 55.4 %collective-permute-start.17 = (f32[1,64,1024]{2,1,0:T(8,128)S(1)}, f32[1,64,1024]{2,1,0:T(8,128)S(1)}, u32[]{:S(2)}, u32[]{:S(2)}) collective-permute-start(f32[1,64,1024]{2,1,0:T(8,128)S(1)} %collective-permute-done.13.refs_6_), channel_id=1, source_target_pairs={{0,1},{1,2},{2,3},{3,0},{4,5},{5,6},{6,7},{7,4},{8,9},{9,10},{10,1... | collective-permute-start | bytes 786440 | tf_op jit(solution)/shard_map/ppermute | solution.py:985
  189.2 20.6 %collective-permute-start.20 = (f32[3,64,1024]{2,1,0:T(8,128)}, f32[3,64,1024]{2,1,0:T(8,128)S(1)}, u32[]{:S(2)}, u32[]{:S(2)}) collective-permute-start(f32[3,64,1024]{2,1,0:T(8,128)} %gate.16.refs_6_.refs_1_), channel_id=1, source_target_pairs={{0,16},{4,12},{8,24},{12,4},{16,0},{20,28},{24,8},{28,20},{1,17},{... | collective-permute-start | bytes 2359304 | tf_op jit(solution)/shard_map/ppermute | solution.py:981
  190.7 21.3 %collective-permute-start.19 = (f32[3,64,1024]{2,1,0:T(8,128)}, f32[3,64,1024]{2,1,0:T(8,128)S(1)}, u32[]{:S(2)}, u32[]{:S(2)}) collective-permute-start(f32[3,64,1024]{2,1,0:T(8,128)} %gate.16.refs_6_.refs_1_), channel_id=1, source_target_pairs={{0,8},{4,20},{8,0},{12,28},{16,24},{20,4},{24,16},{28,12},{1,9},{5... | collective-permute-start | bytes 2359304 | tf_op jit(solution)/shard_map/ppermute | solution.py:977
  210.7 12.3 %collective-permute-start.21 = (f32[3,64,1024]{2,1,0:T(8,128)}, f32[3,64,1024]{2,1,0:T(8,128)S(1)}, u32[]{:S(2)}, u32[]{:S(2)}) collective-permute-start(f32[3,64,1024]{2,1,0:T(8,128)} %gate.17.refs_3_), channel_id=1, source_target_pairs={{0,8},{4,20},{8,0},{12,28},{16,24},{20,4},{24,16},{28,12},{1,9},{5... | collective-permute-start | bytes 2359304 | tf_op jit(solution)/shard_map/ppermute | solution.py:977
  226.6 6.1 %collective-permute-start.22 = (f32[3,256,1024]{2,1,0:T(8,128)}, f32[3,256,1024]{2,1,0:T(8,128)}, u32[]{:S(2)}, u32[]{:S(2)}) collective-permute-start(f32[3,256,1024]{2,1,0:T(8,128)} %join.9.refs_22_), channel_id=1, source_target_pairs={{0,4},{4,0},{8,12},{12,8},{16,20},{20,16},{24,28},{28,24},{1,5},{5... | collective-permute-start | bytes 9437192 | tf_op jit(solution)/shard_map/ppermute | solution.py:968
  227.7 48.3 %collective-permute-start.24 = (f32[2,256,1024]{2,1,0:T(8,128)}, f32[2,256,1024]{2,1,0:T(8,128)S(1)}, u32[]{:S(2)}, u32[]{:S(2)}) collective-permute-start(f32[2,256,1024]{2,1,0:T(8,128)} %gate.18.refs_24_.refs_1_), channel_id=1, source_target_pairs={{0,16},{4,12},{8,24},{12,4},{16,0},{20,28},{24,8},{28,20},{1,17},{... | collective-permute-start | bytes 6291464 | tf_op jit(solution)/shard_map/ppermute | solution.py:981
  229.0 50.0 %collective-permute-start.23 = (f32[2,256,1024]{2,1,0:T(8,128)}, f32[2,256,1024]{2,1,0:T(8,128)}, u32[]{:S(2)}, u32[]{:S(2)}) collective-permute-start(f32[2,256,1024]{2,1,0:T(8,128)} %gate.18.refs_24_.refs_1_), channel_id=1, source_target_pairs={{0,8},{4,20},{8,0},{12,28},{16,24},{20,4},{24,16},{28,12},{1,9},{5... | collective-permute-start | bytes 6291464 | tf_op jit(solution)/shard_map/ppermute | solution.py:977
  232.0 32.7 %collective-permute-start.25 = (f32[1,256,1024]{2,1,0:T(8,128)S(1)}, f32[1,256,1024]{2,1,0:T(8,128)S(1)}, u32[]{:S(2)}, u32[]{:S(2)}) collective-permute-start(f32[1,256,1024]{2,1,0:T(8,128)S(1)} %constant_dynamic-slice_fusion), channel_id=1, source_target_pairs={{0,1},{1,2},{2,3},{3,0},{4,7},{5,4},{6,5},{7,6},{8,9},{9,10},{10,1... | collective-permute-start | bytes 3145736 | tf_op jit(solution)/shard_map/ppermute | solution.py:989
  265.8 45.8 %collective-permute-start.27 = (f32[1,256,1024]{2,1,0:T(8,128)}, f32[1,256,1024]{2,1,0:T(8,128)}, u32[]{:S(2)}, u32[]{:S(2)}) collective-permute-start(f32[1,256,1024]{2,1,0:T(8,128)} %gate.20.refs_8_.refs_1_), channel_id=1, source_target_pairs={{0,8},{4,20},{8,0},{12,28},{16,24},{20,4},{24,16},{28,12},{1,9},{5... | collective-permute-start | bytes 3145736 | tf_op jit(solution)/shard_map/ppermute | solution.py:977
  267.0 44.6 %collective-permute-start.28 = (f32[1,256,1024]{2,1,0:T(8,128)}, f32[1,256,1024]{2,1,0:T(8,128)S(1)}, u32[]{:S(2)}, u32[]{:S(2)}) collective-permute-start(f32[1,256,1024]{2,1,0:T(8,128)} %gate.20.refs_8_.refs_1_), channel_id=1, source_target_pairs={{0,16},{4,12},{8,24},{12,4},{16,0},{20,28},{24,8},{28,20},{1,17},{... | collective-permute-start | bytes 3145736 | tf_op jit(solution)/shard_map/ppermute | solution.py:981
  277.3 43.5 %collective-permute-start.26 = (f32[2,256,1024]{2,1,0:T(8,128)}, f32[2,256,1024]{2,1,0:T(8,128)S(1)}, u32[]{:S(2)}, u32[]{:S(2)}) collective-permute-start(f32[2,256,1024]{2,1,0:T(8,128)} %gate.19.refs_7_.refs_3_), channel_id=1, source_target_pairs={{0,8},{4,20},{8,0},{12,28},{16,24},{20,4},{24,16},{28,12},{1,9},{5... | collective-permute-start | bytes 6291464 | tf_op jit(solution)/shard_map/ppermute | solution.py:977
  279.0 43.1 %copy-start.4 = (f32[2,256,1024]{2,1,0:T(8,128)S(1)}, f32[2,256,1024]{2,1,0:T(8,128)}, u32[]{:S(2)}) copy-start(f32[2,256,1024]{2,1,0:T(8,128)} %gate.19.refs_7_.refs_3_) | copy-start | bytes 6291460
  279.0 43.1 %copy-start.22 = (s32[2]{0:T(128)S(1)}, s32[2]{0:T(128)}, u32[]{:S(2)}) copy-start(s32[2]{0:T(128)} %copy-done.20) | copy-start | bytes 28
  333.5 13.6 %collective-permute-start.29 = (f32[2,1024,1024]{2,1,0:T(8,128)}, f32[2,1024,1024]{2,1,0:T(8,128)}, u32[]{:S(2)}, u32[]{:S(2)}) collective-permute-start(f32[2,1024,1024]{2,1,0:T(8,128)} %join.10.refs_4_), channel_id=1, source_target_pairs={{0,4},{4,0},{8,12},{12,8},{16,20},{20,16},{24,28},{28,24},{1,5},{5... | collective-permute-start | bytes 25165832 | tf_op jit(solution)/shard_map/ppermute | solution.py:968
  333.9 46.3 %collective-permute-start.30 = (f32[1,256,1024]{2,1,0:T(8,128)}, f32[1,256,1024]{2,1,0:T(8,128)S(1)}, u32[]{:S(2)}, u32[]{:S(2)}) collective-permute-start(f32[1,256,1024]{2,1,0:T(8,128)} %gate.21.refs_7_.refs_3_), channel_id=1, source_target_pairs={{0,8},{4,20},{8,0},{12,28},{16,24},{20,4},{24,16},{28,12},{1,9},{5... | collective-permute-start | bytes 3145736 | tf_op jit(solution)/shard_map/ppermute | solution.py:977
  347.1 33.2 %copy-start.9 = (f32[1,256,1024]{2,1,0:T(8,128)S(1)}, f32[1,256,1024]{2,1,0:T(8,128)}, u32[]{:S(2)}) copy-start(f32[1,256,1024]{2,1,0:T(8,128)} %gate.20.refs_8_.refs_1_) | copy-start | bytes 3145732
  379.9 7.5 %collective-permute-start.32 = (f32[4,2,128,1024]{3,2,1,0:T(8,128)}, f32[4,2,128,1024]{3,2,1,0:T(8,128)}, u32[]{:S(2)}, u32[]{:S(2)}) collective-permute-start(f32[4,2,128,1024]{3,2,1,0:T(8,128)} %get-tuple-element.105), channel_id=1, source_target_pairs={{0,4},{4,0},{8,12},{12,8},{16,20},{20,16},{24,28},{28,24},{1,5},{5... | collective-permute-start | bytes 12582920 | tf_op jit(solution)/shard_map/ppermute | solution.py:968
  386.6 9.0 %collective-permute-start.31 = (f32[1,1024,1024]{2,1,0:T(8,128)}, f32[1,1024,1024]{2,1,0:T(8,128)}, u32[]{:S(2)}, u32[]{:S(2)}) collective-permute-start(f32[1,1024,1024]{2,1,0:T(8,128)} %join.11.refs_5_), channel_id=1, source_target_pairs={{0,4},{4,0},{8,12},{12,8},{16,20},{20,16},{24,28},{28,24},{1,5},{5... | collective-permute-start | bytes 12582920 | tf_op jit(solution)/shard_map/ppermute | solution.py:968
  394.4 58.8 %collective-permute-start.33 = (f32[2,2,128,1024]{3,2,1,0:T(8,128)S(1)}, f32[2,2,128,1024]{3,2,1,0:T(8,128)S(1)}, u32[]{:S(2)}, u32[]{:S(2)}) collective-permute-start(f32[2,2,128,1024]{3,2,1,0:T(8,128)S(1)} %get-tuple-element.148), channel_id=1, source_target_pairs={{0,8},{4,20},{8,0},{12,28},{16,24},{20,4},{24,16},{28,12},{1,9},{5... | collective-permute-start | bytes 6291464 | tf_op jit(solution)/shard_map/ppermute | solution.py:1003
  471.7 23.4 %collective-permute-start.35 = (f32[2,128,1024]{2,1,0:T(8,128)}, f32[2,128,1024]{2,1,0:T(8,128)}, u32[]{:S(2)}, u32[]{:S(2)}) collective-permute-start(f32[2,128,1024]{2,1,0:T(8,128)} %slice_bitcast_fusion.1), channel_id=1, source_target_pairs={{0,16},{4,12},{8,24},{12,4},{16,0},{20,28},{24,8},{28,20},{1,17},{... | collective-permute-start | bytes 3145736 | tf_op jit(solution)/shard_map/ppermute | solution.py:981
  473.4 24.2 %collective-permute-start.34 = (f32[4,5,128,256]{3,2,1,0:T(8,128)}, f32[4,5,128,256]{3,2,1,0:T(8,128)S(1)}, u32[]{:S(2)}, u32[]{:S(2)}) collective-permute-start(f32[4,5,128,256]{3,2,1,0:T(8,128)} %get-tuple-element.116), channel_id=1, source_target_pairs={{0,4},{4,0},{8,12},{12,8},{16,20},{20,16},{24,28},{28,24},{1,5},{5... | collective-permute-start | bytes 7864328 | tf_op jit(solution)/shard_map/ppermute | solution.py:968
  495.0 28.2 %collective-permute-start.37 = (f32[4,3,128,256]{3,2,1,0:T(8,128)}, f32[4,3,128,256]{3,2,1,0:T(8,128)}, u32[]{:S(2)}, u32[]{:S(2)}) collective-permute-start(f32[4,3,128,256]{3,2,1,0:T(8,128)} %get-tuple-element.120), channel_id=1, source_target_pairs={{0,4},{4,0},{8,12},{12,8},{16,20},{20,16},{24,28},{28,24},{1,5},{5... | collective-permute-start | bytes 4718600 | tf_op jit(solution)/shard_map/ppermute | solution.py:968
  502.9 24.7 %collective-permute-start.36 = (f32[2,5,128,256]{3,2,1,0:T(8,128)}, f32[2,5,128,256]{3,2,1,0:T(8,128)}, u32[]{:S(2)}, u32[]{:S(2)}) collective-permute-start(f32[2,5,128,256]{3,2,1,0:T(8,128)} %get-tuple-element.150), channel_id=1, source_target_pairs={{0,8},{4,20},{8,0},{12,28},{16,24},{20,4},{24,16},{28,12},{1,9},{5... | collective-permute-start | bytes 3932168 | tf_op jit(solution)/shard_map/ppermute | solution.py:1003
  527.7 41.9 %collective-permute-start.41 = (f32[2,3,128,256]{3,2,1,0:T(8,128)}, f32[2,3,128,256]{3,2,1,0:T(8,128)S(1)}, u32[]{:S(2)}, u32[]{:S(2)}) collective-permute-start(f32[2,3,128,256]{3,2,1,0:T(8,128)} %get-tuple-element.152), channel_id=1, source_target_pairs={{0,8},{4,20},{8,0},{12,28},{16,24},{20,4},{24,16},{28,12},{1,9},{5... | collective-permute-start | bytes 2359304 | tf_op jit(solution)/shard_map/ppermute | solution.py:1003
  531.2 51.4 %collective-permute-start.43 = (f32[5,128,256]{2,1,0:T(8,128)S(1)}, f32[5,128,256]{2,1,0:T(8,128)}, u32[]{:S(2)}, u32[]{:S(2)}) collective-permute-start(f32[5,128,256]{2,1,0:T(8,128)S(1)} %get-tuple-element.154), channel_id=1, source_target_pairs={{0,16},{4,12},{8,24},{12,4},{16,0},{20,28},{24,8},{28,20},{1,17},{... | collective-permute-start | bytes 1966088 | tf_op jit(solution)/shard_map/ppermute | solution.py:981
  569.4 3.0 collective-permute-start.38
  572.5 4.3 collective-permute-start.39
  572.6 9.1 %collective-permute-start.42 = (f32[3,128,256]{2,1,0:T(8,128)S(1)}, f32[3,128,256]{2,1,0:T(8,128)S(1)}, u32[]{:S(2)}, u32[]{:S(2)}) collective-permute-start(f32[3,128,256]{2,1,0:T(8,128)S(1)} %slice_bitcast_fusion.6), channel_id=1, source_target_pairs={{0,16},{4,12},{8,24},{12,4},{16,0},{20,28},{24,8},{28,20},{1,17},{... | collective-permute-start | bytes 1179656 | tf_op jit(solution)/shard_map/ppermute | solution.py:981
  576.8 4.4 collective-permute-start.40
  (48 other events, 310.0 us)

commit v5 on v4

--- a/solution.py
+++ b/solution.py
@@ -30,7 +30,7 @@
 
 def cost(us):
     return pl.CostEstimate(
-        flops=int(us * 1.15e9), transcendentals=0, bytes_accessed=int(us * 3.6e6)
+        flops=int(us * 4.6e8), transcendentals=0, bytes_accessed=int(us * 1.4e6)
     )
 
 
@@ -192,12 +192,12 @@
     )[0]
 
 
-def take(targets, source, flip=1):
-    for k, target in enumerate(targets[::flip]):
+def take(targets, source):
+    for k, target in enumerate(targets):
         target[...] = source[k].astype(BF16)
 
 
-def take_two(first, second, mine, other, core, flip=1):
+def take_two(first, second, mine, other, core):
     @pl.when(core == 0)
     def _():
         take(first, mine)
@@ -205,8 +205,8 @@
 
     @pl.when(core == 1)
     def _():
-        take(second, mine, flip)
-        take(first, other, flip)
+        take(second, mine)
+        take(first, other)
 
 
 def planes(ref):
@@ -312,8 +312,8 @@
     )
 
 
-def front_own(lengths, first, weights, wait):
-    return front_call(front_body, "front_own", 15, (lengths,), first, [weights], 0, [], wait)
+def front_own(lengths, first, weights, wait, carry):
+    return front_call(front_body, "front_own", 15, (lengths,), first, [weights], 0, [], wait, carry)
 
 
 def front(lengths, first, shard, wait, carry):
@@ -356,11 +356,21 @@
     )
 
 
+def unfold_into(target, first, source):
+    width = source.shape[2]
+    rows = width // 4
+    for piece in range(4):
+        for part in range(4):
+            target[pl.ds(first + piece * rows, rows), part * width : (part + 1) * width] = source[
+                0, pl.ds(piece * width + part * rows, rows), :
+            ].astype(BF16)
+
+
 def middle_kernel(me, lengths, live, tokens, gain1, shift1, gain2, shift2, own_out, own_co, *refs):
     mixed, refs = refs[:4], refs[4:]
     queries, refs = refs[:4], refs[4:]
     pairs, refs = refs[:4], refs[4:]
-    mine, other, *refs = refs
+    outs, cos, (out_two, co_two), refs = refs[:2], refs[2:4], refs[4:6], refs[6:]
     w_out, w_co, after_self, after_cross, second, third, cross_query, looked, logs, turned = refs
     step = pl.program_id(0)
 
@@ -369,10 +379,20 @@
         width = own_out.shape[0]
         w_out[:width, :] = own_out[...]
         w_co[:width, :] = own_co[...]
-        parts = [
-            [target.at[pl.ds((j + 1) * width, width)] for j in range(3)] for target in (w_out, w_co)
-        ]
-        take_two(*parts, mine, other, me[1], flip=-1)
+        for place, out_part, co_part in ((1, outs[0], cos[0]), (3, outs[1], cos[1])):
+            unfold_into(w_out, place * width, out_part)
+            unfold_into(w_co, place * width, co_part)
+
+        @pl.when(me[1] == 0)
+        def _():
+            unfold_into(w_out, 2 * width, out_two)
+            unfold_into(w_co, 2 * width, co_two)
+
+        @pl.when(me[1] == 1)
+        def _():
+            unfold_into(w_co, 2 * width, out_two)
+            unfold_into(w_out, 2 * width, co_two)
+
         for j in range(4):
             turned[j] = pairs[j][1].T
 
@@ -414,22 +434,28 @@
 TEXT = 128
 
 
-def middle(me, lengths, live, tokens, norms, own_out, own_co, mixed, crosses, pairs, arrays, wait):
+def middle(me, lengths, live, tokens, norms, own_out, own_co, mixed, crosses, pairs, g_cross, g_two, wait):
     rows, depth = tokens.shape
     width = own_out.shape[0]
     text_rows = live.shape[0]
     inner = 4 * width
     row = whole((1, depth))
+
+    def plane_at(k):
+        dims = (1, depth, width)
+        return pl.BlockSpec(dims, lambda *_: (k, 0, 0), pipeline_mode=pl.Buffered(1))
+
     return launch(
         middle_kernel,
-        [me, lengths, live, tokens, *norms, own_out, own_co, *mixed, *crosses, *pairs, *arrays],
+        [me, lengths, live, tokens, *norms, own_out, own_co, *mixed, *crosses, *pairs]
+        + [*g_cross, *g_cross, *g_two],
         [smem(), smem(), whole((text_rows, 1)), rows_of(BLK, depth)]
         + [row] * 4
         + [once((width, depth))] * 2
         + [rows_of(BLK, width)] * 4
         + [at((1, depth, width), (0, 0, 0))] * 4
         + [whole((2, text_rows, width))] * 4
-        + [once(arrays[0].shape)] * 2,
+        + [plane_at(k) for k in (3, 3, 4, 4, 3, 3)],
         [whole((inner, depth))] * 2
         + [rows_of(BLK, depth)] * 4
         + [rows_of(BLK, inner)] * 2
@@ -968,6 +994,15 @@
     return lax.ppermute(value, "dp", [(i, i ^ 1) for i in range(DP)])
 
 
+def fold(piece):
+    width = piece.shape[1] // 4
+    return jnp.concatenate([piece[:, k * width : (k + 1) * width] for k in range(4)], axis=0)
+
+
+def fold_whole(shard):
+    return jnp.concatenate([fold(piece) for piece in jnp.split(shard, 4)], axis=0)
+
+
 def cut(shard, chip):
     rows = shard.shape[1] // 4
     return lax.dynamic_slice_in_dim(shard, chip * rows, rows, 1).astype(F32)
@@ -1029,7 +1064,7 @@
     live = ((text_mask == 1) | (position == 0)).astype(F32).reshape(-1, 1)
     own_qkv = jnp.transpose(w_qkv, (1, 0, 2))
     own_cross = jnp.concatenate([w_cross_q[None], jnp.transpose(w_cross_kv, (1, 0, 2))], axis=0)
-    outer, feeds = jnp.stack([w_out, w_cross_out]), jnp.stack([w_up, w_down])
+    feeds = jnp.stack([w_up, w_down])
     first = norm_first(tokens, gains[0], shifts[0])
     qkvs, mixeds, logs, weights = ([None] * 4 for _ in range(4))
     weights[0] = own_qkv
@@ -1037,25 +1072,41 @@
     def shards(value):
         return along(value.astype(F32), 1), along(value.astype(F32), 3)
 
-    if planar:
+    wait, carry = [], []
+    if planar:
+        rows = w_out.shape[0] // 4
+        outer = [
+            fold(lax.dynamic_slice_in_dim(value, chip * rows, rows, 0))[None].astype(F32)
+            for value in (w_out, w_cross_out)
+        ]
         qkv_one = around(cut(own_qkv, chip))
         qkv_near, qkv_side = near_of(qkv_one), side_of(qkv_one)
-        own_piece = gate([qkv_one], cut(own_cross, chip))
+        own_piece = gate([qkv_one], jnp.concatenate([cut(own_cross, chip), *outer], axis=0))
         cross_one = around(own_piece)
-        wait = [qkv_one]
-    else:
-        wait = []
-    qkvs[0], mixeds[0], logs[0] = front_own(lengths, first, own_qkv, wait)
-    carry = []
-    if planar:
-        mine = join(me, [qkv_one, qkv_near, qkv_side, near_of(qkv_side)], [logs[0], cross_one])
+        wait = [qkv_one, own_piece]
+    qkvs[0], mixeds[0], logs[0] = front_own(lengths, first, own_qkv, wait, [])
+    if planar:
+        mine = join(me, [qkv_one, qkv_near, qkv_side, near_of(qkv_side)], [logs[0]])
         g_qkv = mine, swap(mine)
         cross_near, cross_side = near_of(cross_one), side_of(cross_one)
-        two = around(jnp.where(core == 0, qkv_one, cross_one))
+        two = jnp.where(
+            core == 0,
+            jnp.concatenate([qkv_one, cross_one[3:4]], axis=0),
+            jnp.concatenate([cross_one[:3], cross_one[4:5]], axis=0),
+        )
+        two = around(two)
         wait = [cross_one]
-        carry = [cut(lax.dynamic_slice_in_dim(outer, core, 1, 0), chip)]
+        carry = [cut(feeds, chip)]
     else:
+        folded = [fold_whole(value)[None] for value in (w_out, w_cross_out)]
         g_qkv = shards(own_qkv)
+        g_cross = shards(jnp.concatenate([own_cross, *folded], axis=0))
+        g_two = [
+            along(jnp.concatenate(parts, axis=0).astype(F32), 2)
+            for parts in ((own_qkv, folded[0]), (own_cross, folded[1]))
+        ]
+        g_feed = shards(feeds)
+        g_last = along(feeds[:1].astype(F32), 2), along(feeds[1:].astype(F32), 2)
     weights[1], qkvs[1], mixeds[1], logs[1], *carried = front(
         lengths, first, g_qkv[0], wait, carry
     )
@@ -1063,75 +1114,50 @@
         cross_side, two = gate([logs[1]], cross_side), gate([logs[1]], two)
         cross_far = near_of(cross_side)
         two_near, two_side = near_of(two), side_of(two)
-        outer_one, outer_three = along(carried[0], 1), along(carried[0], 3)
+        feed_one = around(carried[0])
         wait = [two, cross_near, cross_side, logs[1]]
-        carry = [cut(feeds, chip)]
-    weights[3], qkvs[3], mixeds[3], logs[3], *carried = front(
-        lengths, first, g_qkv[1], wait, carry
-    )
-    if planar:
-        mine = join(me, [cross_one, cross_near, cross_side, cross_far], [logs[3], outer_one, outer_three])
+    weights[3], qkvs[3], mixeds[3], logs[3] = front(lengths, first, g_qkv[1], wait, [])
+    if planar:
+        mine = join(me, [cross_one, cross_near, cross_side, cross_far], [logs[3], feed_one, two_near, two_side])
         g_cross = mine, swap(mine)
-        mine = join(me, [two, two_near, two_side, near_of(two_side)], [mine])
+        two_far = near_of(two_side)
+        feed_near, feed_side = near_of(feed_one), side_of(feed_one)
+        feed_two = around(lax.dynamic_slice_in_dim(feed_one, core, 1, 0))
+        wait = [two_near, two_side]
+    cross_a, cross_b, *pairs = text_front(text, own_cross, g_cross, wait)
+    if planar:
+        mine = join(me, [two, two_near, two_side, two_far], [cross_a])
         g_two = mine, swap(mine)
-        outer_two = along(outer_one, 1)
-        feed_one = around(carried[0])
-        wait = [two_near, two_side]
-    else:
-        g_cross = shards(own_cross)
-        g_two = along(own_qkv.astype(F32), 2), along(own_cross.astype(F32), 2)
-    cross_a, cross_b, *pairs = text_front(text, own_cross, g_cross, wait)
-    if planar:
-        outers = jnp.concatenate([outer_one, outer_two, outer_three], axis=0)
-        outers = gate([cross_a], outers)
-        outer_near, outer_side = near_of(outers), side_of(outers)
-        wait = [outers, feed_one]
+        wait = []
     weights[2], cross_two, qkvs[2], mixeds[2], logs[2], pair_two = front_two(
         me, lengths, first, g_two, text, wait
     )
     pairs = [pairs[0], pairs[1], pair_two, pairs[2]]
     crosses = [own_cross, cross_a, cross_two, cross_b]
     if planar:
-        outer_side, feed_one = gate([logs[2]], outer_side), gate([logs[2]], feed_one)
-        mine = join(me, [outers, outer_near, outer_side, near_of(outer_side)], [logs[2]])
-        g_outer = mine, swap(mine)
-        feed_near, feed_side = near_of(feed_one), side_of(feed_one)
-        feed_two = around(lax.dynamic_slice_in_dim(feed_one, core, 1, 0))
-        wait = [feed_one]
-    else:
-        g_outer = [
-            jnp.stack([along(value.astype(F32), step) for step in (1, 2, 3)])
-            for value in (w_out, w_cross_out)
-        ]
-    full_out, full_co, after_self, after_cross, second, third, cross_query, looked, cross_logs = middle(
-        me, lengths, live, tokens, (gains[1], shifts[1], gains[2], shifts[2]), w_out, w_cross_out,
-        mixeds, crosses, pairs, g_outer, wait,
-    )
-    if planar:
-        feed_side, feed_two = gate([third], feed_side), gate([third], feed_two)
+        feed_side, feed_two = gate([logs[2]], feed_side), gate([logs[2]], feed_two)
         feed_far = near_of(feed_side)
         last_near, last_side = near_of(feed_two), side_of(feed_two)
         wait = [feed_near, feed_side, feed_two]
+    full_out, full_co, after_self, after_cross, second, third, cross_query, looked, cross_logs = middle(
+        me, lengths, live, tokens, (gains[1], shifts[1], gains[2], shifts[2]), w_out, w_cross_out,
+        mixeds, crosses, pairs, g_cross, g_two, wait,
+    )
+    if planar:
+        mine = join(me, [feed_one, feed_near, feed_side, feed_far], [third, last_near, last_side])
+        g_feed = mine, swap(mine)
+        last_far = near_of(last_side)
+        wait = [mine]
     out, grad, both_keep, both_send = feed_own(
         me, third, cotangent, after_cross, w_up, w_down, wait
     )
     if planar:
-        mine = join(me, [feed_one, feed_near, feed_side, feed_far], [out, last_near, last_side])
-        g_feed = mine, swap(mine)
-        last_side = gate([out], last_side)
-        last_far = near_of(last_side)
-        wait = [last_near, last_side]
-    else:
-        g_feed = shards(feeds)
+        mine = join(me, [feed_two, last_near, last_side, last_far], [out])
+        g_last = mine, swap(mine)
+        wait = [mine]
     out, grad, both_send = feed_pair(
         third, cotangent, out, grad, g_feed, wait, [both_send]
     )
-    if planar:
-        mine = join(me, [feed_two, last_near, last_side, last_far], [out])
-        g_last = mine, swap(mine)
-    else:
-        g_last = along(feeds[:1].astype(F32), 2), along(feeds[1:].astype(F32), 2)
-        wait = []
     out, grad = feed_last(me, third, cotangent, out, grad, g_last, [])
     if planar:
         both_part, both_near = sum_near(both_keep, swap(both_send))

time: 592 us -> 561 us (0.948)
  Pallas kernels: 333 us -> 305 us
  starting transfers between devices: 49.9 us -> 58.9 us
  waiting for transfers between devices: 129 us -> 122 us
    ppermute x3 -> x0, waiting for transfers between devices: 50.6 us -> none  [along(): return lax.ppermute(value, 'mp', straight(step))]
    ppermute x9 -> x8, waiting for transfers between devices: 16.6 us -> 60.4 us  [side_of(): return lax.ppermute(piece, 'dp', beside(False))]
    pallas_call x34 -> x29, Pallas kernels: 333 us -> 305 us  [launch(): pl.pallas_call(body, in_specs=list(in_specs) + [anywhere()] * extra, out_...]
    ppermute x3, starting transfers between devices: 0.14 us -> 12.5 us  [plane_sum(): value = value + lax.ppermute(value, 'dp', [(i, i ^ bit) for i in range(DP)])]
    ppermute x3 -> x0, starting transfers between devices: 7.47 us -> none  [along(): return lax.ppermute(value, 'mp', straight(step))]
    unnamed x108 -> x70, local copies, waits for them, and re-layouts: 32.1 us -> 24.9 us
    ppermute x9 -> x8, waiting for transfers between devices: 12.7 us -> 8.37 us  [swap(): return lax.ppermute(value, 'dp', [(i, i ^ 1) for i in range(DP)])]
    ppermute x12 -> x10, waiting for transfers between devices: 21 us -> 25.1 us  [near_of(): return lax.ppermute(piece, 'dp', beside(True))]
  transfers between devices with their start and end apart: 44 -> 37, of which waited for: 16 -> 13; matrix products, arithmetic and copies ran while one was open for 6% -> 6% of each run, Pallas kernels for 53% -> 50%
where the time goes in v5:
time: 561 us; the launch traced here: 553 us
  Pallas kernels  305 us (54%)
  waiting for transfers between devices  122 us (22%)
  starting transfers between devices  58.9 us (10%)
  local copies, waits for them, and re-layouts  40 us (7%)
  other arithmetic  26 us (5%)
    pallas_call x29, Pallas kernels, launch(): pl.pallas_call(body, in_specs=list(in_specs) + [anywhere()] * extra, out_...  305 us
    ppermute x8, waiting for transfers between devices, side_of(): return lax.ppermute(piece, 'dp', beside(False))  60.4 us
    ppermute x10, waiting for transfers between devices, near_of(): return lax.ppermute(piece, 'dp', beside(True))  25.1 us
    unnamed x70, local copies, waits for them, and re-layouts  24.9 us
    ppermute x5, waiting for transfers between devices, around(): return lax.ppermute(value, ('dp', 'mp'), ring(1))  24.3 us
    ppermute x10, starting transfers between devices, near_of(): return lax.ppermute(piece, 'dp', beside(True))  16.1 us
    ppermute x8, starting transfers between devices, side_of(): return lax.ppermute(piece, 'dp', beside(False))  15.2 us
    ppermute x3, starting transfers between devices, plane_sum(): value = value + lax.ppermute(value, 'dp', [(i, i ^ bit) for i in range(DP)])  12.5 us
  transfers between devices with their start and end apart: 37, of which 13 were waited for; matrix products, arithmetic and copies ran while one was open for 6% of the time, Pallas kernels for 50%

profile of v5, /device:TPU:0, one launch (start us, length us, event | category | flops | bytes accessed | tf_op | source)
XLA Modules:
  0.0 553.0 jit_solution(3772177585782243975)
XLA Ops:
  1.8 3.1 collective-permute-start
  7.6 17.1 %collective-permute-done.refs_0_.refs_3_.refs_1_ = f32[3,256,256]{2,1,0:T(8,128)} collective-permute-done((f32[3,256,256]{2,1,0:T(8,128)S(1)}, f32[3,256,256]{2,1,0:T(8,128)}, u32[]{:S(2)}, u32[]{:S(2)}) %collective-permute-start) | collective-permute-done | bytes 786464 | tf_op jit(solution)/shard_map/ppermute | solution.py:1024
  28.6 5.5 %norm_first.1.refs_1_.refs_2_.refs_7_ = bf16[1280,1024]{1,0:T(8,128)(2,1)} custom-call(bf16[1280,1024]{1,0:T(8,128)(2,1)} %refs_11_.1, f32[1,1024]{1,0:T(1,128)} %get-tuple-element.183.refs_1_.refs_13_, f32[1,1024]{1,0:T(1,128)} %get-tuple-element.180.refs_2_), custom_call_target="tpu_custom_call" | custom-call | flops 2760000000 | bytes 8400000 | tf_op jit(solution)/shard_map/norm_first/pallas_call | solution.py:71
  35.6 3.2 collective-permute-done.2.refs_3_
  38.9 2.4 collective-permute-start.3
  41.4 9.7 %front_own.1 = (bf16[3,1280,256]{2,1,0:T(8,128)(2,1)}, bf16[1280,256]{1,0:T(8,128)(2,1)}, f32[8,1280]{1,0:T(8,128)}) custom-call(s32[5]{0:T(128)} %refs_0_.13, bf16[1280,1024]{1,0:T(8,128)(2,1)} %norm_first.1.refs_1_.refs_2_.refs_7_, bf16[3,1024,256]{2,1,0:T(8,128)(2,1)} %bitcast.93, f32[3,256,256]{2,1,0:T(8,128)} %collective-permute-done.refs_0_.refs_3_.refs_1_, ...), custom_call_target="tpu_custom_call" | custom-call | flops 6899999744 | bytes 21000000 | tf_op jit(solution)/shard_map/front_own/pallas_call | solution.py:71
  51.1 3.7 collective-permute-done.3.refs_4_
  55.6 3.4 join.5.refs_2_
  59.1 2.8 fusion.1.refs_4_
  61.9 7.2 %collective-permute-done.4.refs_3_.refs_1_ = f32[5,256,256]{2,1,0:T(8,128)} collective-permute-done((f32[5,256,256]{2,1,0:T(8,128)}, f32[5,256,256]{2,1,0:T(8,128)}, u32[]{:S(2)}, u32[]{:S(2)}) %collective-permute-start.4) | collective-permute-done | bytes 1310752 | tf_op jit(solution)/shard_map/ppermute | solution.py:1024
  71.3 2.2 maximum_select_fusion
  73.5 2.2 collective-permute-start.5
  77.7 10.6 %front.2 = (bf16[3,1024,256]{2,1,0:T(8,128)(2,1)}, bf16[3,1280,256]{2,1,0:T(8,128)(2,1)}, bf16[1280,256]{1,0:T(8,128)(2,1)}, f32[8,1280]{1,0:T(8,128)}, f32[2,256,1024]{2,1,0:T(8,128)}) custom-call(s32[5]{0:T(128)} %refs_0_.13, bf16[1280,1024]{1,0:T(8,128)(2,1)} %norm_first.1.refs_1_.refs_2_.refs_7_, ...), custom_call_target="tpu_custom_call", output_to_operand_aliasing={{4}: (4, {})} | custom-call | flops 7360000000 | bytes 22400000 | tf_op jit(solution)/shard_map/front/pallas_call | solution.py:71
  90.4 17.0 %collective-permute-done.10.refs_1_ = f32[5,256,256]{2,1,0:T(8,128)} collective-permute-done((f32[5,256,256]{2,1,0:T(8,128)}, f32[5,256,256]{2,1,0:T(8,128)}, u32[]{:S(2)}, u32[]{:S(2)}) %collective-permute-start.10) | collective-permute-done | bytes 1310752 | tf_op jit(solution)/shard_map/ppermute | solution.py:1016
  110.0 10.6 %front.3 = (bf16[3,1024,256]{2,1,0:T(8,128)(2,1)}, bf16[3,1280,256]{2,1,0:T(8,128)(2,1)}, bf16[1280,256]{1,0:T(8,128)(2,1)}, f32[8,1280]{1,0:T(8,128)}) custom-call(s32[5]{0:T(128)} %refs_0_.13, bf16[1280,1024]{1,0:T(8,128)(2,1)} %norm_first.1.refs_1_.refs_2_.refs_7_, f32[3,1024,256]{2,1,0:T(8,128)} %collective-permute-done.12.refs_2_, ...), custom_call_target="tpu_custom_call" | custom-call | flops 7360000000 | bytes 22400000 | tf_op jit(solution)/shard_map/front/pallas_call | solution.py:71
  120.6 14.2 %collective-permute-done.7.refs_8_.refs_5_.refs_3_ = f32[4,256,256]{2,1,0:T(8,128)} collective-permute-done((f32[4,256,256]{2,1,0:T(8,128)}, f32[4,256,256]{2,1,0:T(8,128)}, u32[]{:S(2)}, u32[]{:S(2)}) %collective-permute-start.7) | collective-permute-done | bytes 1048608 | tf_op jit(solution)/shard_map/ppermute | solution.py:1016
  134.8 10.0 %collective-permute-done.6.refs_7_.refs_4_.refs_2_ = f32[4,256,256]{2,1,0:T(8,128)S(1)} collective-permute-done((f32[4,256,256]{2,1,0:T(8,128)}, f32[4,256,256]{2,1,0:T(8,128)S(1)}, u32[]{:S(2)}, u32[]{:S(2)}) %collective-permute-start.6) | collective-permute-done | bytes 1048608 | tf_op jit(solution)/shard_map/ppermute | solution.py:1012
  147.8 3.2 join.6.refs_2_.refs_22_.refs_24_
  154.3 5.5 collective-permute-done.14.refs_3_.refs_23_.refs_25_
  159.8 2.3 copy-done.22
  162.1 9.1 %text_front.1 = (bf16[3,1024,256]{2,1,0:T(8,128)(2,1)}, bf16[3,1024,256]{2,1,0:T(8,128)(2,1)}, bf16[2,640,256]{2,1,0:T(8,128)(2,1)}, bf16[2,640,256]{2,1,0:T(8,128)(2,1)}, bf16[2,640,256]{2,1,0:T(8,128)(2,1)}) custom-call(bf16[640,1024]{1,0:T(8,128)(2,1)} %bitcast.88, bf16[3,1024,256]{2,1,0:T(8,128)(2,1)} %pad_maximum_fusion.refs_1_.refs_14_.refs_6_, ...), custom_call_target="tpu_custom_call" | custom-call | flops 3220000000 | bytes 9800000 | tf_op jit(solution)/shard_map/text_front/pallas_call | solution.py:71
  173.8 4.6 join.7.refs_3_.refs_26_
  183.1 2.8 collective-permute-done.15.refs_4_.refs_27_
  186.0 14.4 %front_two.1 = (bf16[3,1024,256]{2,1,0:T(8,128)(2,1)}, bf16[3,1024,256]{2,1,0:T(8,128)(2,1)}, bf16[3,1280,256]{2,1,0:T(8,128)(2,1)}, bf16[1280,256]{1,0:T(8,128)...) custom-call(s32[2]{0:T(128)} %copy-done.12, s32[5]{0:T(128)} %refs_0_.13, ...), custom_call_target="tpu_custom_call" | custom-call | flops 8280000000 | bytes 25200000 | tf_op jit(solution)/shard_map/front_two/pallas_call | solution.py:71
  200.4 26.0 %collective-permute-done.17.refs_1_ = f32[2,256,1024]{2,1,0:T(8,128)} collective-permute-done((f32[2,256,1024]{2,1,0:T(8,128)S(1)}, f32[2,256,1024]{2,1,0:T(8,128)}, u32[]{:S(2)}, u32[]{:S(2)}) %collective-permute-start.17) | collective-permute-done | bytes 2097184 | tf_op jit(solution)/shard_map/ppermute | solution.py:1016
  231.7 32.1 %middle.1 = (bf16[1024,1024]{1,0:T(8,128)(2,1)}, bf16[1024,1024]{1,0:T(8,128)(2,1)}, f32[1280,1024]{1,0:T(8,128)}, f32[1280,1024]{1,0:T(8,128)}, bf16[1280,1024]...) custom-call(s32[2]{0:T(128)} %copy-done.12, ...), custom_call_target="tpu_custom_call" | custom-call | flops 19779999744 | bytes 60200000 | tf_op jit(solution)/shard_map/middle/pallas_call | solution.py:71
  263.7 11.3 %collective-permute-done.20.refs_6_.refs_2_ = f32[1,256,1024]{2,1,0:T(8,128)S(1)} collective-permute-done((f32[1,256,1024]{2,1,0:T(8,128)}, f32[1,256,1024]{2,1,0:T(8,128)S(1)}, u32[]{:S(2)}, u32[]{:S(2)}) %collective-permute-start.20) | collective-permute-done | bytes 1048608 | tf_op jit(solution)/shard_map/ppermute | solution.py:1012
  275.1 2.1 copy-done.8
  277.2 6.9 %join.8.refs_6_.refs_4_ = f32[2,1024,1024]{2,1,0:T(8,128)} custom-call(s32[2]{0:T(128)S(1)} %copy-done.13, f32[2,256,1024]{2,1,0:T(8,128)S(1)} %collective-permute-done.13.refs_6_.refs_1_, f32[2,256,1024]{2,1,0:T(8,128)} %collective-permute-done.16.refs_28_.refs_2_, f32[2,256,1024]{2,1,0:T(8,128)} %gate.12.refs_29_.refs_3_, ...), custom_call_target="tpu_custom_call" | custom-call | flops 920000000 | bytes 2800000 | tf_op jit(solution)/shard_map/join/pallas_call | solution.py:71
  284.2 2.1 collective-permute-start.23
  286.3 32.9 %feed_own.1 = (f32[1280,1024]{1,0:T(8,128)}, f32[1280,1024]{1,0:T(8,128)}, f32[4,2,128,1024]{3,2,1,0:T(8,128)}, f32[4,2,128,1024]{3,2,1,0:T(8,128)}) custom-call(s32[2]{0:T(128)} %copy-done.12, bf16[1280,1024]{1,0:T(8,128)(2,1)} %get-tuple-element.83.refs_5_.refs_1_.refs_0_, bf16[1280,1024]{1,0:T(8,128)(2,1)} %refs_3_.3, ...), custom_call_target="tpu_custom_call" | custom-call | flops 14720000000 | bytes 44800000 | tf_op jit(solution)/shard_map/feed_own/pallas_call | solution.py:71
  319.2 2.5 copy-done.4
  325.5 32.8 %feed_pair.1 = (f32[1280,1024]{1,0:T(8,128)}, f32[1280,1024]{1,0:T(8,128)}, f32[4,2,128,1024]{3,2,1,0:T(8,128)}) custom-call(bf16[1280,1024]{1,0:T(8,128)(2,1)} %get-tuple-element.83.refs_5_.refs_1_.refs_0_, bf16[1280,1024]{1,0:T(8,128)(2,1)} %refs_3_.3, f32[1280,1024]{1,0:T(8,128)} %get-tuple-element.85.refs_5_.refs_2_, ...), custom_call_target="tpu_custom_call", output_to_operand_aliasing={{2}: (7, {})} | custom-call | flops 13799999488 | bytes 42000000 | tf_op jit(solution)/shard_map/feed_pair/pallas_call | solution.py:71
  358.3 18.4 %feed_last.1 = (bf16[1280,1024]{1,0:T(8,128)(2,1)}, f32[1280,1024]{1,0:T(8,128)}) custom-call(s32[2]{0:T(128)} %copy-done.12, bf16[1280,1024]{1,0:T(8,128)(2,1)} %get-tuple-element.83.refs_5_.refs_1_.refs_0_, bf16[1280,1024]{1,0:T(8,128)(2,1)} %refs_3_.3, f32[1280,1024]{1,0:T(8,128)} %get-tuple-element.88.refs_3_, f32[1280,1024]{1,0:T(8,128)} %get-tuple-element.89.refs_4_, ...), custom_call_target="tpu_custom_call" | custom-call | flops 8280000000 | bytes 25200000 | tf_op jit(solution)/shard_map/feed_last/pallas_call | solution.py:71
  376.7 3.1 add.60
  385.1 39.3 %back.1 = (f32[1280,1024]{1,0:T(8,128)}, bf16[1280,1024]{1,0:T(8,128)(2,1)}, bf16[4,2,640,256]{3,2,1,0:T(8,128)(2,1)}, f32[2,256,1024]{2,1,0:T(8,128)}, bf16[1280,256]{1,0:T(8,128)(2,1)}, /*index=5*/f32[8,1024]{1,0:T(8,128)}) custom-call(s32[5]{0:T(128)} %refs_0_.13, f32[640,1]{1,0:T(8,128)} %bitcast.92, f32[1280,1024]{1,0:T(8,128)} %get-tuple-element.95.refs_2_, ...), custom_call_target="tpu_custom_call" | custom-call | flops 24380000256 | bytes 74200000 | tf_op jit(solution)/shard_map/back/pallas_call | solution.py:71
  424.4 13.3 %text_back.1 = (f32[640,1024]{1,0:T(8,128)}, f32[4,5,128,256]{3,2,1,0:T(8,128)}, f32[4,5,128,256]{3,2,1,0:T(8,128)}) custom-call(s32[2]{0:T(128)} %copy-done.12, bf16[640,1024]{1,0:T(8,128)(2,1)} %bitcast.90, bf16[4,2,640,256]{3,2,1,0:T(8,128)(2,1)} %get-tuple-element.109.refs_2_, bf16[1280,1024]{1,0:T(8,128)(2,1)} %get-tuple-element.110.refs_3_, ...), custom_call_target="tpu_custom_call" | custom-call | flops 6899999744 | bytes 21000000 | tf_op jit(solution)/shard_map/text_back/pallas_call | solution.py:71
  437.8 2.8 slice_add_fusion.2
  441.3 16.5 %self_own.1 = (f32[1280,1024]{1,0:T(8,128)}, f32[4,3,128,256]{3,2,1,0:T(8,128)}, f32[4,3,128,256]{3,2,1,0:T(8,128)}) custom-call(s32[2]{0:T(128)} %copy-done.12, s32[5]{0:T(128)} %refs_0_.13, bf16[3,1280,256]{2,1,0:T(8,128)(2,1)} %get-tuple-element.107.refs_2_, bf16[1280,256]{1,0:T(8,128)(2,1)} %get-tuple-element.67.refs_10_.refs_8_.refs_3_, ...), custom_call_target="tpu_custom_call" | custom-call | flops 10119999488 | bytes 30800000 | tf_op jit(solution)/shard_map/self_own/pallas_call | solution.py:71
  460.3 2.1 add.61
  464.2 5.6 %collective-permute-start.29 = (f32[2,5,128,256]{3,2,1,0:T(8,128)}, f32[2,5,128,256]{3,2,1,0:T(8,128)}, u32[]{:S(2)}, u32[]{:S(2)}) collective-permute-start(f32[2,5,128,256]{3,2,1,0:T(8,128)} %get-tuple-element.148), channel_id=1, source_target_pairs={{0,8},{4,20},{8,0},{12,28},{16,24},{20,4},{24,16},{28,12},{1,9},{5... | collective-permute-start | bytes 3932168 | tf_op jit(solution)/shard_map/ppermute | solution.py:1038
  469.8 14.5 %self_back.1.refs_0_.refs_10_ = f32[1280,1024]{1,0:T(8,128)} custom-call(s32[5]{0:T(128)} %refs_0_.13, bf16[3,1280,256]{2,1,0:T(8,128)(2,1)} %get-tuple-element.105.refs_1_, bf16[1280,256]{1,0:T(8,128)(2,1)} %get-tuple-element.69.refs_11_.refs_2_, bf16[1280,1024]{1,0:T(8,128)(2,1)} %get-tuple-element.104.refs_4_.refs_3_.refs_9_, ...), custom_call_target="tpu_custom_call" | custom-call | flops 11960000512 | bytes 36400000 | tf_op jit(solution)/shard_map/self_back/pallas_call | solution.py:71
  484.3 2.1 add.64
  492.6 8.0 %collective-permute-start.36 = (f32[5,128,256]{2,1,0:T(8,128)}, f32[5,128,256]{2,1,0:T(8,128)}, u32[]{:S(2)}, u32[]{:S(2)}) collective-permute-start(f32[5,128,256]{2,1,0:T(8,128)} %get-tuple-element.152), channel_id=1, source_target_pairs={{0,16},{4,12},{8,24},{12,4},{16,0},{20,28},{24,8},{28,20},{1,17},{... | collective-permute-start | bytes 1966088 | tf_op jit(solution)/shard_map/ppermute | solution.py:1016
  500.7 25.1 %self_rest.1 = (f32[1280,1024]{1,0:T(8,128)}, f32[8,1024]{1,0:T(8,128)}) custom-call(s32[5]{0:T(128)} %refs_0_.13, bf16[3,1280,256]{2,1,0:T(8,128)(2,1)} %get-tuple-element.91.refs_1_, bf16[1280,256]{1,0:T(8,128)(2,1)} %get-tuple-element.74.refs_12_.refs_2_, f32[8,1280]{1,0:T(8,128)} %get-tuple-element.82.refs_0_.refs_3_, ...), custom_call_target="tpu_custom_call" | custom-call | flops 18400000000 | bytes 56000000 | tf_op jit(solution)/shard_map/self_rest/pallas_call | solution.py:71
  529.0 9.8 %collective-permute-start.32 = (f32[6,1024]{1,0:T(8,128)S(1)}, f32[6,1024]{1,0:T(8,128)S(1)}, u32[]{:S(2)}, u32[]{:S(2)}) collective-permute-start(f32[6,1024]{1,0:T(8,128)S(1)} %add.65), channel_id=1, source_target_pairs={{0,8},{4,12},{8,0},{12,4},{16,24},{20,28},{24,16},{28,20},{1,9},{5... | collective-permute-start | bytes 73736 | tf_op jit(solution)/shard_map/ppermute | solution.py:1048
  540.6 2.7 collective-permute-start.33
  544.4 2.9 collective-permute-done.33
  (168 shorter events, 69.9 us)
Async XLA Ops:
  1.8 22.9 %collective-permute-start = (f32[3,256,256]{2,1,0:T(8,128)S(1)}, f32[3,256,256]{2,1,0:T(8,128)}, u32[]{:S(2)}, u32[]{:S(2)}) collective-permute-start(f32[3,256,256]{2,1,0:T(8,128)S(1)} %convert_bitcast_fusion), channel_id=1, source_target_pairs={{0,1},{1,2},{2,3},{3,0},{4,7},{5,4},{6,5},{7,6},{8,9},{9,10},{10,1... | collective-permute-start | bytes 2359304 | tf_op jit(solution)/shard_map/ppermute | solution.py:1024
  7.5 19.9 %copy-start.30 = (f32[3,1024]{1,0:T(4,128)S(1)}, f32[3,1024]{1,0:T(4,128)}, u32[]{:S(2)}) copy-start(f32[3,1024]{1,0:T(4,128)} %param.18) | copy-start | bytes 36868
  7.5 20.5 %copy-start.31 = (f32[3,1024]{1,0:T(4,128)S(1)}, f32[3,1024]{1,0:T(4,128)}, u32[]{:S(2)}) copy-start(f32[3,1024]{1,0:T(4,128)} %param.19) | copy-start | bytes 36868
  24.7 14.2 %collective-permute-start.2 = (f32[3,256,256]{2,1,0:T(8,128)}, f32[3,256,256]{2,1,0:T(8,128)S(1)}, u32[]{:S(2)}, u32[]{:S(2)}) collective-permute-start(f32[3,256,256]{2,1,0:T(8,128)} %collective-permute-done.refs_0_.refs_3_.refs_1_), channel_id=1, source_target_pairs={{0,16},{4,12},{8,24},{12,4},{16,0},{20,28},{24,8},{28,20},{1,17},{... | collective-permute-start | bytes 2359304 | tf_op jit(solution)/shard_map/ppermute | solution.py:1016
  34.2 16.9 %collective-permute-start.1 = (f32[3,256,256]{2,1,0:T(8,128)}, f32[3,256,256]{2,1,0:T(8,128)S(1)}, u32[]{:S(2)}, u32[]{:S(2)}) collective-permute-start(f32[3,256,256]{2,1,0:T(8,128)} %collective-permute-done.refs_0_.refs_3_.refs_1_), channel_id=1, source_target_pairs={{0,8},{4,20},{8,0},{12,28},{16,24},{20,4},{24,16},{28,12},{1,9},{5... | collective-permute-start | bytes 2359304 | tf_op jit(solution)/shard_map/ppermute | solution.py:1012
  38.9 15.9 %collective-permute-start.3 = (f32[3,256,256]{2,1,0:T(8,128)S(1)}, f32[3,256,256]{2,1,0:T(8,128)S(1)}, u32[]{:S(2)}, u32[]{:S(2)}) collective-permute-start(f32[3,256,256]{2,1,0:T(8,128)S(1)} %collective-permute-done.2.refs_3_), channel_id=1, source_target_pairs={{0,8},{4,20},{8,0},{12,28},{16,24},{20,4},{24,16},{28,12},{1,9},{5... | collective-permute-start | bytes 2359304 | tf_op jit(solution)/shard_map/ppermute | solution.py:1012
  41.4 129.8 %copy-start.12 = (s32[2]{0:T(128)}, s32[2]{0:T(128)S(1)}, u32[]{:S(2)}) copy-start(s32[2]{0:T(128)S(1)} %pad_add_fusion.refs_0_) | copy-start | bytes 28
  41.4 27.6 %collective-permute-start.4 = (f32[5,256,256]{2,1,0:T(8,128)}, f32[5,256,256]{2,1,0:T(8,128)}, u32[]{:S(2)}, u32[]{:S(2)}) collective-permute-start(f32[5,256,256]{2,1,0:T(8,128)} %gate.9.refs_4_), channel_id=1, source_target_pairs={{0,1},{1,2},{2,3},{3,0},{4,7},{5,4},{6,5},{7,6},{8,9},{9,10},{10,1... | collective-permute-start | bytes 3932168 | tf_op jit(solution)/shard_map/ppermute | solution.py:1024
  59.0 51.0 %collective-permute-start.12 = (f32[3,1024,256]{2,1,0:T(8,128)}, f32[3,1024,256]{2,1,0:T(8,128)}, u32[]{:S(2)}, u32[]{:S(2)}) collective-permute-start(f32[3,1024,256]{2,1,0:T(8,128)} %join.5.refs_2_), channel_id=1, source_target_pairs={{0,4},{4,0},{8,12},{12,8},{16,20},{20,16},{24,28},{28,24},{1,5},{5... | collective-permute-start | bytes 9437192 | tf_op jit(solution)/shard_map/ppermute | solution.py:994
  73.5 34.9 %collective-permute-start.5 = (f32[4,256,256]{2,1,0:T(8,128)}, f32[4,256,256]{2,1,0:T(8,128)}, u32[]{:S(2)}, u32[]{:S(2)}) collective-permute-start(f32[4,256,256]{2,1,0:T(8,128)} %maximum_select_fusion), channel_id=1, source_target_pairs={{0,1},{1,2},{2,3},{3,0},{4,7},{5,4},{6,5},{7,6},{8,9},{9,10},{10,1... | collective-permute-start | bytes 3145736 | tf_op jit(solution)/shard_map/ppermute | solution.py:1024
  75.7 31.6 %collective-permute-start.10 = (f32[5,256,256]{2,1,0:T(8,128)}, f32[5,256,256]{2,1,0:T(8,128)}, u32[]{:S(2)}, u32[]{:S(2)}) collective-permute-start(f32[5,256,256]{2,1,0:T(8,128)} %collective-permute-done.4.refs_3_.refs_1_), channel_id=1, source_target_pairs={{0,16},{4,12},{8,24},{12,4},{16,0},{20,28},{24,8},{28,20},{1,17},{... | collective-permute-start | bytes 3932168 | tf_op jit(solution)/shard_map/ppermute | solution.py:1016
  76.2 32.5 %collective-permute-start.9 = (f32[5,256,256]{2,1,0:T(8,128)}, f32[5,256,256]{2,1,0:T(8,128)}, u32[]{:S(2)}, u32[]{:S(2)}) collective-permute-start(f32[5,256,256]{2,1,0:T(8,128)} %collective-permute-done.4.refs_3_.refs_1_), channel_id=1, source_target_pairs={{0,8},{4,20},{8,0},{12,28},{16,24},{20,4},{24,16},{28,12},{1,9},{5... | collective-permute-start | bytes 3932168 | tf_op jit(solution)/shard_map/ppermute | solution.py:1012
  88.4 57.5 %collective-permute-start.13 = (f32[2,256,1024]{2,1,0:T(8,128)}, f32[2,256,1024]{2,1,0:T(8,128)S(1)}, u32[]{:S(2)}, u32[]{:S(2)}) collective-permute-start(f32[2,256,1024]{2,1,0:T(8,128)} %get-tuple-element.72), channel_id=1, source_target_pairs={{0,1},{1,2},{2,3},{3,0},{4,7},{5,4},{6,5},{7,6},{8,9},{9,10},{10,1... | collective-permute-start | bytes 6291464 | tf_op jit(solution)/shard_map/ppermute | solution.py:1024
  107.3 38.5 %collective-permute-start.11 = (f32[5,256,256]{2,1,0:T(8,128)}, f32[5,256,256]{2,1,0:T(8,128)}, u32[]{:S(2)}, u32[]{:S(2)}) collective-permute-start(f32[5,256,256]{2,1,0:T(8,128)} %gate.11.refs_5_.refs_3_), channel_id=1, source_target_pairs={{0,8},{4,20},{8,0},{12,28},{16,24},{20,4},{24,16},{28,12},{1,9},{5... | collective-permute-start | bytes 3932168 | tf_op jit(solution)/shard_map/ppermute | solution.py:1012
  108.4 26.4 %collective-permute-start.7 = (f32[4,256,256]{2,1,0:T(8,128)}, f32[4,256,256]{2,1,0:T(8,128)}, u32[]{:S(2)}, u32[]{:S(2)}) collective-permute-start(f32[4,256,256]{2,1,0:T(8,128)} %gate.10.refs_3_.refs_1_), channel_id=1, source_target_pairs={{0,16},{4,12},{8,24},{12,4},{16,0},{20,28},{24,8},{28,20},{1,17},{... | collective-permute-start | bytes 3145736 | tf_op jit(solution)/shard_map/ppermute | solution.py:1016
  108.7 36.1 %collective-permute-start.6 = (f32[4,256,256]{2,1,0:T(8,128)}, f32[4,256,256]{2,1,0:T(8,128)S(1)}, u32[]{:S(2)}, u32[]{:S(2)}) collective-permute-start(f32[4,256,256]{2,1,0:T(8,128)} %gate.10.refs_3_.refs_1_), channel_id=1, source_target_pairs={{0,8},{4,20},{8,0},{12,28},{16,24},{20,4},{24,16},{28,12},{1,9},{5... | collective-permute-start | bytes 3145736 | tf_op jit(solution)/shard_map/ppermute | solution.py:1012
  151.0 11.1 %copy-start = (f32[5,1024,256]{2,1,0:T(8,128)}, f32[5,1024,256]{2,1,0:T(8,128)S(1)}, u32[]{:S(2)}) copy-start(f32[5,1024,256]{2,1,0:T(8,128)S(1)} %join.6.refs_2_.refs_22_.refs_24_) | copy-start | bytes 15728644
  151.0 8.7 %collective-permute-start.14 = (f32[5,1024,256]{2,1,0:T(8,128)S(1)}, f32[5,1024,256]{2,1,0:T(8,128)S(1)}, u32[]{:S(2)}, u32[]{:S(2)}) collective-permute-start(f32[5,1024,256]{2,1,0:T(8,128)S(1)} %join.6.refs_2_.refs_22_.refs_24_), channel_id=1, source_target_pairs={{0,4},{4,0},{8,12},{12,8},{16,20},{20,16},{24,28},{28,24},{1,5},{5... | collective-permute-start | bytes 15728648 | tf_op jit(solution)/shard_map/ppermute | solution.py:994
  151.1 20.1 %collective-permute-start.8 = (f32[4,256,256]{2,1,0:T(8,128)}, f32[4,256,256]{2,1,0:T(8,128)}, u32[]{:S(2)}, u32[]{:S(2)}) collective-permute-start(f32[4,256,256]{2,1,0:T(8,128)} %collective-permute-done.7.refs_8_.refs_5_.refs_3_), channel_id=1, source_target_pairs={{0,8},{4,20},{8,0},{12,28},{16,24},{20,4},{24,16},{28,12},{1,9},{5... | collective-permute-start | bytes 3145736 | tf_op jit(solution)/shard_map/ppermute | solution.py:1012
  178.4 7.6 %collective-permute-start.15 = (f32[4,1024,256]{2,1,0:T(8,128)}, f32[4,1024,256]{2,1,0:T(8,128)}, u32[]{:S(2)}, u32[]{:S(2)}) collective-permute-start(f32[4,1024,256]{2,1,0:T(8,128)} %join.7.refs_3_.refs_26_), channel_id=1, source_target_pairs={{0,4},{4,0},{8,12},{12,8},{16,20},{20,16},{24,28},{28,24},{1,5},{5... | collective-permute-start | bytes 12582920 | tf_op jit(solution)/shard_map/ppermute | solution.py:994
  178.6 47.8 %collective-permute-start.17 = (f32[2,256,1024]{2,1,0:T(8,128)S(1)}, f32[2,256,1024]{2,1,0:T(8,128)}, u32[]{:S(2)}, u32[]{:S(2)}) collective-permute-start(f32[2,256,1024]{2,1,0:T(8,128)S(1)} %collective-permute-done.13.refs_6_.refs_1_), channel_id=1, source_target_pairs={{0,16},{4,12},{8,24},{12,4},{16,0},{20,28},{24,8},{28,20},{1,17},{... | collective-permute-start | bytes 6291464 | tf_op jit(solution)/shard_map/ppermute | solution.py:1016
  180.3 51.4 %collective-permute-start.16 = (f32[2,256,1024]{2,1,0:T(8,128)S(1)}, f32[2,256,1024]{2,1,0:T(8,128)}, u32[]{:S(2)}, u32[]{:S(2)}) collective-permute-start(f32[2,256,1024]{2,1,0:T(8,128)S(1)} %collective-permute-done.13.refs_6_.refs_1_), channel_id=1, source_target_pairs={{0,8},{4,20},{8,0},{12,28},{16,24},{20,4},{24,16},{28,12},{1,9},{5... | collective-permute-start | bytes 6291464 | tf_op jit(solution)/shard_map/ppermute | solution.py:1012
  183.1 46.2 %collective-permute-start.18 = (f32[1,256,1024]{2,1,0:T(8,128)}, f32[1,256,1024]{2,1,0:T(8,128)}, u32[]{:S(2)}, u32[]{:S(2)}) collective-permute-start(f32[1,256,1024]{2,1,0:T(8,128)} %constant_dynamic-slice_fusion), channel_id=1, source_target_pairs={{0,1},{1,2},{2,3},{3,0},{4,7},{5,4},{6,5},{7,6},{8,9},{9,10},{10,1... | collective-permute-start | bytes 3145736 | tf_op jit(solution)/shard_map/ppermute | solution.py:1024
  226.4 48.7 %collective-permute-start.19 = (f32[2,256,1024]{2,1,0:T(8,128)}, f32[2,256,1024]{2,1,0:T(8,128)}, u32[]{:S(2)}, u32[]{:S(2)}) collective-permute-start(f32[2,256,1024]{2,1,0:T(8,128)} %gate.12.refs_29_.refs_3_), channel_id=1, source_target_pairs={{0,8},{4,20},{8,0},{12,28},{16,24},{20,4},{24,16},{28,12},{1,9},{5... | collective-permute-start | bytes 6291464 | tf_op jit(solution)/shard_map/ppermute | solution.py:1012
  229.3 34.4 %collective-permute-start.21 = (f32[1,256,1024]{2,1,0:T(8,128)}, f32[1,256,1024]{2,1,0:T(8,128)S(1)}, u32[]{:S(2)}, u32[]{:S(2)}) collective-permute-start(f32[1,256,1024]{2,1,0:T(8,128)} %gate.13.refs_30_.refs_1_), channel_id=1, source_target_pairs={{0,16},{4,12},{8,24},{12,4},{16,0},{20,28},{24,8},{28,20},{1,17},{... | collective-permute-start | bytes 3145736 | tf_op jit(solution)/shard_map/ppermute | solution.py:1016
  231.0 44.1 %collective-permute-start.20 = (f32[1,256,1024]{2,1,0:T(8,128)}, f32[1,256,1024]{2,1,0:T(8,128)S(1)}, u32[]{:S(2)}, u32[]{:S(2)}) collective-permute-start(f32[1,256,1024]{2,1,0:T(8,128)} %gate.13.refs_30_.refs_1_), channel_id=1, source_target_pairs={{0,8},{4,20},{8,0},{12,28},{16,24},{20,4},{24,16},{28,12},{1,9},{5... | collective-permute-start | bytes 3145736 | tf_op jit(solution)/shard_map/ppermute | solution.py:1012
  231.7 43.4 %copy-start.13 = (s32[2]{0:T(128)S(1)}, s32[2]{0:T(128)}, u32[]{:S(2)}) copy-start(s32[2]{0:T(128)} %copy-done.12) | copy-start | bytes 28
  284.1 39.5 %collective-permute-start.22 = (f32[2,1024,1024]{2,1,0:T(8,128)}, f32[2,1024,1024]{2,1,0:T(8,128)}, u32[]{:S(2)}, u32[]{:S(2)}) collective-permute-start(f32[2,1024,1024]{2,1,0:T(8,128)} %join.8.refs_6_.refs_4_), channel_id=1, source_target_pairs={{0,4},{4,0},{8,12},{12,8},{16,20},{20,16},{24,28},{28,24},{1,5},{5... | collective-permute-start | bytes 25165832 | tf_op jit(solution)/shard_map/ppermute | solution.py:994
  284.2 35.0 %collective-permute-start.23 = (f32[1,256,1024]{2,1,0:T(8,128)S(1)}, f32[1,256,1024]{2,1,0:T(8,128)S(1)}, u32[]{:S(2)}, u32[]{:S(2)}) collective-permute-start(f32[1,256,1024]{2,1,0:T(8,128)S(1)} %collective-permute-done.21.refs_7_.refs_3_), channel_id=1, source_target_pairs={{0,8},{4,20},{8,0},{12,28},{16,24},{20,4},{24,16},{28,12},{1,9},{5... | collective-permute-start | bytes 3145736 | tf_op jit(solution)/shard_map/ppermute | solution.py:1012
  286.3 32.9 %copy-start.7 = (f32[1,256,1024]{2,1,0:T(8,128)S(1)}, f32[1,256,1024]{2,1,0:T(8,128)}, u32[]{:S(2)}) copy-start(f32[1,256,1024]{2,1,0:T(8,128)} %copy-done.6) | copy-start | bytes 3145732
  286.3 32.9 %copy-start.14 = (s32[2]{0:T(128)S(1)}, s32[2]{0:T(128)}, u32[]{:S(2)}) copy-start(s32[2]{0:T(128)} %copy-done.12) | copy-start | bytes 28
  323.5 34.7 %collective-permute-start.24 = (f32[1,1024,1024]{2,1,0:T(8,128)S(1)}, f32[1,1024,1024]{2,1,0:T(8,128)}, u32[]{:S(2)}, u32[]{:S(2)}) collective-permute-start(f32[1,1024,1024]{2,1,0:T(8,128)S(1)} %join.9.refs_6_.refs_5_), channel_id=1, source_target_pairs={{0,4},{4,0},{8,12},{12,8},{16,20},{20,16},{24,28},{28,24},{1,5},{5... | collective-permute-start | bytes 12582920 | tf_op jit(solution)/shard_map/ppermute | solution.py:994
  358.3 18.5 %collective-permute-start.25 = (f32[4,2,128,1024]{3,2,1,0:T(8,128)}, f32[4,2,128,1024]{3,2,1,0:T(8,128)}, u32[]{:S(2)}, u32[]{:S(2)}) collective-permute-start(f32[4,2,128,1024]{3,2,1,0:T(8,128)} %get-tuple-element.103), channel_id=1, source_target_pairs={{0,4},{4,0},{8,12},{12,8},{16,20},{20,16},{24,28},{28,24},{1,5},{5... | collective-permute-start | bytes 12582920 | tf_op jit(solution)/shard_map/ppermute | solution.py:994
  358.3 18.4 %copy-start.23 = (f32[4,2,128,1024]{3,2,1,0:T(8,128)S(1)}, f32[4,2,128,1024]{3,2,1,0:T(8,128)}, u32[]{:S(2)}) copy-start(f32[4,2,128,1024]{3,2,1,0:T(8,128)} %get-tuple-element.102) | copy-start | bytes 12582916
  383.5 40.9 %collective-permute-start.26 = (f32[2,2,128,1024]{3,2,1,0:T(8,128)S(1)}, f32[2,2,128,1024]{3,2,1,0:T(8,128)}, u32[]{:S(2)}, u32[]{:S(2)}) collective-permute-start(f32[2,2,128,1024]{3,2,1,0:T(8,128)S(1)} %get-tuple-element.146), channel_id=1, source_target_pairs={{0,8},{4,20},{8,0},{12,28},{16,24},{20,4},{24,16},{28,12},{1,9},{5... | collective-permute-start | bytes 6291464 | tf_op jit(solution)/shard_map/ppermute | solution.py:1038
  437.7 21.3 %collective-permute-start.27 = (f32[4,5,128,256]{3,2,1,0:T(8,128)}, f32[4,5,128,256]{3,2,1,0:T(8,128)}, u32[]{:S(2)}, u32[]{:S(2)}) collective-permute-start(f32[4,5,128,256]{3,2,1,0:T(8,128)} %get-tuple-element.114), channel_id=1, source_target_pairs={{0,4},{4,0},{8,12},{12,8},{16,20},{20,16},{24,28},{28,24},{1,5},{5... | collective-permute-start | bytes 7864328 | tf_op jit(solution)/shard_map/ppermute | solution.py:994
  440.7 17.2 %collective-permute-start.28 = (f32[2,128,1024]{2,1,0:T(8,128)S(1)}, f32[2,128,1024]{2,1,0:T(8,128)S(1)}, u32[]{:S(2)}, u32[]{:S(2)}) collective-permute-start(f32[2,128,1024]{2,1,0:T(8,128)S(1)} %slice_bitcast_fusion.1), channel_id=1, source_target_pairs={{0,16},{4,12},{8,24},{12,4},{16,0},{20,28},{24,8},{28,20},{1,17},{... | collective-permute-start | bytes 3145736 | tf_op jit(solution)/shard_map/ppermute | solution.py:1016
  441.3 16.5 %copy-start.29 = (f32[8,1024]{1,0:T(8,128)S(1)}, f32[8,1024]{1,0:T(8,128)}, u32[]{:S(2)}) copy-start(f32[8,1024]{1,0:T(8,128)} %get-tuple-element.115.refs_0_) | copy-start | bytes 98308
  457.8 26.4 %collective-permute-start.30 = (f32[4,3,128,256]{3,2,1,0:T(8,128)}, f32[4,3,128,256]{3,2,1,0:T(8,128)}, u32[]{:S(2)}, u32[]{:S(2)}) collective-permute-start(f32[4,3,128,256]{3,2,1,0:T(8,128)} %get-tuple-element.118), channel_id=1, source_target_pairs={{0,4},{4,0},{8,12},{12,8},{16,20},{20,16},{24,28},{28,24},{1,5},{5... | collective-permute-start | bytes 4718600 | tf_op jit(solution)/shard_map/ppermute | solution.py:994
  464.2 24.7 %collective-permute-start.29 = (f32[2,5,128,256]{3,2,1,0:T(8,128)}, f32[2,5,128,256]{3,2,1,0:T(8,128)}, u32[]{:S(2)}, u32[]{:S(2)}) collective-permute-start(f32[2,5,128,256]{3,2,1,0:T(8,128)} %get-tuple-element.148), channel_id=1, source_target_pairs={{0,8},{4,20},{8,0},{12,28},{16,24},{20,4},{24,16},{28,12},{1,9},{5... | collective-permute-start | bytes 3932168 | tf_op jit(solution)/shard_map/ppermute | solution.py:1038
  488.8 38.0 %collective-permute-start.34 = (f32[2,3,128,256]{3,2,1,0:T(8,128)}, f32[2,3,128,256]{3,2,1,0:T(8,128)S(1)}, u32[]{:S(2)}, u32[]{:S(2)}) collective-permute-start(f32[2,3,128,256]{3,2,1,0:T(8,128)} %get-tuple-element.150), channel_id=1, source_target_pairs={{0,8},{4,20},{8,0},{12,28},{16,24},{20,4},{24,16},{28,12},{1,9},{5... | collective-permute-start | bytes 2359304 | tf_op jit(solution)/shard_map/ppermute | solution.py:1038
  492.6 56.1 %collective-permute-start.36 = (f32[5,128,256]{2,1,0:T(8,128)}, f32[5,128,256]{2,1,0:T(8,128)}, u32[]{:S(2)}, u32[]{:S(2)}) collective-permute-start(f32[5,128,256]{2,1,0:T(8,128)} %get-tuple-element.152), channel_id=1, source_target_pairs={{0,16},{4,12},{8,24},{12,4},{16,0},{20,28},{24,8},{28,20},{1,17},{... | collective-permute-start | bytes 1966088 | tf_op jit(solution)/shard_map/ppermute | solution.py:1016
  526.7 16.7 %copy-start.24 = (f32[2,128,1024]{2,1,0:T(8,128)S(1)}, f32[2,128,1024]{2,1,0:T(8,128)}, u32[]{:S(2)}) copy-start(f32[2,128,1024]{2,1,0:T(8,128)} %fusion.2) | copy-start | bytes 3145732
  526.7 2.2 collective-permute-start.31
  529.0 19.7 %copy-start.21 = (f32[2,5,128,256]{3,2,1,0:T(8,128)S(1)}, f32[2,5,128,256]{3,2,1,0:T(8,128)}, u32[]{:S(2)}) copy-start(f32[2,5,128,256]{3,2,1,0:T(8,128)} %copy-done.20) | copy-start | bytes 3932164
  529.0 11.7 %collective-permute-start.32 = (f32[6,1024]{1,0:T(8,128)S(1)}, f32[6,1024]{1,0:T(8,128)S(1)}, u32[]{:S(2)}, u32[]{:S(2)}) collective-permute-start(f32[6,1024]{1,0:T(8,128)S(1)} %add.65), channel_id=1, source_target_pairs={{0,8},{4,12},{8,0},{12,4},{16,24},{20,28},{24,16},{28,20},{1,9},{5... | collective-permute-start | bytes 73736 | tf_op jit(solution)/shard_map/ppermute | solution.py:1048
  538.8 9.1 %collective-permute-start.35 = (f32[3,128,256]{2,1,0:T(8,128)S(1)}, f32[3,128,256]{2,1,0:T(8,128)S(1)}, u32[]{:S(2)}, u32[]{:S(2)}) collective-permute-start(f32[3,128,256]{2,1,0:T(8,128)S(1)} %slice_bitcast_fusion.6), channel_id=1, source_target_pairs={{0,16},{4,12},{8,24},{12,4},{16,0},{20,28},{24,8},{28,20},{1,17},{... | collective-permute-start | bytes 1179656 | tf_op jit(solution)/shard_map/ppermute | solution.py:1016
  540.6 6.7 %collective-permute-start.33 = (f32[6,1024]{1,0:T(8,128)S(1)}, f32[6,1024]{1,0:T(8,128)S(1)}, u32[]{:S(2)}, u32[]{:S(2)}) collective-permute-start(f32[6,1024]{1,0:T(8,128)S(1)} %add.66), channel_id=1, source_target_pairs={{0,16},{4,20},{8,24},{12,28},{16,0},{20,4},{24,8},{28,12},{1,17},{... | collective-permute-start | bytes 73736 | tf_op jit(solution)/shard_map/ppermute | solution.py:1048
  (22 other events, 50.7 us)

commit v6 on v5

--- a/solution.py
+++ b/solution.py
@@ -81,7 +81,7 @@
 
 def gate(wait, carry):
     return launch(
-        lambda: None, [], [], [], [], wait=wait, carry=[carry], name="gate", cost_estimate=cost(1)
+        lambda: None, [], [], [], [], wait=wait, carry=[carry], name="gate", cost_estimate=cost(0.1)
     )[0]
 
 
@@ -207,6 +207,28 @@
     def _():
         take(second, mine)
         take(first, other)
+
+
+def fill(targets, parts, chip, core):
+    for part, offset in zip(parts, offsets(core)):
+        rows = part.shape[1]
+        place = pl.multiple_of((chip ^ offset) * rows, rows)
+        for k, target in enumerate(targets):
+            target[pl.ds(place, rows), :] = part[k].astype(BF16)
+
+
+def fill_two(first, second, mine, other, me):
+    chip, core = me[0], me[1]
+
+    @pl.when(core == 0)
+    def _():
+        fill(first, mine, chip, 0)
+        fill(second, other, chip, 1)
+
+    @pl.when(core == 1)
+    def _():
+        fill(second, mine, chip, 1)
+        fill(first, other, chip, 0)
 
 
 def planes(ref):
@@ -497,26 +519,21 @@
     return hidden, pre_grad, dot(hidden, down), dot(pre_grad, up, NT)
 
 
-def feed_own_kernel(me, third, cot, after, up, down, out, grad, keep, send, both):
-    hidden, pre_grad, result, pushed = feed_rows(third[...], cot[...], up[...], down[...])
+def feed_own_kernel(
+    me, third, cot, after, up, down, out, grad, keep, send, hidden_rows, grad_rows, both
+):
+    step = pl.program_id(0)
+    part = pl.ds(pl.multiple_of(step * FEED, FEED), FEED)
+    hidden, pre_grad, result, pushed = feed_rows(third[part, :], cot[part, :], up[...], down[...])
     out[...] = after[...] + result
     grad[...] = pushed
-    step = pl.program_id(0)
-    more_up = dot(third[...], pre_grad, TN)
-    more_down = dot(hidden, cot[...], TN)
-
-    @pl.when(step == 0)
-    def _():
-        both[0] = more_up
-        both[1] = more_down
-
-    @pl.when(step > 0)
-    def _():
-        both[0] += more_up
-        both[1] += more_down
+    hidden_rows[part, :] = hidden
+    grad_rows[part, :] = pre_grad
 
     @pl.when(step == pl.num_programs(0) - 1)
     def _():
+        both[0] = dot(third[...], grad_rows[...], TN)
+        both[1] = dot(hidden_rows[...], cot[...], TN)
         put_pieces(both, keep, send, me)
 
 
@@ -541,10 +558,11 @@
     return launch(
         feed_own_kernel,
         [me, third, cot, after, up, down],
-        [smem(), tile, tile, tile, once((depth, inner)), once((inner, depth))],
+        [smem(), once(third.shape), once(cot.shape), tile]
+        + [once((depth, inner)), once((inner, depth))],
         [tile, tile, once(pieces), once(pieces)],
         [shape((rows, depth)), shape((rows, depth)), shape(pieces), shape(pieces)],
-        scratch=[pltpu.VMEM((2, depth, inner), F32)],
+        scratch=[pltpu.VMEM((rows, inner), BF16)] * 2 + [pltpu.VMEM((2, depth, inner), F32)],
         wait=wait,
         grid=(rows // FEED,),
         compiler_params=params(),
@@ -553,11 +571,13 @@
     )
 
 
-def feed_pair_kernel(third, cot, out_in, grad_in, mine, other, out, grad, one, two):
+def feed_pair_kernel(me, third, cot, out_in, grad_in, *refs):
+    mine, other, (out, grad, one, two) = refs[:4], refs[4:8], refs[8:]
+
     @pl.when(pl.program_id(0) == 0)
     def _():
-        take(planes(one), mine)
-        take(planes(two), other)
+        fill(planes(one), mine, me[0], me[1])
+        fill(planes(two), other, me[0], 1 - me[1])
 
     _, _, result, pushed = feed_rows(third[...], cot[...], one[0], one[1])
     _, _, more_result, more_pushed = feed_rows(third[...], cot[...], two[0], two[1])
@@ -565,11 +585,13 @@
     grad[...] = grad_in[...] + (pushed + more_pushed)
 
 
-def feed_last_kernel(me, third, cot, out_in, grad_in, mine, other, out, grad, both):
+def feed_last_kernel(me, third, cot, out_in, grad_in, *refs):
+    mine, other, (out, grad, both) = refs[:4], refs[4:8], refs[8:]
+
     @pl.when(pl.program_id(0) == 0)
     def _():
         up, down = planes(both)
-        take_two([up], [down], mine, other, me[1])
+        fill_two([up], [down], mine, other, me)
 
     _, _, result, pushed = feed_rows(third[...], cot[...], both[0], both[1])
     out[...] = (out_in[...] + result).astype(BF16)
@@ -579,13 +601,14 @@
 def feed_call(kernel, name, us, prefix, dtype, copies, third, cot, out, grad, arrays, wait, carry=()):
     rows, depth = third.shape
     tile = rows_of(FEED, depth)
+    inner = arrays[0].shape[2]
     return launch(
         kernel,
         [*prefix, third, cot, out, grad, *arrays],
-        [smem()] * len(prefix) + [tile] * 4 + [once(arrays[0].shape)] * 2,
+        [smem()] * len(prefix) + [tile] * 4 + [once(arrays[0].shape)] * 8,
         [tile, tile],
         [shape((rows, depth), dtype), shape((rows, depth))],
-        scratch=[pltpu.VMEM((2,) + arrays[0].shape[1:], BF16)] * copies,
+        scratch=[pltpu.VMEM((2, inner, depth), BF16)] * copies,
         wait=wait,
         carry=carry,
         grid=(rows // FEED,),
@@ -595,8 +618,8 @@
     )
 
 
-def feed_pair(*operands):
-    return feed_call(feed_pair_kernel, "feed_pair", 30, (), F32, 2, *operands)
+def feed_pair(me, *operands):
+    return feed_call(feed_pair_kernel, "feed_pair", 33, (me,), F32, 2, *operands)
 
 
 def feed_last(me, *operands):
@@ -1033,14 +1056,21 @@
     return lax.psum_scatter(value, "dp", scatter_dimension=axis, tiled=True)
 
 
+def pieces_of(mine, other):
+    mine, other = jnp.split(mine, 4, axis=1), jnp.split(other, 4, axis=1)
+    return mine + [other[k] for k in (0, 2, 1, 3)]
+
+
 def sum_near(keep, sent):
-    part = keep + sent
-    return part[:2], lax.ppermute(part[2:], "dp", beside(True))
-
-
-def sum_side(part, near):
-    part = part + near
-    return part[0], side_of(part[1])
+    return lax.ppermute(keep[2:] + sent[2:], "dp", beside(True))
+
+
+def sum_side(keep, sent, near):
+    return side_of(keep[1] + sent[1] + near[1])
+
+
+def sum_last(keep, sent, near, side):
+    return keep[0] + sent[0] + near[0] + side
 
 
 def plane_sum(value):
@@ -1105,8 +1135,8 @@
             along(jnp.concatenate(parts, axis=0).astype(F32), 2)
             for parts in ((own_qkv, folded[0]), (own_cross, folded[1]))
         ]
-        g_feed = shards(feeds)
-        g_last = along(feeds[:1].astype(F32), 2), along(feeds[1:].astype(F32), 2)
+        g_feed = pieces_of(*shards(feeds))
+        g_last = pieces_of(*[along(feeds[k : k + 1].astype(F32), 2) for k in range(2)])
     weights[1], qkvs[1], mixeds[1], logs[1], *carried = front(
         lengths, first, g_qkv[0], wait, carry
     )
@@ -1135,40 +1165,44 @@
     pairs = [pairs[0], pairs[1], pair_two, pairs[2]]
     crosses = [own_cross, cross_a, cross_two, cross_b]
     if planar:
-        feed_side, feed_two = gate([logs[2]], feed_side), gate([logs[2]], feed_two)
+        wait = [feed_one, feed_two]
+    full_out, full_co, after_self, after_cross, second, third, cross_query, looked, cross_logs = middle(
+        me, lengths, live, tokens, (gains[1], shifts[1], gains[2], shifts[2]), w_out, w_cross_out,
+        mixeds, crosses, pairs, g_cross, g_two, wait,
+    )
+    if planar:
+        feed_side, feed_two = gate([third], feed_side), gate([third], feed_two)
         feed_far = near_of(feed_side)
         last_near, last_side = near_of(feed_two), side_of(feed_two)
         wait = [feed_near, feed_side, feed_two]
-    full_out, full_co, after_self, after_cross, second, third, cross_query, looked, cross_logs = middle(
-        me, lengths, live, tokens, (gains[1], shifts[1], gains[2], shifts[2]), w_out, w_cross_out,
-        mixeds, crosses, pairs, g_cross, g_two, wait,
-    )
-    if planar:
-        mine = join(me, [feed_one, feed_near, feed_side, feed_far], [third, last_near, last_side])
-        g_feed = mine, swap(mine)
-        last_far = near_of(last_side)
-        wait = [mine]
     out, grad, both_keep, both_send = feed_own(
         me, third, cotangent, after_cross, w_up, w_down, wait
     )
     if planar:
-        mine = join(me, [feed_two, last_near, last_side, last_far], [out])
-        g_last = mine, swap(mine)
-        wait = [mine]
+        g_feed = [feed_one, feed_near, feed_side, gate([out], feed_far)]
+        g_feed = g_feed + [swap(value) for value in g_feed]
+        last_far = near_of(last_side)
+        last_swaps = [swap(value) for value in (feed_two, last_near, last_side)]
+        wait = last_swaps
     out, grad, both_send = feed_pair(
-        third, cotangent, out, grad, g_feed, wait, [both_send]
-    )
+        me, third, cotangent, out, grad, g_feed, wait, [both_send]
+    )
+    if planar:
+        last_far = gate([out], last_far)
+        g_last = [feed_two, last_near, last_side, last_far, *last_swaps, swap(last_far)]
     out, grad = feed_last(me, third, cotangent, out, grad, g_last, [])
     if planar:
-        both_part, both_near = sum_near(both_keep, swap(both_send))
+        both_swap = swap(both_send)
+        both_near = sum_near(both_keep, both_swap)
     upstream, mixed_grad, pair_grad, row_grads, query_grad, sums = back(
         lengths, live, grad, cotangent, after_cross, after_self, cross_query, looked, mixeds[0],
         cross_logs, gains[1], gains[2], full_out, full_co, crosses, pairs,
-        [both_part] if planar else [],
+        [both_swap] if planar else [],
     )
     wait = []
     if planar:
-        both_part, both_side = sum_side(both_part, gate([sums], both_near))
+        both_near = gate([sums], both_near)
+        both_side = sum_side(both_keep, both_swap, both_near)
         wait = [both_near]
     text_grad, keep, send = text_back(
         me, text, pair_grad, second, query_grad, row_grads, crosses, wait
@@ -1180,28 +1214,31 @@
         me, lengths, qkvs[0], mixeds[0], mixed_grad, logs[0], weights[0], first, wait
     )
     if planar:
-        late_part, late_near = sum_near(keep, late_swap)
+        late_near = sum_near(keep, late_swap)
         qkv_swap = swap(qkv_send)
-        wait = [late_part, both_side]
+        wait = [late_swap, both_side]
     first_grad = self_back(
         lengths, qkvs[1], mixeds[1], mixed_grad, logs[1], weights[1], first_grad, 1, wait
     )
     if planar:
-        late_one, late_side = sum_side(late_part, gate([first_grad], late_near))
-        qkv_part, qkv_near = sum_near(qkv_keep, gate([first_grad], qkv_swap))
-        wait = [late_one, qkv_part]
+        late_near, qkv_swap = gate([first_grad], late_near), gate([first_grad], qkv_swap)
+        late_side = sum_side(keep, late_swap, late_near)
+        qkv_near = sum_near(qkv_keep, qkv_swap)
+        wait = [late_near, qkv_swap]
     token_grad, last_sums = self_rest(
         (2, 3), lengths, [[qkvs[j], mixeds[j], logs[j], weights[j]] for j in (2, 3)],
         mixed_grad, first_grad, tokens, upstream, gains[0], wait,
     )
     if planar:
-        qkv_one, qkv_side = sum_side(qkv_part, gate([last_sums], qkv_near))
+        qkv_near = gate([last_sums], qkv_near)
+        qkv_side = sum_side(qkv_keep, qkv_swap, qkv_near)
     norm_sums = jnp.concatenate(
         [last_sums[0:1], sums[2:3], sums[0:1], last_sums[1:2], sums[3:4], sums[1:2]], axis=0
     )
     if planar:
-        both_sum, late_sum = both_part + both_side, late_one + late_side
-        qkv_sum = qkv_one + qkv_side
+        both_sum = sum_last(both_keep, both_swap, both_near, both_side)
+        late_sum = sum_last(keep, late_swap, late_near, late_side)
+        qkv_sum = sum_last(qkv_keep, qkv_swap, qkv_near, qkv_side)
         row_sum = [unfold(late_sum[k]) for k in (3, 4)]
         width = norm_sums.shape[1] // DP
         norm_sum = lax.dynamic_slice_in_dim(plane_sum(norm_sums), place * width, width, 1)

time: 561 us -> 548 us (0.977)
  Pallas kernels: 305 us -> 290 us
  local copies, waits for them, and re-layouts: 40 us -> 32 us
  waiting for transfers between devices: 122 us -> 130 us
    ppermute x8, waiting for transfers between devices: 60.4 us -> 21.9 us  [side_of(): return lax.ppermute(piece, 'dp', beside(False))]
    ppermute x10, waiting for transfers between devices: 25.1 us -> 53.6 us  [near_of(): return lax.ppermute(piece, 'dp', beside(True))]
    pallas_call x29, Pallas kernels: 305 us -> 290 us  [launch(): pl.pallas_call(body, in_specs=list(in_specs) + [anywhere()] * extra, out_...]
    ppermute x8, starting transfers between devices: 15.2 us -> 6.52 us  [side_of(): return lax.ppermute(piece, 'dp', beside(False))]
    ppermute x8 -> x14, starting transfers between devices: 0.59 us -> 7.75 us  [swap(): return lax.ppermute(value, 'dp', [(i, i ^ 1) for i in range(DP)])]
    ppermute x8 -> x14, waiting for transfers between devices: 8.37 us -> 15.2 us  [swap(): return lax.ppermute(value, 'dp', [(i, i ^ 1) for i in range(DP)])]
    ppermute x3, waiting for transfers between devices: 3.93 us -> 9.93 us  [plane_sum(): value = value + lax.ppermute(value, 'dp', [(i, i ^ bit) for i in range(DP)])]
    unnamed x70 -> x82, local copies, waits for them, and re-layouts: 24.9 us -> 22.2 us
  transfers between devices with their start and end apart: 37 -> 43, of which waited for: 13 -> 16; matrix products, arithmetic and copies ran while one was open for 6% -> 6% of each run, Pallas kernels for 50% -> 44%
where the time goes in v6:
time: 548 us; the launch traced here: 541 us
  Pallas kernels  290 us (53%)
  waiting for transfers between devices  130 us (24%)
  starting transfers between devices  57.2 us (10%)
  local copies, waits for them, and re-layouts  32 us (6%)
  other arithmetic  30.7 us (6%)
    pallas_call x29, Pallas kernels, launch(): pl.pallas_call(body, in_specs=list(in_specs) + [anywhere()] * extra, out_...  290 us
    ppermute x10, waiting for transfers between devices, near_of(): return lax.ppermute(piece, 'dp', beside(True))  53.6 us
    ppermute x5, waiting for transfers between devices, around(): return lax.ppermute(value, ('dp', 'mp'), ring(1))  29.8 us
    unnamed x82, local copies, waits for them, and re-layouts  22.2 us
    ppermute x8, waiting for transfers between devices, side_of(): return lax.ppermute(piece, 'dp', beside(False))  21.9 us
    ppermute x10, starting transfers between devices, near_of(): return lax.ppermute(piece, 'dp', beside(True))  16.1 us
    ppermute x3, starting transfers between devices, plane_sum(): value = value + lax.ppermute(value, 'dp', [(i, i ^ bit) for i in range(DP)])  15.3 us
    ppermute x14, waiting for transfers between devices, swap(): return lax.ppermute(value, 'dp', [(i, i ^ 1) for i in range(DP)])  15.2 us
  transfers between devices with their start and end apart: 43, of which 16 were waited for; matrix products, arithmetic and copies ran while one was open for 6% of the time, Pallas kernels for 44%

profile of v6, /device:TPU:0, one launch (start us, length us, event | category | flops | bytes accessed | tf_op | source)
XLA Modules:
  0.0 541.3 jit_solution(2626889846095827742)
XLA Ops:
  1.8 3.1 collective-permute-start
  8.2 16.6 %collective-permute-done.refs_0_.refs_3_.refs_1_ = f32[3,256,256]{2,1,0:T(8,128)} collective-permute-done((f32[3,256,256]{2,1,0:T(8,128)S(1)}, f32[3,256,256]{2,1,0:T(8,128)}, u32[]{:S(2)}, u32[]{:S(2)}) %collective-permute-start) | collective-permute-done | bytes 786464 | tf_op jit(solution)/shard_map/ppermute | solution.py:1047
  27.5 5.6 %norm_first.1.refs_1_.refs_2_.refs_7_ = bf16[1280,1024]{1,0:T(8,128)(2,1)} custom-call(bf16[1280,1024]{1,0:T(8,128)(2,1)} %refs_11_.1, f32[1,1024]{1,0:T(1,128)} %get-tuple-element.175.refs_1_.refs_13_, f32[1,1024]{1,0:T(1,128)} %get-tuple-element.172.refs_2_), custom_call_target="tpu_custom_call" | custom-call | flops 2760000000 | bytes 8400000 | tf_op jit(solution)/shard_map/norm_first/pallas_call | solution.py:71
  34.6 5.4 collective-permute-done.2.refs_3_
  40.0 2.4 collective-permute-start.3
  44.3 9.6 %front_own.1 = (bf16[3,1280,256]{2,1,0:T(8,128)(2,1)}, bf16[1280,256]{1,0:T(8,128)(2,1)}, f32[8,1280]{1,0:T(8,128)}) custom-call(s32[5]{0:T(128)} %refs_0_.13, bf16[1280,1024]{1,0:T(8,128)(2,1)} %norm_first.1.refs_1_.refs_2_.refs_7_, bf16[3,1024,256]{2,1,0:T(8,128)(2,1)} %bitcast.93, f32[3,256,256]{2,1,0:T(8,128)} %collective-permute-done.refs_0_.refs_3_.refs_1_, ...), custom_call_target="tpu_custom_call" | custom-call | flops 6899999744 | bytes 21000000 | tf_op jit(solution)/shard_map/front_own/pallas_call | solution.py:71
  54.8 3.4 join.3.refs_2_
  58.3 2.8 fusion.1.refs_4_
  61.1 9.8 %collective-permute-done.4.refs_3_.refs_1_ = f32[5,256,256]{2,1,0:T(8,128)} collective-permute-done((f32[5,256,256]{2,1,0:T(8,128)}, f32[5,256,256]{2,1,0:T(8,128)}, u32[]{:S(2)}, u32[]{:S(2)}) %collective-permute-start.4) | collective-permute-done | bytes 1310752 | tf_op jit(solution)/shard_map/ppermute | solution.py:1047
  73.1 2.2 maximum_select_fusion
  75.4 2.2 collective-permute-start.5
  79.6 10.7 %front.2 = (bf16[3,1024,256]{2,1,0:T(8,128)(2,1)}, bf16[3,1280,256]{2,1,0:T(8,128)(2,1)}, bf16[1280,256]{1,0:T(8,128)(2,1)}, f32[8,1280]{1,0:T(8,128)}, f32[2,256,1024]{2,1,0:T(8,128)}) custom-call(s32[5]{0:T(128)} %refs_0_.13, bf16[1280,1024]{1,0:T(8,128)(2,1)} %norm_first.1.refs_1_.refs_2_.refs_7_, ...), custom_call_target="tpu_custom_call", output_to_operand_aliasing={{4}: (4, {})} | custom-call | flops 7360000000 | bytes 22400000 | tf_op jit(solution)/shard_map/front/pallas_call | solution.py:71
  92.3 16.5 %collective-permute-done.10.refs_1_ = f32[5,256,256]{2,1,0:T(8,128)S(1)} collective-permute-done((f32[5,256,256]{2,1,0:T(8,128)}, f32[5,256,256]{2,1,0:T(8,128)S(1)}, u32[]{:S(2)}, u32[]{:S(2)}) %collective-permute-start.10) | collective-permute-done | bytes 1310752 | tf_op jit(solution)/shard_map/ppermute | solution.py:1039
  113.2 10.6 %front.3 = (bf16[3,1024,256]{2,1,0:T(8,128)(2,1)}, bf16[3,1280,256]{2,1,0:T(8,128)(2,1)}, bf16[1280,256]{1,0:T(8,128)(2,1)}, f32[8,1280]{1,0:T(8,128)}) custom-call(s32[5]{0:T(128)} %refs_0_.13, bf16[1280,1024]{1,0:T(8,128)(2,1)} %norm_first.1.refs_1_.refs_2_.refs_7_, f32[3,1024,256]{2,1,0:T(8,128)} %collective-permute-done.12.refs_2_, ...), custom_call_target="tpu_custom_call" | custom-call | flops 7360000000 | bytes 22400000 | tf_op jit(solution)/shard_map/front/pallas_call | solution.py:71
  123.9 24.1 %collective-permute-done.6.refs_7_.refs_4_.refs_2_ = f32[4,256,256]{2,1,0:T(8,128)S(1)} collective-permute-done((f32[4,256,256]{2,1,0:T(8,128)}, f32[4,256,256]{2,1,0:T(8,128)S(1)}, u32[]{:S(2)}, u32[]{:S(2)}) %collective-permute-start.6) | collective-permute-done | bytes 1048608 | tf_op jit(solution)/shard_map/ppermute | solution.py:1035
  151.2 2.4 join.4.refs_2_.refs_22_.refs_24_
  156.8 5.5 %collective-permute-done.14.refs_3_.refs_23_.refs_25_ = f32[5,1024,256]{2,1,0:T(8,128)S(1)} collective-permute-done((f32[5,1024,256]{2,1,0:T(8,128)S(1)}, f32[5,1024,256]{2,1,0:T(8,128)S(1)}, u32[]{:S(2)}, u32[]{:S(2)}) %collective-permute-start.14) | collective-permute-done | bytes 5242912 | tf_op jit(solution)/shard_map/ppermute | solution.py:1017
  162.3 2.2 copy-done.17
  164.6 9.3 %text_front.1 = (bf16[3,1024,256]{2,1,0:T(8,128)(2,1)}, bf16[3,1024,256]{2,1,0:T(8,128)(2,1)}, bf16[2,640,256]{2,1,0:T(8,128)(2,1)}, bf16[2,640,256]{2,1,0:T(8,128)(2,1)}, bf16[2,640,256]{2,1,0:T(8,128)(2,1)}) custom-call(bf16[640,1024]{1,0:T(8,128)(2,1)} %bitcast.88, bf16[3,1024,256]{2,1,0:T(8,128)(2,1)} %pad_maximum_fusion.refs_1_.refs_14_.refs_6_, ...), custom_call_target="tpu_custom_call" | custom-call | flops 3220000000 | bytes 9800000 | tf_op jit(solution)/shard_map/text_front/pallas_call | solution.py:71
  175.3 4.3 join.5.refs_3_.refs_26_
  184.2 3.0 collective-permute-done.15.refs_4_.refs_27_
  187.2 14.4 %front_two.1 = (bf16[3,1024,256]{2,1,0:T(8,128)(2,1)}, bf16[3,1024,256]{2,1,0:T(8,128)(2,1)}, bf16[3,1280,256]{2,1,0:T(8,128)(2,1)}, bf16[1280,256]{1,0:T(8,128)...) custom-call(s32[2]{0:T(128)} %copy-done.12, s32[5]{0:T(128)} %refs_0_.13, ...), custom_call_target="tpu_custom_call" | custom-call | flops 8280000000 | bytes 25200000 | tf_op jit(solution)/shard_map/front_two/pallas_call | solution.py:71
  201.6 3.4 collective-permute-done.16.refs_29_.refs_1_
  205.0 32.1 %middle.1 = (bf16[1024,1024]{1,0:T(8,128)(2,1)}, bf16[1024,1024]{1,0:T(8,128)(2,1)}, f32[1280,1024]{1,0:T(8,128)}, f32[1280,1024]{1,0:T(8,128)}, bf16[1280,1024]...) custom-call(s32[2]{0:T(128)} %copy-done.12, ...), custom_call_target="tpu_custom_call" | custom-call | flops 19779999744 | bytes 60200000 | tf_op jit(solution)/shard_map/middle/pallas_call | solution.py:71
  238.4 3.0 collective-permute-start.19
  243.7 27.3 %feed_own.1 = (f32[1280,1024]{1,0:T(8,128)}, f32[1280,1024]{1,0:T(8,128)}, f32[4,2,128,1024]{3,2,1,0:T(8,128)}, f32[4,2,128,1024]{3,2,1,0:T(8,128)}) custom-call(s32[2]{0:T(128)} %copy-done.12, bf16[1280,1024]{1,0:T(8,128)(2,1)} %get-tuple-element.82.refs_0_.refs_1_, bf16[1280,1024]{1,0:T(8,128)(2,1)} %refs_3_.3, ...), custom_call_target="tpu_custom_call" | custom-call | flops 14720000000 | bytes 44800000 | tf_op jit(solution)/shard_map/feed_own/pallas_call | solution.py:71
  271.0 6.0 %collective-permute-done.19.refs_1_ = f32[2,256,1024]{2,1,0:T(8,128)} collective-permute-done((f32[2,256,1024]{2,1,0:T(8,128)}, f32[2,256,1024]{2,1,0:T(8,128)}, u32[]{:S(2)}, u32[]{:S(2)}) %collective-permute-start.19) | collective-permute-done | bytes 2097184 | tf_op jit(solution)/shard_map/ppermute | solution.py:1035
  277.6 10.5 %collective-permute-done.25.refs_6_ = f32[1,256,1024]{2,1,0:T(8,128)S(1)} collective-permute-done((f32[1,256,1024]{2,1,0:T(8,128)}, f32[1,256,1024]{2,1,0:T(8,128)S(1)}, u32[]{:S(2)}, u32[]{:S(2)}) %collective-permute-start.25) | collective-permute-done | bytes 1048608 | tf_op jit(solution)/shard_map/ppermute | solution.py:1035
  288.6 2.9 collective-permute-done.26.refs_14_.refs_10_
  294.8 32.9 %feed_pair.1 = (f32[1280,1024]{1,0:T(8,128)}, f32[1280,1024]{1,0:T(8,128)}, f32[4,2,128,1024]{3,2,1,0:T(8,128)}) custom-call(s32[2]{0:T(128)} %copy-done.12, bf16[1280,1024]{1,0:T(8,128)(2,1)} %get-tuple-element.82.refs_0_.refs_1_, bf16[1280,1024]{1,0:T(8,128)(2,1)} %refs_3_.3, ...), custom_call_target="tpu_custom_call", output_to_operand_aliasing={{2}: (16, {})} | custom-call | flops 15180000256 | bytes 46200000 | tf_op jit(solution)/shard_map/feed_pair/pallas_call | solution.py:71
  327.9 2.0 collective-permute-start.29
  329.9 13.0 %collective-permute-done.29.refs_1_ = f32[1,256,1024]{2,1,0:T(8,128)S(1)} collective-permute-done((f32[1,256,1024]{2,1,0:T(8,128)}, f32[1,256,1024]{2,1,0:T(8,128)S(1)}, u32[]{:S(2)}, u32[]{:S(2)}) %collective-permute-start.29) | collective-permute-done | bytes 1048608 | tf_op jit(solution)/shard_map/ppermute | solution.py:1035
  343.9 2.9 collective-permute-done.30.refs_12_
  347.8 18.4 %feed_last.1 = (bf16[1280,1024]{1,0:T(8,128)(2,1)}, f32[1280,1024]{1,0:T(8,128)}) custom-call(s32[2]{0:T(128)} %copy-done.12, bf16[1280,1024]{1,0:T(8,128)(2,1)} %get-tuple-element.82.refs_0_.refs_1_, bf16[1280,1024]{1,0:T(8,128)(2,1)} %refs_3_.3, f32[1280,1024]{1,0:T(8,128)} %get-tuple-element.87.refs_0_.refs_3_, f32[1280,1024]{1,0:T(8,128)} %get-tuple-element.88.refs_4_, ...), custom_call_target="tpu_custom_call" | custom-call | flops 8280000000 | bytes 25200000 | tf_op jit(solution)/shard_map/feed_last/pallas_call | solution.py:71
  366.2 3.5 slice_add_fusion
  371.7 39.3 %back.1 = (f32[1280,1024]{1,0:T(8,128)}, bf16[1280,1024]{1,0:T(8,128)(2,1)}, bf16[4,2,640,256]{3,2,1,0:T(8,128)(2,1)}, f32[2,256,1024]{2,1,0:T(8,128)}, bf16[1280,256]{1,0:T(8,128)(2,1)}, /*index=5*/f32[8,1024]{1,0:T(8,128)}) custom-call(s32[5]{0:T(128)} %refs_0_.13, f32[640,1]{1,0:T(8,128)} %bitcast.92, f32[1280,1024]{1,0:T(8,128)} %get-tuple-element.95.refs_2_, ...), custom_call_target="tpu_custom_call" | custom-call | flops 24380000256 | bytes 74200000 | tf_op jit(solution)/shard_map/back/pallas_call | solution.py:71
  412.3 13.4 %text_back.1 = (f32[640,1024]{1,0:T(8,128)}, f32[4,5,128,256]{3,2,1,0:T(8,128)}, f32[4,5,128,256]{3,2,1,0:T(8,128)}) custom-call(s32[2]{0:T(128)} %copy-done.12, bf16[640,1024]{1,0:T(8,128)(2,1)} %bitcast.90, bf16[4,2,640,256]{3,2,1,0:T(8,128)(2,1)} %get-tuple-element.108.refs_2_, bf16[1280,1024]{1,0:T(8,128)(2,1)} %get-tuple-element.109.refs_3_, ...), custom_call_target="tpu_custom_call" | custom-call | flops 6899999744 | bytes 21000000 | tf_op jit(solution)/shard_map/text_back/pallas_call | solution.py:71
  427.6 16.4 %self_own.1 = (f32[1280,1024]{1,0:T(8,128)}, f32[4,3,128,256]{3,2,1,0:T(8,128)}, f32[4,3,128,256]{3,2,1,0:T(8,128)}) custom-call(s32[2]{0:T(128)} %copy-done.12, s32[5]{0:T(128)} %refs_0_.13, bf16[3,1280,256]{2,1,0:T(8,128)(2,1)} %get-tuple-element.106.refs_2_, bf16[1280,256]{1,0:T(8,128)(2,1)} %get-tuple-element.67.refs_10_.refs_8_.refs_3_, ...), custom_call_target="tpu_custom_call" | custom-call | flops 10119999488 | bytes 30800000 | tf_op jit(solution)/shard_map/self_own/pallas_call | solution.py:71
  444.1 5.6 %collective-permute-start.36 = (f32[4,3,128,256]{3,2,1,0:T(8,128)}, f32[4,3,128,256]{3,2,1,0:T(8,128)}, u32[]{:S(2)}, u32[]{:S(2)}) collective-permute-start(f32[4,3,128,256]{3,2,1,0:T(8,128)} %get-tuple-element.117), channel_id=1, source_target_pairs={{0,4},{4,0},{8,12},{12,8},{16,20},{20,16},{24,28},{28,24},{1,5},{5... | collective-permute-start | bytes 4718600 | tf_op jit(solution)/shard_map/ppermute | solution.py:1017
  449.7 2.4 fusion.3
  452.4 2.6 slice_add_fusion.1
  456.8 14.5 %self_back.1.refs_0_.refs_10_ = f32[1280,1024]{1,0:T(8,128)} custom-call(s32[5]{0:T(128)} %refs_0_.13, bf16[3,1280,256]{2,1,0:T(8,128)(2,1)} %get-tuple-element.104.refs_1_, bf16[1280,256]{1,0:T(8,128)(2,1)} %get-tuple-element.69.refs_11_.refs_2_, bf16[1280,1024]{1,0:T(8,128)(2,1)} %get-tuple-element.103.refs_4_.refs_3_.refs_9_, ...), custom_call_target="tpu_custom_call" | custom-call | flops 11960000512 | bytes 36400000 | tf_op jit(solution)/shard_map/self_back/pallas_call | solution.py:71
  471.2 2.4 slice_add_fusion.6
  475.0 25.0 %self_rest.1 = (f32[1280,1024]{1,0:T(8,128)}, f32[8,1024]{1,0:T(8,128)}) custom-call(s32[5]{0:T(128)} %refs_0_.13, bf16[3,1280,256]{2,1,0:T(8,128)(2,1)} %get-tuple-element.90.refs_1_, bf16[1280,256]{1,0:T(8,128)(2,1)} %get-tuple-element.74.refs_12_.refs_2_, f32[8,1280]{1,0:T(8,128)} %get-tuple-element.91.refs_3_, ...), custom_call_target="tpu_custom_call" | custom-call | flops 18400000000 | bytes 56000000 | tf_op jit(solution)/shard_map/self_rest/pallas_call | solution.py:71
  501.0 15.0 %collective-permute-start.37 = (f32[6,1024]{1,0:T(8,128)S(1)}, f32[6,1024]{1,0:T(8,128)S(1)}, u32[]{:S(2)}, u32[]{:S(2)}) collective-permute-start(f32[6,1024]{1,0:T(8,128)S(1)} %concatenate.74), channel_id=1, source_target_pairs={{0,4},{4,0},{8,12},{12,8},{16,20},{20,16},{24,28},{28,24},{1,5},{5... | collective-permute-start | bytes 73736 | tf_op jit(solution)/shard_map/ppermute | solution.py:1078
  516.0 2.2 fusion.5
  522.7 2.6 collective-permute-done.38
  526.6 7.3 %collective-permute-done.39 = f32[6,1024]{1,0:T(8,128)S(1)} collective-permute-done((f32[6,1024]{1,0:T(8,128)S(1)}, f32[6,1024]{1,0:T(8,128)S(1)}, u32[]{:S(2)}, u32[]{:S(2)}) %collective-permute-start.39) | collective-permute-done | bytes 24608 | tf_op jit(solution)/shard_map/ppermute | solution.py:1078
  (186 shorter events, 67.3 us)
Async XLA Ops:
  1.8 22.9 %collective-permute-start = (f32[3,256,256]{2,1,0:T(8,128)S(1)}, f32[3,256,256]{2,1,0:T(8,128)}, u32[]{:S(2)}, u32[]{:S(2)}) collective-permute-start(f32[3,256,256]{2,1,0:T(8,128)S(1)} %convert_bitcast_fusion), channel_id=1, source_target_pairs={{0,1},{1,2},{2,3},{3,0},{4,7},{5,4},{6,5},{7,6},{8,9},{9,10},{10,1... | collective-permute-start | bytes 2359304 | tf_op jit(solution)/shard_map/ppermute | solution.py:1047
  24.7 15.3 %collective-permute-start.2 = (f32[3,256,256]{2,1,0:T(8,128)}, f32[3,256,256]{2,1,0:T(8,128)S(1)}, u32[]{:S(2)}, u32[]{:S(2)}) collective-permute-start(f32[3,256,256]{2,1,0:T(8,128)} %collective-permute-done.refs_0_.refs_3_.refs_1_), channel_id=1, source_target_pairs={{0,16},{4,12},{8,24},{12,4},{16,0},{20,28},{24,8},{28,20},{1,17},{... | collective-permute-start | bytes 2359304 | tf_op jit(solution)/shard_map/ppermute | solution.py:1039
  26.3 147.5 %copy-start.12 = (s32[2]{0:T(128)}, s32[2]{0:T(128)S(1)}, u32[]{:S(2)}) copy-start(s32[2]{0:T(128)S(1)} %pad_add_fusion.refs_0_) | copy-start | bytes 28
  33.1 20.9 %collective-permute-start.1 = (f32[3,256,256]{2,1,0:T(8,128)}, f32[3,256,256]{2,1,0:T(8,128)S(1)}, u32[]{:S(2)}, u32[]{:S(2)}) collective-permute-start(f32[3,256,256]{2,1,0:T(8,128)} %collective-permute-done.refs_0_.refs_3_.refs_1_), channel_id=1, source_target_pairs={{0,8},{4,20},{8,0},{12,28},{16,24},{20,4},{24,16},{28,12},{1,9},{5... | collective-permute-start | bytes 2359304 | tf_op jit(solution)/shard_map/ppermute | solution.py:1035
  40.0 14.0 %collective-permute-start.3 = (f32[3,256,256]{2,1,0:T(8,128)S(1)}, f32[3,256,256]{2,1,0:T(8,128)S(1)}, u32[]{:S(2)}, u32[]{:S(2)}) collective-permute-start(f32[3,256,256]{2,1,0:T(8,128)S(1)} %collective-permute-done.2.refs_3_), channel_id=1, source_target_pairs={{0,8},{4,20},{8,0},{12,28},{16,24},{20,4},{24,16},{28,12},{1,9},{5... | collective-permute-start | bytes 2359304 | tf_op jit(solution)/shard_map/ppermute | solution.py:1035
  44.3 26.5 %collective-permute-start.4 = (f32[5,256,256]{2,1,0:T(8,128)}, f32[5,256,256]{2,1,0:T(8,128)}, u32[]{:S(2)}, u32[]{:S(2)}) collective-permute-start(f32[5,256,256]{2,1,0:T(8,128)} %gate.11.refs_4_), channel_id=1, source_target_pairs={{0,1},{1,2},{2,3},{3,0},{4,7},{5,4},{6,5},{7,6},{8,9},{9,10},{10,1... | collective-permute-start | bytes 3932168 | tf_op jit(solution)/shard_map/ppermute | solution.py:1047
  58.2 55.0 %collective-permute-start.12 = (f32[3,1024,256]{2,1,0:T(8,128)}, f32[3,1024,256]{2,1,0:T(8,128)}, u32[]{:S(2)}, u32[]{:S(2)}) collective-permute-start(f32[3,1024,256]{2,1,0:T(8,128)} %join.3.refs_2_), channel_id=1, source_target_pairs={{0,4},{4,0},{8,12},{12,8},{16,20},{20,16},{24,28},{28,24},{1,5},{5... | collective-permute-start | bytes 9437192 | tf_op jit(solution)/shard_map/ppermute | solution.py:1017
  75.4 34.7 %collective-permute-start.5 = (f32[4,256,256]{2,1,0:T(8,128)}, f32[4,256,256]{2,1,0:T(8,128)S(1)}, u32[]{:S(2)}, u32[]{:S(2)}) collective-permute-start(f32[4,256,256]{2,1,0:T(8,128)} %maximum_select_fusion), channel_id=1, source_target_pairs={{0,1},{1,2},{2,3},{3,0},{4,7},{5,4},{6,5},{7,6},{8,9},{9,10},{10,1... | collective-permute-start | bytes 3145736 | tf_op jit(solution)/shard_map/ppermute | solution.py:1047
  77.6 31.2 %collective-permute-start.10 = (f32[5,256,256]{2,1,0:T(8,128)}, f32[5,256,256]{2,1,0:T(8,128)S(1)}, u32[]{:S(2)}, u32[]{:S(2)}) collective-permute-start(f32[5,256,256]{2,1,0:T(8,128)} %collective-permute-done.4.refs_3_.refs_1_), channel_id=1, source_target_pairs={{0,16},{4,12},{8,24},{12,4},{16,0},{20,28},{24,8},{28,20},{1,17},{... | collective-permute-start | bytes 3932168 | tf_op jit(solution)/shard_map/ppermute | solution.py:1039
  78.1 34.8 %collective-permute-start.9 = (f32[5,256,256]{2,1,0:T(8,128)}, f32[5,256,256]{2,1,0:T(8,128)}, u32[]{:S(2)}, u32[]{:S(2)}) collective-permute-start(f32[5,256,256]{2,1,0:T(8,128)} %collective-permute-done.4.refs_3_.refs_1_), channel_id=1, source_target_pairs={{0,8},{4,20},{8,0},{12,28},{16,24},{20,4},{24,16},{28,12},{1,9},{5... | collective-permute-start | bytes 3932168 | tf_op jit(solution)/shard_map/ppermute | solution.py:1035
  90.2 57.7 %collective-permute-start.13 = (f32[2,256,1024]{2,1,0:T(8,128)}, f32[2,256,1024]{2,1,0:T(8,128)}, u32[]{:S(2)}, u32[]{:S(2)}) collective-permute-start(f32[2,256,1024]{2,1,0:T(8,128)} %get-tuple-element.72), channel_id=1, source_target_pairs={{0,1},{1,2},{2,3},{3,0},{4,7},{5,4},{6,5},{7,6},{8,9},{9,10},{10,1... | collective-permute-start | bytes 6291464 | tf_op jit(solution)/shard_map/ppermute | solution.py:1047
  109.8 38.1 %collective-permute-start.11 = (f32[5,256,256]{2,1,0:T(8,128)}, f32[5,256,256]{2,1,0:T(8,128)S(1)}, u32[]{:S(2)}, u32[]{:S(2)}) collective-permute-start(f32[5,256,256]{2,1,0:T(8,128)} %gate.13.refs_5_.refs_3_), channel_id=1, source_target_pairs={{0,8},{4,20},{8,0},{12,28},{16,24},{20,4},{24,16},{28,12},{1,9},{5... | collective-permute-start | bytes 3932168 | tf_op jit(solution)/shard_map/ppermute | solution.py:1035
  111.1 38.0 %copy-start.4 = (f32[5,256,256]{2,1,0:T(8,128)S(1)}, f32[5,256,256]{2,1,0:T(8,128)}, u32[]{:S(2)}) copy-start(f32[5,256,256]{2,1,0:T(8,128)} %gate.13.refs_5_.refs_3_) | copy-start | bytes 3932164
  111.1 36.8 %collective-permute-start.6 = (f32[4,256,256]{2,1,0:T(8,128)}, f32[4,256,256]{2,1,0:T(8,128)S(1)}, u32[]{:S(2)}, u32[]{:S(2)}) collective-permute-start(f32[4,256,256]{2,1,0:T(8,128)} %gate.12.refs_3_.refs_1_), channel_id=1, source_target_pairs={{0,8},{4,20},{8,0},{12,28},{16,24},{20,4},{24,16},{28,12},{1,9},{5... | collective-permute-start | bytes 3145736 | tf_op jit(solution)/shard_map/ppermute | solution.py:1035
  112.9 35.0 %collective-permute-start.7 = (f32[4,256,256]{2,1,0:T(8,128)}, f32[4,256,256]{2,1,0:T(8,128)}, u32[]{:S(2)}, u32[]{:S(2)}) collective-permute-start(f32[4,256,256]{2,1,0:T(8,128)} %gate.12.refs_3_.refs_1_), channel_id=1, source_target_pairs={{0,16},{4,12},{8,24},{12,4},{16,0},{20,28},{24,8},{28,20},{1,17},{... | collective-permute-start | bytes 3145736 | tf_op jit(solution)/shard_map/ppermute | solution.py:1039
  153.6 8.7 %collective-permute-start.14 = (f32[5,1024,256]{2,1,0:T(8,128)S(1)}, f32[5,1024,256]{2,1,0:T(8,128)S(1)}, u32[]{:S(2)}, u32[]{:S(2)}) collective-permute-start(f32[5,1024,256]{2,1,0:T(8,128)S(1)} %join.4.refs_2_.refs_22_.refs_24_), channel_id=1, source_target_pairs={{0,4},{4,0},{8,12},{12,8},{16,20},{20,16},{24,28},{28,24},{1,5},{5... | collective-permute-start | bytes 15728648 | tf_op jit(solution)/shard_map/ppermute | solution.py:1017
  153.7 20.2 %collective-permute-start.8 = (f32[4,256,256]{2,1,0:T(8,128)}, f32[4,256,256]{2,1,0:T(8,128)}, u32[]{:S(2)}, u32[]{:S(2)}) collective-permute-start(f32[4,256,256]{2,1,0:T(8,128)} %collective-permute-done.7.refs_8_.refs_5_.refs_3_), channel_id=1, source_target_pairs={{0,8},{4,20},{8,0},{12,28},{16,24},{20,4},{24,16},{28,12},{1,9},{5... | collective-permute-start | bytes 3145736 | tf_op jit(solution)/shard_map/ppermute | solution.py:1035
  179.6 7.6 %collective-permute-start.15 = (f32[4,1024,256]{2,1,0:T(8,128)}, f32[4,1024,256]{2,1,0:T(8,128)}, u32[]{:S(2)}, u32[]{:S(2)}) collective-permute-start(f32[4,1024,256]{2,1,0:T(8,128)} %join.5.refs_3_.refs_26_), channel_id=1, source_target_pairs={{0,4},{4,0},{8,12},{12,8},{16,20},{20,16},{24,28},{28,24},{1,5},{5... | collective-permute-start | bytes 12582920 | tf_op jit(solution)/shard_map/ppermute | solution.py:1017
  181.1 23.9 %collective-permute-start.16 = (f32[1,256,1024]{2,1,0:T(8,128)S(1)}, f32[1,256,1024]{2,1,0:T(8,128)}, u32[]{:S(2)}, u32[]{:S(2)}) collective-permute-start(f32[1,256,1024]{2,1,0:T(8,128)S(1)} %constant_dynamic-slice_fusion), channel_id=1, source_target_pairs={{0,1},{1,2},{2,3},{3,0},{4,7},{5,4},{6,5},{7,6},{8,9},{9,10},{10,1... | collective-permute-start | bytes 3145736 | tf_op jit(solution)/shard_map/ppermute | solution.py:1047
  182.1 54.9 %collective-permute-start.18 = (f32[2,256,1024]{2,1,0:T(8,128)}, f32[2,256,1024]{2,1,0:T(8,128)S(1)}, u32[]{:S(2)}, u32[]{:S(2)}) collective-permute-start(f32[2,256,1024]{2,1,0:T(8,128)} %collective-permute-done.13.refs_6_.refs_28_.refs_5_), channel_id=1, source_target_pairs={{0,16},{4,12},{8,24},{12,4},{16,0},{20,28},{24,8},{28,20},{1,17},{... | collective-permute-start | bytes 6291464 | tf_op jit(solution)/shard_map/ppermute | solution.py:1039
  182.5 59.0 %collective-permute-start.17 = (f32[2,256,1024]{2,1,0:T(8,128)}, f32[2,256,1024]{2,1,0:T(8,128)}, u32[]{:S(2)}, u32[]{:S(2)}) collective-permute-start(f32[2,256,1024]{2,1,0:T(8,128)} %collective-permute-done.13.refs_6_.refs_28_.refs_5_), channel_id=1, source_target_pairs={{0,8},{4,20},{8,0},{12,28},{16,24},{20,4},{24,16},{28,12},{1,9},{5... | collective-permute-start | bytes 6291464 | tf_op jit(solution)/shard_map/ppermute | solution.py:1035
  238.4 38.6 %collective-permute-start.19 = (f32[2,256,1024]{2,1,0:T(8,128)}, f32[2,256,1024]{2,1,0:T(8,128)}, u32[]{:S(2)}, u32[]{:S(2)}) collective-permute-start(f32[2,256,1024]{2,1,0:T(8,128)} %gate.14.refs_7_), channel_id=1, source_target_pairs={{0,8},{4,20},{8,0},{12,28},{16,24},{20,4},{24,16},{28,12},{1,9},{5... | collective-permute-start | bytes 6291464 | tf_op jit(solution)/shard_map/ppermute | solution.py:1035
  241.4 35.6 %collective-permute-start.20 = (f32[2,256,1024]{2,1,0:T(8,128)}, f32[2,256,1024]{2,1,0:T(8,128)}, u32[]{:S(2)}, u32[]{:S(2)}) collective-permute-start(f32[2,256,1024]{2,1,0:T(8,128)} %collective-permute-done.13.refs_6_.refs_28_.refs_5_), channel_id=1, source_target_pairs={{0,4},{4,0},{8,12},{12,8},{16,20},{20,16},{24,28},{28,24},{1,5},{5... | collective-permute-start | bytes 6291464 | tf_op jit(solution)/shard_map/ppermute | solution.py:1017
  241.4 36.1 %collective-permute-start.21 = (f32[2,256,1024]{2,1,0:T(8,128)}, f32[2,256,1024]{2,1,0:T(8,128)}, u32[]{:S(2)}, u32[]{:S(2)}) collective-permute-start(f32[2,256,1024]{2,1,0:T(8,128)} %collective-permute-done.17.refs_6_), channel_id=1, source_target_pairs={{0,4},{4,0},{8,12},{12,8},{16,20},{20,16},{24,28},{28,24},{1,5},{5... | collective-permute-start | bytes 6291464 | tf_op jit(solution)/shard_map/ppermute | solution.py:1017
  241.9 46.2 %collective-permute-start.25 = (f32[1,256,1024]{2,1,0:T(8,128)}, f32[1,256,1024]{2,1,0:T(8,128)S(1)}, u32[]{:S(2)}, u32[]{:S(2)}) collective-permute-start(f32[1,256,1024]{2,1,0:T(8,128)} %gate.15.refs_8_.refs_5_), channel_id=1, source_target_pairs={{0,8},{4,20},{8,0},{12,28},{16,24},{20,4},{24,16},{28,12},{1,9},{5... | collective-permute-start | bytes 3145736 | tf_op jit(solution)/shard_map/ppermute | solution.py:1035
  242.0 46.1 %collective-permute-start.27 = (f32[1,256,1024]{2,1,0:T(8,128)}, f32[1,256,1024]{2,1,0:T(8,128)}, u32[]{:S(2)}, u32[]{:S(2)}) collective-permute-start(f32[1,256,1024]{2,1,0:T(8,128)} %gate.15.refs_8_.refs_5_), channel_id=1, source_target_pairs={{0,16},{4,12},{8,24},{12,4},{16,0},{20,28},{24,8},{28,20},{1,17},{... | collective-permute-start | bytes 3145736 | tf_op jit(solution)/shard_map/ppermute | solution.py:1039
  243.7 33.3 %copy-start.25 = (f32[2,256,1024]{2,1,0:T(8,128)S(1)}, f32[2,256,1024]{2,1,0:T(8,128)}, u32[]{:S(2)}) copy-start(f32[2,256,1024]{2,1,0:T(8,128)} %gate.14.refs_7_) | copy-start | bytes 6291460
  277.0 11.7 %collective-permute-start.22 = (f32[2,256,1024]{2,1,0:T(8,128)S(1)}, f32[2,256,1024]{2,1,0:T(8,128)}, u32[]{:S(2)}, u32[]{:S(2)}) collective-permute-start(f32[2,256,1024]{2,1,0:T(8,128)S(1)} %copy-done.25), channel_id=1, source_target_pairs={{0,4},{4,0},{8,12},{12,8},{16,20},{20,16},{24,28},{28,24},{1,5},{5... | collective-permute-start | bytes 6291464 | tf_op jit(solution)/shard_map/ppermute | solution.py:1017
  277.0 15.5 %collective-permute-start.23 = (f32[2,256,1024]{2,1,0:T(8,128)}, f32[2,256,1024]{2,1,0:T(8,128)S(1)}, u32[]{:S(2)}, u32[]{:S(2)}) collective-permute-start(f32[2,256,1024]{2,1,0:T(8,128)} %gate.16.refs_8_), channel_id=1, source_target_pairs={{0,4},{4,0},{8,12},{12,8},{16,20},{20,16},{24,28},{28,24},{1,5},{5... | collective-permute-start | bytes 6291464 | tf_op jit(solution)/shard_map/ppermute | solution.py:1017
  277.5 11.1 %collective-permute-start.24 = (f32[1,256,1024]{2,1,0:T(8,128)}, f32[1,256,1024]{2,1,0:T(8,128)S(1)}, u32[]{:S(2)}, u32[]{:S(2)}) collective-permute-start(f32[1,256,1024]{2,1,0:T(8,128)} %gate.15.refs_8_.refs_5_), channel_id=1, source_target_pairs={{0,4},{4,0},{8,12},{12,8},{16,20},{20,16},{24,28},{28,24},{1,5},{5... | collective-permute-start | bytes 3145736 | tf_op jit(solution)/shard_map/ppermute | solution.py:1017
  288.1 39.6 %copy-start.34 = (f32[1,256,1024]{2,1,0:T(8,128)}, f32[1,256,1024]{2,1,0:T(8,128)S(1)}, u32[]{:S(2)}) copy-start(f32[1,256,1024]{2,1,0:T(8,128)S(1)} %collective-permute-done.25.refs_6_) | copy-start | bytes 3145732
  288.1 3.4 collective-permute-start.26
  288.1 4.4 collective-permute-start.28
  327.7 38.5 %collective-permute-start.31 = (f32[4,2,128,1024]{3,2,1,0:T(8,128)}, f32[4,2,128,1024]{3,2,1,0:T(8,128)}, u32[]{:S(2)}, u32[]{:S(2)}) collective-permute-start(f32[4,2,128,1024]{3,2,1,0:T(8,128)} %get-tuple-element.102), channel_id=1, source_target_pairs={{0,4},{4,0},{8,12},{12,8},{16,20},{20,16},{24,28},{28,24},{1,5},{5... | collective-permute-start | bytes 12582920 | tf_op jit(solution)/shard_map/ppermute | solution.py:1017
  327.9 15.0 %collective-permute-start.29 = (f32[1,256,1024]{2,1,0:T(8,128)}, f32[1,256,1024]{2,1,0:T(8,128)S(1)}, u32[]{:S(2)}, u32[]{:S(2)}) collective-permute-start(f32[1,256,1024]{2,1,0:T(8,128)} %collective-permute-done.27.refs_7_), channel_id=1, source_target_pairs={{0,8},{4,20},{8,0},{12,28},{16,24},{20,4},{24,16},{28,12},{1,9},{5... | collective-permute-start | bytes 3145736 | tf_op jit(solution)/shard_map/ppermute | solution.py:1035
  343.9 2.9 collective-permute-start.30
  369.7 41.3 %collective-permute-start.32 = (f32[2,2,128,1024]{3,2,1,0:T(8,128)}, f32[2,2,128,1024]{3,2,1,0:T(8,128)S(1)}, u32[]{:S(2)}, u32[]{:S(2)}) collective-permute-start(f32[2,2,128,1024]{3,2,1,0:T(8,128)} %slice_add_fusion), channel_id=1, source_target_pairs={{0,8},{4,20},{8,0},{12,28},{16,24},{20,4},{24,16},{28,12},{1,9},{5... | collective-permute-start | bytes 6291464 | tf_op jit(solution)/shard_map/ppermute | solution.py:1065
  425.7 26.4 %collective-permute-start.33 = (f32[4,5,128,256]{3,2,1,0:T(8,128)}, f32[4,5,128,256]{3,2,1,0:T(8,128)}, u32[]{:S(2)}, u32[]{:S(2)}) collective-permute-start(f32[4,5,128,256]{3,2,1,0:T(8,128)} %get-tuple-element.114), channel_id=1, source_target_pairs={{0,4},{4,0},{8,12},{12,8},{16,20},{20,16},{24,28},{28,24},{1,5},{5... | collective-permute-start | bytes 7864328 | tf_op jit(solution)/shard_map/ppermute | solution.py:1017
  427.5 22.2 %collective-permute-start.34 = (f32[2,128,1024]{2,1,0:T(8,128)S(1)}, f32[2,128,1024]{2,1,0:T(8,128)S(1)}, u32[]{:S(2)}, u32[]{:S(2)}) collective-permute-start(f32[2,128,1024]{2,1,0:T(8,128)S(1)} %fusion.4), channel_id=1, source_target_pairs={{0,16},{4,12},{8,24},{12,4},{16,0},{20,28},{24,8},{28,20},{1,17},{... | collective-permute-start | bytes 3145736 | tf_op jit(solution)/shard_map/ppermute | solution.py:1039
  444.1 27.2 %collective-permute-start.36 = (f32[4,3,128,256]{3,2,1,0:T(8,128)}, f32[4,3,128,256]{3,2,1,0:T(8,128)}, u32[]{:S(2)}, u32[]{:S(2)}) collective-permute-start(f32[4,3,128,256]{3,2,1,0:T(8,128)} %get-tuple-element.117), channel_id=1, source_target_pairs={{0,4},{4,0},{8,12},{12,8},{16,20},{20,16},{24,28},{28,24},{1,5},{5... | collective-permute-start | bytes 4718600 | tf_op jit(solution)/shard_map/ppermute | solution.py:1017
  455.1 18.8 %collective-permute-start.35 = (f32[2,5,128,256]{3,2,1,0:T(8,128)}, f32[2,5,128,256]{3,2,1,0:T(8,128)S(1)}, u32[]{:S(2)}, u32[]{:S(2)}) collective-permute-start(f32[2,5,128,256]{3,2,1,0:T(8,128)} %slice_add_fusion.1), channel_id=1, source_target_pairs={{0,8},{4,20},{8,0},{12,28},{16,24},{20,4},{24,16},{28,12},{1,9},{5... | collective-permute-start | bytes 3932168 | tf_op jit(solution)/shard_map/ppermute | solution.py:1065
  473.6 46.4 %collective-permute-start.40 = (f32[2,3,128,256]{3,2,1,0:T(8,128)}, f32[2,3,128,256]{3,2,1,0:T(8,128)S(1)}, u32[]{:S(2)}, u32[]{:S(2)}) collective-permute-start(f32[2,3,128,256]{3,2,1,0:T(8,128)} %slice_add_fusion.6), channel_id=1, source_target_pairs={{0,8},{4,20},{8,0},{12,28},{16,24},{20,4},{24,16},{28,12},{1,9},{5... | collective-permute-start | bytes 2359304 | tf_op jit(solution)/shard_map/ppermute | solution.py:1065
  475.0 40.9 %copy-start.19 = (f32[2,5,128,256]{3,2,1,0:T(8,128)S(1)}, f32[2,5,128,256]{3,2,1,0:T(8,128)}, u32[]{:S(2)}) copy-start(f32[2,5,128,256]{3,2,1,0:T(8,128)} %gate.19.refs_14_) | copy-start | bytes 3932164
  501.0 19.9 %collective-permute-start.37 = (f32[6,1024]{1,0:T(8,128)S(1)}, f32[6,1024]{1,0:T(8,128)S(1)}, u32[]{:S(2)}, u32[]{:S(2)}) collective-permute-start(f32[6,1024]{1,0:T(8,128)S(1)} %concatenate.74), channel_id=1, source_target_pairs={{0,4},{4,0},{8,12},{12,8},{16,20},{20,16},{24,28},{28,24},{1,5},{5... | collective-permute-start | bytes 73736 | tf_op jit(solution)/shard_map/ppermute | solution.py:1078
  518.2 18.3 %collective-permute-start.42 = (f32[5,128,256]{2,1,0:T(8,128)}, f32[5,128,256]{2,1,0:T(8,128)}, u32[]{:S(2)}, u32[]{:S(2)}) collective-permute-start(f32[5,128,256]{2,1,0:T(8,128)} %fusion.5), channel_id=1, source_target_pairs={{0,16},{4,12},{8,24},{12,4},{16,0},{20,28},{24,8},{28,20},{1,17},{... | collective-permute-start | bytes 1966088 | tf_op jit(solution)/shard_map/ppermute | solution.py:1039
  520.9 4.4 collective-permute-start.38
  522.3 12.2 %collective-permute-start.41 = (f32[3,128,256]{2,1,0:T(8,128)S(1)}, f32[3,128,256]{2,1,0:T(8,128)S(1)}, u32[]{:S(2)}, u32[]{:S(2)}) collective-permute-start(f32[3,128,256]{2,1,0:T(8,128)S(1)} %fusion.9), channel_id=1, source_target_pairs={{0,16},{4,12},{8,24},{12,4},{16,0},{20,28},{24,8},{28,20},{1,17},{... | collective-permute-start | bytes 1179656 | tf_op jit(solution)/shard_map/ppermute | solution.py:1039
  525.3 8.7 %collective-permute-start.39 = (f32[6,1024]{1,0:T(8,128)S(1)}, f32[6,1024]{1,0:T(8,128)S(1)}, u32[]{:S(2)}, u32[]{:S(2)}) collective-permute-start(f32[6,1024]{1,0:T(8,128)S(1)} %add.117), channel_id=1, source_target_pairs={{0,16},{4,20},{8,24},{12,28},{16,0},{20,4},{24,8},{28,12},{1,17},{... | collective-permute-start | bytes 73736 | tf_op jit(solution)/shard_map/ppermute | solution.py:1078
  (34 other events, 192.1 us)

commit v7 on v6

--- a/solution.py
+++ b/solution.py
@@ -571,18 +571,16 @@
     )
 
 
-def feed_pair_kernel(me, third, cot, out_in, grad_in, *refs):
-    mine, other, (out, grad, one, two) = refs[:4], refs[4:8], refs[8:]
+def feed_kernel(own, me, third, cot, out_in, grad_in, *refs):
+    parts, (out, grad, both) = refs[:4], refs[4:]
 
     @pl.when(pl.program_id(0) == 0)
     def _():
-        fill(planes(one), mine, me[0], me[1])
-        fill(planes(two), other, me[0], 1 - me[1])
-
-    _, _, result, pushed = feed_rows(third[...], cot[...], one[0], one[1])
-    _, _, more_result, more_pushed = feed_rows(third[...], cot[...], two[0], two[1])
-    out[...] = out_in[...] + (result + more_result)
-    grad[...] = grad_in[...] + (pushed + more_pushed)
+        fill(planes(both), parts, me[0], me[1] if own else 1 - me[1])
+
+    _, _, result, pushed = feed_rows(third[...], cot[...], both[0], both[1])
+    out[...] = out_in[...] + result
+    grad[...] = grad_in[...] + pushed
 
 
 def feed_last_kernel(me, third, cot, out_in, grad_in, *refs):
@@ -598,17 +596,17 @@
     grad[...] = grad_in[...] + pushed
 
 
-def feed_call(kernel, name, us, prefix, dtype, copies, third, cot, out, grad, arrays, wait, carry=()):
+def feed_call(kernel, name, us, prefix, dtype, third, cot, out, grad, arrays, wait, carry=()):
     rows, depth = third.shape
     tile = rows_of(FEED, depth)
     inner = arrays[0].shape[2]
     return launch(
         kernel,
         [*prefix, third, cot, out, grad, *arrays],
-        [smem()] * len(prefix) + [tile] * 4 + [once(arrays[0].shape)] * 8,
+        [smem()] * len(prefix) + [tile] * 4 + [once(arrays[0].shape)] * len(arrays),
         [tile, tile],
         [shape((rows, depth), dtype), shape((rows, depth))],
-        scratch=[pltpu.VMEM((2, inner, depth), BF16)] * copies,
+        scratch=[pltpu.VMEM((2, inner, depth), BF16)],
         wait=wait,
         carry=carry,
         grid=(rows // FEED,),
@@ -618,12 +616,12 @@
     )
 
 
-def feed_pair(me, *operands):
-    return feed_call(feed_pair_kernel, "feed_pair", 33, (me,), F32, 2, *operands)
+def feed(own, me, *operands):
+    return feed_call(partial(feed_kernel, own), "feed", 18, (me,), F32, *operands)
 
 
 def feed_last(me, *operands):
-    return feed_call(feed_last_kernel, "feed_last", 18, (me,), BF16, 1, *operands)
+    return feed_call(feed_last_kernel, "feed_last", 18, (me,), BF16, *operands)
 
 
 def back_kernel(
@@ -1074,9 +1072,9 @@
 
 
 def plane_sum(value):
-    for bit in (1, 2, 4):
-        value = value + lax.ppermute(value, "dp", [(i, i ^ bit) for i in range(DP)])
-    return value
+    chips = [lax.ppermute(value, "dp", [(i, i ^ bit) for i in range(DP)]) for bit in (2, 4, 6)]
+    value = value + chips[0] + (chips[1] + chips[2])
+    return value + swap(value)
 
 
 def local(
@@ -1178,32 +1176,32 @@
     out, grad, both_keep, both_send = feed_own(
         me, third, cotangent, after_cross, w_up, w_down, wait
     )
+    wait, carry = [], [both_send]
     if planar:
         g_feed = [feed_one, feed_near, feed_side, gate([out], feed_far)]
         g_feed = g_feed + [swap(value) for value in g_feed]
-        last_far = near_of(last_side)
-        last_swaps = [swap(value) for value in (feed_two, last_near, last_side)]
-        wait = last_swaps
-    out, grad, both_send = feed_pair(
-        me, third, cotangent, out, grad, g_feed, wait, [both_send]
-    )
-    if planar:
-        last_far = gate([out], last_far)
-        g_last = [feed_two, last_near, last_side, last_far, *last_swaps, swap(last_far)]
-    out, grad = feed_last(me, third, cotangent, out, grad, g_last, [])
+        wait = g_feed[4:7]
+    out, grad = feed(True, me, third, cotangent, out, grad, g_feed[:4], wait)
+    if planar:
+        last_far = near_of(gate([out], last_side))
+    out, grad = feed(False, me, third, cotangent, out, grad, g_feed[4:], [])
+    if planar:
+        g_last = [feed_two, last_near, last_side, gate([out], last_far)]
+        g_last = g_last + [swap(value) for value in g_last]
+    out, grad, both_send = feed_last(
+        me, third, cotangent, out, grad, g_last, [], [both_send]
+    )
     if planar:
         both_swap = swap(both_send)
-        both_near = sum_near(both_keep, both_swap)
     upstream, mixed_grad, pair_grad, row_grads, query_grad, sums = back(
         lengths, live, grad, cotangent, after_cross, after_self, cross_query, looked, mixeds[0],
         cross_logs, gains[1], gains[2], full_out, full_co, crosses, pairs,
-        [both_swap] if planar else [],
+        [],
     )
     wait = []
     if planar:
-        both_near = gate([sums], both_near)
-        both_side = sum_side(both_keep, both_swap, both_near)
-        wait = [both_near]
+        both_swap = gate([sums], both_swap)
+        both_near = sum_near(both_keep, both_swap)
     text_grad, keep, send = text_back(
         me, text, pair_grad, second, query_grad, row_grads, crosses, wait
     )
@@ -1214,9 +1212,11 @@
         me, lengths, qkvs[0], mixeds[0], mixed_grad, logs[0], weights[0], first, wait
     )
     if planar:
+        both_near = gate([first_grad], both_near)
+        both_side = sum_side(both_keep, both_swap, both_near)
         late_near = sum_near(keep, late_swap)
         qkv_swap = swap(qkv_send)
-        wait = [late_swap, both_side]
+        wait = [late_swap, both_near]
     first_grad = self_back(
         lengths, qkvs[1], mixeds[1], mixed_grad, logs[1], weights[1], first_grad, 1, wait
     )
@@ -1231,6 +1231,9 @@
     )
     if planar:
         qkv_near = gate([last_sums], qkv_near)
+        late_side = gate([last_sums], late_side)
+        both_side = gate([last_sums], both_side)
+        last_sums = gate([late_side, both_side, qkv_near], last_sums)
         qkv_side = sum_side(qkv_keep, qkv_swap, qkv_near)
     norm_sums = jnp.concatenate(
         [last_sums[0:1], sums[2:3], sums[0:1], last_sums[1:2], sums[3:4], sums[1:2]], axis=0

time: 548 us -> 524 us (0.956)
  waiting for transfers between devices: 130 us -> 91.3 us
  Pallas kernels: 290 us -> 323 us
  starting transfers between devices: 57.2 us -> 38.1 us
    pallas_call x29 -> x35, Pallas kernels: 290 us -> 323 us  [launch(): pl.pallas_call(body, in_specs=list(in_specs) + [anywhere()] * extra, out_...]
    ppermute x10, waiting for transfers between devices: 53.6 us -> 29.4 us  [near_of(): return lax.ppermute(piece, 'dp', beside(True))]
    ppermute x3, starting transfers between devices: 15.3 us -> 3.77 us  [plane_sum(): lax.ppermute(value, 'dp', [(i, i ^ bit) for i in range(DP)])]
    ppermute x3, waiting for transfers between devices: 9.93 us -> 1.02 us  [plane_sum(): lax.ppermute(value, 'dp', [(i, i ^ bit) for i in range(DP)])]
    ppermute x14 -> x15, starting transfers between devices: 7.75 us -> 2.27 us  [swap(): return lax.ppermute(value, 'dp', [(i, i ^ 1) for i in range(DP)])]
    ppermute x14 -> x15, waiting for transfers between devices: 15.2 us -> 11.3 us  [swap(): return lax.ppermute(value, 'dp', [(i, i ^ 1) for i in range(DP)])]
    unnamed x82 -> x71, local copies, waits for them, and re-layouts: 22.2 us -> 21.5 us
  transfers between devices with their start and end apart: 43 -> 44, of which waited for: 16 -> 15; matrix products, arithmetic and copies ran while one was open for 6% -> 8% of each run, Pallas kernels for 44% -> 57%
where the time goes in v7:
time: 524 us; the launch traced here: 518 us
  Pallas kernels  323 us (62%)
  waiting for transfers between devices  91.3 us (17%)
  starting transfers between devices  38.1 us (7%)
  other arithmetic  32.8 us (6%)
  local copies, waits for them, and re-layouts  31.4 us (6%)
    pallas_call x35, Pallas kernels, launch(): pl.pallas_call(body, in_specs=list(in_specs) + [anywhere()] * extra, out_...  323 us
    ppermute x10, waiting for transfers between devices, near_of(): return lax.ppermute(piece, 'dp', beside(True))  29.4 us
    ppermute x5, waiting for transfers between devices, around(): return lax.ppermute(value, ('dp', 'mp'), ring(1))  25.1 us
    unnamed x71, local copies, waits for them, and re-layouts  21.5 us
    ppermute x8, waiting for transfers between devices, side_of(): return lax.ppermute(piece, 'dp', beside(False))  19.7 us
    ppermute x10, starting transfers between devices, near_of(): return lax.ppermute(piece, 'dp', beside(True))  16.2 us
    ppermute x15, waiting for transfers between devices, swap(): return lax.ppermute(value, 'dp', [(i, i ^ 1) for i in range(DP)])  11.3 us
  transfers between devices with their start and end apart: 44, of which 15 were waited for; matrix products, arithmetic and copies ran while one was open for 8% of the time, Pallas kernels for 57%

profile of v7, /device:TPU:0, one launch (start us, length us, event | category | flops | bytes accessed | tf_op | source)
XLA Modules:
  0.0 517.6 jit_solution(6195094219308844964)
XLA Ops:
  1.8 3.1 collective-permute-start
  8.2 16.6 %collective-permute-done.refs_0_.refs_3_.refs_1_ = f32[3,256,256]{2,1,0:T(8,128)} collective-permute-done((f32[3,256,256]{2,1,0:T(8,128)S(1)}, f32[3,256,256]{2,1,0:T(8,128)}, u32[]{:S(2)}, u32[]{:S(2)}) %collective-permute-start) | collective-permute-done | bytes 786464 | tf_op jit(solution)/shard_map/ppermute | solution.py:1045
  27.5 5.5 %norm_first.1.refs_1_.refs_2_.refs_7_ = bf16[1280,1024]{1,0:T(8,128)(2,1)} custom-call(bf16[1280,1024]{1,0:T(8,128)(2,1)} %refs_11_.1, f32[1,1024]{1,0:T(1,128)} %get-tuple-element.179.refs_1_.refs_13_, f32[1,1024]{1,0:T(1,128)} %get-tuple-element.176.refs_2_), custom_call_target="tpu_custom_call" | custom-call | flops 2760000000 | bytes 8400000 | tf_op jit(solution)/shard_map/norm_first/pallas_call | solution.py:71
  34.6 5.4 %collective-permute-done.2.refs_3_ = f32[3,256,256]{2,1,0:T(8,128)S(1)} collective-permute-done((f32[3,256,256]{2,1,0:T(8,128)}, f32[3,256,256]{2,1,0:T(8,128)S(1)}, u32[]{:S(2)}, u32[]{:S(2)}) %collective-permute-start.2) | collective-permute-done | bytes 786464 | tf_op jit(solution)/shard_map/ppermute | solution.py:1037
  40.0 2.5 collective-permute-start.3
  42.4 1.9 maximum_convert_fusion.refs_1_
  44.4 11.8 %front_own.1 = (bf16[3,1280,256]{2,1,0:T(8,128)(2,1)}, bf16[1280,256]{1,0:T(8,128)(2,1)}, f32[8,1280]{1,0:T(8,128)}) custom-call(s32[5]{0:T(128)} %refs_0_.13, bf16[1280,1024]{1,0:T(8,128)(2,1)} %norm_first.1.refs_1_.refs_2_.refs_7_, bf16[3,1024,256]{2,1,0:T(8,128)(2,1)} %bitcast.93, f32[3,256,256]{2,1,0:T(8,128)} %collective-permute-done.refs_0_.refs_3_.refs_1_, ...), custom_call_target="tpu_custom_call" | custom-call | flops 6899999744 | bytes 21000000 | tf_op jit(solution)/shard_map/front_own/pallas_call | solution.py:71
  57.0 3.4 join.3.refs_2_
  60.5 2.8 fusion.1.refs_4_
  63.3 7.6 %collective-permute-done.4.refs_3_.refs_1_ = f32[5,256,256]{2,1,0:T(8,128)} collective-permute-done((f32[5,256,256]{2,1,0:T(8,128)}, f32[5,256,256]{2,1,0:T(8,128)}, u32[]{:S(2)}, u32[]{:S(2)}) %collective-permute-start.4) | collective-permute-done | bytes 1310752 | tf_op jit(solution)/shard_map/ppermute | solution.py:1045
  73.1 2.3 maximum_select_fusion
  75.4 1.9 collective-permute-start.5
  79.3 12.9 %front.2 = (bf16[3,1024,256]{2,1,0:T(8,128)(2,1)}, bf16[3,1280,256]{2,1,0:T(8,128)(2,1)}, bf16[1280,256]{1,0:T(8,128)(2,1)}, f32[8,1280]{1,0:T(8,128)}, f32[2,256,1024]{2,1,0:T(8,128)}) custom-call(s32[5]{0:T(128)} %refs_0_.13, bf16[1280,1024]{1,0:T(8,128)(2,1)} %norm_first.1.refs_1_.refs_2_.refs_7_, ...), custom_call_target="tpu_custom_call", output_to_operand_aliasing={{4}: (4, {})} | custom-call | flops 7360000000 | bytes 22400000 | tf_op jit(solution)/shard_map/front/pallas_call | solution.py:71
  92.2 2.1 collective-permute-start.13
  94.2 14.3 %collective-permute-done.10.refs_1_ = f32[5,256,256]{2,1,0:T(8,128)S(1)} collective-permute-done((f32[5,256,256]{2,1,0:T(8,128)}, f32[5,256,256]{2,1,0:T(8,128)S(1)}, u32[]{:S(2)}, u32[]{:S(2)}) %collective-permute-start.10) | collective-permute-done | bytes 1310752 | tf_op jit(solution)/shard_map/ppermute | solution.py:1037
  112.9 12.8 %front.3 = (bf16[3,1024,256]{2,1,0:T(8,128)(2,1)}, bf16[3,1280,256]{2,1,0:T(8,128)(2,1)}, bf16[1280,256]{1,0:T(8,128)(2,1)}, f32[8,1280]{1,0:T(8,128)}) custom-call(s32[5]{0:T(128)} %refs_0_.13, bf16[1280,1024]{1,0:T(8,128)(2,1)} %norm_first.1.refs_1_.refs_2_.refs_7_, f32[3,1024,256]{2,1,0:T(8,128)} %collective-permute-done.12.refs_2_, ...), custom_call_target="tpu_custom_call" | custom-call | flops 7360000000 | bytes 22400000 | tf_op jit(solution)/shard_map/front/pallas_call | solution.py:71
  125.7 21.8 %collective-permute-done.6.refs_7_.refs_4_.refs_2_ = f32[4,256,256]{2,1,0:T(8,128)S(1)} collective-permute-done((f32[4,256,256]{2,1,0:T(8,128)}, f32[4,256,256]{2,1,0:T(8,128)S(1)}, u32[]{:S(2)}, u32[]{:S(2)}) %collective-permute-start.6) | collective-permute-done | bytes 1048608 | tf_op jit(solution)/shard_map/ppermute | solution.py:1033
  150.8 2.4 join.4.refs_2_.refs_22_.refs_24_
  156.4 5.5 %collective-permute-done.14.refs_3_.refs_23_.refs_25_ = f32[5,1024,256]{2,1,0:T(8,128)S(1)} collective-permute-done((f32[5,1024,256]{2,1,0:T(8,128)S(1)}, f32[5,1024,256]{2,1,0:T(8,128)S(1)}, u32[]{:S(2)}, u32[]{:S(2)}) %collective-permute-start.14) | collective-permute-done | bytes 5242912 | tf_op jit(solution)/shard_map/ppermute | solution.py:1015
  162.0 2.3 copy-done.20
  164.2 9.2 %text_front.1 = (bf16[3,1024,256]{2,1,0:T(8,128)(2,1)}, bf16[3,1024,256]{2,1,0:T(8,128)(2,1)}, bf16[2,640,256]{2,1,0:T(8,128)(2,1)}, bf16[2,640,256]{2,1,0:T(8,128)(2,1)}, bf16[2,640,256]{2,1,0:T(8,128)(2,1)}) custom-call(bf16[640,1024]{1,0:T(8,128)(2,1)} %bitcast.88, bf16[3,1024,256]{2,1,0:T(8,128)(2,1)} %pad_maximum_fusion.refs_1_.refs_14_.refs_6_, ...), custom_call_target="tpu_custom_call" | custom-call | flops 3220000000 | bytes 9800000 | tf_op jit(solution)/shard_map/text_front/pallas_call | solution.py:71
  174.9 4.3 join.5.refs_3_.refs_26_
  183.8 3.0 collective-permute-done.15.refs_4_.refs_27_
  186.8 16.9 %front_two.1 = (bf16[3,1024,256]{2,1,0:T(8,128)(2,1)}, bf16[3,1024,256]{2,1,0:T(8,128)(2,1)}, bf16[3,1280,256]{2,1,0:T(8,128)(2,1)}, bf16[1280,256]{1,0:T(8,128)...) custom-call(s32[2]{0:T(128)} %copy-done.12, s32[5]{0:T(128)} %refs_0_.13, ...), custom_call_target="tpu_custom_call" | custom-call | flops 8280000000 | bytes 25200000 | tf_op jit(solution)/shard_map/front_two/pallas_call | solution.py:71
  204.7 32.1 %middle.1 = (bf16[1024,1024]{1,0:T(8,128)(2,1)}, bf16[1024,1024]{1,0:T(8,128)(2,1)}, f32[1280,1024]{1,0:T(8,128)}, f32[1280,1024]{1,0:T(8,128)}, bf16[1280,1024]...) custom-call(s32[2]{0:T(128)} %copy-done.12, ...), custom_call_target="tpu_custom_call" | custom-call | flops 19779999744 | bytes 60200000 | tf_op jit(solution)/shard_map/middle/pallas_call | solution.py:71
  238.1 3.0 collective-permute-start.19
  242.1 26.9 %feed_own.1 = (f32[1280,1024]{1,0:T(8,128)}, f32[1280,1024]{1,0:T(8,128)}, f32[4,2,128,1024]{3,2,1,0:T(8,128)}, f32[4,2,128,1024]{3,2,1,0:T(8,128)}) custom-call(s32[2]{0:T(128)} %copy-done.12, bf16[1280,1024]{1,0:T(8,128)(2,1)} %get-tuple-element.84.refs_0_.refs_1_, bf16[1280,1024]{1,0:T(8,128)(2,1)} %refs_3_.3, ...), custom_call_target="tpu_custom_call" | custom-call | flops 14720000000 | bytes 44800000 | tf_op jit(solution)/shard_map/feed_own/pallas_call | solution.py:71
  269.0 7.5 %collective-permute-done.19.refs_1_ = f32[2,256,1024]{2,1,0:T(8,128)S(1)} collective-permute-done((f32[2,256,1024]{2,1,0:T(8,128)}, f32[2,256,1024]{2,1,0:T(8,128)S(1)}, u32[]{:S(2)}, u32[]{:S(2)}) %collective-permute-start.19) | collective-permute-done | bytes 2097184 | tf_op jit(solution)/shard_map/ppermute | solution.py:1033
  277.9 2.1 collective-permute-start.24
  280.9 18.4 %feed.2 = (f32[1280,1024]{1,0:T(8,128)}, f32[1280,1024]{1,0:T(8,128)}) custom-call(s32[2]{0:T(128)} %copy-done.12, bf16[1280,1024]{1,0:T(8,128)(2,1)} %get-tuple-element.84.refs_0_.refs_1_, bf16[1280,1024]{1,0:T(8,128)(2,1)} %refs_3_.3, f32[1280,1024]{1,0:T(8,128)} %get-tuple-element.86.refs_0_.refs_3_, f32[1280,1024]{1,0:T(8,128)} %get-tuple-element.87.refs_4_, ...), custom_call_target="tpu_custom_call" | custom-call | flops 8280000000 | bytes 25200000 | tf_op jit(solution)/shard_map/feed/pallas_call | solution.py:71
  300.1 18.6 %feed.3 = (f32[1280,1024]{1,0:T(8,128)}, f32[1280,1024]{1,0:T(8,128)}) custom-call(s32[2]{0:T(128)} %copy-done.12, bf16[1280,1024]{1,0:T(8,128)(2,1)} %get-tuple-element.84.refs_0_.refs_1_, bf16[1280,1024]{1,0:T(8,128)(2,1)} %refs_3_.3, f32[1280,1024]{1,0:T(8,128)} %get-tuple-element.88.refs_3_.refs_0_, f32[1280,1024]{1,0:T(8,128)} %get-tuple-element.89.refs_4_, ...), custom_call_target="tpu_custom_call" | custom-call | flops 8280000000 | bytes 25200000 | tf_op jit(solution)/shard_map/feed/pallas_call | solution.py:71
  319.9 2.7 collective-permute-done.30.refs_12_
  323.6 18.3 %feed_last.1 = (bf16[1280,1024]{1,0:T(8,128)(2,1)}, f32[1280,1024]{1,0:T(8,128)}, f32[4,2,128,1024]{3,2,1,0:T(8,128)}) custom-call(s32[2]{0:T(128)} %copy-done.12, bf16[1280,1024]{1,0:T(8,128)(2,1)} %get-tuple-element.84.refs_0_.refs_1_, bf16[1280,1024]{1,0:T(8,128)(2,1)} %refs_3_.3, ...), custom_call_target="tpu_custom_call", output_to_operand_aliasing={{2}: (13, {})} | custom-call | flops 8280000000 | bytes 25200000 | tf_op jit(solution)/shard_map/feed_last/pallas_call | solution.py:71
  342.2 39.5 %back.1 = (f32[1280,1024]{1,0:T(8,128)}, bf16[1280,1024]{1,0:T(8,128)(2,1)}, bf16[4,2,640,256]{3,2,1,0:T(8,128)(2,1)}, f32[2,256,1024]{2,1,0:T(8,128)}, bf16[1280,256]{1,0:T(8,128)(2,1)}, /*index=5*/f32[8,1024]{1,0:T(8,128)}) custom-call(s32[5]{0:T(128)} %refs_0_.13, f32[640,1]{1,0:T(8,128)} %bitcast.92, f32[1280,1024]{1,0:T(8,128)} %get-tuple-element.99.refs_2_, ...), custom_call_target="tpu_custom_call" | custom-call | flops 24380000256 | bytes 74200000 | tf_op jit(solution)/shard_map/back/pallas_call | solution.py:71
  381.6 13.3 %text_back.1 = (f32[640,1024]{1,0:T(8,128)}, f32[4,5,128,256]{3,2,1,0:T(8,128)}, f32[4,5,128,256]{3,2,1,0:T(8,128)}) custom-call(s32[2]{0:T(128)} %copy-done.12, bf16[640,1024]{1,0:T(8,128)(2,1)} %bitcast.90, bf16[4,2,640,256]{3,2,1,0:T(8,128)(2,1)} %get-tuple-element.111.refs_2_, bf16[1280,1024]{1,0:T(8,128)(2,1)} %get-tuple-element.112.refs_3_, ...), custom_call_target="tpu_custom_call" | custom-call | flops 6899999744 | bytes 21000000 | tf_op jit(solution)/shard_map/text_back/pallas_call | solution.py:71
  395.2 4.1 slice_add_fusion
  399.3 1.9 collective-permute-start.33
  401.3 21.4 %self_own.1 = (f32[1280,1024]{1,0:T(8,128)}, f32[4,3,128,256]{3,2,1,0:T(8,128)}, f32[4,3,128,256]{3,2,1,0:T(8,128)}) custom-call(s32[2]{0:T(128)} %copy-done.12, s32[5]{0:T(128)} %refs_0_.13, bf16[3,1280,256]{2,1,0:T(8,128)(2,1)} %get-tuple-element.109.refs_2_, bf16[1280,256]{1,0:T(8,128)(2,1)} %get-tuple-element.69.refs_10_.refs_8_.refs_3_, ...), custom_call_target="tpu_custom_call" | custom-call | flops 10119999488 | bytes 30800000 | tf_op jit(solution)/shard_map/self_own/pallas_call | solution.py:71
  422.7 2.6 slice_add_fusion.1
  425.7 3.2 fusion.4
  430.4 19.5 %self_back.1.refs_0_.refs_10_ = f32[1280,1024]{1,0:T(8,128)} custom-call(s32[5]{0:T(128)} %refs_0_.13, bf16[3,1280,256]{2,1,0:T(8,128)(2,1)} %get-tuple-element.107.refs_1_, bf16[1280,256]{1,0:T(8,128)(2,1)} %get-tuple-element.71.refs_11_.refs_2_, bf16[1280,1024]{1,0:T(8,128)(2,1)} %get-tuple-element.106.refs_4_.refs_3_.refs_9_, ...), custom_call_target="tpu_custom_call" | custom-call | flops 11960000512 | bytes 36400000 | tf_op jit(solution)/shard_map/self_back/pallas_call | solution.py:71
  449.9 4.5 collective-permute-done.34.refs_1_
  454.4 2.4 fusion.7
  458.1 2.4 slice_add_fusion.6
  462.3 35.2 %self_rest.1 = (f32[1280,1024]{1,0:T(8,128)}, f32[8,1024]{1,0:T(8,128)}) custom-call(s32[5]{0:T(128)} %refs_0_.13, bf16[3,1280,256]{2,1,0:T(8,128)(2,1)} %get-tuple-element.94.refs_1_, bf16[1280,256]{1,0:T(8,128)(2,1)} %get-tuple-element.76.refs_12_.refs_2_, f32[8,1280]{1,0:T(8,128)} %get-tuple-element.95.refs_3_, ...), custom_call_target="tpu_custom_call" | custom-call | flops 18400000000 | bytes 56000000 | tf_op jit(solution)/shard_map/self_rest/pallas_call | solution.py:71
  506.4 2.2 collective-permute-start.39
  510.2 2.3 fusion.3
  515.4 2.0 fusion.12
  (182 shorter events, 58.0 us)
Async XLA Ops:
  1.8 22.9 %collective-permute-start = (f32[3,256,256]{2,1,0:T(8,128)S(1)}, f32[3,256,256]{2,1,0:T(8,128)}, u32[]{:S(2)}, u32[]{:S(2)}) collective-permute-start(f32[3,256,256]{2,1,0:T(8,128)S(1)} %convert_bitcast_fusion), channel_id=1, source_target_pairs={{0,1},{1,2},{2,3},{3,0},{4,7},{5,4},{6,5},{7,6},{8,9},{9,10},{10,1... | collective-permute-start | bytes 2359304 | tf_op jit(solution)/shard_map/ppermute | solution.py:1045
  4.9 22.0 %copy-start.29 = (f32[3,1024]{1,0:T(4,128)S(1)}, f32[3,1024]{1,0:T(4,128)}, u32[]{:S(2)}) copy-start(f32[3,1024]{1,0:T(4,128)} %param.19) | copy-start | bytes 36868
  24.7 15.3 %collective-permute-start.2 = (f32[3,256,256]{2,1,0:T(8,128)}, f32[3,256,256]{2,1,0:T(8,128)S(1)}, u32[]{:S(2)}, u32[]{:S(2)}) collective-permute-start(f32[3,256,256]{2,1,0:T(8,128)} %collective-permute-done.refs_0_.refs_3_.refs_1_), channel_id=1, source_target_pairs={{0,16},{4,12},{8,24},{12,4},{16,0},{20,28},{24,8},{28,20},{1,17},{... | collective-permute-start | bytes 2359304 | tf_op jit(solution)/shard_map/ppermute | solution.py:1037
  26.3 147.2 %copy-start.12 = (s32[2]{0:T(128)}, s32[2]{0:T(128)S(1)}, u32[]{:S(2)}) copy-start(s32[2]{0:T(128)S(1)} %pad_add_fusion.refs_0_) | copy-start | bytes 28
  33.1 23.1 %collective-permute-start.1 = (f32[3,256,256]{2,1,0:T(8,128)}, f32[3,256,256]{2,1,0:T(8,128)S(1)}, u32[]{:S(2)}, u32[]{:S(2)}) collective-permute-start(f32[3,256,256]{2,1,0:T(8,128)} %collective-permute-done.refs_0_.refs_3_.refs_1_), channel_id=1, source_target_pairs={{0,8},{4,20},{8,0},{12,28},{16,24},{20,4},{24,16},{28,12},{1,9},{5... | collective-permute-start | bytes 2359304 | tf_op jit(solution)/shard_map/ppermute | solution.py:1033
  40.0 16.2 %collective-permute-start.3 = (f32[3,256,256]{2,1,0:T(8,128)S(1)}, f32[3,256,256]{2,1,0:T(8,128)S(1)}, u32[]{:S(2)}, u32[]{:S(2)}) collective-permute-start(f32[3,256,256]{2,1,0:T(8,128)S(1)} %collective-permute-done.2.refs_3_), channel_id=1, source_target_pairs={{0,8},{4,20},{8,0},{12,28},{16,24},{20,4},{24,16},{28,12},{1,9},{5... | collective-permute-start | bytes 2359304 | tf_op jit(solution)/shard_map/ppermute | solution.py:1033
  44.4 26.5 %collective-permute-start.4 = (f32[5,256,256]{2,1,0:T(8,128)}, f32[5,256,256]{2,1,0:T(8,128)}, u32[]{:S(2)}, u32[]{:S(2)}) collective-permute-start(f32[5,256,256]{2,1,0:T(8,128)} %gate.16.refs_4_), channel_id=1, source_target_pairs={{0,1},{1,2},{2,3},{3,0},{4,7},{5,4},{6,5},{7,6},{8,9},{9,10},{10,1... | collective-permute-start | bytes 3932168 | tf_op jit(solution)/shard_map/ppermute | solution.py:1045
  60.4 52.5 %collective-permute-start.12 = (f32[3,1024,256]{2,1,0:T(8,128)}, f32[3,1024,256]{2,1,0:T(8,128)}, u32[]{:S(2)}, u32[]{:S(2)}) collective-permute-start(f32[3,1024,256]{2,1,0:T(8,128)} %join.3.refs_2_), channel_id=1, source_target_pairs={{0,4},{4,0},{8,12},{12,8},{16,20},{20,16},{24,28},{28,24},{1,5},{5... | collective-permute-start | bytes 9437192 | tf_op jit(solution)/shard_map/ppermute | solution.py:1015
  75.4 34.4 %collective-permute-start.5 = (f32[4,256,256]{2,1,0:T(8,128)}, f32[4,256,256]{2,1,0:T(8,128)S(1)}, u32[]{:S(2)}, u32[]{:S(2)}) collective-permute-start(f32[4,256,256]{2,1,0:T(8,128)} %maximum_select_fusion), channel_id=1, source_target_pairs={{0,1},{1,2},{2,3},{3,0},{4,7},{5,4},{6,5},{7,6},{8,9},{9,10},{10,1... | collective-permute-start | bytes 3145736 | tf_op jit(solution)/shard_map/ppermute | solution.py:1045
  77.3 31.2 %collective-permute-start.10 = (f32[5,256,256]{2,1,0:T(8,128)}, f32[5,256,256]{2,1,0:T(8,128)S(1)}, u32[]{:S(2)}, u32[]{:S(2)}) collective-permute-start(f32[5,256,256]{2,1,0:T(8,128)} %collective-permute-done.4.refs_3_.refs_1_), channel_id=1, source_target_pairs={{0,16},{4,12},{8,24},{12,4},{16,0},{20,28},{24,8},{28,20},{1,17},{... | collective-permute-start | bytes 3932168 | tf_op jit(solution)/shard_map/ppermute | solution.py:1037
  77.8 34.8 %collective-permute-start.9 = (f32[5,256,256]{2,1,0:T(8,128)}, f32[5,256,256]{2,1,0:T(8,128)}, u32[]{:S(2)}, u32[]{:S(2)}) collective-permute-start(f32[5,256,256]{2,1,0:T(8,128)} %collective-permute-done.4.refs_3_.refs_1_), channel_id=1, source_target_pairs={{0,8},{4,20},{8,0},{12,28},{16,24},{20,4},{24,16},{28,12},{1,9},{5... | collective-permute-start | bytes 3932168 | tf_op jit(solution)/shard_map/ppermute | solution.py:1033
  92.2 55.4 %collective-permute-start.13 = (f32[2,256,1024]{2,1,0:T(8,128)}, f32[2,256,1024]{2,1,0:T(8,128)}, u32[]{:S(2)}, u32[]{:S(2)}) collective-permute-start(f32[2,256,1024]{2,1,0:T(8,128)} %get-tuple-element.74), channel_id=1, source_target_pairs={{0,1},{1,2},{2,3},{3,0},{4,7},{5,4},{6,5},{7,6},{8,9},{9,10},{10,1... | collective-permute-start | bytes 6291464 | tf_op jit(solution)/shard_map/ppermute | solution.py:1045
  109.6 38.0 %collective-permute-start.11 = (f32[5,256,256]{2,1,0:T(8,128)}, f32[5,256,256]{2,1,0:T(8,128)S(1)}, u32[]{:S(2)}, u32[]{:S(2)}) collective-permute-start(f32[5,256,256]{2,1,0:T(8,128)} %gate.18.refs_5_.refs_3_), channel_id=1, source_target_pairs={{0,8},{4,20},{8,0},{12,28},{16,24},{20,4},{24,16},{28,12},{1,9},{5... | collective-permute-start | bytes 3932168 | tf_op jit(solution)/shard_map/ppermute | solution.py:1033
  110.8 37.9 %copy-start.4 = (f32[5,256,256]{2,1,0:T(8,128)S(1)}, f32[5,256,256]{2,1,0:T(8,128)}, u32[]{:S(2)}) copy-start(f32[5,256,256]{2,1,0:T(8,128)} %gate.18.refs_5_.refs_3_) | copy-start | bytes 3932164
  110.8 36.8 %collective-permute-start.6 = (f32[4,256,256]{2,1,0:T(8,128)}, f32[4,256,256]{2,1,0:T(8,128)S(1)}, u32[]{:S(2)}, u32[]{:S(2)}) collective-permute-start(f32[4,256,256]{2,1,0:T(8,128)} %gate.17.refs_3_.refs_1_), channel_id=1, source_target_pairs={{0,8},{4,20},{8,0},{12,28},{16,24},{20,4},{24,16},{28,12},{1,9},{5... | collective-permute-start | bytes 3145736 | tf_op jit(solution)/shard_map/ppermute | solution.py:1033
  112.6 35.0 %collective-permute-start.7 = (f32[4,256,256]{2,1,0:T(8,128)}, f32[4,256,256]{2,1,0:T(8,128)}, u32[]{:S(2)}, u32[]{:S(2)}) collective-permute-start(f32[4,256,256]{2,1,0:T(8,128)} %gate.17.refs_3_.refs_1_), channel_id=1, source_target_pairs={{0,16},{4,12},{8,24},{12,4},{16,0},{20,28},{24,8},{28,20},{1,17},{... | collective-permute-start | bytes 3145736 | tf_op jit(solution)/shard_map/ppermute | solution.py:1037
  153.2 8.7 %collective-permute-start.14 = (f32[5,1024,256]{2,1,0:T(8,128)S(1)}, f32[5,1024,256]{2,1,0:T(8,128)S(1)}, u32[]{:S(2)}, u32[]{:S(2)}) collective-permute-start(f32[5,1024,256]{2,1,0:T(8,128)S(1)} %join.4.refs_2_.refs_22_.refs_24_), channel_id=1, source_target_pairs={{0,4},{4,0},{8,12},{12,8},{16,20},{20,16},{24,28},{28,24},{1,5},{5... | collective-permute-start | bytes 15728648 | tf_op jit(solution)/shard_map/ppermute | solution.py:1015
  153.3 20.2 %collective-permute-start.8 = (f32[4,256,256]{2,1,0:T(8,128)}, f32[4,256,256]{2,1,0:T(8,128)}, u32[]{:S(2)}, u32[]{:S(2)}) collective-permute-start(f32[4,256,256]{2,1,0:T(8,128)} %collective-permute-done.7.refs_8_.refs_5_.refs_3_), channel_id=1, source_target_pairs={{0,8},{4,20},{8,0},{12,28},{16,24},{20,4},{24,16},{28,12},{1,9},{5... | collective-permute-start | bytes 3145736 | tf_op jit(solution)/shard_map/ppermute | solution.py:1033
  179.2 7.6 %collective-permute-start.15 = (f32[4,1024,256]{2,1,0:T(8,128)}, f32[4,1024,256]{2,1,0:T(8,128)}, u32[]{:S(2)}, u32[]{:S(2)}) collective-permute-start(f32[4,1024,256]{2,1,0:T(8,128)} %join.5.refs_3_.refs_26_), channel_id=1, source_target_pairs={{0,4},{4,0},{8,12},{12,8},{16,20},{20,16},{24,28},{28,24},{1,5},{5... | collective-permute-start | bytes 12582920 | tf_op jit(solution)/shard_map/ppermute | solution.py:1015
  180.7 23.9 %collective-permute-start.16 = (f32[1,256,1024]{2,1,0:T(8,128)S(1)}, f32[1,256,1024]{2,1,0:T(8,128)}, u32[]{:S(2)}, u32[]{:S(2)}) collective-permute-start(f32[1,256,1024]{2,1,0:T(8,128)S(1)} %constant_dynamic-slice_fusion), channel_id=1, source_target_pairs={{0,1},{1,2},{2,3},{3,0},{4,7},{5,4},{6,5},{7,6},{8,9},{9,10},{10,1... | collective-permute-start | bytes 3145736 | tf_op jit(solution)/shard_map/ppermute | solution.py:1045
  181.8 55.0 %collective-permute-start.18 = (f32[2,256,1024]{2,1,0:T(8,128)}, f32[2,256,1024]{2,1,0:T(8,128)S(1)}, u32[]{:S(2)}, u32[]{:S(2)}) collective-permute-start(f32[2,256,1024]{2,1,0:T(8,128)} %collective-permute-done.13.refs_6_.refs_28_.refs_5_), channel_id=1, source_target_pairs={{0,16},{4,12},{8,24},{12,4},{16,0},{20,28},{24,8},{28,20},{1,17},{... | collective-permute-start | bytes 6291464 | tf_op jit(solution)/shard_map/ppermute | solution.py:1037
  182.1 59.0 %collective-permute-start.17 = (f32[2,256,1024]{2,1,0:T(8,128)}, f32[2,256,1024]{2,1,0:T(8,128)}, u32[]{:S(2)}, u32[]{:S(2)}) collective-permute-start(f32[2,256,1024]{2,1,0:T(8,128)} %collective-permute-done.13.refs_6_.refs_28_.refs_5_), channel_id=1, source_target_pairs={{0,8},{4,20},{8,0},{12,28},{16,24},{20,4},{24,16},{28,12},{1,9},{5... | collective-permute-start | bytes 6291464 | tf_op jit(solution)/shard_map/ppermute | solution.py:1033
  238.1 38.4 %collective-permute-start.19 = (f32[2,256,1024]{2,1,0:T(8,128)}, f32[2,256,1024]{2,1,0:T(8,128)S(1)}, u32[]{:S(2)}, u32[]{:S(2)}) collective-permute-start(f32[2,256,1024]{2,1,0:T(8,128)} %gate.19.refs_7_), channel_id=1, source_target_pairs={{0,8},{4,20},{8,0},{12,28},{16,24},{20,4},{24,16},{28,12},{1,9},{5... | collective-permute-start | bytes 6291464 | tf_op jit(solution)/shard_map/ppermute | solution.py:1033
  241.1 39.9 %collective-permute-start.20 = (f32[2,256,1024]{2,1,0:T(8,128)}, f32[2,256,1024]{2,1,0:T(8,128)}, u32[]{:S(2)}, u32[]{:S(2)}) collective-permute-start(f32[2,256,1024]{2,1,0:T(8,128)} %collective-permute-done.13.refs_6_.refs_28_.refs_5_), channel_id=1, source_target_pairs={{0,4},{4,0},{8,12},{12,8},{16,20},{20,16},{24,28},{28,24},{1,5},{5... | collective-permute-start | bytes 6291464 | tf_op jit(solution)/shard_map/ppermute | solution.py:1015
  241.1 39.9 %collective-permute-start.21 = (f32[2,256,1024]{2,1,0:T(8,128)}, f32[2,256,1024]{2,1,0:T(8,128)}, u32[]{:S(2)}, u32[]{:S(2)}) collective-permute-start(f32[2,256,1024]{2,1,0:T(8,128)} %collective-permute-done.17.refs_6_), channel_id=1, source_target_pairs={{0,4},{4,0},{8,12},{12,8},{16,20},{20,16},{24,28},{28,24},{1,5},{5... | collective-permute-start | bytes 6291464 | tf_op jit(solution)/shard_map/ppermute | solution.py:1015
  241.6 39.4 %collective-permute-start.22 = (f32[2,256,1024]{2,1,0:T(8,128)}, f32[2,256,1024]{2,1,0:T(8,128)}, u32[]{:S(2)}, u32[]{:S(2)}) collective-permute-start(f32[2,256,1024]{2,1,0:T(8,128)} %gate.19.refs_7_), channel_id=1, source_target_pairs={{0,4},{4,0},{8,12},{12,8},{16,20},{20,16},{24,28},{28,24},{1,5},{5... | collective-permute-start | bytes 6291464 | tf_op jit(solution)/shard_map/ppermute | solution.py:1015
  241.6 36.3 %collective-permute-start.25 = (f32[1,256,1024]{2,1,0:T(8,128)}, f32[1,256,1024]{2,1,0:T(8,128)S(1)}, u32[]{:S(2)}, u32[]{:S(2)}) collective-permute-start(f32[1,256,1024]{2,1,0:T(8,128)} %gate.20.refs_8_.refs_5_), channel_id=1, source_target_pairs={{0,16},{4,12},{8,24},{12,4},{16,0},{20,28},{24,8},{28,20},{1,17},{... | collective-permute-start | bytes 3145736 | tf_op jit(solution)/shard_map/ppermute | solution.py:1037
  277.9 22.3 %collective-permute-start.23 = (f32[2,256,1024]{2,1,0:T(8,128)}, f32[2,256,1024]{2,1,0:T(8,128)}, u32[]{:S(2)}, u32[]{:S(2)}) collective-permute-start(f32[2,256,1024]{2,1,0:T(8,128)} %gate.21.refs_8_), channel_id=1, source_target_pairs={{0,4},{4,0},{8,12},{12,8},{16,20},{20,16},{24,28},{28,24},{1,5},{5... | collective-permute-start | bytes 6291464 | tf_op jit(solution)/shard_map/ppermute | solution.py:1015
  277.9 21.7 %copy-start.26 = (f32[1,256,1024]{2,1,0:T(8,128)}, f32[1,256,1024]{2,1,0:T(8,128)S(1)}, u32[]{:S(2)}) copy-start(f32[1,256,1024]{2,1,0:T(8,128)S(1)} %collective-permute-done.25.refs_7_) | copy-start | bytes 3145732
  277.9 22.2 %collective-permute-start.24 = (f32[1,256,1024]{2,1,0:T(8,128)}, f32[1,256,1024]{2,1,0:T(8,128)S(1)}, u32[]{:S(2)}, u32[]{:S(2)}) collective-permute-start(f32[1,256,1024]{2,1,0:T(8,128)} %gate.20.refs_8_.refs_5_), channel_id=1, source_target_pairs={{0,8},{4,20},{8,0},{12,28},{16,24},{20,4},{24,16},{28,12},{1,9},{5... | collective-permute-start | bytes 3145736 | tf_op jit(solution)/shard_map/ppermute | solution.py:1033
  299.3 19.4 %collective-permute-start.26 = (f32[1,256,1024]{2,1,0:T(8,128)}, f32[1,256,1024]{2,1,0:T(8,128)S(1)}, u32[]{:S(2)}, u32[]{:S(2)}) collective-permute-start(f32[1,256,1024]{2,1,0:T(8,128)} %gate.22), channel_id=1, source_target_pairs={{0,8},{4,20},{8,0},{12,28},{16,24},{20,4},{24,16},{28,12},{1,9},{5... | collective-permute-start | bytes 3145736 | tf_op jit(solution)/shard_map/ppermute | solution.py:1033
  299.5 20.4 %collective-permute-start.27 = (f32[1,256,1024]{2,1,0:T(8,128)}, f32[1,256,1024]{2,1,0:T(8,128)}, u32[]{:S(2)}, u32[]{:S(2)}) collective-permute-start(f32[1,256,1024]{2,1,0:T(8,128)} %gate.20.refs_8_.refs_5_), channel_id=1, source_target_pairs={{0,4},{4,0},{8,12},{12,8},{16,20},{20,16},{24,28},{28,24},{1,5},{5... | collective-permute-start | bytes 3145736 | tf_op jit(solution)/shard_map/ppermute | solution.py:1015
  299.5 20.4 %collective-permute-start.29 = (f32[1,256,1024]{2,1,0:T(8,128)S(1)}, f32[1,256,1024]{2,1,0:T(8,128)}, u32[]{:S(2)}, u32[]{:S(2)}) collective-permute-start(f32[1,256,1024]{2,1,0:T(8,128)S(1)} %collective-permute-done.25.refs_7_), channel_id=1, source_target_pairs={{0,4},{4,0},{8,12},{12,8},{16,20},{20,16},{24,28},{28,24},{1,5},{5... | collective-permute-start | bytes 3145736 | tf_op jit(solution)/shard_map/ppermute | solution.py:1015
  300.0 19.9 %collective-permute-start.28 = (f32[1,256,1024]{2,1,0:T(8,128)S(1)}, f32[1,256,1024]{2,1,0:T(8,128)}, u32[]{:S(2)}, u32[]{:S(2)}) collective-permute-start(f32[1,256,1024]{2,1,0:T(8,128)S(1)} %collective-permute-done.24.refs_6_), channel_id=1, source_target_pairs={{0,4},{4,0},{8,12},{12,8},{16,20},{20,16},{24,28},{28,24},{1,5},{5... | collective-permute-start | bytes 3145736 | tf_op jit(solution)/shard_map/ppermute | solution.py:1015
  319.7 2.9 collective-permute-start.30
  341.9 53.3 %collective-permute-start.32 = (f32[4,2,128,1024]{3,2,1,0:T(8,128)}, f32[4,2,128,1024]{3,2,1,0:T(8,128)}, u32[]{:S(2)}, u32[]{:S(2)}) collective-permute-start(f32[4,2,128,1024]{3,2,1,0:T(8,128)} %get-tuple-element.118), channel_id=1, source_target_pairs={{0,4},{4,0},{8,12},{12,8},{16,20},{20,16},{24,28},{28,24},{1,5},{5... | collective-permute-start | bytes 12582920 | tf_op jit(solution)/shard_map/ppermute | solution.py:1015
  394.9 27.8 %collective-permute-start.31 = (f32[4,5,128,256]{3,2,1,0:T(8,128)}, f32[4,5,128,256]{3,2,1,0:T(8,128)}, u32[]{:S(2)}, u32[]{:S(2)}) collective-permute-start(f32[4,5,128,256]{3,2,1,0:T(8,128)} %get-tuple-element.115), channel_id=1, source_target_pairs={{0,4},{4,0},{8,12},{12,8},{16,20},{20,16},{24,28},{28,24},{1,5},{5... | collective-permute-start | bytes 7864328 | tf_op jit(solution)/shard_map/ppermute | solution.py:1015
  399.3 26.4 %collective-permute-start.33 = (f32[2,2,128,1024]{3,2,1,0:T(8,128)}, f32[2,2,128,1024]{3,2,1,0:T(8,128)}, u32[]{:S(2)}, u32[]{:S(2)}) collective-permute-start(f32[2,2,128,1024]{3,2,1,0:T(8,128)} %slice_add_fusion), channel_id=1, source_target_pairs={{0,8},{4,20},{8,0},{12,28},{16,24},{20,4},{24,16},{28,12},{1,9},{5... | collective-permute-start | bytes 6291464 | tf_op jit(solution)/shard_map/ppermute | solution.py:1063
  422.7 34.2 %collective-permute-start.35 = (f32[4,3,128,256]{3,2,1,0:T(8,128)}, f32[4,3,128,256]{3,2,1,0:T(8,128)S(1)}, u32[]{:S(2)}, u32[]{:S(2)}) collective-permute-start(f32[4,3,128,256]{3,2,1,0:T(8,128)} %get-tuple-element.121), channel_id=1, source_target_pairs={{0,4},{4,0},{8,12},{12,8},{16,20},{20,16},{24,28},{28,24},{1,5},{5... | collective-permute-start | bytes 4718600 | tf_op jit(solution)/shard_map/ppermute | solution.py:1015
  425.3 29.2 %collective-permute-start.34 = (f32[2,5,128,256]{3,2,1,0:T(8,128)}, f32[2,5,128,256]{3,2,1,0:T(8,128)}, u32[]{:S(2)}, u32[]{:S(2)}) collective-permute-start(f32[2,5,128,256]{3,2,1,0:T(8,128)} %slice_add_fusion.1), channel_id=1, source_target_pairs={{0,8},{4,20},{8,0},{12,28},{16,24},{20,4},{24,16},{28,12},{1,9},{5... | collective-permute-start | bytes 3932168 | tf_op jit(solution)/shard_map/ppermute | solution.py:1063
  428.9 75.6 %collective-permute-start.37 = (f32[2,128,1024]{2,1,0:T(8,128)}, f32[2,128,1024]{2,1,0:T(8,128)S(1)}, u32[]{:S(2)}, u32[]{:S(2)}) collective-permute-start(f32[2,128,1024]{2,1,0:T(8,128)} %fusion.4), channel_id=1, source_target_pairs={{0,16},{4,12},{8,24},{12,4},{16,0},{20,28},{24,8},{28,20},{1,17},{... | collective-permute-start | bytes 3145736 | tf_op jit(solution)/shard_map/ppermute | solution.py:1037
  456.9 40.6 %collective-permute-start.36 = (f32[5,128,256]{2,1,0:T(8,128)}, f32[5,128,256]{2,1,0:T(8,128)S(1)}, u32[]{:S(2)}, u32[]{:S(2)}) collective-permute-start(f32[5,128,256]{2,1,0:T(8,128)} %fusion.7), channel_id=1, source_target_pairs={{0,16},{4,12},{8,24},{12,4},{16,0},{20,28},{24,8},{28,20},{1,17},{... | collective-permute-start | bytes 1966088 | tf_op jit(solution)/shard_map/ppermute | solution.py:1037
  460.5 42.8 %collective-permute-start.38 = (f32[2,3,128,256]{3,2,1,0:T(8,128)}, f32[2,3,128,256]{3,2,1,0:T(8,128)}, u32[]{:S(2)}, u32[]{:S(2)}) collective-permute-start(f32[2,3,128,256]{3,2,1,0:T(8,128)} %slice_add_fusion.6), channel_id=1, source_target_pairs={{0,8},{4,20},{8,0},{12,28},{16,24},{20,4},{24,16},{28,12},{1,9},{5... | collective-permute-start | bytes 2359304 | tf_op jit(solution)/shard_map/ppermute | solution.py:1063
  504.4 11.0 %collective-permute-start.43 = (f32[3,128,256]{2,1,0:T(8,128)S(1)}, f32[3,128,256]{2,1,0:T(8,128)S(1)}, u32[]{:S(2)}, u32[]{:S(2)}) collective-permute-start(f32[3,128,256]{2,1,0:T(8,128)S(1)} %fusion.9), channel_id=1, source_target_pairs={{0,16},{4,12},{8,24},{12,4},{16,0},{20,28},{24,8},{28,20},{1,17},{... | collective-permute-start | bytes 1179656 | tf_op jit(solution)/shard_map/ppermute | solution.py:1037
  506.4 6.0 %collective-permute-start.39 = (f32[6,1024]{1,0:T(8,128)S(1)}, f32[6,1024]{1,0:T(8,128)S(1)}, u32[]{:S(2)}, u32[]{:S(2)}) collective-permute-start(f32[6,1024]{1,0:T(8,128)S(1)} %concatenate.74), channel_id=1, source_target_pairs={{0,8},{4,12},{8,0},{12,4},{16,24},{20,28},{24,16},{28,20},{1,9},{5... | collective-permute-start | bytes 73736 | tf_op jit(solution)/shard_map/ppermute | solution.py:1075
  508.7 4.3 collective-permute-start.40
  508.7 4.8 collective-permute-start.41
  513.5 1.3 collective-permute-start.42
  (29 other events, 158.4 us)

commit v8 on v7

--- a/solution.py
+++ b/solution.py
@@ -121,7 +121,7 @@
     first_ref[...] = norm_forward(tokens_ref[...].astype(F32), gain_ref[...], shift_ref[...])
 
 
-def norm_first(tokens, gain, shift):
+def norm_first(tokens, gain, shift, wait):
     rows, width = tokens.shape
     return launch(
         norm_kernel,
@@ -129,6 +129,7 @@
         [rows_of(BLK, width), whole((1, width)), whole((1, width))],
         [rows_of(BLK, width)],
         [shape((rows, width), BF16)],
+        wait=wait,
         grid=(rows // BLK,),
         name="norm_first",
         cost_estimate=cost(6),
@@ -188,7 +189,7 @@
         wait=wait,
         compiler_params=params(24),
         name="join",
-        cost_estimate=cost(2),
+        cost_estimate=cost(0.1),
     )[0]
 
 
@@ -1093,7 +1094,6 @@
     own_qkv = jnp.transpose(w_qkv, (1, 0, 2))
     own_cross = jnp.concatenate([w_cross_q[None], jnp.transpose(w_cross_kv, (1, 0, 2))], axis=0)
     feeds = jnp.stack([w_up, w_down])
-    first = norm_first(tokens, gains[0], shifts[0])
     qkvs, mixeds, logs, weights = ([None] * 4 for _ in range(4))
     weights[0] = own_qkv
 
@@ -1101,6 +1101,7 @@
         return along(value.astype(F32), 1), along(value.astype(F32), 3)
 
     wait, carry = [], []
+    first = None if planar else norm_first(tokens, gains[0], shifts[0], [])
     if planar:
         rows = w_out.shape[0] // 4
         outer = [
@@ -1108,10 +1109,11 @@
             for value in (w_out, w_cross_out)
         ]
         qkv_one = around(cut(own_qkv, chip))
-        qkv_near, qkv_side = near_of(qkv_one), side_of(qkv_one)
         own_piece = gate([qkv_one], jnp.concatenate([cut(own_cross, chip), *outer], axis=0))
         cross_one = around(own_piece)
-        wait = [qkv_one, own_piece]
+        first = norm_first(tokens, gains[0], shifts[0], [own_piece])
+        qkv_near, qkv_side = near_of(qkv_one), gate([first], side_of(qkv_one))
+        wait = [qkv_one, cross_one]
     qkvs[0], mixeds[0], logs[0] = front_own(lengths, first, own_qkv, wait, [])
     if planar:
         mine = join(me, [qkv_one, qkv_near, qkv_side, near_of(qkv_side)], [logs[0]])
@@ -1123,7 +1125,7 @@
             jnp.concatenate([cross_one[:3], cross_one[4:5]], axis=0),
         )
         two = around(two)
-        wait = [cross_one]
+        wait = [cross_near, cross_side]
         carry = [cut(feeds, chip)]
     else:
         folded = [fold_whole(value)[None] for value in (w_out, w_cross_out)]
@@ -1139,7 +1141,7 @@
         lengths, first, g_qkv[0], wait, carry
     )
     if planar:
-        cross_side, two = gate([logs[1]], cross_side), gate([logs[1]], two)
+        two = gate([logs[1]], two)
         cross_far = near_of(cross_side)
         two_near, two_side = near_of(two), side_of(two)
         feed_one = around(carried[0])

time: 524 us -> 530 us (1.011)
  waiting for transfers between devices: 91.3 us -> 104 us
    ppermute x5, waiting for transfers between devices: 25.1 us -> 45.5 us  [around(): return lax.ppermute(value, ('dp', 'mp'), ring(1))]
    ppermute x8, waiting for transfers between devices: 19.7 us -> 7.21 us  [side_of(): return lax.ppermute(piece, 'dp', beside(False))]
    unnamed x71 -> x75, local copies, waits for them, and re-layouts: 21.5 us -> 20.9 us
  transfers between devices with their start and end apart: 44 -> 44, of which waited for: 15 -> 16; matrix products, arithmetic and copies ran while one was open for 8% -> 8% of each run, Pallas kernels for 57% -> 57%
where the time goes in v8:
time: 530 us; the launch traced here: 524 us
  Pallas kernels  323 us (61%)
  waiting for transfers between devices  104 us (20%)
  starting transfers between devices  34 us (6%)
  other arithmetic  31.2 us (6%)
  local copies, waits for them, and re-layouts  30.1 us (6%)
    pallas_call x35, Pallas kernels, launch(): pl.pallas_call(body, in_specs=list(in_specs) + [anywhere()] * extra, out_...  323 us
    ppermute x5, waiting for transfers between devices, around(): return lax.ppermute(value, ('dp', 'mp'), ring(1))  45.5 us
    ppermute x10, waiting for transfers between devices, near_of(): return lax.ppermute(piece, 'dp', beside(True))  33.1 us
    unnamed x75, local copies, waits for them, and re-layouts  20.9 us
    ppermute x15, waiting for transfers between devices, swap(): return lax.ppermute(value, 'dp', [(i, i ^ 1) for i in range(DP)])  13.2 us
    ppermute x10, starting transfers between devices, near_of(): return lax.ppermute(piece, 'dp', beside(True))  11.3 us
  transfers between devices with their start and end apart: 44, of which 16 were waited for; matrix products, arithmetic and copies ran while one was open for 8% of the time, Pallas kernels for 57%

profile of v8, /device:TPU:0, one launch (start us, length us, event | category | flops | bytes accessed | tf_op | source)
XLA Modules:
  0.0 523.8 jit_solution(11735028977520483080)
XLA Ops:
  0.7 2.0 convert_bitcast_fusion
  2.7 3.0 collective-permute-start
  9.5 16.1 %collective-permute-done.refs_0_.refs_3_.refs_1_ = f32[3,256,256]{2,1,0:T(8,128)S(1)} collective-permute-done((f32[3,256,256]{2,1,0:T(8,128)}, f32[3,256,256]{2,1,0:T(8,128)S(1)}, u32[]{:S(2)}, u32[]{:S(2)}) %collective-permute-start) | collective-permute-done | bytes 786464 | tf_op jit(solution)/shard_map/ppermute | solution.py:1046
  30.8 5.5 %norm_first.1.refs_1_.refs_0_.refs_2_.refs_7_ = bf16[1280,1024]{1,0:T(8,128)(2,1)} custom-call(bf16[1280,1024]{1,0:T(8,128)(2,1)} %refs_11_.1, f32[1,1024]{1,0:T(1,128)} %get-tuple-element.179.refs_1_.refs_13_, f32[1,1024]{1,0:T(1,128)} %get-tuple-element.176.refs_2_, f32[5,256,256]{2,1,0:T(8,128)} %gate.16.refs_3_), custom_call_target="tpu_custom_call" | custom-call | flops 2760000000 | bytes 8400000 | tf_op jit(solution)/shard_map/norm_first/pallas_call | solution.py:71
  36.3 7.2 %collective-permute-done.3.refs_1_ = f32[3,256,256]{2,1,0:T(8,128)S(1)} collective-permute-done((f32[3,256,256]{2,1,0:T(8,128)}, f32[3,256,256]{2,1,0:T(8,128)S(1)}, u32[]{:S(2)}, u32[]{:S(2)}) %collective-permute-start.3) | collective-permute-done | bytes 786464 | tf_op jit(solution)/shard_map/ppermute | solution.py:1038
  44.4 2.5 collective-permute-start.4
  46.9 11.3 %collective-permute-done.1.refs_4_.refs_1_ = f32[5,256,256]{2,1,0:T(8,128)} collective-permute-done((f32[5,256,256]{2,1,0:T(8,128)}, f32[5,256,256]{2,1,0:T(8,128)}, u32[]{:S(2)}, u32[]{:S(2)}) %collective-permute-start.1) | collective-permute-done | bytes 1310752 | tf_op jit(solution)/shard_map/ppermute | solution.py:1046
  61.2 12.0 %front_own.1 = (bf16[3,1280,256]{2,1,0:T(8,128)(2,1)}, bf16[1280,256]{1,0:T(8,128)(2,1)}, f32[8,1280]{1,0:T(8,128)}) custom-call(s32[5]{0:T(128)} %refs_0_.13, bf16[1280,1024]{1,0:T(8,128)(2,1)} %norm_first.1.refs_1_.refs_0_.refs_2_.refs_7_, bf16[3,1024,256]{2,1,0:T(8,128)(2,1)} %bitcast.93, f32[3,256,256]{2,1,0:T(8,128)} %copy-done.3, ...), custom_call_target="tpu_custom_call" | custom-call | flops 6899999744 | bytes 21000000 | tf_op jit(solution)/shard_map/front_own/pallas_call | solution.py:71
  74.0 3.7 join.3.refs_2_
  77.8 2.8 fusion.1.refs_5_
  83.3 5.0 collective-permute-done.5.refs_3_.refs_4_.refs_2_
  89.4 12.9 %front.2 = (bf16[3,1024,256]{2,1,0:T(8,128)(2,1)}, bf16[3,1280,256]{2,1,0:T(8,128)(2,1)}, bf16[1280,256]{1,0:T(8,128)(2,1)}, f32[8,1280]{1,0:T(8,128)}, f32[2,256,1024]{2,1,0:T(8,128)}) custom-call(s32[5]{0:T(128)} %refs_0_.13, bf16[1280,1024]{1,0:T(8,128)(2,1)} %norm_first.1.refs_1_.refs_0_.refs_2_.refs_7_, ...), custom_call_target="tpu_custom_call", output_to_operand_aliasing={{4}: (5, {})} | custom-call | flops 7360000000 | bytes 22400000 | tf_op jit(solution)/shard_map/front/pallas_call | solution.py:71
  102.3 2.4 collective-permute-start.13
  106.3 4.8 collective-permute-done.7.refs_1_
  113.1 12.9 %front.3 = (bf16[3,1024,256]{2,1,0:T(8,128)(2,1)}, bf16[3,1280,256]{2,1,0:T(8,128)(2,1)}, bf16[1280,256]{1,0:T(8,128)(2,1)}, f32[8,1280]{1,0:T(8,128)}) custom-call(s32[5]{0:T(128)} %refs_0_.13, bf16[1280,1024]{1,0:T(8,128)(2,1)} %norm_first.1.refs_1_.refs_0_.refs_2_.refs_7_, f32[3,1024,256]{2,1,0:T(8,128)} %collective-permute-done.12.refs_2_, ...), custom_call_target="tpu_custom_call" | custom-call | flops 7360000000 | bytes 22400000 | tf_op jit(solution)/shard_map/front/pallas_call | solution.py:71
  125.9 19.0 %collective-permute-done.8.refs_7_.refs_4_.refs_2_ = f32[4,256,256]{2,1,0:T(8,128)S(1)} collective-permute-done((f32[4,256,256]{2,1,0:T(8,128)}, f32[4,256,256]{2,1,0:T(8,128)S(1)}, u32[]{:S(2)}, u32[]{:S(2)}) %collective-permute-start.8) | collective-permute-done | bytes 1048608 | tf_op jit(solution)/shard_map/ppermute | solution.py:1034
  145.0 10.3 %collective-permute-done.13.refs_6_.refs_28_.refs_5_ = f32[2,256,1024]{2,1,0:T(8,128)} collective-permute-done((f32[2,256,1024]{2,1,0:T(8,128)}, f32[2,256,1024]{2,1,0:T(8,128)}, u32[]{:S(2)}, u32[]{:S(2)}) %collective-permute-start.13) | collective-permute-done | bytes 2097184 | tf_op jit(solution)/shard_map/ppermute | solution.py:1046
  156.0 2.8 join.4.refs_2_.refs_22_.refs_24_
  159.5 1.8 pad_maximum_fusion.refs_1_.refs_14_.refs_6_
  161.3 6.3 %collective-permute-done.14.refs_3_.refs_23_.refs_25_ = f32[5,1024,256]{2,1,0:T(8,128)S(1)} collective-permute-done((f32[5,1024,256]{2,1,0:T(8,128)S(1)}, f32[5,1024,256]{2,1,0:T(8,128)S(1)}, u32[]{:S(2)}, u32[]{:S(2)}) %collective-permute-start.14) | collective-permute-done | bytes 5242912 | tf_op jit(solution)/shard_map/ppermute | solution.py:1016
  167.6 2.3 copy-done.22
  169.9 9.3 %text_front.1 = (bf16[3,1024,256]{2,1,0:T(8,128)(2,1)}, bf16[3,1024,256]{2,1,0:T(8,128)(2,1)}, bf16[2,640,256]{2,1,0:T(8,128)(2,1)}, bf16[2,640,256]{2,1,0:T(8,128)(2,1)}, bf16[2,640,256]{2,1,0:T(8,128)(2,1)}) custom-call(bf16[640,1024]{1,0:T(8,128)(2,1)} %bitcast.88, bf16[3,1024,256]{2,1,0:T(8,128)(2,1)} %pad_maximum_fusion.refs_1_.refs_14_.refs_6_, ...), custom_call_target="tpu_custom_call" | custom-call | flops 3220000000 | bytes 9800000 | tf_op jit(solution)/shard_map/text_front/pallas_call | solution.py:71
  180.6 4.3 join.5.refs_3_.refs_26_
  188.5 4.0 collective-permute-done.15.refs_4_.refs_27_
  192.5 16.9 %front_two.1 = (bf16[3,1024,256]{2,1,0:T(8,128)(2,1)}, bf16[3,1024,256]{2,1,0:T(8,128)(2,1)}, bf16[3,1280,256]{2,1,0:T(8,128)(2,1)}, bf16[1280,256]{1,0:T(8,128)...) custom-call(s32[2]{0:T(128)} %copy-done.14, s32[5]{0:T(128)} %refs_0_.13, ...), custom_call_target="tpu_custom_call" | custom-call | flops 8280000000 | bytes 25200000 | tf_op jit(solution)/shard_map/front_two/pallas_call | solution.py:71
  209.4 3.1 collective-permute-done.16.refs_29_.refs_1_
  212.5 32.0 %middle.1 = (bf16[1024,1024]{1,0:T(8,128)(2,1)}, bf16[1024,1024]{1,0:T(8,128)(2,1)}, f32[1280,1024]{1,0:T(8,128)}, f32[1280,1024]{1,0:T(8,128)}, bf16[1280,1024]...) custom-call(s32[2]{0:T(128)} %copy-done.14, ...), custom_call_target="tpu_custom_call" | custom-call | flops 19779999744 | bytes 60200000 | tf_op jit(solution)/shard_map/middle/pallas_call | solution.py:71
  247.4 26.9 %feed_own.1 = (f32[1280,1024]{1,0:T(8,128)}, f32[1280,1024]{1,0:T(8,128)}, f32[4,2,128,1024]{3,2,1,0:T(8,128)}, f32[4,2,128,1024]{3,2,1,0:T(8,128)}) custom-call(s32[2]{0:T(128)} %copy-done.14, bf16[1280,1024]{1,0:T(8,128)(2,1)} %get-tuple-element.84.refs_0_.refs_1_, bf16[1280,1024]{1,0:T(8,128)(2,1)} %refs_3_.3, ...), custom_call_target="tpu_custom_call" | custom-call | flops 14720000000 | bytes 44800000 | tf_op jit(solution)/shard_map/feed_own/pallas_call | solution.py:71
  274.3 9.1 %collective-permute-done.19.refs_1_ = f32[2,256,1024]{2,1,0:T(8,128)S(1)} collective-permute-done((f32[2,256,1024]{2,1,0:T(8,128)}, f32[2,256,1024]{2,1,0:T(8,128)S(1)}, u32[]{:S(2)}, u32[]{:S(2)}) %collective-permute-start.19) | collective-permute-done | bytes 2097184 | tf_op jit(solution)/shard_map/ppermute | solution.py:1034
  286.3 18.4 %feed.2 = (f32[1280,1024]{1,0:T(8,128)}, f32[1280,1024]{1,0:T(8,128)}) custom-call(s32[2]{0:T(128)} %copy-done.14, bf16[1280,1024]{1,0:T(8,128)(2,1)} %get-tuple-element.84.refs_0_.refs_1_, bf16[1280,1024]{1,0:T(8,128)(2,1)} %refs_3_.3, f32[1280,1024]{1,0:T(8,128)} %get-tuple-element.86.refs_0_.refs_3_, f32[1280,1024]{1,0:T(8,128)} %get-tuple-element.87.refs_4_, ...), custom_call_target="tpu_custom_call" | custom-call | flops 8280000000 | bytes 25200000 | tf_op jit(solution)/shard_map/feed/pallas_call | solution.py:71
  306.8 18.6 %feed.3 = (f32[1280,1024]{1,0:T(8,128)}, f32[1280,1024]{1,0:T(8,128)}) custom-call(s32[2]{0:T(128)} %copy-done.14, bf16[1280,1024]{1,0:T(8,128)(2,1)} %get-tuple-element.84.refs_0_.refs_1_, bf16[1280,1024]{1,0:T(8,128)(2,1)} %refs_3_.3, f32[1280,1024]{1,0:T(8,128)} %get-tuple-element.88.refs_3_.refs_0_, f32[1280,1024]{1,0:T(8,128)} %get-tuple-element.89.refs_4_, ...), custom_call_target="tpu_custom_call" | custom-call | flops 8280000000 | bytes 25200000 | tf_op jit(solution)/shard_map/feed/pallas_call | solution.py:71
  326.6 2.7 collective-permute-done.30.refs_12_
  330.3 18.3 %feed_last.1 = (bf16[1280,1024]{1,0:T(8,128)(2,1)}, f32[1280,1024]{1,0:T(8,128)}, f32[4,2,128,1024]{3,2,1,0:T(8,128)}) custom-call(s32[2]{0:T(128)} %copy-done.14, bf16[1280,1024]{1,0:T(8,128)(2,1)} %get-tuple-element.84.refs_0_.refs_1_, bf16[1280,1024]{1,0:T(8,128)(2,1)} %refs_3_.3, ...), custom_call_target="tpu_custom_call", output_to_operand_aliasing={{2}: (13, {})} | custom-call | flops 8280000000 | bytes 25200000 | tf_op jit(solution)/shard_map/feed_last/pallas_call | solution.py:71
  348.8 39.5 %back.1 = (f32[1280,1024]{1,0:T(8,128)}, bf16[1280,1024]{1,0:T(8,128)(2,1)}, bf16[4,2,640,256]{3,2,1,0:T(8,128)(2,1)}, f32[2,256,1024]{2,1,0:T(8,128)}, bf16[1280,256]{1,0:T(8,128)(2,1)}, /*index=5*/f32[8,1024]{1,0:T(8,128)}) custom-call(s32[5]{0:T(128)} %refs_0_.13, f32[640,1]{1,0:T(8,128)} %bitcast.92, f32[1280,1024]{1,0:T(8,128)} %get-tuple-element.99.refs_2_, ...), custom_call_target="tpu_custom_call" | custom-call | flops 24380000256 | bytes 74200000 | tf_op jit(solution)/shard_map/back/pallas_call | solution.py:71
  388.3 13.2 %text_back.1 = (f32[640,1024]{1,0:T(8,128)}, f32[4,5,128,256]{3,2,1,0:T(8,128)}, f32[4,5,128,256]{3,2,1,0:T(8,128)}) custom-call(s32[2]{0:T(128)} %copy-done.14, bf16[640,1024]{1,0:T(8,128)(2,1)} %bitcast.90, bf16[4,2,640,256]{3,2,1,0:T(8,128)(2,1)} %get-tuple-element.111.refs_2_, bf16[1280,1024]{1,0:T(8,128)(2,1)} %get-tuple-element.112.refs_3_, ...), custom_call_target="tpu_custom_call" | custom-call | flops 6899999744 | bytes 21000000 | tf_op jit(solution)/shard_map/text_back/pallas_call | solution.py:71
  401.9 4.1 slice_add_fusion
  406.5 21.4 %self_own.1 = (f32[1280,1024]{1,0:T(8,128)}, f32[4,3,128,256]{3,2,1,0:T(8,128)}, f32[4,3,128,256]{3,2,1,0:T(8,128)}) custom-call(s32[2]{0:T(128)} %copy-done.14, s32[5]{0:T(128)} %refs_0_.13, bf16[3,1280,256]{2,1,0:T(8,128)(2,1)} %get-tuple-element.109.refs_2_, bf16[1280,256]{1,0:T(8,128)(2,1)} %get-tuple-element.69.refs_10_.refs_8_.refs_3_, ...), custom_call_target="tpu_custom_call" | custom-call | flops 10119999488 | bytes 30800000 | tf_op jit(solution)/shard_map/self_own/pallas_call | solution.py:71
  428.0 2.6 slice_add_fusion.1
  432.3 3.2 fusion.4
  436.0 19.5 %self_back.1.refs_0_.refs_10_ = f32[1280,1024]{1,0:T(8,128)} custom-call(s32[5]{0:T(128)} %refs_0_.13, bf16[3,1280,256]{2,1,0:T(8,128)(2,1)} %get-tuple-element.107.refs_1_, bf16[1280,256]{1,0:T(8,128)(2,1)} %get-tuple-element.71.refs_11_.refs_2_, bf16[1280,1024]{1,0:T(8,128)(2,1)} %get-tuple-element.106.refs_4_.refs_3_.refs_9_, ...), custom_call_target="tpu_custom_call" | custom-call | flops 11960000512 | bytes 36400000 | tf_op jit(solution)/shard_map/self_back/pallas_call | solution.py:71
  455.6 3.6 collective-permute-done.34.refs_1_
  459.2 2.5 fusion.7
  464.4 2.4 slice_add_fusion.6
  467.0 35.2 %self_rest.1 = (f32[1280,1024]{1,0:T(8,128)}, f32[8,1024]{1,0:T(8,128)}) custom-call(s32[5]{0:T(128)} %refs_0_.13, bf16[3,1280,256]{2,1,0:T(8,128)(2,1)} %get-tuple-element.94.refs_1_, bf16[1280,256]{1,0:T(8,128)(2,1)} %get-tuple-element.76.refs_12_.refs_2_, f32[8,1280]{1,0:T(8,128)} %get-tuple-element.95.refs_3_, ...), custom_call_target="tpu_custom_call" | custom-call | flops 18400000000 | bytes 56000000 | tf_op jit(solution)/shard_map/self_rest/pallas_call | solution.py:71
  503.1 1.9 fusion.6
  509.1 2.1 collective-permute-start.43
  516.7 2.3 fusion.3
  521.6 2.0 fusion.12
  (186 shorter events, 57.1 us)
Async XLA Ops:
  2.7 23.0 %collective-permute-start = (f32[3,256,256]{2,1,0:T(8,128)}, f32[3,256,256]{2,1,0:T(8,128)S(1)}, u32[]{:S(2)}, u32[]{:S(2)}) collective-permute-start(f32[3,256,256]{2,1,0:T(8,128)} %convert_bitcast_fusion), channel_id=1, source_target_pairs={{0,1},{1,2},{2,3},{3,0},{4,7},{5,4},{6,5},{7,6},{8,9},{9,10},{10,1... | collective-permute-start | bytes 2359304 | tf_op jit(solution)/shard_map/ppermute | solution.py:1046
  26.5 31.7 %collective-permute-start.1 = (f32[5,256,256]{2,1,0:T(8,128)}, f32[5,256,256]{2,1,0:T(8,128)}, u32[]{:S(2)}, u32[]{:S(2)}) collective-permute-start(f32[5,256,256]{2,1,0:T(8,128)} %gate.16.refs_3_), channel_id=1, source_target_pairs={{0,1},{1,2},{2,3},{3,0},{4,7},{5,4},{6,5},{7,6},{8,9},{9,10},{10,1... | collective-permute-start | bytes 3932168 | tf_op jit(solution)/shard_map/ppermute | solution.py:1046
  26.5 17.0 %collective-permute-start.3 = (f32[3,256,256]{2,1,0:T(8,128)}, f32[3,256,256]{2,1,0:T(8,128)S(1)}, u32[]{:S(2)}, u32[]{:S(2)}) collective-permute-start(f32[3,256,256]{2,1,0:T(8,128)} %copy-done.3), channel_id=1, source_target_pairs={{0,16},{4,12},{8,24},{12,4},{16,0},{20,28},{24,8},{28,20},{1,17},{... | collective-permute-start | bytes 2359304 | tf_op jit(solution)/shard_map/ppermute | solution.py:1038
  29.3 43.9 %collective-permute-start.2 = (f32[3,256,256]{2,1,0:T(8,128)}, f32[3,256,256]{2,1,0:T(8,128)}, u32[]{:S(2)}, u32[]{:S(2)}) collective-permute-start(f32[3,256,256]{2,1,0:T(8,128)} %copy-done.3), channel_id=1, source_target_pairs={{0,8},{4,20},{8,0},{12,28},{16,24},{20,4},{24,16},{28,12},{1,9},{5... | collective-permute-start | bytes 2359304 | tf_op jit(solution)/shard_map/ppermute | solution.py:1034
  44.4 28.8 %collective-permute-start.4 = (f32[3,256,256]{2,1,0:T(8,128)}, f32[3,256,256]{2,1,0:T(8,128)}, u32[]{:S(2)}, u32[]{:S(2)}) collective-permute-start(f32[3,256,256]{2,1,0:T(8,128)} %gate.17.refs_3_), channel_id=1, source_target_pairs={{0,8},{4,20},{8,0},{12,28},{16,24},{20,4},{24,16},{28,12},{1,9},{5... | collective-permute-start | bytes 2359304 | tf_op jit(solution)/shard_map/ppermute | solution.py:1034
  46.9 132.2 %copy-start.14 = (s32[2]{0:T(128)}, s32[2]{0:T(128)S(1)}, u32[]{:S(2)}) copy-start(s32[2]{0:T(128)S(1)} %pad_add_fusion.refs_0_) | copy-start | bytes 28
  58.2 30.1 %collective-permute-start.5 = (f32[5,256,256]{2,1,0:T(8,128)}, f32[5,256,256]{2,1,0:T(8,128)S(1)}, u32[]{:S(2)}, u32[]{:S(2)}) collective-permute-start(f32[5,256,256]{2,1,0:T(8,128)} %collective-permute-done.1.refs_4_.refs_1_), channel_id=1, source_target_pairs={{0,8},{4,20},{8,0},{12,28},{16,24},{20,4},{24,16},{28,12},{1,9},{5... | collective-permute-start | bytes 3932168 | tf_op jit(solution)/shard_map/ppermute | solution.py:1034
  59.7 28.6 %collective-permute-start.6 = (f32[5,256,256]{2,1,0:T(8,128)}, f32[5,256,256]{2,1,0:T(8,128)}, u32[]{:S(2)}, u32[]{:S(2)}) collective-permute-start(f32[5,256,256]{2,1,0:T(8,128)} %collective-permute-done.1.refs_4_.refs_1_), channel_id=1, source_target_pairs={{0,16},{4,12},{8,24},{12,4},{16,0},{20,28},{24,8},{28,20},{1,17},{... | collective-permute-start | bytes 3932168 | tf_op jit(solution)/shard_map/ppermute | solution.py:1038
  77.7 35.3 %collective-permute-start.12 = (f32[3,1024,256]{2,1,0:T(8,128)}, f32[3,1024,256]{2,1,0:T(8,128)}, u32[]{:S(2)}, u32[]{:S(2)}) collective-permute-start(f32[3,1024,256]{2,1,0:T(8,128)} %join.3.refs_2_), channel_id=1, source_target_pairs={{0,4},{4,0},{8,12},{12,8},{16,20},{20,16},{24,28},{28,24},{1,5},{5... | collective-permute-start | bytes 9437192 | tf_op jit(solution)/shard_map/ppermute | solution.py:1016
  83.0 28.0 %collective-permute-start.7 = (f32[4,256,256]{2,1,0:T(8,128)S(1)}, f32[4,256,256]{2,1,0:T(8,128)S(1)}, u32[]{:S(2)}, u32[]{:S(2)}) collective-permute-start(f32[4,256,256]{2,1,0:T(8,128)S(1)} %maximum_select_fusion), channel_id=1, source_target_pairs={{0,1},{1,2},{2,3},{3,0},{4,7},{5,4},{6,5},{7,6},{8,9},{9,10},{10,1... | collective-permute-start | bytes 3145736 | tf_op jit(solution)/shard_map/ppermute | solution.py:1046
  102.3 53.0 %collective-permute-start.13 = (f32[2,256,1024]{2,1,0:T(8,128)}, f32[2,256,1024]{2,1,0:T(8,128)}, u32[]{:S(2)}, u32[]{:S(2)}) collective-permute-start(f32[2,256,1024]{2,1,0:T(8,128)} %get-tuple-element.74), channel_id=1, source_target_pairs={{0,1},{1,2},{2,3},{3,0},{4,7},{5,4},{6,5},{7,6},{8,9},{9,10},{10,1... | collective-permute-start | bytes 6291464 | tf_op jit(solution)/shard_map/ppermute | solution.py:1046
  104.7 40.3 %collective-permute-start.11 = (f32[5,256,256]{2,1,0:T(8,128)}, f32[5,256,256]{2,1,0:T(8,128)}, u32[]{:S(2)}, u32[]{:S(2)}) collective-permute-start(f32[5,256,256]{2,1,0:T(8,128)} %collective-permute-done.6.refs_4_.refs_5_.refs_3_), channel_id=1, source_target_pairs={{0,8},{4,20},{8,0},{12,28},{16,24},{20,4},{24,16},{28,12},{1,9},{5... | collective-permute-start | bytes 3932168 | tf_op jit(solution)/shard_map/ppermute | solution.py:1034
  112.0 43.2 %copy-start.11 = (f32[5,256,256]{2,1,0:T(8,128)S(1)}, f32[5,256,256]{2,1,0:T(8,128)}, u32[]{:S(2)}) copy-start(f32[5,256,256]{2,1,0:T(8,128)} %copy-done.10) | copy-start | bytes 3932164
  112.0 32.9 %collective-permute-start.8 = (f32[4,256,256]{2,1,0:T(8,128)}, f32[4,256,256]{2,1,0:T(8,128)S(1)}, u32[]{:S(2)}, u32[]{:S(2)}) collective-permute-start(f32[4,256,256]{2,1,0:T(8,128)} %gate.18.refs_3_.refs_1_), channel_id=1, source_target_pairs={{0,8},{4,20},{8,0},{12,28},{16,24},{20,4},{24,16},{28,12},{1,9},{5... | collective-permute-start | bytes 3145736 | tf_op jit(solution)/shard_map/ppermute | solution.py:1034
  112.6 32.4 %collective-permute-start.9 = (f32[4,256,256]{2,1,0:T(8,128)}, f32[4,256,256]{2,1,0:T(8,128)}, u32[]{:S(2)}, u32[]{:S(2)}) collective-permute-start(f32[4,256,256]{2,1,0:T(8,128)} %gate.18.refs_3_.refs_1_), channel_id=1, source_target_pairs={{0,16},{4,12},{8,24},{12,4},{16,0},{20,28},{24,8},{28,20},{1,17},{... | collective-permute-start | bytes 3145736 | tf_op jit(solution)/shard_map/ppermute | solution.py:1038
  158.9 8.7 %collective-permute-start.14 = (f32[5,1024,256]{2,1,0:T(8,128)S(1)}, f32[5,1024,256]{2,1,0:T(8,128)S(1)}, u32[]{:S(2)}, u32[]{:S(2)}) collective-permute-start(f32[5,1024,256]{2,1,0:T(8,128)S(1)} %join.4.refs_2_.refs_22_.refs_24_), channel_id=1, source_target_pairs={{0,4},{4,0},{8,12},{12,8},{16,20},{20,16},{24,28},{28,24},{1,5},{5... | collective-permute-start | bytes 15728648 | tf_op jit(solution)/shard_map/ppermute | solution.py:1016
  159.0 20.2 %collective-permute-start.10 = (f32[4,256,256]{2,1,0:T(8,128)}, f32[4,256,256]{2,1,0:T(8,128)}, u32[]{:S(2)}, u32[]{:S(2)}) collective-permute-start(f32[4,256,256]{2,1,0:T(8,128)} %collective-permute-done.9.refs_8_.refs_5_.refs_3_), channel_id=1, source_target_pairs={{0,8},{4,20},{8,0},{12,28},{16,24},{20,4},{24,16},{28,12},{1,9},{5... | collective-permute-start | bytes 3145736 | tf_op jit(solution)/shard_map/ppermute | solution.py:1034
  184.9 7.6 %collective-permute-start.15 = (f32[4,1024,256]{2,1,0:T(8,128)}, f32[4,1024,256]{2,1,0:T(8,128)}, u32[]{:S(2)}, u32[]{:S(2)}) collective-permute-start(f32[4,1024,256]{2,1,0:T(8,128)} %join.5.refs_3_.refs_26_), channel_id=1, source_target_pairs={{0,4},{4,0},{8,12},{12,8},{16,20},{20,16},{24,28},{28,24},{1,5},{5... | collective-permute-start | bytes 12582920 | tf_op jit(solution)/shard_map/ppermute | solution.py:1016
  186.4 26.1 %collective-permute-start.16 = (f32[1,256,1024]{2,1,0:T(8,128)S(1)}, f32[1,256,1024]{2,1,0:T(8,128)}, u32[]{:S(2)}, u32[]{:S(2)}) collective-permute-start(f32[1,256,1024]{2,1,0:T(8,128)S(1)} %constant_dynamic-slice_fusion), channel_id=1, source_target_pairs={{0,1},{1,2},{2,3},{3,0},{4,7},{5,4},{6,5},{7,6},{8,9},{9,10},{10,1... | collective-permute-start | bytes 3145736 | tf_op jit(solution)/shard_map/ppermute | solution.py:1046
  187.4 57.1 %collective-permute-start.18 = (f32[2,256,1024]{2,1,0:T(8,128)}, f32[2,256,1024]{2,1,0:T(8,128)S(1)}, u32[]{:S(2)}, u32[]{:S(2)}) collective-permute-start(f32[2,256,1024]{2,1,0:T(8,128)} %collective-permute-done.13.refs_6_.refs_28_.refs_5_), channel_id=1, source_target_pairs={{0,16},{4,12},{8,24},{12,4},{16,0},{20,28},{24,8},{28,20},{1,17},{... | collective-permute-start | bytes 6291464 | tf_op jit(solution)/shard_map/ppermute | solution.py:1038
  187.9 58.5 %collective-permute-start.17 = (f32[2,256,1024]{2,1,0:T(8,128)}, f32[2,256,1024]{2,1,0:T(8,128)}, u32[]{:S(2)}, u32[]{:S(2)}) collective-permute-start(f32[2,256,1024]{2,1,0:T(8,128)} %collective-permute-done.13.refs_6_.refs_28_.refs_5_), channel_id=1, source_target_pairs={{0,8},{4,20},{8,0},{12,28},{16,24},{20,4},{24,16},{28,12},{1,9},{5... | collective-permute-start | bytes 6291464 | tf_op jit(solution)/shard_map/ppermute | solution.py:1034
  245.9 37.5 %collective-permute-start.19 = (f32[2,256,1024]{2,1,0:T(8,128)}, f32[2,256,1024]{2,1,0:T(8,128)S(1)}, u32[]{:S(2)}, u32[]{:S(2)}) collective-permute-start(f32[2,256,1024]{2,1,0:T(8,128)} %gate.19.refs_7_), channel_id=1, source_target_pairs={{0,8},{4,20},{8,0},{12,28},{16,24},{20,4},{24,16},{28,12},{1,9},{5... | collective-permute-start | bytes 6291464 | tf_op jit(solution)/shard_map/ppermute | solution.py:1034
  246.4 39.8 %collective-permute-start.20 = (f32[2,256,1024]{2,1,0:T(8,128)}, f32[2,256,1024]{2,1,0:T(8,128)}, u32[]{:S(2)}, u32[]{:S(2)}) collective-permute-start(f32[2,256,1024]{2,1,0:T(8,128)} %collective-permute-done.13.refs_6_.refs_28_.refs_5_), channel_id=1, source_target_pairs={{0,4},{4,0},{8,12},{12,8},{16,20},{20,16},{24,28},{28,24},{1,5},{5... | collective-permute-start | bytes 6291464 | tf_op jit(solution)/shard_map/ppermute | solution.py:1016
  246.4 39.8 %collective-permute-start.21 = (f32[2,256,1024]{2,1,0:T(8,128)}, f32[2,256,1024]{2,1,0:T(8,128)}, u32[]{:S(2)}, u32[]{:S(2)}) collective-permute-start(f32[2,256,1024]{2,1,0:T(8,128)} %collective-permute-done.17.refs_6_), channel_id=1, source_target_pairs={{0,4},{4,0},{8,12},{12,8},{16,20},{20,16},{24,28},{28,24},{1,5},{5... | collective-permute-start | bytes 6291464 | tf_op jit(solution)/shard_map/ppermute | solution.py:1016
  246.9 39.3 %collective-permute-start.22 = (f32[2,256,1024]{2,1,0:T(8,128)}, f32[2,256,1024]{2,1,0:T(8,128)}, u32[]{:S(2)}, u32[]{:S(2)}) collective-permute-start(f32[2,256,1024]{2,1,0:T(8,128)} %gate.19.refs_7_), channel_id=1, source_target_pairs={{0,4},{4,0},{8,12},{12,8},{16,20},{20,16},{24,28},{28,24},{1,5},{5... | collective-permute-start | bytes 6291464 | tf_op jit(solution)/shard_map/ppermute | solution.py:1016
  246.9 37.8 %collective-permute-start.25 = (f32[1,256,1024]{2,1,0:T(8,128)}, f32[1,256,1024]{2,1,0:T(8,128)S(1)}, u32[]{:S(2)}, u32[]{:S(2)}) collective-permute-start(f32[1,256,1024]{2,1,0:T(8,128)} %gate.20.refs_8_.refs_5_), channel_id=1, source_target_pairs={{0,16},{4,12},{8,24},{12,4},{16,0},{20,28},{24,8},{28,20},{1,17},{... | collective-permute-start | bytes 3145736 | tf_op jit(solution)/shard_map/ppermute | solution.py:1038
  284.7 22.1 %collective-permute-start.23 = (f32[2,256,1024]{2,1,0:T(8,128)}, f32[2,256,1024]{2,1,0:T(8,128)}, u32[]{:S(2)}, u32[]{:S(2)}) collective-permute-start(f32[2,256,1024]{2,1,0:T(8,128)} %gate.21.refs_8_), channel_id=1, source_target_pairs={{0,4},{4,0},{8,12},{12,8},{16,20},{20,16},{24,28},{28,24},{1,5},{5... | collective-permute-start | bytes 6291464 | tf_op jit(solution)/shard_map/ppermute | solution.py:1016
  284.7 21.5 %copy-start.28 = (f32[1,256,1024]{2,1,0:T(8,128)}, f32[1,256,1024]{2,1,0:T(8,128)S(1)}, u32[]{:S(2)}) copy-start(f32[1,256,1024]{2,1,0:T(8,128)S(1)} %collective-permute-done.25.refs_7_) | copy-start | bytes 3145732
  284.7 22.0 %collective-permute-start.24 = (f32[1,256,1024]{2,1,0:T(8,128)}, f32[1,256,1024]{2,1,0:T(8,128)S(1)}, u32[]{:S(2)}, u32[]{:S(2)}) collective-permute-start(f32[1,256,1024]{2,1,0:T(8,128)} %gate.20.refs_8_.refs_5_), channel_id=1, source_target_pairs={{0,8},{4,20},{8,0},{12,28},{16,24},{20,4},{24,16},{28,12},{1,9},{5... | collective-permute-start | bytes 3145736 | tf_op jit(solution)/shard_map/ppermute | solution.py:1034
  304.7 20.8 %collective-permute-start.26 = (f32[1,256,1024]{2,1,0:T(8,128)}, f32[1,256,1024]{2,1,0:T(8,128)S(1)}, u32[]{:S(2)}, u32[]{:S(2)}) collective-permute-start(f32[1,256,1024]{2,1,0:T(8,128)} %gate.22), channel_id=1, source_target_pairs={{0,8},{4,20},{8,0},{12,28},{16,24},{20,4},{24,16},{28,12},{1,9},{5... | collective-permute-start | bytes 3145736 | tf_op jit(solution)/shard_map/ppermute | solution.py:1034
  306.2 20.4 %collective-permute-start.27 = (f32[1,256,1024]{2,1,0:T(8,128)}, f32[1,256,1024]{2,1,0:T(8,128)}, u32[]{:S(2)}, u32[]{:S(2)}) collective-permute-start(f32[1,256,1024]{2,1,0:T(8,128)} %gate.20.refs_8_.refs_5_), channel_id=1, source_target_pairs={{0,4},{4,0},{8,12},{12,8},{16,20},{20,16},{24,28},{28,24},{1,5},{5... | collective-permute-start | bytes 3145736 | tf_op jit(solution)/shard_map/ppermute | solution.py:1016
  306.2 20.4 %collective-permute-start.29 = (f32[1,256,1024]{2,1,0:T(8,128)S(1)}, f32[1,256,1024]{2,1,0:T(8,128)}, u32[]{:S(2)}, u32[]{:S(2)}) collective-permute-start(f32[1,256,1024]{2,1,0:T(8,128)S(1)} %collective-permute-done.25.refs_7_), channel_id=1, source_target_pairs={{0,4},{4,0},{8,12},{12,8},{16,20},{20,16},{24,28},{28,24},{1,5},{5... | collective-permute-start | bytes 3145736 | tf_op jit(solution)/shard_map/ppermute | solution.py:1016
  306.7 19.9 %collective-permute-start.28 = (f32[1,256,1024]{2,1,0:T(8,128)S(1)}, f32[1,256,1024]{2,1,0:T(8,128)}, u32[]{:S(2)}, u32[]{:S(2)}) collective-permute-start(f32[1,256,1024]{2,1,0:T(8,128)S(1)} %collective-permute-done.24.refs_6_), channel_id=1, source_target_pairs={{0,4},{4,0},{8,12},{12,8},{16,20},{20,16},{24,28},{28,24},{1,5},{5... | collective-permute-start | bytes 3145736 | tf_op jit(solution)/shard_map/ppermute | solution.py:1016
  326.4 2.9 collective-permute-start.30
  348.6 53.3 %collective-permute-start.32 = (f32[4,2,128,1024]{3,2,1,0:T(8,128)}, f32[4,2,128,1024]{3,2,1,0:T(8,128)}, u32[]{:S(2)}, u32[]{:S(2)}) collective-permute-start(f32[4,2,128,1024]{3,2,1,0:T(8,128)} %get-tuple-element.118), channel_id=1, source_target_pairs={{0,4},{4,0},{8,12},{12,8},{16,20},{20,16},{24,28},{28,24},{1,5},{5... | collective-permute-start | bytes 12582920 | tf_op jit(solution)/shard_map/ppermute | solution.py:1016
  401.6 26.4 %collective-permute-start.31 = (f32[4,5,128,256]{3,2,1,0:T(8,128)}, f32[4,5,128,256]{3,2,1,0:T(8,128)}, u32[]{:S(2)}, u32[]{:S(2)}) collective-permute-start(f32[4,5,128,256]{3,2,1,0:T(8,128)} %get-tuple-element.115), channel_id=1, source_target_pairs={{0,4},{4,0},{8,12},{12,8},{16,20},{20,16},{24,28},{28,24},{1,5},{5... | collective-permute-start | bytes 7864328 | tf_op jit(solution)/shard_map/ppermute | solution.py:1016
  406.0 26.4 %collective-permute-start.33 = (f32[2,2,128,1024]{3,2,1,0:T(8,128)}, f32[2,2,128,1024]{3,2,1,0:T(8,128)}, u32[]{:S(2)}, u32[]{:S(2)}) collective-permute-start(f32[2,2,128,1024]{3,2,1,0:T(8,128)} %slice_add_fusion), channel_id=1, source_target_pairs={{0,8},{4,20},{8,0},{12,28},{16,24},{20,4},{24,16},{28,12},{1,9},{5... | collective-permute-start | bytes 6291464 | tf_op jit(solution)/shard_map/ppermute | solution.py:1064
  406.5 21.5 %copy-start.23 = (f32[4,5,128,256]{3,2,1,0:T(8,128)S(1)}, f32[4,5,128,256]{3,2,1,0:T(8,128)}, u32[]{:S(2)}) copy-start(f32[4,5,128,256]{3,2,1,0:T(8,128)} %get-tuple-element.120) | copy-start | bytes 7864324
  427.9 35.2 %collective-permute-start.35 = (f32[4,3,128,256]{3,2,1,0:T(8,128)}, f32[4,3,128,256]{3,2,1,0:T(8,128)S(1)}, u32[]{:S(2)}, u32[]{:S(2)}) collective-permute-start(f32[4,3,128,256]{3,2,1,0:T(8,128)} %get-tuple-element.121), channel_id=1, source_target_pairs={{0,4},{4,0},{8,12},{12,8},{16,20},{20,16},{24,28},{28,24},{1,5},{5... | collective-permute-start | bytes 4718600 | tf_op jit(solution)/shard_map/ppermute | solution.py:1016
  430.6 28.6 %collective-permute-start.34 = (f32[2,5,128,256]{3,2,1,0:T(8,128)}, f32[2,5,128,256]{3,2,1,0:T(8,128)}, u32[]{:S(2)}, u32[]{:S(2)}) collective-permute-start(f32[2,5,128,256]{3,2,1,0:T(8,128)} %slice_add_fusion.1), channel_id=1, source_target_pairs={{0,8},{4,20},{8,0},{12,28},{16,24},{20,4},{24,16},{28,12},{1,9},{5... | collective-permute-start | bytes 3932168 | tf_op jit(solution)/shard_map/ppermute | solution.py:1064
  435.5 75.7 %collective-permute-start.37 = (f32[2,128,1024]{2,1,0:T(8,128)}, f32[2,128,1024]{2,1,0:T(8,128)S(1)}, u32[]{:S(2)}, u32[]{:S(2)}) collective-permute-start(f32[2,128,1024]{2,1,0:T(8,128)} %fusion.4), channel_id=1, source_target_pairs={{0,16},{4,12},{8,24},{12,4},{16,0},{20,28},{24,8},{28,20},{1,17},{... | collective-permute-start | bytes 3145736 | tf_op jit(solution)/shard_map/ppermute | solution.py:1038
  461.6 40.6 %collective-permute-start.36 = (f32[5,128,256]{2,1,0:T(8,128)}, f32[5,128,256]{2,1,0:T(8,128)S(1)}, u32[]{:S(2)}, u32[]{:S(2)}) collective-permute-start(f32[5,128,256]{2,1,0:T(8,128)} %fusion.7), channel_id=1, source_target_pairs={{0,16},{4,12},{8,24},{12,4},{16,0},{20,28},{24,8},{28,20},{1,17},{... | collective-permute-start | bytes 1966088 | tf_op jit(solution)/shard_map/ppermute | solution.py:1038
  466.7 41.2 %collective-permute-start.38 = (f32[2,3,128,256]{3,2,1,0:T(8,128)}, f32[2,3,128,256]{3,2,1,0:T(8,128)}, u32[]{:S(2)}, u32[]{:S(2)}) collective-permute-start(f32[2,3,128,256]{3,2,1,0:T(8,128)} %slice_add_fusion.6), channel_id=1, source_target_pairs={{0,8},{4,20},{8,0},{12,28},{16,24},{20,4},{24,16},{28,12},{1,9},{5... | collective-permute-start | bytes 2359304 | tf_op jit(solution)/shard_map/ppermute | solution.py:1064
  509.1 12.5 %collective-permute-start.43 = (f32[3,128,256]{2,1,0:T(8,128)S(1)}, f32[3,128,256]{2,1,0:T(8,128)S(1)}, u32[]{:S(2)}, u32[]{:S(2)}) collective-permute-start(f32[3,128,256]{2,1,0:T(8,128)S(1)} %fusion.9), channel_id=1, source_target_pairs={{0,16},{4,12},{8,24},{12,4},{16,0},{20,28},{24,8},{28,20},{1,17},{... | collective-permute-start | bytes 1179656 | tf_op jit(solution)/shard_map/ppermute | solution.py:1038
  513.1 5.8 %collective-permute-start.39 = (f32[6,1024]{1,0:T(8,128)S(1)}, f32[6,1024]{1,0:T(8,128)S(1)}, u32[]{:S(2)}, u32[]{:S(2)}) collective-permute-start(f32[6,1024]{1,0:T(8,128)S(1)} %concatenate.74), channel_id=1, source_target_pairs={{0,8},{4,12},{8,0},{12,4},{16,24},{20,28},{24,16},{28,20},{1,9},{5... | collective-permute-start | bytes 73736 | tf_op jit(solution)/shard_map/ppermute | solution.py:1076
  513.4 5.6 %collective-permute-start.40 = (f32[6,1024]{1,0:T(8,128)S(1)}, f32[6,1024]{1,0:T(8,128)S(1)}, u32[]{:S(2)}, u32[]{:S(2)}) collective-permute-start(f32[6,1024]{1,0:T(8,128)S(1)} %concatenate.74), channel_id=1, source_target_pairs={{0,16},{4,20},{8,24},{12,28},{16,0},{20,4},{24,8},{28,12},{1,17},{... | collective-permute-start | bytes 73736 | tf_op jit(solution)/shard_map/ppermute | solution.py:1076
  514.9 4.8 collective-permute-start.41
  519.8 1.3 collective-permute-start.42
  (31 other events, 184.6 us)

commit v9 on v8

--- a/solution.py
+++ b/solution.py
@@ -1125,7 +1125,7 @@
             jnp.concatenate([cross_one[:3], cross_one[4:5]], axis=0),
         )
         two = around(two)
-        wait = [cross_near, cross_side]
+        wait = [cross_near, cross_side, two]
         carry = [cut(feeds, chip)]
     else:
         folded = [fold_whole(value)[None] for value in (w_out, w_cross_out)]

time: 530 us -> 528 us (level)
  Pallas kernels: 323 us -> 293 us
  starting transfers between devices: 34 us -> 61.3 us
    pallas_call x35, Pallas kernels: 323 us -> 293 us  [launch(): pl.pallas_call(body, in_specs=list(in_specs) + [anywhere()] * extra, out_...]
    ppermute x10, starting transfers between devices: 11.3 us -> 21.2 us  [near_of(): return lax.ppermute(piece, 'dp', beside(True))]
    ppermute x3, starting transfers between devices: 3.55 us -> 12.8 us  [plane_sum(): lax.ppermute(value, 'dp', [(i, i ^ bit) for i in range(DP)])]
    ppermute x15, waiting for transfers between devices: 13.2 us -> 5.46 us  [swap(): return lax.ppermute(value, 'dp', [(i, i ^ 1) for i in range(DP)])]
    ppermute x10, waiting for transfers between devices: 33.1 us -> 39.8 us  [near_of(): return lax.ppermute(piece, 'dp', beside(True))]
    unnamed x75 -> x91, local copies, waits for them, and re-layouts: 20.9 us -> 22.6 us
  transfers between devices with their start and end apart: 44 -> 44, of which waited for: 16 -> 16; matrix products, arithmetic and copies ran while one was open for 8% -> 7% of each run, Pallas kernels for 57% -> 51%
where the time goes in v9:
time: 528 us; the launch traced here: 524 us
  Pallas kernels  293 us (55%)
  waiting for transfers between devices  108 us (20%)
  starting transfers between devices  61.3 us (12%)
  other arithmetic  29.9 us (6%)
  local copies, waits for them, and re-layouts  29.6 us (6%)
    pallas_call x35, Pallas kernels, launch(): pl.pallas_call(body, in_specs=list(in_specs) + [anywhere()] * extra, out_...  293 us
    ppermute x5, waiting for transfers between devices, around(): return lax.ppermute(value, ('dp', 'mp'), ring(1))  42.5 us
    ppermute x10, waiting for transfers between devices, near_of(): return lax.ppermute(piece, 'dp', beside(True))  39.8 us
    unnamed x91, local copies, waits for them, and re-layouts  22.6 us
    ppermute x10, starting transfers between devices, near_of(): return lax.ppermute(piece, 'dp', beside(True))  21.2 us
    ppermute x3, starting transfers between devices, plane_sum(): lax.ppermute(value, 'dp', [(i, i ^ bit) for i in range(DP)])  12.8 us
    ppermute x8, starting transfers between devices, side_of(): return lax.ppermute(piece, 'dp', beside(False))  10.6 us
  transfers between devices with their start and end apart: 44, of which 16 were waited for; matrix products, arithmetic and copies ran while one was open for 7% of the time, Pallas kernels for 51%

profile of v9, /device:TPU:0, one launch (start us, length us, event | category | flops | bytes accessed | tf_op | source)
XLA Modules:
  0.0 523.5 jit_solution(10752786884476506065)
XLA Ops:
  1.8 3.1 collective-permute-start
  8.7 15.9 %collective-permute-done.refs_0_.refs_3_.refs_1_ = f32[3,256,256]{2,1,0:T(8,128)S(1)} collective-permute-done((f32[3,256,256]{2,1,0:T(8,128)S(1)}, f32[3,256,256]{2,1,0:T(8,128)S(1)}, u32[]{:S(2)}, u32[]{:S(2)}) %collective-permute-start) | collective-permute-done | bytes 786464 | tf_op jit(solution)/shard_map/ppermute | solution.py:1046
  29.8 5.6 %norm_first.1.refs_1_.refs_0_.refs_2_.refs_7_ = bf16[1280,1024]{1,0:T(8,128)(2,1)} custom-call(bf16[1280,1024]{1,0:T(8,128)(2,1)} %refs_11_.1, f32[1,1024]{1,0:T(1,128)} %get-tuple-element.179.refs_1_.refs_13_, f32[1,1024]{1,0:T(1,128)} %get-tuple-element.176.refs_2_, f32[5,256,256]{2,1,0:T(8,128)} %gate.16.refs_3_), custom_call_target="tpu_custom_call" | custom-call | flops 2760000000 | bytes 8400000 | tf_op jit(solution)/shard_map/norm_first/pallas_call | solution.py:71
  35.4 7.0 %collective-permute-done.3.refs_1_ = f32[3,256,256]{2,1,0:T(8,128)S(1)} collective-permute-done((f32[3,256,256]{2,1,0:T(8,128)}, f32[3,256,256]{2,1,0:T(8,128)S(1)}, u32[]{:S(2)}, u32[]{:S(2)}) %collective-permute-start.3) | collective-permute-done | bytes 786464 | tf_op jit(solution)/shard_map/ppermute | solution.py:1038
  43.3 2.4 collective-permute-start.4
  45.8 11.3 %collective-permute-done.1.refs_4_.refs_1_ = f32[5,256,256]{2,1,0:T(8,128)S(1)} collective-permute-done((f32[5,256,256]{2,1,0:T(8,128)}, f32[5,256,256]{2,1,0:T(8,128)S(1)}, u32[]{:S(2)}, u32[]{:S(2)}) %collective-permute-start.1) | collective-permute-done | bytes 1310752 | tf_op jit(solution)/shard_map/ppermute | solution.py:1046
  61.6 9.9 %front_own.1 = (bf16[3,1280,256]{2,1,0:T(8,128)(2,1)}, bf16[1280,256]{1,0:T(8,128)(2,1)}, f32[8,1280]{1,0:T(8,128)}) custom-call(s32[5]{0:T(128)} %refs_0_.13, bf16[1280,1024]{1,0:T(8,128)(2,1)} %norm_first.1.refs_1_.refs_0_.refs_2_.refs_7_, bf16[3,1024,256]{2,1,0:T(8,128)(2,1)} %bitcast.93, f32[3,256,256]{2,1,0:T(8,128)} %copy-done.3, f32[5,256,256]{2,1,0:T(8,128)} %copy-done.6), custom_call_target="tpu_custom_call" | custom-call | flops 6899999744 | bytes 21000000 | tf_op jit(solution)/shard_map/front_own/pallas_call | solution.py:71
  72.4 2.6 join.3.refs_2_
  77.6 6.4 %collective-permute-done.7.refs_5_.refs_1_ = f32[4,256,256]{2,1,0:T(8,128)S(1)} collective-permute-done((f32[4,256,256]{2,1,0:T(8,128)}, f32[4,256,256]{2,1,0:T(8,128)S(1)}, u32[]{:S(2)}, u32[]{:S(2)}) %collective-permute-start.7) | collective-permute-done | bytes 1048608 | tf_op jit(solution)/shard_map/ppermute | solution.py:1046
  84.0 4.3 collective-permute-done.5.refs_3_.refs_4_.refs_2_
  88.3 2.7 collective-permute-done.6.refs_4_.refs_5_.refs_3_
  91.0 10.6 %front.2 = (bf16[3,1024,256]{2,1,0:T(8,128)(2,1)}, bf16[3,1280,256]{2,1,0:T(8,128)(2,1)}, bf16[1280,256]{1,0:T(8,128)(2,1)}, f32[8,1280]{1,0:T(8,128)}, f32[2,256,1024]{2,1,0:T(8,128)}) custom-call(s32[5]{0:T(128)} %refs_0_.13, bf16[1280,1024]{1,0:T(8,128)(2,1)} %norm_first.1.refs_1_.refs_0_.refs_2_.refs_7_, ...), custom_call_target="tpu_custom_call", output_to_operand_aliasing={{4}: (6, {})} | custom-call | flops 7360000000 | bytes 22400000 | tf_op jit(solution)/shard_map/front/pallas_call | solution.py:71
  102.1 3.7 collective-permute-start.11
  105.8 10.7 %front.3 = (bf16[3,1024,256]{2,1,0:T(8,128)(2,1)}, bf16[3,1280,256]{2,1,0:T(8,128)(2,1)}, bf16[1280,256]{1,0:T(8,128)(2,1)}, f32[8,1280]{1,0:T(8,128)}) custom-call(s32[5]{0:T(128)} %refs_0_.13, bf16[1280,1024]{1,0:T(8,128)(2,1)} %norm_first.1.refs_1_.refs_0_.refs_2_.refs_7_, f32[3,1024,256]{2,1,0:T(8,128)} %collective-permute-done.12.refs_2_, ...), custom_call_target="tpu_custom_call" | custom-call | flops 7360000000 | bytes 22400000 | tf_op jit(solution)/shard_map/front/pallas_call | solution.py:71
  116.6 27.5 %collective-permute-done.8.refs_7_.refs_4_.refs_2_ = f32[4,256,256]{2,1,0:T(8,128)S(1)} collective-permute-done((f32[4,256,256]{2,1,0:T(8,128)}, f32[4,256,256]{2,1,0:T(8,128)S(1)}, u32[]{:S(2)}, u32[]{:S(2)}) %collective-permute-start.8) | collective-permute-done | bytes 1048608 | tf_op jit(solution)/shard_map/ppermute | solution.py:1034
  145.2 3.0 collective-permute-done.13.refs_6_.refs_28_.refs_5_
  155.6 4.3 collective-permute-start.10
  161.3 2.6 collective-permute-done.14.refs_3_.refs_23_.refs_25_
  163.8 2.3 copy-done.27
  166.1 9.3 %text_front.1 = (bf16[3,1024,256]{2,1,0:T(8,128)(2,1)}, bf16[3,1024,256]{2,1,0:T(8,128)(2,1)}, bf16[2,640,256]{2,1,0:T(8,128)(2,1)}, bf16[2,640,256]{2,1,0:T(8,128)(2,1)}, bf16[2,640,256]{2,1,0:T(8,128)(2,1)}) custom-call(bf16[640,1024]{1,0:T(8,128)(2,1)} %bitcast.88, bf16[3,1024,256]{2,1,0:T(8,128)(2,1)} %pad_maximum_fusion.refs_1_.refs_14_.refs_6_, ...), custom_call_target="tpu_custom_call" | custom-call | flops 3220000000 | bytes 9800000 | tf_op jit(solution)/shard_map/text_front/pallas_call | solution.py:71
  176.9 4.3 join.5.refs_3_.refs_26_
  184.5 3.2 collective-permute-start.18
  188.8 14.7 %front_two.1 = (bf16[3,1024,256]{2,1,0:T(8,128)(2,1)}, bf16[3,1024,256]{2,1,0:T(8,128)(2,1)}, bf16[3,1280,256]{2,1,0:T(8,128)(2,1)}, bf16[1280,256]{1,0:T(8,128)...) custom-call(s32[2]{0:T(128)} %copy-done.19, s32[5]{0:T(128)} %refs_0_.13, ...), custom_call_target="tpu_custom_call" | custom-call | flops 8280000000 | bytes 25200000 | tf_op jit(solution)/shard_map/front_two/pallas_call | solution.py:71
  203.5 5.9 %collective-permute-done.16.refs_29_.refs_1_ = f32[1,256,1024]{2,1,0:T(8,128)} collective-permute-done((f32[1,256,1024]{2,1,0:T(8,128)S(1)}, f32[1,256,1024]{2,1,0:T(8,128)}, u32[]{:S(2)}, u32[]{:S(2)}) %collective-permute-start.16) | collective-permute-done | bytes 1048608 | tf_op jit(solution)/shard_map/ppermute | solution.py:1046
  209.5 32.1 %middle.1 = (bf16[1024,1024]{1,0:T(8,128)(2,1)}, bf16[1024,1024]{1,0:T(8,128)(2,1)}, f32[1280,1024]{1,0:T(8,128)}, f32[1280,1024]{1,0:T(8,128)}, bf16[1280,1024]...) custom-call(s32[2]{0:T(128)} %copy-done.19, ...), custom_call_target="tpu_custom_call" | custom-call | flops 19779999744 | bytes 60200000 | tf_op jit(solution)/shard_map/middle/pallas_call | solution.py:71
  242.9 4.3 collective-permute-start.19
  247.7 26.9 %feed_own.1 = (f32[1280,1024]{1,0:T(8,128)}, f32[1280,1024]{1,0:T(8,128)}, f32[4,2,128,1024]{3,2,1,0:T(8,128)}, f32[4,2,128,1024]{3,2,1,0:T(8,128)}) custom-call(s32[2]{0:T(128)} %copy-done.19, bf16[1280,1024]{1,0:T(8,128)(2,1)} %get-tuple-element.84.refs_0_.refs_1_, bf16[1280,1024]{1,0:T(8,128)(2,1)} %refs_3_.3, ...), custom_call_target="tpu_custom_call" | custom-call | flops 14720000000 | bytes 44800000 | tf_op jit(solution)/shard_map/feed_own/pallas_call | solution.py:71
  274.6 8.0 %collective-permute-done.19.refs_1_ = f32[2,256,1024]{2,1,0:T(8,128)S(1)} collective-permute-done((f32[2,256,1024]{2,1,0:T(8,128)}, f32[2,256,1024]{2,1,0:T(8,128)S(1)}, u32[]{:S(2)}, u32[]{:S(2)}) %collective-permute-start.19) | collective-permute-done | bytes 2097184 | tf_op jit(solution)/shard_map/ppermute | solution.py:1034
  287.0 18.4 %feed.2 = (f32[1280,1024]{1,0:T(8,128)}, f32[1280,1024]{1,0:T(8,128)}) custom-call(s32[2]{0:T(128)} %copy-done.19, bf16[1280,1024]{1,0:T(8,128)(2,1)} %get-tuple-element.84.refs_0_.refs_1_, bf16[1280,1024]{1,0:T(8,128)(2,1)} %refs_3_.3, f32[1280,1024]{1,0:T(8,128)} %get-tuple-element.86.refs_0_.refs_3_, f32[1280,1024]{1,0:T(8,128)} %get-tuple-element.87.refs_4_, ...), custom_call_target="tpu_custom_call" | custom-call | flops 8280000000 | bytes 25200000 | tf_op jit(solution)/shard_map/feed/pallas_call | solution.py:71
  306.2 18.6 %feed.3 = (f32[1280,1024]{1,0:T(8,128)}, f32[1280,1024]{1,0:T(8,128)}) custom-call(s32[2]{0:T(128)} %copy-done.19, bf16[1280,1024]{1,0:T(8,128)(2,1)} %get-tuple-element.84.refs_0_.refs_1_, bf16[1280,1024]{1,0:T(8,128)(2,1)} %refs_3_.3, f32[1280,1024]{1,0:T(8,128)} %get-tuple-element.88.refs_3_.refs_0_, f32[1280,1024]{1,0:T(8,128)} %get-tuple-element.89.refs_4_, ...), custom_call_target="tpu_custom_call" | custom-call | flops 8280000000 | bytes 25200000 | tf_op jit(solution)/shard_map/feed/pallas_call | solution.py:71
  326.0 2.7 collective-permute-done.30.refs_12_
  329.6 18.3 %feed_last.1 = (bf16[1280,1024]{1,0:T(8,128)(2,1)}, f32[1280,1024]{1,0:T(8,128)}, f32[4,2,128,1024]{3,2,1,0:T(8,128)}) custom-call(s32[2]{0:T(128)} %copy-done.19, bf16[1280,1024]{1,0:T(8,128)(2,1)} %get-tuple-element.84.refs_0_.refs_1_, bf16[1280,1024]{1,0:T(8,128)(2,1)} %refs_3_.3, ...), custom_call_target="tpu_custom_call", output_to_operand_aliasing={{2}: (13, {})} | custom-call | flops 8280000000 | bytes 25200000 | tf_op jit(solution)/shard_map/feed_last/pallas_call | solution.py:71
  348.2 39.5 %back.1 = (f32[1280,1024]{1,0:T(8,128)}, bf16[1280,1024]{1,0:T(8,128)(2,1)}, bf16[4,2,640,256]{3,2,1,0:T(8,128)(2,1)}, f32[2,256,1024]{2,1,0:T(8,128)}, bf16[1280,256]{1,0:T(8,128)(2,1)}, /*index=5*/f32[8,1024]{1,0:T(8,128)}) custom-call(s32[5]{0:T(128)} %refs_0_.13, f32[640,1]{1,0:T(8,128)} %bitcast.92, f32[1280,1024]{1,0:T(8,128)} %get-tuple-element.99.refs_2_, ...), custom_call_target="tpu_custom_call" | custom-call | flops 24380000256 | bytes 74200000 | tf_op jit(solution)/shard_map/back/pallas_call | solution.py:71
  387.7 13.3 %text_back.1 = (f32[640,1024]{1,0:T(8,128)}, f32[4,5,128,256]{3,2,1,0:T(8,128)}, f32[4,5,128,256]{3,2,1,0:T(8,128)}) custom-call(s32[2]{0:T(128)} %copy-done.19, bf16[640,1024]{1,0:T(8,128)(2,1)} %bitcast.90, bf16[4,2,640,256]{3,2,1,0:T(8,128)(2,1)} %get-tuple-element.111.refs_2_, bf16[1280,1024]{1,0:T(8,128)(2,1)} %get-tuple-element.112.refs_3_, ...), custom_call_target="tpu_custom_call" | custom-call | flops 6899999744 | bytes 21000000 | tf_op jit(solution)/shard_map/text_back/pallas_call | solution.py:71
  401.3 4.1 slice_add_fusion
  407.4 16.3 %self_own.1 = (f32[1280,1024]{1,0:T(8,128)}, f32[4,3,128,256]{3,2,1,0:T(8,128)}, f32[4,3,128,256]{3,2,1,0:T(8,128)}) custom-call(s32[2]{0:T(128)} %copy-done.19, s32[5]{0:T(128)} %refs_0_.13, bf16[3,1280,256]{2,1,0:T(8,128)(2,1)} %get-tuple-element.109.refs_2_, bf16[1280,256]{1,0:T(8,128)(2,1)} %get-tuple-element.69.refs_10_.refs_8_.refs_3_, ...), custom_call_target="tpu_custom_call" | custom-call | flops 10119999488 | bytes 30800000 | tf_op jit(solution)/shard_map/self_own/pallas_call | solution.py:71
  423.7 2.6 slice_add_fusion.1
  426.3 5.3 %collective-permute-start.34 = (f32[2,5,128,256]{3,2,1,0:T(8,128)}, f32[2,5,128,256]{3,2,1,0:T(8,128)}, u32[]{:S(2)}, u32[]{:S(2)}) collective-permute-start(f32[2,5,128,256]{3,2,1,0:T(8,128)} %slice_add_fusion.1), channel_id=1, source_target_pairs={{0,8},{4,20},{8,0},{12,28},{16,24},{20,4},{24,16},{28,12},{1,9},{5... | collective-permute-start | bytes 3932168 | tf_op jit(solution)/shard_map/ppermute | solution.py:1064
  431.8 3.2 fusion.4
  435.0 14.5 %self_back.1.refs_0_.refs_10_ = f32[1280,1024]{1,0:T(8,128)} custom-call(s32[5]{0:T(128)} %refs_0_.13, bf16[3,1280,256]{2,1,0:T(8,128)(2,1)} %get-tuple-element.107.refs_1_, bf16[1280,256]{1,0:T(8,128)(2,1)} %get-tuple-element.71.refs_11_.refs_2_, bf16[1280,1024]{1,0:T(8,128)(2,1)} %get-tuple-element.106.refs_4_.refs_3_.refs_9_, ...), custom_call_target="tpu_custom_call" | custom-call | flops 11960000512 | bytes 36400000 | tf_op jit(solution)/shard_map/self_back/pallas_call | solution.py:71
  449.5 8.1 %collective-permute-done.34.refs_1_ = f32[2,5,128,256]{3,2,1,0:T(8,128)} collective-permute-done((f32[2,5,128,256]{3,2,1,0:T(8,128)}, f32[2,5,128,256]{3,2,1,0:T(8,128)}, u32[]{:S(2)}, u32[]{:S(2)}) %collective-permute-start.34) | collective-permute-done | bytes 1310752 | tf_op jit(solution)/shard_map/ppermute | solution.py:1064
  457.5 2.5 fusion.7
  460.0 3.0 collective-permute-start.36
  464.1 2.4 slice_add_fusion.6
  466.5 25.1 %self_rest.1 = (f32[1280,1024]{1,0:T(8,128)}, f32[8,1024]{1,0:T(8,128)}) custom-call(s32[5]{0:T(128)} %refs_0_.13, bf16[3,1280,256]{2,1,0:T(8,128)(2,1)} %get-tuple-element.94.refs_1_, bf16[1280,256]{1,0:T(8,128)(2,1)} %get-tuple-element.76.refs_12_.refs_2_, f32[8,1280]{1,0:T(8,128)} %get-tuple-element.95.refs_3_, ...), custom_call_target="tpu_custom_call" | custom-call | flops 18400000000 | bytes 56000000 | tf_op jit(solution)/shard_map/self_rest/pallas_call | solution.py:71
  501.8 10.8 %collective-permute-start.39 = (f32[6,1024]{1,0:T(8,128)S(1)}, f32[6,1024]{1,0:T(8,128)S(1)}, u32[]{:S(2)}, u32[]{:S(2)}) collective-permute-start(f32[6,1024]{1,0:T(8,128)S(1)} %concatenate.74), channel_id=1, source_target_pairs={{0,8},{4,12},{8,0},{12,4},{16,24},{20,28},{24,16},{28,20},{1,9},{5... | collective-permute-start | bytes 73736 | tf_op jit(solution)/shard_map/ppermute | solution.py:1076
  514.6 2.3 fusion.3
  516.9 2.5 collective-permute-done.41
  (202 shorter events, 64.3 us)
Async XLA Ops:
  1.8 22.8 %collective-permute-start = (f32[3,256,256]{2,1,0:T(8,128)S(1)}, f32[3,256,256]{2,1,0:T(8,128)S(1)}, u32[]{:S(2)}, u32[]{:S(2)}) collective-permute-start(f32[3,256,256]{2,1,0:T(8,128)S(1)} %convert_bitcast_fusion), channel_id=1, source_target_pairs={{0,1},{1,2},{2,3},{3,0},{4,7},{5,4},{6,5},{7,6},{8,9},{9,10},{10,1... | collective-permute-start | bytes 2359304 | tf_op jit(solution)/shard_map/ppermute | solution.py:1046
  8.7 19.0 %copy-start.39 = (f32[3,1024]{1,0:T(4,128)S(1)}, f32[3,1024]{1,0:T(4,128)}, u32[]{:S(2)}) copy-start(f32[3,1024]{1,0:T(4,128)} %param.19) | copy-start | bytes 36868
  25.5 31.6 %collective-permute-start.1 = (f32[5,256,256]{2,1,0:T(8,128)}, f32[5,256,256]{2,1,0:T(8,128)S(1)}, u32[]{:S(2)}, u32[]{:S(2)}) collective-permute-start(f32[5,256,256]{2,1,0:T(8,128)} %gate.16.refs_3_), channel_id=1, source_target_pairs={{0,1},{1,2},{2,3},{3,0},{4,7},{5,4},{6,5},{7,6},{8,9},{9,10},{10,1... | collective-permute-start | bytes 3932168 | tf_op jit(solution)/shard_map/ppermute | solution.py:1046
  25.5 16.9 %collective-permute-start.3 = (f32[3,256,256]{2,1,0:T(8,128)}, f32[3,256,256]{2,1,0:T(8,128)S(1)}, u32[]{:S(2)}, u32[]{:S(2)}) collective-permute-start(f32[3,256,256]{2,1,0:T(8,128)} %copy-done.3), channel_id=1, source_target_pairs={{0,16},{4,12},{8,24},{12,4},{16,0},{20,28},{24,8},{28,20},{1,17},{... | collective-permute-start | bytes 2359304 | tf_op jit(solution)/shard_map/ppermute | solution.py:1038
  27.1 148.3 %copy-start.19 = (s32[2]{0:T(128)}, s32[2]{0:T(128)S(1)}, u32[]{:S(2)}) copy-start(s32[2]{0:T(128)S(1)} %pad_add_fusion.refs_0_) | copy-start | bytes 28
  28.3 43.3 %collective-permute-start.2 = (f32[3,256,256]{2,1,0:T(8,128)}, f32[3,256,256]{2,1,0:T(8,128)S(1)}, u32[]{:S(2)}, u32[]{:S(2)}) collective-permute-start(f32[3,256,256]{2,1,0:T(8,128)} %copy-done.3), channel_id=1, source_target_pairs={{0,8},{4,20},{8,0},{12,28},{16,24},{20,4},{24,16},{28,12},{1,9},{5... | collective-permute-start | bytes 2359304 | tf_op jit(solution)/shard_map/ppermute | solution.py:1034
  43.3 28.3 %collective-permute-start.4 = (f32[3,256,256]{2,1,0:T(8,128)}, f32[3,256,256]{2,1,0:T(8,128)S(1)}, u32[]{:S(2)}, u32[]{:S(2)}) collective-permute-start(f32[3,256,256]{2,1,0:T(8,128)} %gate.17.refs_3_), channel_id=1, source_target_pairs={{0,8},{4,20},{8,0},{12,28},{16,24},{20,4},{24,16},{28,12},{1,9},{5... | collective-permute-start | bytes 2359304 | tf_op jit(solution)/shard_map/ppermute | solution.py:1034
  58.4 25.6 %collective-permute-start.7 = (f32[4,256,256]{2,1,0:T(8,128)}, f32[4,256,256]{2,1,0:T(8,128)S(1)}, u32[]{:S(2)}, u32[]{:S(2)}) collective-permute-start(f32[4,256,256]{2,1,0:T(8,128)} %maximum_select_fusion), channel_id=1, source_target_pairs={{0,1},{1,2},{2,3},{3,0},{4,7},{5,4},{6,5},{7,6},{8,9},{9,10},{10,1... | collective-permute-start | bytes 3145736 | tf_op jit(solution)/shard_map/ppermute | solution.py:1046
  58.6 29.7 %collective-permute-start.5 = (f32[5,256,256]{2,1,0:T(8,128)S(1)}, f32[5,256,256]{2,1,0:T(8,128)S(1)}, u32[]{:S(2)}, u32[]{:S(2)}) collective-permute-start(f32[5,256,256]{2,1,0:T(8,128)S(1)} %collective-permute-done.1.refs_4_.refs_1_), channel_id=1, source_target_pairs={{0,8},{4,20},{8,0},{12,28},{16,24},{20,4},{24,16},{28,12},{1,9},{5... | collective-permute-start | bytes 3932168 | tf_op jit(solution)/shard_map/ppermute | solution.py:1034
  60.1 30.9 %collective-permute-start.6 = (f32[5,256,256]{2,1,0:T(8,128)S(1)}, f32[5,256,256]{2,1,0:T(8,128)}, u32[]{:S(2)}, u32[]{:S(2)}) collective-permute-start(f32[5,256,256]{2,1,0:T(8,128)S(1)} %collective-permute-done.1.refs_4_.refs_1_), channel_id=1, source_target_pairs={{0,16},{4,12},{8,24},{12,4},{16,0},{20,28},{24,8},{28,20},{1,17},{... | collective-permute-start | bytes 3932168 | tf_op jit(solution)/shard_map/ppermute | solution.py:1038
  75.0 30.9 %collective-permute-start.12 = (f32[3,1024,256]{2,1,0:T(8,128)}, f32[3,1024,256]{2,1,0:T(8,128)}, u32[]{:S(2)}, u32[]{:S(2)}) collective-permute-start(f32[3,1024,256]{2,1,0:T(8,128)} %join.3.refs_2_), channel_id=1, source_target_pairs={{0,4},{4,0},{8,12},{12,8},{16,20},{20,16},{24,28},{28,24},{1,5},{5... | collective-permute-start | bytes 9437192 | tf_op jit(solution)/shard_map/ppermute | solution.py:1016
  101.7 46.5 %collective-permute-start.13 = (f32[2,256,1024]{2,1,0:T(8,128)}, f32[2,256,1024]{2,1,0:T(8,128)}, u32[]{:S(2)}, u32[]{:S(2)}) collective-permute-start(f32[2,256,1024]{2,1,0:T(8,128)} %get-tuple-element.74), channel_id=1, source_target_pairs={{0,1},{1,2},{2,3},{3,0},{4,7},{5,4},{6,5},{7,6},{8,9},{9,10},{10,1... | collective-permute-start | bytes 6291464 | tf_op jit(solution)/shard_map/ppermute | solution.py:1046
  102.1 42.0 %collective-permute-start.11 = (f32[5,256,256]{2,1,0:T(8,128)}, f32[5,256,256]{2,1,0:T(8,128)S(1)}, u32[]{:S(2)}, u32[]{:S(2)}) collective-permute-start(f32[5,256,256]{2,1,0:T(8,128)} %collective-permute-done.6.refs_4_.refs_5_.refs_3_), channel_id=1, source_target_pairs={{0,8},{4,20},{8,0},{12,28},{16,24},{20,4},{24,16},{28,12},{1,9},{5... | collective-permute-start | bytes 3932168 | tf_op jit(solution)/shard_map/ppermute | solution.py:1034
  105.8 42.4 %copy-start.7 = (f32[5,256,256]{2,1,0:T(8,128)S(1)}, f32[5,256,256]{2,1,0:T(8,128)}, u32[]{:S(2)}) copy-start(f32[5,256,256]{2,1,0:T(8,128)} %copy-done.6) | copy-start | bytes 3932164
  105.8 38.3 %collective-permute-start.8 = (f32[4,256,256]{2,1,0:T(8,128)}, f32[4,256,256]{2,1,0:T(8,128)S(1)}, u32[]{:S(2)}, u32[]{:S(2)}) collective-permute-start(f32[4,256,256]{2,1,0:T(8,128)} %gate.18.refs_3_.refs_1_), channel_id=1, source_target_pairs={{0,8},{4,20},{8,0},{12,28},{16,24},{20,4},{24,16},{28,12},{1,9},{5... | collective-permute-start | bytes 3145736 | tf_op jit(solution)/shard_map/ppermute | solution.py:1034
  105.8 38.2 %collective-permute-start.9 = (f32[4,256,256]{2,1,0:T(8,128)}, f32[4,256,256]{2,1,0:T(8,128)}, u32[]{:S(2)}, u32[]{:S(2)}) collective-permute-start(f32[4,256,256]{2,1,0:T(8,128)} %gate.18.refs_3_.refs_1_), channel_id=1, source_target_pairs={{0,16},{4,12},{8,24},{12,4},{16,0},{20,28},{24,8},{28,20},{1,17},{... | collective-permute-start | bytes 3145736 | tf_op jit(solution)/shard_map/ppermute | solution.py:1038
  153.8 10.0 %collective-permute-start.14 = (f32[5,1024,256]{2,1,0:T(8,128)S(1)}, f32[5,1024,256]{2,1,0:T(8,128)S(1)}, u32[]{:S(2)}, u32[]{:S(2)}) collective-permute-start(f32[5,1024,256]{2,1,0:T(8,128)S(1)} %join.4.refs_2_.refs_22_.refs_24_), channel_id=1, source_target_pairs={{0,4},{4,0},{8,12},{12,8},{16,20},{20,16},{24,28},{28,24},{1,5},{5... | collective-permute-start | bytes 15728648 | tf_op jit(solution)/shard_map/ppermute | solution.py:1016
  155.6 19.9 %collective-permute-start.10 = (f32[4,256,256]{2,1,0:T(8,128)}, f32[4,256,256]{2,1,0:T(8,128)}, u32[]{:S(2)}, u32[]{:S(2)}) collective-permute-start(f32[4,256,256]{2,1,0:T(8,128)} %collective-permute-done.9.refs_8_.refs_5_.refs_3_), channel_id=1, source_target_pairs={{0,8},{4,20},{8,0},{12,28},{16,24},{20,4},{24,16},{28,12},{1,9},{5... | collective-permute-start | bytes 3145736 | tf_op jit(solution)/shard_map/ppermute | solution.py:1034
  181.2 7.6 %collective-permute-start.15 = (f32[4,1024,256]{2,1,0:T(8,128)}, f32[4,1024,256]{2,1,0:T(8,128)}, u32[]{:S(2)}, u32[]{:S(2)}) collective-permute-start(f32[4,1024,256]{2,1,0:T(8,128)} %join.5.refs_3_.refs_26_), channel_id=1, source_target_pairs={{0,4},{4,0},{8,12},{12,8},{16,20},{20,16},{24,28},{28,24},{1,5},{5... | collective-permute-start | bytes 12582920 | tf_op jit(solution)/shard_map/ppermute | solution.py:1016
  182.9 26.5 %collective-permute-start.16 = (f32[1,256,1024]{2,1,0:T(8,128)S(1)}, f32[1,256,1024]{2,1,0:T(8,128)}, u32[]{:S(2)}, u32[]{:S(2)}) collective-permute-start(f32[1,256,1024]{2,1,0:T(8,128)S(1)} %constant_dynamic-slice_fusion), channel_id=1, source_target_pairs={{0,1},{1,2},{2,3},{3,0},{4,7},{5,4},{6,5},{7,6},{8,9},{9,10},{10,1... | collective-permute-start | bytes 3145736 | tf_op jit(solution)/shard_map/ppermute | solution.py:1046
  184.5 57.1 %collective-permute-start.18 = (f32[2,256,1024]{2,1,0:T(8,128)}, f32[2,256,1024]{2,1,0:T(8,128)S(1)}, u32[]{:S(2)}, u32[]{:S(2)}) collective-permute-start(f32[2,256,1024]{2,1,0:T(8,128)} %collective-permute-done.13.refs_6_.refs_28_.refs_5_), channel_id=1, source_target_pairs={{0,16},{4,12},{8,24},{12,4},{16,0},{20,28},{24,8},{28,20},{1,17},{... | collective-permute-start | bytes 6291464 | tf_op jit(solution)/shard_map/ppermute | solution.py:1038
  187.7 59.5 %collective-permute-start.17 = (f32[2,256,1024]{2,1,0:T(8,128)}, f32[2,256,1024]{2,1,0:T(8,128)}, u32[]{:S(2)}, u32[]{:S(2)}) collective-permute-start(f32[2,256,1024]{2,1,0:T(8,128)} %collective-permute-done.13.refs_6_.refs_28_.refs_5_), channel_id=1, source_target_pairs={{0,8},{4,20},{8,0},{12,28},{16,24},{20,4},{24,16},{28,12},{1,9},{5... | collective-permute-start | bytes 6291464 | tf_op jit(solution)/shard_map/ppermute | solution.py:1034
  242.9 39.7 %collective-permute-start.19 = (f32[2,256,1024]{2,1,0:T(8,128)}, f32[2,256,1024]{2,1,0:T(8,128)S(1)}, u32[]{:S(2)}, u32[]{:S(2)}) collective-permute-start(f32[2,256,1024]{2,1,0:T(8,128)} %gate.19.refs_7_), channel_id=1, source_target_pairs={{0,8},{4,20},{8,0},{12,28},{16,24},{20,4},{24,16},{28,12},{1,9},{5... | collective-permute-start | bytes 6291464 | tf_op jit(solution)/shard_map/ppermute | solution.py:1034
  247.2 39.9 %collective-permute-start.20 = (f32[2,256,1024]{2,1,0:T(8,128)}, f32[2,256,1024]{2,1,0:T(8,128)}, u32[]{:S(2)}, u32[]{:S(2)}) collective-permute-start(f32[2,256,1024]{2,1,0:T(8,128)} %collective-permute-done.13.refs_6_.refs_28_.refs_5_), channel_id=1, source_target_pairs={{0,4},{4,0},{8,12},{12,8},{16,20},{20,16},{24,28},{28,24},{1,5},{5... | collective-permute-start | bytes 6291464 | tf_op jit(solution)/shard_map/ppermute | solution.py:1016
  247.2 39.8 %collective-permute-start.21 = (f32[2,256,1024]{2,1,0:T(8,128)}, f32[2,256,1024]{2,1,0:T(8,128)}, u32[]{:S(2)}, u32[]{:S(2)}) collective-permute-start(f32[2,256,1024]{2,1,0:T(8,128)} %collective-permute-done.17.refs_6_), channel_id=1, source_target_pairs={{0,4},{4,0},{8,12},{12,8},{16,20},{20,16},{24,28},{28,24},{1,5},{5... | collective-permute-start | bytes 6291464 | tf_op jit(solution)/shard_map/ppermute | solution.py:1016
  247.7 39.3 %collective-permute-start.22 = (f32[2,256,1024]{2,1,0:T(8,128)}, f32[2,256,1024]{2,1,0:T(8,128)}, u32[]{:S(2)}, u32[]{:S(2)}) collective-permute-start(f32[2,256,1024]{2,1,0:T(8,128)} %gate.19.refs_7_), channel_id=1, source_target_pairs={{0,4},{4,0},{8,12},{12,8},{16,20},{20,16},{24,28},{28,24},{1,5},{5... | collective-permute-start | bytes 6291464 | tf_op jit(solution)/shard_map/ppermute | solution.py:1016
  247.7 36.3 %collective-permute-start.25 = (f32[1,256,1024]{2,1,0:T(8,128)}, f32[1,256,1024]{2,1,0:T(8,128)S(1)}, u32[]{:S(2)}, u32[]{:S(2)}) collective-permute-start(f32[1,256,1024]{2,1,0:T(8,128)} %gate.20.refs_8_.refs_5_), channel_id=1, source_target_pairs={{0,16},{4,12},{8,24},{12,4},{16,0},{20,28},{24,8},{28,20},{1,17},{... | collective-permute-start | bytes 3145736 | tf_op jit(solution)/shard_map/ppermute | solution.py:1038
  283.9 22.2 %collective-permute-start.23 = (f32[2,256,1024]{2,1,0:T(8,128)}, f32[2,256,1024]{2,1,0:T(8,128)}, u32[]{:S(2)}, u32[]{:S(2)}) collective-permute-start(f32[2,256,1024]{2,1,0:T(8,128)} %gate.21.refs_8_), channel_id=1, source_target_pairs={{0,4},{4,0},{8,12},{12,8},{16,20},{20,16},{24,28},{28,24},{1,5},{5... | collective-permute-start | bytes 6291464 | tf_op jit(solution)/shard_map/ppermute | solution.py:1016
  283.9 21.6 %copy-start.36 = (f32[1,256,1024]{2,1,0:T(8,128)}, f32[1,256,1024]{2,1,0:T(8,128)S(1)}, u32[]{:S(2)}) copy-start(f32[1,256,1024]{2,1,0:T(8,128)S(1)} %collective-permute-done.25.refs_7_) | copy-start | bytes 3145732
  283.9 22.1 %collective-permute-start.24 = (f32[1,256,1024]{2,1,0:T(8,128)}, f32[1,256,1024]{2,1,0:T(8,128)S(1)}, u32[]{:S(2)}, u32[]{:S(2)}) collective-permute-start(f32[1,256,1024]{2,1,0:T(8,128)} %gate.20.refs_8_.refs_5_), channel_id=1, source_target_pairs={{0,8},{4,20},{8,0},{12,28},{16,24},{20,4},{24,16},{28,12},{1,9},{5... | collective-permute-start | bytes 3145736 | tf_op jit(solution)/shard_map/ppermute | solution.py:1034
  305.4 19.4 %collective-permute-start.26 = (f32[1,256,1024]{2,1,0:T(8,128)}, f32[1,256,1024]{2,1,0:T(8,128)S(1)}, u32[]{:S(2)}, u32[]{:S(2)}) collective-permute-start(f32[1,256,1024]{2,1,0:T(8,128)} %gate.22), channel_id=1, source_target_pairs={{0,8},{4,20},{8,0},{12,28},{16,24},{20,4},{24,16},{28,12},{1,9},{5... | collective-permute-start | bytes 3145736 | tf_op jit(solution)/shard_map/ppermute | solution.py:1034
  305.6 20.4 %collective-permute-start.27 = (f32[1,256,1024]{2,1,0:T(8,128)}, f32[1,256,1024]{2,1,0:T(8,128)}, u32[]{:S(2)}, u32[]{:S(2)}) collective-permute-start(f32[1,256,1024]{2,1,0:T(8,128)} %gate.20.refs_8_.refs_5_), channel_id=1, source_target_pairs={{0,4},{4,0},{8,12},{12,8},{16,20},{20,16},{24,28},{28,24},{1,5},{5... | collective-permute-start | bytes 3145736 | tf_op jit(solution)/shard_map/ppermute | solution.py:1016
  305.6 20.4 %collective-permute-start.29 = (f32[1,256,1024]{2,1,0:T(8,128)S(1)}, f32[1,256,1024]{2,1,0:T(8,128)}, u32[]{:S(2)}, u32[]{:S(2)}) collective-permute-start(f32[1,256,1024]{2,1,0:T(8,128)S(1)} %collective-permute-done.25.refs_7_), channel_id=1, source_target_pairs={{0,4},{4,0},{8,12},{12,8},{16,20},{20,16},{24,28},{28,24},{1,5},{5... | collective-permute-start | bytes 3145736 | tf_op jit(solution)/shard_map/ppermute | solution.py:1016
  306.1 19.9 %collective-permute-start.28 = (f32[1,256,1024]{2,1,0:T(8,128)S(1)}, f32[1,256,1024]{2,1,0:T(8,128)}, u32[]{:S(2)}, u32[]{:S(2)}) collective-permute-start(f32[1,256,1024]{2,1,0:T(8,128)S(1)} %collective-permute-done.24.refs_6_), channel_id=1, source_target_pairs={{0,4},{4,0},{8,12},{12,8},{16,20},{20,16},{24,28},{28,24},{1,5},{5... | collective-permute-start | bytes 3145736 | tf_op jit(solution)/shard_map/ppermute | solution.py:1016
  325.8 2.9 collective-permute-start.30
  348.0 53.3 %collective-permute-start.32 = (f32[4,2,128,1024]{3,2,1,0:T(8,128)}, f32[4,2,128,1024]{3,2,1,0:T(8,128)}, u32[]{:S(2)}, u32[]{:S(2)}) collective-permute-start(f32[4,2,128,1024]{3,2,1,0:T(8,128)} %get-tuple-element.118), channel_id=1, source_target_pairs={{0,4},{4,0},{8,12},{12,8},{16,20},{20,16},{24,28},{28,24},{1,5},{5... | collective-permute-start | bytes 12582920 | tf_op jit(solution)/shard_map/ppermute | solution.py:1016
  401.0 22.7 %collective-permute-start.31 = (f32[4,5,128,256]{3,2,1,0:T(8,128)}, f32[4,5,128,256]{3,2,1,0:T(8,128)}, u32[]{:S(2)}, u32[]{:S(2)}) collective-permute-start(f32[4,5,128,256]{3,2,1,0:T(8,128)} %get-tuple-element.115), channel_id=1, source_target_pairs={{0,4},{4,0},{8,12},{12,8},{16,20},{20,16},{24,28},{28,24},{1,5},{5... | collective-permute-start | bytes 7864328 | tf_op jit(solution)/shard_map/ppermute | solution.py:1016
  405.4 26.4 %collective-permute-start.33 = (f32[2,2,128,1024]{3,2,1,0:T(8,128)}, f32[2,2,128,1024]{3,2,1,0:T(8,128)}, u32[]{:S(2)}, u32[]{:S(2)}) collective-permute-start(f32[2,2,128,1024]{3,2,1,0:T(8,128)} %slice_add_fusion), channel_id=1, source_target_pairs={{0,8},{4,20},{8,0},{12,28},{16,24},{20,4},{24,16},{28,12},{1,9},{5... | collective-permute-start | bytes 6291464 | tf_op jit(solution)/shard_map/ppermute | solution.py:1064
  423.7 39.2 %collective-permute-start.35 = (f32[4,3,128,256]{3,2,1,0:T(8,128)}, f32[4,3,128,256]{3,2,1,0:T(8,128)S(1)}, u32[]{:S(2)}, u32[]{:S(2)}) collective-permute-start(f32[4,3,128,256]{3,2,1,0:T(8,128)} %get-tuple-element.121), channel_id=1, source_target_pairs={{0,4},{4,0},{8,12},{12,8},{16,20},{20,16},{24,28},{28,24},{1,5},{5... | collective-permute-start | bytes 4718600 | tf_op jit(solution)/shard_map/ppermute | solution.py:1016
  426.3 31.2 %collective-permute-start.34 = (f32[2,5,128,256]{3,2,1,0:T(8,128)}, f32[2,5,128,256]{3,2,1,0:T(8,128)}, u32[]{:S(2)}, u32[]{:S(2)}) collective-permute-start(f32[2,5,128,256]{3,2,1,0:T(8,128)} %slice_add_fusion.1), channel_id=1, source_target_pairs={{0,8},{4,20},{8,0},{12,28},{16,24},{20,4},{24,16},{28,12},{1,9},{5... | collective-permute-start | bytes 3932168 | tf_op jit(solution)/shard_map/ppermute | solution.py:1064
  435.0 64.9 %collective-permute-start.37 = (f32[2,128,1024]{2,1,0:T(8,128)}, f32[2,128,1024]{2,1,0:T(8,128)S(1)}, u32[]{:S(2)}, u32[]{:S(2)}) collective-permute-start(f32[2,128,1024]{2,1,0:T(8,128)} %fusion.4), channel_id=1, source_target_pairs={{0,16},{4,12},{8,24},{12,4},{16,0},{20,28},{24,8},{28,20},{1,17},{... | collective-permute-start | bytes 3145736 | tf_op jit(solution)/shard_map/ppermute | solution.py:1038
  460.0 31.6 %collective-permute-start.36 = (f32[5,128,256]{2,1,0:T(8,128)}, f32[5,128,256]{2,1,0:T(8,128)S(1)}, u32[]{:S(2)}, u32[]{:S(2)}) collective-permute-start(f32[5,128,256]{2,1,0:T(8,128)} %fusion.7), channel_id=1, source_target_pairs={{0,16},{4,12},{8,24},{12,4},{16,0},{20,28},{24,8},{28,20},{1,17},{... | collective-permute-start | bytes 1966088 | tf_op jit(solution)/shard_map/ppermute | solution.py:1038
  466.5 30.8 %collective-permute-start.38 = (f32[2,3,128,256]{3,2,1,0:T(8,128)}, f32[2,3,128,256]{3,2,1,0:T(8,128)}, u32[]{:S(2)}, u32[]{:S(2)}) collective-permute-start(f32[2,3,128,256]{3,2,1,0:T(8,128)} %slice_add_fusion.6), channel_id=1, source_target_pairs={{0,8},{4,20},{8,0},{12,28},{16,24},{20,4},{24,16},{28,12},{1,9},{5... | collective-permute-start | bytes 2359304 | tf_op jit(solution)/shard_map/ppermute | solution.py:1064
  498.4 22.9 %collective-permute-start.43 = (f32[3,128,256]{2,1,0:T(8,128)S(1)}, f32[3,128,256]{2,1,0:T(8,128)S(1)}, u32[]{:S(2)}, u32[]{:S(2)}) collective-permute-start(f32[3,128,256]{2,1,0:T(8,128)S(1)} %fusion.9), channel_id=1, source_target_pairs={{0,16},{4,12},{8,24},{12,4},{16,0},{20,28},{24,8},{28,20},{1,17},{... | collective-permute-start | bytes 1179656 | tf_op jit(solution)/shard_map/ppermute | solution.py:1038
  501.8 15.1 %collective-permute-start.39 = (f32[6,1024]{1,0:T(8,128)S(1)}, f32[6,1024]{1,0:T(8,128)S(1)}, u32[]{:S(2)}, u32[]{:S(2)}) collective-permute-start(f32[6,1024]{1,0:T(8,128)S(1)} %concatenate.74), channel_id=1, source_target_pairs={{0,8},{4,12},{8,0},{12,4},{16,24},{20,28},{24,16},{28,20},{1,9},{5... | collective-permute-start | bytes 73736 | tf_op jit(solution)/shard_map/ppermute | solution.py:1076
  512.6 4.3 collective-permute-start.40
  514.6 4.8 collective-permute-start.41
  519.5 1.3 collective-permute-start.42
  (39 other events, 227.6 us)
